TPU v7x, 32 devices: a whole 2x2x4 slice. The times are simulated.
32 devices in a mesh: mode: 8 (over z, x), space: 4 (over y, core).
Axes of the slice: x: 2, y: 2, z: 4, core: 2. Of those that a mesh axis runs over, the one named last changes fastest.
Arguments:
- right_side: float32 [288, 3, 12, 8, 128], P('mode', None, 'space'), as said below
- mean_stiffness: float32 [12, 8, 128], P('space'), may hold values from 1 to 4
- ply_stiffness: float32 [10], replicated, may hold values from 0.1 to 0.4
- fibre_weights: float32 [3, 3], replicated, may hold values from 0.5 to 2
- ply_map: int32 [12, 8, 128], P('space'), may hold values from 0 to 9
- coupling_table: int32 [660, 4], replicated, may hold values from 0 to 285, as said below
Outputs:
- solution_field: float32 [288, 3, 12, 8, 128], P('mode', None, 'space')
- residual: float32 [288, 3, 12, 8, 128], P('mode', None, 'space')
Inputs may be any that keep to these rules, and one draw needn't show every extreme that they name: `coupling_table`: the modes below 286 number the multi-indices of total degree at most 3 in 10 variables in some order; for every multi-index alpha of degree at most 2 and every variable k there is one row (mode of alpha, mode of alpha + e_k, k, alpha_k + 1), in some order of rows, and no other rows. `right_side`: mode slots 286 and above are zero.
All inputs are finite; a program needn't handle non-finite values.
Results may differ from a plain program's by a relative error of at most 0.015.
Values sent between devices are 32-bit elements; how exact they have to be, the bound alone decides.
No kernel may reach another device: no remote copies, remote signals or barrier semaphores. Data moves between devices by JAX's collectives and lax.ppermute only.
A program may use at most 192 MiB of HBM per device.

v0:
```python
import functools

import jax
import jax.numpy as jnp
from jax import lax
from jax.experimental import pallas as pl
from jax.experimental.pallas import tpu as pltpu
from jax.sharding import PartitionSpec as P

VARS = 10
ITERS = 2


def extended(array, sides, width):
    for axis, dim in sides:
        devices, length = (lax.axis_size(axis), array.shape[dim])
        up = [(i, (i + 1) % devices) for i in range(devices - 1)]
        down = [(j, i) for i, j in up]
        last = lax.slice_in_dim(array, length - width, length, axis=dim)
        leading = lax.slice_in_dim(array, 0, width, axis=dim)
        before = lax.ppermute(last, axis, up)
        after = lax.ppermute(leading, axis, down)
        array = jnp.concatenate([before, array, after], axis=dim)
    return array


def window(array_in, dim_index, offset):
    slicers = [slice(None)] * (array_in.ndim - 3)
    for which in range(3):
        shift_by = offset if which == dim_index else 0
        length_here = array_in.shape[array_in.ndim - 3 + which] - 2
        slicers.append(slice(1 + shift_by, 1 + shift_by + length_here))
    return array_in[tuple(slicers)]


def diffuse(vector, stiffness, fibre_weights):
    vector_pads = [(0, 0)] * (vector.ndim - 2) + [(1, 1), (1, 1)]
    stiff_pads = [(0, 0)] * (stiffness.ndim - 2) + [(1, 1), (1, 1)]
    padded_v = jnp.pad(vector, vector_pads)
    padded_c = jnp.pad(stiffness, stiff_pads)
    centre = window(padded_v, 0, 0)
    middle = window(padded_c, 0, 0)
    result = None
    for dim_index in range(3):
        upper = (
            0.5
            * (middle + window(padded_c, dim_index, 1))
            * (centre - window(padded_v, dim_index, 1))
        )
        lower = (
            0.5
            * (middle + window(padded_c, dim_index, -1))
            * (centre - window(padded_v, dim_index, -1))
        )
        column = fibre_weights[:, dim_index].reshape(3, 1, 1, 1)
        term = column * (upper + lower)
        result = term if result is None else result + term
    return result


def squares(vector):
    return lax.psum(jnp.sum(vector * vector), ("mode", "space"))


def row_table(both_rows, both_cols, both_vars, both_weights, base, mode_dev, slots):
    local_rows = both_rows - base
    valid_rows = (local_rows >= 0) & (local_rows < mode_dev)
    local_rows = jnp.where(valid_rows, local_rows, mode_dev)
    row_coupling = jnp.zeros((VARS, mode_dev, slots), jnp.float32)
    row_coupling = row_coupling.at[both_vars, local_rows, both_cols].add(both_weights, mode="drop")
    return row_coupling.reshape(VARS * mode_dev, slots)


def plain(right_side, mean_stiffness, ply_stiffness, fibre_weights, ply_map, coupling_table):
    mode_dev = right_side.shape[0]
    slots = mode_dev * lax.axis_size("mode")
    base = lax.axis_index("mode") * mode_dev
    first_mode = coupling_table[:, 0]
    second_mode = coupling_table[:, 1]
    variable = coupling_table[:, 2]
    entry_weight = jnp.sqrt(coupling_table[:, 3].astype(jnp.float32))
    both_rows = jnp.concatenate([first_mode, second_mode])
    both_cols = jnp.concatenate([second_mode, first_mode])
    both_vars = jnp.concatenate([variable, variable])
    both_weights = jnp.concatenate([entry_weight, entry_weight])
    plies = jnp.arange(VARS, dtype=jnp.int32).reshape(VARS, 1, 1, 1)
    ply_fields = (ply_map[None] == plies).astype(jnp.float32) * ply_stiffness.reshape(VARS, 1, 1, 1)
    stiff_stack = jnp.concatenate([mean_stiffness[None], ply_fields], axis=0)
    stiff_rims = extended(stiff_stack, (("space", 1),), 1)
    stiff_rims = stiff_rims[:, None]
    row_coupling = row_table(both_rows, both_cols, both_vars, both_weights, base, mode_dev, slots)
    solution_field = jnp.zeros_like(right_side)
    residual = right_side
    direction = right_side
    norm_now = squares(residual)
    for iteration in range(ITERS):
        shard_piece = lax.all_gather(direction, "mode", axis=0, tiled=True)
        mixed = jnp.dot(
            row_coupling,
            shard_piece.reshape(shard_piece.shape[0], -1),
            precision=lax.Precision.HIGHEST,
            preferred_element_type=jnp.float32,
        )
        stacked = jnp.concatenate(
            [direction[None], mixed.reshape((VARS,) + direction.shape)], axis=0
        )
        padded = extended(stacked, (("space", 3),), 1)
        terms = diffuse(padded, stiff_rims[:, None], fibre_weights)
        image = direction + jnp.sum(terms, axis=0)
        step_size = norm_now / lax.psum(jnp.sum(direction * image), ("mode", "space"))
        solution_field = solution_field + step_size * direction
        residual = residual - step_size * image
        norm_next = squares(residual)
        direction = residual + norm_next / norm_now * direction
        norm_now = norm_next
    return (solution_field, residual)


COMPS = 3
SLAB = 3
PARTS = 8
WIDE = 16
ROWS = 4
EVEN = 1 + VARS * (VARS + 1) // 2
SPAN = VARS * EVEN
FULL = 624
INNER = 6
TILES = 8
LANES = 128
VMEM = 56 * 1024 * 1024


def lane_id():
    return lax.broadcasted_iota(jnp.int32, (8, LANES), 1)


def swap_out(tile):
    block = lane_id() // WIDE
    tile = pltpu.roll(tile, 0, 1, stride=WIDE, stride_axis=0)
    for bit in (1, 2, 4):
        tile = jnp.where((block & bit) != 0, pltpu.roll(tile, 8 - bit, 0), tile)
    return tile


def swap_back(tile):
    block = lane_id() // WIDE
    row = lax.broadcasted_iota(jnp.int32, (8, LANES), 0)
    for bit in (1, 2, 4):
        tile = jnp.where((block & bit) != 0, pltpu.roll(tile, bit, 0), tile)
    for bit in (1, 2, 4):
        tile = jnp.where((row & bit) != 0, pltpu.roll(tile, LANES - WIDE * bit, 1), tile)
    return tile


def halo_row(planes):
    lane = lane_id()
    slot = lane % WIDE
    halo = jnp.zeros((8, LANES), jnp.float32)
    for x, plane in planes.items():
        places = [(-1, x + 1), (WIDE, x + 6)]
        if 0 <= x < SLAB:
            places += [(-2, x + 10), (WIDE + 1, x + 13)]
        for offset, place in places:
            inside = (lane >= WIDE) if offset < 0 else (lane < LANES - WIDE)
            moved = pltpu.roll(plane, (place - offset) % LANES, 1)
            halo = jnp.where((slot == place) & inside, moved, halo)
    return halo


UNROLL = 3


def pack_kernel(field, mean, ply, *outs):
    modes = field.shape[0]
    both = outs[-1]
    for x in range(SLAB):
        both[0, x] = mean[x]
        both[1, x] = (ply[x] + 1).astype(jnp.float32)

    def body(step, carry):
        for inner in range(UNROLL):
            mode = step * UNROLL + inner
            for comp in range(COMPS):
                planes = [field[mode, comp, x] for x in range(SLAB)]
                halo = halo_row(dict(enumerate(planes)))
                for p, tile in enumerate(planes + [halo]):
                    place = pl.ds(mode * ROWS + p, PARTS, stride=ROWS * modes)
                    outs[comp][place, :] = swap_out(tile)
        return carry

    lax.fori_loop(0, modes // UNROLL, body, 0)


def estimate(micros):
    return pl.CostEstimate(flops=int(micros * 1e9), bytes_accessed=int(micros * 3e6), transcendentals=0)


def pack(field, mean, ply):
    modes = field.shape[0]
    shape = jax.ShapeDtypeStruct((PARTS * modes * ROWS, LANES), jnp.float32)
    return pl.pallas_call(
        pack_kernel,
        out_shape=[shape] * COMPS + [jax.ShapeDtypeStruct((2,) + mean.shape, jnp.float32)],
        compiler_params=pltpu.CompilerParams(vmem_limit_bytes=VMEM),
        cost_estimate=estimate(5),
        name="pack",
    )(field, mean, ply)


def stiffness_kernel(place, before, both, after, ply_stiffness, fields, wide):
    rows = []
    for kind in range(2):
        planes = {-2: before[kind, 1], -1: before[kind, 2], 3: after[kind, 0], 4: after[kind, 1]}
        planes.update({x: both[kind, x] for x in range(SLAB)})
        halo = halo_row({x: planes[x] for x in range(-1, 4)})
        ordered = [planes[0], planes[1], planes[2], planes[-1], planes[3], halo, planes[-2], planes[4]]
        for t, tile in enumerate(ordered):
            wide[...] = swap_out(tile)
            rows.append(wide[pl.ds(place[0], 1), :])
    for t in range(TILES):
        mean, ply = rows[t], rows[TILES + t]
        cols = slice(LANES * t, LANES * (t + 1))
        for k in range(VARS):
            fields[k : k + 1, cols] = jnp.where(ply == k + 1.0, ply_stiffness[k], 0.0)
        fields[VARS : VARS + 1, cols] = mean
        fields[VARS + 1 : VARS + 2, cols] = jnp.where(ply > 0.0, 1.0, 0.0)
        fields[VARS + 2 : 16, cols] = jnp.zeros((4, LANES), jnp.float32)


def stiffness_fields(place, before, both, after, ply_stiffness):
    vmem = pl.BlockSpec(memory_space=pltpu.VMEM)
    smem = pl.BlockSpec(memory_space=pltpu.SMEM)
    return pl.pallas_call(
        stiffness_kernel,
        out_shape=jax.ShapeDtypeStruct((16, TILES * LANES), jnp.float32),
        in_specs=[smem, vmem, vmem, vmem, smem],
        out_specs=vmem,
        scratch_shapes=[pltpu.VMEM((8, LANES), jnp.float32)],
        cost_estimate=estimate(2),
        name="stiffness_fields",
    )(place, before, both, after, ply_stiffness)


AT = {0: 0, 1: 1, 2: 2, -1: 3, 3: 4, -2: 6, 4: 7}
PLACE = {index: x for x, index in AT.items()}
HALO = 5


def neighbour(tiles, index, side, place, full=False):
    t = tiles[index]
    lane = lax.broadcasted_iota(jnp.int32, t.shape, 1)
    slot = lane % WIDE
    roll = lambda v, s: pltpu.roll(v, s % LANES, 1)
    if side in (2, 3):
        y = (place + lane // WIDE) & 7
        if side == 2:
            return jnp.where(y > 0, roll(t, WIDE), 0.0)
        return jnp.where(y < 7, roll(t, -WIDE), 0.0)
    if index == HALO:
        if side < 2:
            return roll(t, 1 if side == 0 else -1)
        result = roll(t, -9) if side == 4 else roll(t, -7)
        for x in range(-1, 4) if full else range(SLAB):
            goal, by = (x + 6, x - 9) if side == 4 else (x + 1, x + 1)
            result = jnp.where(slot == goal, roll(tiles[AT[x]], by), result)
        if full:
            result = jnp.where(slot >= 13, roll(t, 7), result) if side == 4 else jnp.where(
                (slot >= 10) & (slot < 13), roll(t, 9), result
            )
        return result
    x = PLACE[index]
    if side < 2:
        return tiles[AT[x - 1 if side == 0 else x + 1]]
    if side == 4:
        return jnp.where(slot == 0, roll(tiles[HALO], -(x + 1)), roll(t, 1))
    return jnp.where(slot == WIDE - 1, roll(tiles[HALO], 9 - x), roll(t, -1))


def sides_of(index, outer):
    if index < outer:
        return range(6)
    return {3: (1,), 4: (0,), HALO: (4, 5), 6: (1,), 7: (0,)}[index]


def split(array):
    high = array.astype(jnp.bfloat16)
    low = (array - high.astype(jnp.float32)).astype(jnp.bfloat16)
    return jnp.concatenate([high, low], axis=0)


STEP = 32
FACE = 16
EVEN_BLOCKS = ((0, 32), (32, EVEN))


def tile_cols(t):
    return slice(LANES * t, LANES * (t + 1))


def face_stiffness(fields, faces, weights, place):
    tiles = [fields[:, tile_cols(t)] for t in range(TILES)]
    for t in range(TILES):
        for side in sides_of(t, INNER):
            value = (0.5 * weights[side // 2]) * (tiles[t] + neighbour(tiles, t, side, place, True))
            faces[side * FACE : (side + 1) * FACE, tile_cols(t)] = value


def apply_operator(src, dst, mixed, flux, scaled, acc, faces, inside, to_even, to_all, place, inner, outer):
    slots = src.shape[0]
    for start in range(0, inner * LANES, 512):
        cols = slice(start, min(start + 512, inner * LANES))
        mixed[:, cols] = jnp.dot(to_even[...], split(src[:, cols]), preferred_element_type=jnp.float32)

    def face(side, k, t):
        return faces[side * FACE + k : side * FACE + k + 1, tile_cols(t)]

    for low, high in EVEN_BLOCKS:
        flows = {}
        for t in range(inner):
            sides = sides_of(t, outer)
            total = {}
            for k in range(VARS):
                value = mixed[k * EVEN + low : k * EVEN + high, tile_cols(t)]
                for side in sides:
                    term = face(side, k, t) * value
                    total[side] = term if k == 0 else total[side] + term
            for side in sides:
                flux[side, low:high, tile_cols(t)] = total[side]
        even = [mixed[SPAN + low : SPAN + high, tile_cols(t)] for t in range(inner)]
        for t in range(outer):
            steps = [even[t] - neighbour(even, t, side, place) for side in range(6)]
            for k in range(VARS):
                total = face(0, k, t) * steps[0]
                for side in range(1, 6):
                    total = total + face(side, k, t) * steps[side]
                scaled[k * EVEN + low : k * EVEN + high, tile_cols(t)] = total
        for t in range(outer):
            total = None
            for side in range(6):
                opposite = FluxTiles(flux, side ^ 1, low, high)
                term = flux[side, low:high, tile_cols(t)] - neighbour(opposite, t, side, place)
                total = term if total is None else total + term
            scaled[SPAN + low : SPAN + high, tile_cols(t)] = total
    scaled[SPAN + EVEN : FULL, : outer * LANES] = jnp.zeros((FULL - SPAN - EVEN, outer * LANES), jnp.float32)
    for start in range(0, outer * LANES, 512):
        cols = slice(start, min(start + 512, outer * LANES))
        acc[:, cols] = jnp.dot(to_all[...], split(scaled[:, cols]), preferred_element_type=jnp.float32)

    def last(step, carry):
        rows = pl.ds(pl.multiple_of(step * STEP, STEP), STEP)
        tiles = [src[rows, tile_cols(t)] for t in range(inner)]
        for t in range(outer):
            result = tiles[t] + acc[rows, tile_cols(t)]
            for side in range(6):
                result = result + face(side, VARS, t) * (tiles[t] - neighbour(tiles, t, side, place))
            if t >= SLAB:
                result = inside[t] * result
            dst[rows, tile_cols(t)] = result
        return carry

    lax.fori_loop(0, slots // STEP, last, 0)


class FluxTiles:
    def __init__(self, flux, side, low, high):
        self.flux, self.side, self.low, self.high = flux, side, low, high

    def __getitem__(self, t):
        return self.flux[self.side, self.low : self.high, tile_cols(t)]


def apply_kernel(
    place, own, before, after, scale, unscale, to_even, to_all, fields, fibre, so_far,
    out, partial, field, first, second, mixed, flux, scaled, acc, faces, *, comp,
):
    slots = scale.shape[0]
    here = place[0]
    face_stiffness(fields, faces, [fibre[comp, d] for d in range(3)], here)
    lane = lax.broadcasted_iota(jnp.int32, (slots, LANES), 1)
    slot = lane % WIDE
    load = lambda ref, p: ref[pl.ds(p, slots, stride=ROWS), :]
    left = pltpu.roll(load(before, 3), LANES - 3, 1)
    right = pltpu.roll(load(after, 3), 3, 1)
    halo = jnp.where((slot == 0) | (slot == 5), left, load(own, 3))
    halo = jnp.where((slot == 4) | (slot == 9), right, halo)
    ordered = [
        load(own, 0), load(own, 1), load(own, 2), load(before, 2), load(after, 0), halo,
        load(before, 1), load(after, 1),
    ]
    for t, tile in enumerate(ordered):
        field[:, tile_cols(t)] = tile * scale[...]
    inside = {t: fields[VARS + 1 : VARS + 2, tile_cols(t)] for t in range(SLAB, INNER)}
    slot = lax.broadcasted_iota(jnp.int32, (1, LANES), 1) % WIDE
    used = ((slot >= 1) & (slot <= 3)) | ((slot >= 6) & (slot <= 8))
    inside[HALO] = jnp.where(used, inside[HALO], 0.0)
    scratch = (mixed, flux, scaled, acc, faces, inside, to_even, to_all, here)
    apply_operator(field, first, *scratch, TILES, INNER)
    apply_operator(first, second, *scratch, INNER, SLAB)
    sums = [jnp.zeros((1, LANES), jnp.float32)] * 5
    for p in range(SLAB):
        b = load(own, p)
        q = first[:, tile_cols(p)] * unscale[...]
        w = second[:, tile_cols(p)] * unscale[...]
        out[pl.ds(p, slots, stride=2 * SLAB), :] = q
        out[pl.ds(p + SLAB, slots, stride=2 * SLAB), :] = w
        for n, (one, two) in enumerate(((b, b), (b, q), (q, q), (b, w), (q, w))):
            sums[n] = sums[n] + jnp.sum(one * two, axis=0, keepdims=True)
    partial[...] = so_far[...] + jnp.concatenate(sums + [jnp.zeros((3, LANES), jnp.float32)], axis=0)


def apply_twice(comp, place, own, before, after, tables, fields, fibre, so_far):
    scale, unscale, to_even, to_all = tables
    slots = scale.shape[0]
    vmem = pl.BlockSpec(memory_space=pltpu.VMEM)
    smem = pl.BlockSpec(memory_space=pltpu.SMEM)
    f32 = lambda *shape: pltpu.VMEM(shape, jnp.float32)
    return pl.pallas_call(
        functools.partial(apply_kernel, comp=comp),
        out_shape=[
            jax.ShapeDtypeStruct((slots * 2 * SLAB, LANES), jnp.float32),
            jax.ShapeDtypeStruct((8, LANES), jnp.float32),
        ],
        in_specs=[smem] + [vmem] * 8 + [smem, vmem],
        out_specs=[vmem, vmem],
        scratch_shapes=[
            f32(slots, TILES * LANES),
            f32(slots, INNER * LANES),
            f32(slots, SLAB * LANES),
            f32(FULL, TILES * LANES),
            f32(6, EVEN, TILES * LANES),
            f32(FULL, INNER * LANES),
            f32(slots, INNER * LANES),
            f32(6 * FACE, TILES * LANES),
        ],
        compiler_params=pltpu.CompilerParams(vmem_limit_bytes=VMEM),
        cost_estimate=estimate(15),
        name="apply_twice",
    )(place, own, before, after, scale, unscale, to_even, to_all, fields, fibre, so_far)


def finish(field, images, coefs):
    modes = field.shape[0]
    per_part = modes * 2 * SLAB
    steps = 4

    def kernel(field, *refs):
        images, coefs, solution_field, residual = refs[:COMPS], refs[COMPS], refs[-2], refs[-1]
        first = pl.program_id(0) * (modes // steps)

        def body(step, carry):
            for inner in range(UNROLL):
                mode = step * UNROLL + inner
                base = (first + mode) * 2 * SLAB
                for comp in range(COMPS):
                    for p in range(SLAB):
                        b = field[mode, comp, p]
                        q = swap_back(images[comp][pl.ds(base + p, PARTS, stride=per_part), :])
                        w = swap_back(images[comp][pl.ds(base + p + SLAB, PARTS, stride=per_part), :])
                        solution_field[mode, comp, p] = coefs[0] * b + coefs[1] * q
                        residual[mode, comp, p] = b + coefs[2] * q + coefs[3] * w
            return carry

        lax.fori_loop(0, modes // steps // UNROLL, body, 0)

    block = pl.BlockSpec((modes // steps,) + field.shape[1:], lambda i: (i, 0, 0, 0, 0))
    whole = pl.BlockSpec(memory_space=pltpu.VMEM)
    return pl.pallas_call(
        kernel,
        grid=(steps,),
        out_shape=[jax.ShapeDtypeStruct(field.shape, jnp.float32)] * 2,
        in_specs=[block] + [whole] * COMPS + [pl.BlockSpec(memory_space=pltpu.SMEM)],
        out_specs=[block, block],
        compiler_params=pltpu.CompilerParams(vmem_limit_bytes=VMEM),
        cost_estimate=estimate(6),
        name="finish",
    )(field, *images, coefs)


def mode_tables(coupling_table, slots):
    lower, upper, variable, code = (coupling_table[:, n] for n in range(4))
    slot = jnp.arange(slots, dtype=jnp.int32)
    is_lower = lower[:, None] == slot
    is_upper = upper[:, None] == slot
    degree = jnp.sum(jnp.where(is_upper, code[:, None], 0), axis=0)
    factor = jnp.where(code == 3, 6, code).astype(jnp.float32)[:, None]
    factorial = jnp.prod(jnp.where(is_upper, factor, 1.0), axis=0)
    root = (degree == 0) & jnp.any(is_lower, axis=0)
    even = (degree == 2) | root
    rank = jnp.sum(jnp.where(even[:, None] & (slot[:, None] < slot), 1, 0), axis=0)
    lower_even = jnp.any(is_lower & even, axis=1)
    is_even_end = jnp.where(lower_even[:, None], is_lower, is_upper)
    is_odd_end = jnp.where(lower_even[:, None], is_upper, is_lower)
    column = variable * EVEN + jnp.sum(jnp.where(is_even_end, rank, 0), axis=1)
    at_column = column[:, None] == jnp.arange(FULL, dtype=jnp.int32)
    down = code.astype(jnp.float32)[:, None]
    first = jnp.where(lower_even[:, None], 1.0, down)
    second = jnp.where(lower_even[:, None], down, 1.0)
    odd_ends = is_odd_end.astype(jnp.float32)
    columns = at_column.astype(jnp.float32)
    half = jnp.bfloat16
    to_even = jnp.dot(
        columns.astype(half).T, (odd_ends * first).astype(half), preferred_element_type=jnp.float32
    )
    to_odd = jnp.dot(
        odd_ends.astype(half).T, (columns * second).astype(half), preferred_element_type=jnp.float32
    )
    pick = (jnp.arange(FULL, dtype=jnp.int32)[:, None] - SPAN == rank) & even
    pick = pick.astype(jnp.float32)
    to_even = (to_even + pick).astype(half)
    to_all = (to_odd + pick.T).astype(half)
    scale = jnp.sqrt(factorial)
    wide = lambda v: jnp.broadcast_to(v[:, None], (slots, LANES))
    twice = lambda v: jnp.concatenate([v, v], axis=1)
    return wide(scale), wide(1.0 / scale), twice(to_even), twice(to_all)


def all_sum(value):
    for axis in ("space", "mode"):
        devices = lax.axis_size(axis)
        bit = 1
        while bit < devices:
            value = value + lax.ppermute(value, axis, [(i, i ^ bit) for i in range(devices)])
            bit *= 2
    return value


def transposed(right_side, mean_stiffness, ply_stiffness, fibre_weights, ply_map, coupling_table):
    slots = right_side.shape[0] * PARTS
    devices = lax.axis_size("space")
    up = [(i, i + 1) for i in range(devices - 1)]
    down = [(j, i) for i, j in up]
    swap = lambda v: lax.all_to_all(v, "mode", 0, 0, tiled=True)
    *packed, both = pack(right_side, mean_stiffness, ply_map)
    own = [swap(p) for p in packed]
    before = [lax.ppermute(p, "space", up) for p in own]
    after = [lax.ppermute(p, "space", down) for p in own]
    tables = mode_tables(coupling_table, slots)
    place = lax.axis_index("mode").astype(jnp.int32).reshape(1)
    both_before = lax.ppermute(both, "space", up)
    both_after = lax.ppermute(both, "space", down)
    fields = stiffness_fields(place, both_before, both, both_after, ply_stiffness)
    partial = jnp.zeros((8, LANES), jnp.float32)
    images = []
    for comp in range(COMPS):
        out, partial = apply_twice(
            comp, place, own[comp], before[comp], after[comp], tables, fields, fibre_weights, partial
        )
        images.append(swap(out))
    bb, bq, qq, bw, qw = (jnp.sum(all_sum(partial)[n]) for n in range(5))
    step_one = bb / bq
    norm = bb - 2.0 * step_one * bq + step_one * step_one * qq
    beta = norm / bb
    grown = 1.0 + beta
    curve = grown * grown * bq - step_one * grown * (bw + qq) + step_one * step_one * qw
    step_two = norm / curve
    coefs = jnp.stack(
        [
            step_one + step_two * grown,
            -step_one * step_two,
            -step_one - step_two * grown,
            step_one * step_two,
        ]
    )
    return tuple(finish(right_side, images, coefs))


def on_device(right_side, mean_stiffness, ply_stiffness, fibre_weights, ply_map, coupling_table):
    args = (right_side, mean_stiffness, ply_stiffness, fibre_weights, ply_map, coupling_table)
    fits = right_side.shape[1:] == (COMPS, SLAB, 8, 128) and lax.axis_size("mode") == PARTS
    return transposed(*args) if fits else plain(*args)


def solution(mesh):
    return jax.shard_map(
        on_device,
        mesh=mesh,
        in_specs=(
            P("mode", None, "space", None, None),
            P("space", None, None),
            P(),
            P(),
            P("space", None, None),
            P(),
        ),
        out_specs=(P("mode", None, "space", None, None), P("mode", None, "space", None, None)),
        check_vma=False,
    )
```

profile of v0, /device:TPU:0, one launch (start us, length us, event | category | flops | bytes accessed | tf_op | source)
XLA Modules:
  0.0 172.9 jit_solution(17713340321958865273)
XLA Ops:
  0.6 6.6 %pack.1 = (f32[1152,128]{1,0:T(8,128)}, f32[1152,128]{1,0:T(8,128)}, f32[1152,128]{1,0:T(8,128)}, f32[2,3,8,128]{3,2,1,0:T(8,128)}) custom-call(f32[36,3,3,8,128]{4,3,2,1,0:T(8,128)} %field.3, f32[3,8,128]{2,1,0:T(8,128)} %mean.1, s32[3,8,128]{2,1,0:T(8,128)} %ply.1), custom_call_target="tpu_custom_call" | custom-call | flops 5000000000 | bytes 15000000 | tf_op jit(solution)/shard_map/pack/pallas_call | solution.py:201
  7.3 2.3 %collective-permute-start.2 = (f32[2,3,8,128]{3,2,1,0:T(8,128)}, f32[2,3,8,128]{3,2,1,0:T(8,128)S(1)}, u32[]{:S(2)}, u32[]{:S(2)}) collective-permute-start(f32[2,3,8,128]{3,2,1,0:T(8,128)} %get-tuple-element.13.both), channel_id=1, source_target_pairs={{0,1},{1,2},{2,3},{4,5},{5,6},{6,7},{8,9},{9,10},{10,11},{12,13},{... | collective-permute-start | bytes 73736 | tf_op jit(solution)/shard_map/ppermute | solution.py:539
  10.9 6.6 %all-to-all-start = ((f32[8,144,128]{2,1,0:T(8,128)}), f32[8,144,128]{2,1,0:T(8,128)S(1)}, u32[]{:S(2)}, u32[]{:S(2)}) async-start(f32[8,144,128]{2,1,0:T(8,128)} %bitcast.32), calls=%async_computation | async-start | bytes 1179648 | tf_op jit(solution)/shard_map/all_to_all | solution.py:532
  19.9 13.8 %all-to-all-done = f32[8,144,128]{2,1,0:T(8,128)S(1)} async-done(((f32[8,144,128]{2,1,0:T(8,128)}), f32[8,144,128]{2,1,0:T(8,128)S(1)}, u32[]{:S(2)}, u32[]{:S(2)}) %all-to-all-start) | async-done | bytes 589856 | tf_op jit(solution)/shard_map/all_to_all | solution.py:532
  33.7 4.7 %all-to-all-start.2 = ((f32[8,144,128]{2,1,0:T(8,128)}), f32[8,144,128]{2,1,0:T(8,128)S(1)}, u32[]{:S(2)}, u32[]{:S(2)}) async-start(f32[8,144,128]{2,1,0:T(8,128)} %bitcast.5), calls=%async_computation.2 | async-start | bytes 1179648 | tf_op jit(solution)/shard_map/all_to_all | solution.py:532
  39.2 1.8 %collective-permute-start = (f32[1152,128]{1,0:T(8,128)S(1)}, f32[1152,128]{1,0:T(8,128)S(1)}, u32[]{:S(2)}, u32[]{:S(2)}) collective-permute-start(f32[1152,128]{1,0:T(8,128)S(1)} %bitcast.23), channel_id=1, source_target_pairs={{0,1},{1,2},{2,3},{4,5},{5,6},{6,7},{8,9},{9,10},{10,11},{12,13},{... | collective-permute-start | bytes 1769480 | tf_op jit(solution)/shard_map/ppermute | solution.py:535
  46.8 7.8 %all-to-all-done.2 = f32[8,144,128]{2,1,0:T(8,128)S(1)} async-done(((f32[8,144,128]{2,1,0:T(8,128)}), f32[8,144,128]{2,1,0:T(8,128)S(1)}, u32[]{:S(2)}, u32[]{:S(2)}) %all-to-all-start.2) | async-done | bytes 589856 | tf_op jit(solution)/shard_map/all_to_all | solution.py:532
  54.6 3.6 %all-to-all-start.4 = ((f32[8,144,128]{2,1,0:T(8,128)}), f32[8,144,128]{2,1,0:T(8,128)S(1)}, u32[]{:S(2)}, u32[]{:S(2)}) async-start(f32[8,144,128]{2,1,0:T(8,128)} %bitcast.9), calls=%async_computation.4 | async-start | bytes 1179648 | tf_op jit(solution)/shard_map/all_to_all | solution.py:532
  63.6 12.2 %apply_twice.3 = (f32[1728,128]{1,0:T(8,128)}, f32[8,128]{1,0:T(8,128)}) custom-call(s32[1]{0:T(128)} %bitcast.place, f32[1152,128]{1,0:T(8,128)} %bitcast.25, f32[1152,128]{1,0:T(8,128)} %copy-done.8, f32[1152,128]{1,0:T(8,128)} %copy-done.9, f32[288,128]{1,0:T(8,128)} %broadcast_in_dim.99.scale, f32[288,128]{1,0:T(8,128)} %broadcast_in_dim.100.unscale, ...), custom_call_target="tpu_custom_call" | custom-call | flops 15000000512 | bytes 45000000 | tf_op jit(solution)/shard_map/apply_twice/pallas_call | solution.py:417
  75.8 5.7 %all-to-all-start.1 = ((f32[8,216,128]{2,1,0:T(8,128)}), f32[8,216,128]{2,1,0:T(8,128)S(1)}, u32[]{:S(2)}, u32[]{:S(2)}) async-start(f32[8,216,128]{2,1,0:T(8,128)} %bitcast.21), calls=%async_computation.1 | async-start | bytes 1769472 | tf_op jit(solution)/shard_map/all_to_all | solution.py:532
  81.5 4.3 %collective-permute-start.6 = (f32[1152,128]{1,0:T(8,128)S(1)}, f32[1152,128]{1,0:T(8,128)}, u32[]{:S(2)}, u32[]{:S(2)}) collective-permute-start(f32[1152,128]{1,0:T(8,128)S(1)} %bitcast.29), channel_id=1, source_target_pairs={{0,1},{1,2},{2,3},{4,5},{5,6},{6,7},{8,9},{9,10},{10,11},{12,13},{... | collective-permute-start | bytes 1769480 | tf_op jit(solution)/shard_map/ppermute | solution.py:535
  88.1 12.2 %apply_twice.4 = (f32[1728,128]{1,0:T(8,128)}, f32[8,128]{1,0:T(8,128)}) custom-call(s32[1]{0:T(128)} %bitcast.place, f32[1152,128]{1,0:T(8,128)} %bitcast.28, f32[1152,128]{1,0:T(8,128)} %copy-done.10, f32[1152,128]{1,0:T(8,128)} %collective-permute-done.5.after, f32[288,128]{1,0:T(8,128)} %broadcast_in_dim.99.scale, f32[288,128]{1,0:T(8,128)} %broadcast_in_dim.100.unscale, ...), custom_call_target="tpu_custom_call" | custom-call | flops 15000000512 | bytes 45000000 | tf_op jit(solution)/shard_map/apply_twice/pallas_call | solution.py:417
  100.3 4.7 %all-to-all-done.1 = f32[8,216,128]{2,1,0:T(8,128)S(1)} async-done(((f32[8,216,128]{2,1,0:T(8,128)}), f32[8,216,128]{2,1,0:T(8,128)S(1)}, u32[]{:S(2)}, u32[]{:S(2)}) %all-to-all-start.1) | async-done | bytes 884768 | tf_op jit(solution)/shard_map/all_to_all | solution.py:532
  105.0 3.8 %all-to-all-start.3 = ((f32[8,216,128]{2,1,0:T(8,128)}), f32[8,216,128]{2,1,0:T(8,128)S(1)}, u32[]{:S(2)}, u32[]{:S(2)}) async-start(f32[8,216,128]{2,1,0:T(8,128)} %bitcast.22), calls=%async_computation.3 | async-start | bytes 1769472 | tf_op jit(solution)/shard_map/all_to_all | solution.py:532
  108.8 12.2 %apply_twice.5 = (f32[1728,128]{1,0:T(8,128)}, f32[8,128]{1,0:T(8,128)}) custom-call(s32[1]{0:T(128)} %bitcast.place, f32[1152,128]{1,0:T(8,128)} %bitcast.31, f32[1152,128]{1,0:T(8,128)} %collective-permute-done.6.before, f32[1152,128]{1,0:T(8,128)} %collective-permute-done.7.after, f32[288,128]{1,0:T(8,128)} %broadcast_in_dim.99.scale, ...), custom_call_target="tpu_custom_call" | custom-call | flops 15000000512 | bytes 45000000 | tf_op jit(solution)/shard_map/apply_twice/pallas_call | solution.py:417
  121.0 10.6 %all-to-all-done.3 = f32[8,216,128]{2,1,0:T(8,128)S(1)} async-done(((f32[8,216,128]{2,1,0:T(8,128)}), f32[8,216,128]{2,1,0:T(8,128)S(1)}, u32[]{:S(2)}, u32[]{:S(2)}) %all-to-all-start.3) | async-done | bytes 884768 | tf_op jit(solution)/shard_map/all_to_all | solution.py:532
  131.6 3.6 %all-to-all-start.5 = ((f32[8,216,128]{2,1,0:T(8,128)}), f32[8,216,128]{2,1,0:T(8,128)S(1)}, u32[]{:S(2)}, u32[]{:S(2)}) async-start(f32[8,216,128]{2,1,0:T(8,128)} %bitcast.19), calls=%async_computation.5 | async-start | bytes 1769472 | tf_op jit(solution)/shard_map/all_to_all | solution.py:532
  137.9 2.2 %collective-permute-done.9 = f32[8,128]{1,0:T(8,128)S(1)} collective-permute-done((f32[8,128]{1,0:T(8,128)S(1)}, f32[8,128]{1,0:T(8,128)S(1)}, u32[]{:S(2)}, u32[]{:S(2)}) %collective-permute-start.9) | collective-permute-done | bytes 4128 | tf_op jit(solution)/shard_map/ppermute | solution.py:522
  140.1 2.0 %collective-permute-start.10 = (f32[8,128]{1,0:T(8,128)S(1)}, f32[8,128]{1,0:T(8,128)S(1)}, u32[]{:S(2)}, u32[]{:S(2)}) collective-permute-start(f32[8,128]{1,0:T(8,128)S(1)} %add.70), channel_id=1, source_target_pairs={{0,4},{4,0},{8,12},{12,8},{16,20},{20,16},{24,28},{28,24},{1,5},{5... | collective-permute-start | bytes 12296 | tf_op jit(solution)/shard_map/ppermute | solution.py:522
  142.0 1.8 %collective-permute-done.10 = f32[8,128]{1,0:T(8,128)S(1)} collective-permute-done((f32[8,128]{1,0:T(8,128)S(1)}, f32[8,128]{1,0:T(8,128)S(1)}, u32[]{:S(2)}, u32[]{:S(2)}) %collective-permute-start.10) | collective-permute-done | bytes 4128 | tf_op jit(solution)/shard_map/ppermute | solution.py:522
  145.6 4.4 %collective-permute-done.11 = f32[8,128]{1,0:T(8,128)S(1)} collective-permute-done((f32[8,128]{1,0:T(8,128)S(1)}, f32[8,128]{1,0:T(8,128)S(1)}, u32[]{:S(2)}, u32[]{:S(2)}) %collective-permute-start.11) | collective-permute-done | bytes 4128 | tf_op jit(solution)/shard_map/ppermute | solution.py:522
  150.0 4.5 %collective-permute-start.12 = (f32[8,128]{1,0:T(8,128)S(1)}, f32[8,128]{1,0:T(8,128)S(1)}, u32[]{:S(2)}, u32[]{:S(2)}) collective-permute-start(f32[8,128]{1,0:T(8,128)S(1)} %add.72), channel_id=1, source_target_pairs={{0,16},{4,20},{8,24},{12,28},{16,0},{20,4},{24,8},{28,12},{1,17},{... | collective-permute-start | bytes 12296 | tf_op jit(solution)/shard_map/ppermute | solution.py:522
  154.5 3.3 %collective-permute-done.12 = f32[8,128]{1,0:T(8,128)S(1)} collective-permute-done((f32[8,128]{1,0:T(8,128)S(1)}, f32[8,128]{1,0:T(8,128)S(1)}, u32[]{:S(2)}, u32[]{:S(2)}) %collective-permute-start.12) | collective-permute-done | bytes 4128 | tf_op jit(solution)/shard_map/ppermute | solution.py:522
  166.5 6.4 %finish.1 = (f32[36,3,3,8,128]{4,3,2,1,0:T(8,128)}, f32[36,3,3,8,128]{4,3,2,1,0:T(8,128)}) custom-call(f32[36,3,3,8,128]{4,3,2,1,0:T(8,128)} %field.3, f32[1728,128]{1,0:T(8,128)} %bitcast.17, f32[1728,128]{1,0:T(8,128)} %bitcast.18, f32[1728,128]{1,0:T(8,128)} %bitcast.20, f32[4]{0:T(128)} %pad_maximum_fusion.2.refs_3_), custom_call_target="tpu_custom_call" | custom-call | flops 6000000000 | bytes 18000000 | tf_op jit(solution)/shard_map/finish/pallas_call | solution.py:467
  (72 shorter events, 24.4 us)
Async XLA Ops:
  0.6 16.9 %copy-start.6 = (s32[660,4]{0,1:T(4,128)S(1)}, s32[660,4]{0,1:T(4,128)}, u32[]{:S(2)}) copy-start(s32[660,4]{0,1:T(4,128)} %param.11) | copy-start | bytes 31684
  7.3 37.3 %collective-permute-start.2 = (f32[2,3,8,128]{3,2,1,0:T(8,128)}, f32[2,3,8,128]{3,2,1,0:T(8,128)S(1)}, u32[]{:S(2)}, u32[]{:S(2)}) collective-permute-start(f32[2,3,8,128]{3,2,1,0:T(8,128)} %get-tuple-element.13.both), channel_id=1, source_target_pairs={{0,1},{1,2},{2,3},{4,5},{5,6},{6,7},{8,9},{9,10},{10,11},{12,13},{... | collective-permute-start | bytes 73736 | tf_op jit(solution)/shard_map/ppermute | solution.py:539
  9.6 34.9 %collective-permute-start.3 = (f32[2,3,8,128]{3,2,1,0:T(8,128)}, f32[2,3,8,128]{3,2,1,0:T(8,128)S(1)}, u32[]{:S(2)}, u32[]{:S(2)}) collective-permute-start(f32[2,3,8,128]{3,2,1,0:T(8,128)} %get-tuple-element.13.both), channel_id=1, source_target_pairs={{1,0},{2,1},{3,2},{5,4},{6,5},{7,6},{9,8},{10,9},{11,10},{13,12},{... | collective-permute-start | bytes 73736 | tf_op jit(solution)/shard_map/ppermute | solution.py:540
  10.9 22.7 %all-to-all-start = ((f32[8,144,128]{2,1,0:T(8,128)}), f32[8,144,128]{2,1,0:T(8,128)S(1)}, u32[]{:S(2)}, u32[]{:S(2)}) async-start(f32[8,144,128]{2,1,0:T(8,128)} %bitcast.32), calls=%async_computation | async-start | bytes 1179648 | tf_op jit(solution)/shard_map/all_to_all | solution.py:532
  33.7 20.9 %all-to-all-start.2 = ((f32[8,144,128]{2,1,0:T(8,128)}), f32[8,144,128]{2,1,0:T(8,128)S(1)}, u32[]{:S(2)}, u32[]{:S(2)}) async-start(f32[8,144,128]{2,1,0:T(8,128)} %bitcast.5), calls=%async_computation.2 | async-start | bytes 1179648 | tf_op jit(solution)/shard_map/all_to_all | solution.py:532
  39.2 22.0 %collective-permute-start = (f32[1152,128]{1,0:T(8,128)S(1)}, f32[1152,128]{1,0:T(8,128)S(1)}, u32[]{:S(2)}, u32[]{:S(2)}) collective-permute-start(f32[1152,128]{1,0:T(8,128)S(1)} %bitcast.23), channel_id=1, source_target_pairs={{0,1},{1,2},{2,3},{4,5},{5,6},{6,7},{8,9},{9,10},{10,11},{12,13},{... | collective-permute-start | bytes 1769480 | tf_op jit(solution)/shard_map/ppermute | solution.py:535
  41.0 20.3 %collective-permute-start.1 = (f32[1152,128]{1,0:T(8,128)S(1)}, f32[1152,128]{1,0:T(8,128)S(1)}, u32[]{:S(2)}, u32[]{:S(2)}) collective-permute-start(f32[1152,128]{1,0:T(8,128)S(1)} %bitcast.24), channel_id=1, source_target_pairs={{1,0},{2,1},{3,2},{5,4},{6,5},{7,6},{9,8},{10,9},{11,10},{13,12},{... | collective-permute-start | bytes 1769480 | tf_op jit(solution)/shard_map/ppermute | solution.py:536
  54.6 21.2 %copy-start.4 = (f32[8,144,128]{2,1,0:T(8,128)}, f32[8,144,128]{2,1,0:T(8,128)S(1)}, u32[]{:S(2)}) copy-start(f32[8,144,128]{2,1,0:T(8,128)S(1)} %all-to-all-done.2) | copy-start | bytes 1769476
  54.6 21.2 %all-to-all-start.4 = ((f32[8,144,128]{2,1,0:T(8,128)}), f32[8,144,128]{2,1,0:T(8,128)S(1)}, u32[]{:S(2)}, u32[]{:S(2)}) async-start(f32[8,144,128]{2,1,0:T(8,128)} %bitcast.9), calls=%async_computation.4 | async-start | bytes 1179648 | tf_op jit(solution)/shard_map/all_to_all | solution.py:532
  58.2 29.1 %collective-permute-start.4 = (f32[1152,128]{1,0:T(8,128)S(1)}, f32[1152,128]{1,0:T(8,128)S(1)}, u32[]{:S(2)}, u32[]{:S(2)}) collective-permute-start(f32[1152,128]{1,0:T(8,128)S(1)} %bitcast.26), channel_id=1, source_target_pairs={{0,1},{1,2},{2,3},{4,5},{5,6},{6,7},{8,9},{9,10},{10,11},{12,13},{... | collective-permute-start | bytes 1769480 | tf_op jit(solution)/shard_map/ppermute | solution.py:535
  59.9 27.4 %collective-permute-start.5 = (f32[1152,128]{1,0:T(8,128)S(1)}, f32[1152,128]{1,0:T(8,128)}, u32[]{:S(2)}, u32[]{:S(2)}) collective-permute-start(f32[1152,128]{1,0:T(8,128)S(1)} %bitcast.27), channel_id=1, source_target_pairs={{1,0},{2,1},{3,2},{5,4},{6,5},{7,6},{9,8},{10,9},{11,10},{13,12},{... | collective-permute-start | bytes 1769480 | tf_op jit(solution)/shard_map/ppermute | solution.py:536
  75.8 24.5 %copy-start.5 = (f32[8,144,128]{2,1,0:T(8,128)}, f32[8,144,128]{2,1,0:T(8,128)S(1)}, u32[]{:S(2)}) copy-start(f32[8,144,128]{2,1,0:T(8,128)S(1)} %all-to-all-done.4) | copy-start | bytes 1769476
  75.8 29.2 %all-to-all-start.1 = ((f32[8,216,128]{2,1,0:T(8,128)}), f32[8,216,128]{2,1,0:T(8,128)S(1)}, u32[]{:S(2)}, u32[]{:S(2)}) async-start(f32[8,216,128]{2,1,0:T(8,128)} %bitcast.21), calls=%async_computation.1 | async-start | bytes 1769472 | tf_op jit(solution)/shard_map/all_to_all | solution.py:532
  81.5 27.3 %collective-permute-start.6 = (f32[1152,128]{1,0:T(8,128)S(1)}, f32[1152,128]{1,0:T(8,128)}, u32[]{:S(2)}, u32[]{:S(2)}) collective-permute-start(f32[1152,128]{1,0:T(8,128)S(1)} %bitcast.29), channel_id=1, source_target_pairs={{0,1},{1,2},{2,3},{4,5},{5,6},{6,7},{8,9},{9,10},{10,11},{12,13},{... | collective-permute-start | bytes 1769480 | tf_op jit(solution)/shard_map/ppermute | solution.py:535
  85.9 22.9 %collective-permute-start.7 = (f32[1152,128]{1,0:T(8,128)S(1)}, f32[1152,128]{1,0:T(8,128)}, u32[]{:S(2)}, u32[]{:S(2)}) collective-permute-start(f32[1152,128]{1,0:T(8,128)S(1)} %bitcast.30), channel_id=1, source_target_pairs={{1,0},{2,1},{3,2},{5,4},{6,5},{7,6},{9,8},{10,9},{11,10},{13,12},{... | collective-permute-start | bytes 1769480 | tf_op jit(solution)/shard_map/ppermute | solution.py:536
  105.0 15.9 %copy-start = (f32[8,216,128]{2,1,0:T(8,128)}, f32[8,216,128]{2,1,0:T(8,128)S(1)}, u32[]{:S(2)}) copy-start(f32[8,216,128]{2,1,0:T(8,128)S(1)} %all-to-all-done.1) | copy-start | bytes 2654212
  105.0 26.6 %all-to-all-start.3 = ((f32[8,216,128]{2,1,0:T(8,128)}), f32[8,216,128]{2,1,0:T(8,128)S(1)}, u32[]{:S(2)}, u32[]{:S(2)}) async-start(f32[8,216,128]{2,1,0:T(8,128)} %bitcast.22), calls=%async_computation.3 | async-start | bytes 1769472 | tf_op jit(solution)/shard_map/all_to_all | solution.py:532
  131.6 34.0 %copy-start.1 = (f32[8,216,128]{2,1,0:T(8,128)}, f32[8,216,128]{2,1,0:T(8,128)S(1)}, u32[]{:S(2)}) copy-start(f32[8,216,128]{2,1,0:T(8,128)S(1)} %all-to-all-done.3) | copy-start | bytes 2654212
  131.6 34.0 %all-to-all-start.5 = ((f32[8,216,128]{2,1,0:T(8,128)}), f32[8,216,128]{2,1,0:T(8,128)S(1)}, u32[]{:S(2)}, u32[]{:S(2)}) async-start(f32[8,216,128]{2,1,0:T(8,128)} %bitcast.19), calls=%async_computation.5 | async-start | bytes 1769472 | tf_op jit(solution)/shard_map/all_to_all | solution.py:532
  135.2 1.2 collective-permute-start.8
  136.5 3.6 %collective-permute-start.9 = (f32[8,128]{1,0:T(8,128)S(1)}, f32[8,128]{1,0:T(8,128)S(1)}, u32[]{:S(2)}, u32[]{:S(2)}) collective-permute-start(f32[8,128]{1,0:T(8,128)S(1)} %add.69), channel_id=1, source_target_pairs={{0,2},{1,3},{2,0},{3,1},{4,6},{5,7},{6,4},{7,5},{8,10},{9,11},{10,... | collective-permute-start | bytes 12296 | tf_op jit(solution)/shard_map/ppermute | solution.py:522
  140.1 3.8 %collective-permute-start.10 = (f32[8,128]{1,0:T(8,128)S(1)}, f32[8,128]{1,0:T(8,128)S(1)}, u32[]{:S(2)}, u32[]{:S(2)}) collective-permute-start(f32[8,128]{1,0:T(8,128)S(1)} %add.70), channel_id=1, source_target_pairs={{0,4},{4,0},{8,12},{12,8},{16,20},{20,16},{24,28},{28,24},{1,5},{5... | collective-permute-start | bytes 12296 | tf_op jit(solution)/shard_map/ppermute | solution.py:522
  143.9 6.1 %collective-permute-start.11 = (f32[8,128]{1,0:T(8,128)S(1)}, f32[8,128]{1,0:T(8,128)S(1)}, u32[]{:S(2)}, u32[]{:S(2)}) collective-permute-start(f32[8,128]{1,0:T(8,128)S(1)} %add.71), channel_id=1, source_target_pairs={{0,8},{4,12},{8,0},{12,4},{16,24},{20,28},{24,16},{28,20},{1,9},{5... | collective-permute-start | bytes 12296 | tf_op jit(solution)/shard_map/ppermute | solution.py:522
  150.0 7.8 %collective-permute-start.12 = (f32[8,128]{1,0:T(8,128)S(1)}, f32[8,128]{1,0:T(8,128)S(1)}, u32[]{:S(2)}, u32[]{:S(2)}) collective-permute-start(f32[8,128]{1,0:T(8,128)S(1)} %add.72), channel_id=1, source_target_pairs={{0,16},{4,20},{8,24},{12,28},{16,0},{20,4},{24,8},{28,12},{1,17},{... | collective-permute-start | bytes 12296 | tf_op jit(solution)/shard_map/ppermute | solution.py:522
  (8 other events, 29.3 us)
where the time goes:
time: 174 us; the launch traced here: 173 us
  starting transfers between devices  53.3 us (31%)
  Pallas kernels  51.2 us (29%)
  waiting for transfers between devices  49.9 us (29%)
  between operations  7.31 us (4%)
  local copies, waits for them, and re-layouts  4.75 us (3%)
  other arithmetic  4.73 us (3%)
  matrix products  1.79 us (1%)
    all_to_all x6, waiting for transfers between devices, transposed(): swap = lambda v: lax.all_to_all(v, 'mode', 0, 0, tiled=True)  36.9 us
    pallas_call x3, Pallas kernels, apply_twice(): pl.pallas_call(functools.partial(apply_kernel, comp=comp), out_shape=[jax...  36.5 us
    all_to_all x6, starting transfers between devices, transposed(): swap = lambda v: lax.all_to_all(v, 'mode', 0, 0, tiled=True)  28.1 us
    ppermute x5, waiting for transfers between devices, all_sum(): lax.ppermute(value, axis, [(i, i ^ bit) for i in range(devices)])  12.9 us
    ppermute x5, starting transfers between devices, all_sum(): lax.ppermute(value, axis, [(i, i ^ bit) for i in range(devices)])  9.68 us
    ppermute x3, starting transfers between devices, transposed(): before = [lax.ppermute(p, 'space', up) for p in own]  7.77 us
    pallas_call x1, Pallas kernels, pack(): pl.pallas_call(pack_kernel, out_shape=[shape] * COMPS + [jax.ShapeDtypeSt...  6.63 us
    pallas_call x1, Pallas kernels, finish(): pl.pallas_call(kernel, grid=(steps,), out_shape=[jax.ShapeDtypeStruct(fie...  6.43 us
  transfers between devices with their start and end apart: 19, of which 9 were waited for; matrix products, arithmetic and copies ran while one was open for 5% of the time, Pallas kernels for 22%

commit v1 on v0

--- a/solution.py
+++ b/solution.py
@@ -170,22 +170,22 @@
 UNROLL = 3
 
 
-def pack_kernel(field, mean, ply, *outs):
+def pack_kernel(field, *refs):
     modes = field.shape[0]
-    both = outs[-1]
-    for x in range(SLAB):
-        both[0, x] = mean[x]
-        both[1, x] = (ply[x] + 1).astype(jnp.float32)
+    out = refs[-1]
+    if len(refs) > 1:
+        mean, ply, both, out = refs
+        for x in range(SLAB):
+            both[0, x] = mean[x]
+            both[1, x] = (ply[x] + 1).astype(jnp.float32)
 
     def body(step, carry):
         for inner in range(UNROLL):
             mode = step * UNROLL + inner
-            for comp in range(COMPS):
-                planes = [field[mode, comp, x] for x in range(SLAB)]
-                halo = halo_row(dict(enumerate(planes)))
-                for p, tile in enumerate(planes + [halo]):
-                    place = pl.ds(mode * ROWS + p, PARTS, stride=ROWS * modes)
-                    outs[comp][place, :] = swap_out(tile)
+            planes = [field[mode, 0, x] for x in range(SLAB)]
+            halo = halo_row(dict(enumerate(planes)))
+            for p, tile in enumerate(planes + [halo]):
+                out[pl.ds(mode * ROWS + p, PARTS, stride=ROWS * modes), :] = swap_out(tile)
         return carry
 
     lax.fori_loop(0, modes // UNROLL, body, 0)
@@ -195,16 +195,22 @@
     return pl.CostEstimate(flops=int(micros * 1e9), bytes_accessed=int(micros * 3e6), transcendentals=0)
 
 
-def pack(field, mean, ply):
+def pack(field, comp, *stiffness):
     modes = field.shape[0]
-    shape = jax.ShapeDtypeStruct((PARTS * modes * ROWS, LANES), jnp.float32)
+    block = (modes, 1) + field.shape[2:]
+    vmem = pl.BlockSpec(memory_space=pltpu.VMEM)
+    shapes = [jax.ShapeDtypeStruct((2,) + s.shape, jnp.float32) for s in stiffness[:1]]
+    shapes.append(jax.ShapeDtypeStruct((PARTS * modes * ROWS, LANES), jnp.float32))
     return pl.pallas_call(
         pack_kernel,
-        out_shape=[shape] * COMPS + [jax.ShapeDtypeStruct((2,) + mean.shape, jnp.float32)],
+        grid=(1,),
+        out_shape=shapes,
+        in_specs=[pl.BlockSpec(block, lambda i: (0, comp, 0, 0, 0))] + [vmem] * len(stiffness),
+        out_specs=[vmem] * len(shapes),
         compiler_params=pltpu.CompilerParams(vmem_limit_bytes=VMEM),
-        cost_estimate=estimate(5),
+        cost_estimate=estimate(2.5),
         name="pack",
-    )(field, mean, ply)
+    )(field, *stiffness)
 
 
 def stiffness_kernel(place, before, both, after, ply_stiffness, fields, wide):
@@ -443,8 +449,7 @@
     per_part = modes * 2 * SLAB
     steps = 4
 
-    def kernel(field, *refs):
-        images, coefs, solution_field, residual = refs[:COMPS], refs[COMPS], refs[-2], refs[-1]
+    def kernel(field, first_images, other_images, coefs, solution_field, residual):
         first = pl.program_id(0) * (modes // steps)
 
         def body(step, carry):
@@ -452,10 +457,13 @@
                 mode = step * UNROLL + inner
                 base = (first + mode) * 2 * SLAB
                 for comp in range(COMPS):
+                    source, stride, start = first_images, per_part, base
+                    if comp > 0:
+                        source, stride, start = other_images, 2 * per_part, base + (comp - 1) * per_part
                     for p in range(SLAB):
                         b = field[mode, comp, p]
-                        q = swap_back(images[comp][pl.ds(base + p, PARTS, stride=per_part), :])
-                        w = swap_back(images[comp][pl.ds(base + p + SLAB, PARTS, stride=per_part), :])
+                        q = swap_back(source[pl.ds(start + p, PARTS, stride=stride), :])
+                        w = swap_back(source[pl.ds(start + p + SLAB, PARTS, stride=stride), :])
                         solution_field[mode, comp, p] = coefs[0] * b + coefs[1] * q
                         residual[mode, comp, p] = b + coefs[2] * q + coefs[3] * w
             return carry
@@ -468,7 +476,7 @@
         kernel,
         grid=(steps,),
         out_shape=[jax.ShapeDtypeStruct(field.shape, jnp.float32)] * 2,
-        in_specs=[block] + [whole] * COMPS + [pl.BlockSpec(memory_space=pltpu.SMEM)],
+        in_specs=[block, whole, whole, pl.BlockSpec(memory_space=pltpu.SMEM)],
         out_specs=[block, block],
         compiler_params=pltpu.CompilerParams(vmem_limit_bytes=VMEM),
         cost_estimate=estimate(6),
@@ -530,8 +538,10 @@
     up = [(i, i + 1) for i in range(devices - 1)]
     down = [(j, i) for i, j in up]
     swap = lambda v: lax.all_to_all(v, "mode", 0, 0, tiled=True)
-    *packed, both = pack(right_side, mean_stiffness, ply_map)
-    own = [swap(p) for p in packed]
+    (first,) = pack(right_side, 0)
+    both, second = pack(right_side, 1, mean_stiffness, ply_map)
+    (third,) = pack(right_side, 2)
+    own = [swap(p) for p in (first, second, third)]
     before = [lax.ppermute(p, "space", up) for p in own]
     after = [lax.ppermute(p, "space", down) for p in own]
     tables = mode_tables(coupling_table, slots)
@@ -540,12 +550,14 @@
     both_after = lax.ppermute(both, "space", down)
     fields = stiffness_fields(place, both_before, both, both_after, ply_stiffness)
     partial = jnp.zeros((8, LANES), jnp.float32)
-    images = []
+    outs = []
     for comp in range(COMPS):
         out, partial = apply_twice(
             comp, place, own[comp], before[comp], after[comp], tables, fields, fibre_weights, partial
         )
-        images.append(swap(out))
+        outs.append(out)
+    halves = [o.reshape(PARTS, -1, LANES) for o in outs[1:]]
+    images = [swap(outs[0]), swap(jnp.concatenate(halves, axis=1).reshape(-1, LANES))]
     bb, bq, qq, bw, qw = (jnp.sum(all_sum(partial)[n]) for n in range(5))
     step_one = bb / bq
     norm = bb - 2.0 * step_one * bq + step_one * step_one * qq

time: 174 us -> 185 us (1.063)
  Pallas kernels: 51.2 us -> 57.1 us
  other arithmetic: 4.73 us -> 7.22 us
  waiting for transfers between devices: 49.9 us -> 51.9 us
    ppermute x5, waiting for transfers between devices: 12.9 us -> 31.7 us  [all_sum(): lax.ppermute(value, axis, [(i, i ^ bit) for i in range(devices)])]
    all_to_all x6 -> x5, waiting for transfers between devices: 36.9 us -> 20.1 us  [transposed(): swap = lambda v: lax.all_to_all(v, 'mode', 0, 0, tiled=True)]
    pallas_call x1 -> x3, Pallas kernels: 6.63 us -> 12.1 us  [pack(): pl.pallas_call(pack_kernel, grid=(1,), out_shape=shapes, in_specs=[pl.Blo...]
    concatenate x0 -> x1, other arithmetic: none -> 2.5 us  [transposed(): jnp.concatenate(halves, axis=1).reshape(-1, LANES)]
    ppermute x3, starting transfers between devices: 7.77 us -> 9.91 us  [transposed(): before = [lax.ppermute(p, 'space', up) for p in own]]
    all_to_all x6 -> x5, starting transfers between devices: 28.1 us -> 26.5 us  [transposed(): swap = lambda v: lax.all_to_all(v, 'mode', 0, 0, tiled=True)]
  transfers between devices with their start and end apart: 19 -> 18, of which waited for: 9 -> 8; matrix products, arithmetic and copies ran while one was open for 5% -> 6% of each run, Pallas kernels for 22% -> 25%
where the time goes in v1:
time: 185 us; the launch traced here: 184 us
  Pallas kernels  57.1 us (31%)
  starting transfers between devices  53.9 us (29%)
  waiting for transfers between devices  51.9 us (28%)
  between operations  7.46 us (4%)
  other arithmetic  7.22 us (4%)
  local copies, waits for them, and re-layouts  5.02 us (3%)
    pallas_call x3, Pallas kernels, apply_twice(): pl.pallas_call(functools.partial(apply_kernel, comp=comp), out_shape=[jax...  36.5 us
    ppermute x5, waiting for transfers between devices, all_sum(): lax.ppermute(value, axis, [(i, i ^ bit) for i in range(devices)])  31.7 us
    all_to_all x5, starting transfers between devices, transposed(): swap = lambda v: lax.all_to_all(v, 'mode', 0, 0, tiled=True)  26.5 us
    all_to_all x5, waiting for transfers between devices, transposed(): swap = lambda v: lax.all_to_all(v, 'mode', 0, 0, tiled=True)  20.1 us
    pallas_call x3, Pallas kernels, pack(): pl.pallas_call(pack_kernel, grid=(1,), out_shape=shapes, in_specs=[pl.Blo...  12.1 us
    ppermute x5, starting transfers between devices, all_sum(): lax.ppermute(value, axis, [(i, i ^ bit) for i in range(devices)])  10.9 us
    ppermute x3, starting transfers between devices, transposed(): before = [lax.ppermute(p, 'space', up) for p in own]  9.91 us
    pallas_call x1, Pallas kernels, finish(): pl.pallas_call(kernel, grid=(steps,), out_shape=[jax.ShapeDtypeStruct(fie...  6.81 us
  transfers between devices with their start and end apart: 18, of which 8 were waited for; matrix products, arithmetic and copies ran while one was open for 6% of the time, Pallas kernels for 25%

profile of v1, /device:TPU:0, one launch (start us, length us, event | category | flops | bytes accessed | tf_op | source)
XLA Modules:
  0.0 184.3 jit_solution(10779600655254877827)
XLA Ops:
  0.6 4.0 %pack.3 = f32[1152,128]{1,0:T(8,128)} custom-call(f32[36,3,3,8,128]{4,3,2,1,0:T(8,128)} %field.7), custom_call_target="tpu_custom_call" | custom-call | flops 2500000000 | bytes 7500000 | tf_op jit(solution)/shard_map/pack/pallas_call | solution.py:204
  4.7 7.3 %all-to-all-start = ((f32[8,144,128]{2,1,0:T(8,128)}), f32[8,144,128]{2,1,0:T(8,128)S(1)}, u32[]{:S(2)}, u32[]{:S(2)}) async-start(f32[8,144,128]{2,1,0:T(8,128)} %bitcast.31), calls=%async_computation | async-start | bytes 1179648 | tf_op jit(solution)/shard_map/all_to_all | solution.py:540
  11.9 4.0 %pack.4 = (f32[2,3,8,128]{3,2,1,0:T(8,128)}, f32[1152,128]{1,0:T(8,128)}) custom-call(f32[36,3,3,8,128]{4,3,2,1,0:T(8,128)} %field.7, f32[3,8,128]{2,1,0:T(8,128)} %refs_0_.1, s32[3,8,128]{2,1,0:T(8,128)} %refs_1_.1), custom_call_target="tpu_custom_call" | custom-call | flops 2500000000 | bytes 7500000 | tf_op jit(solution)/shard_map/pack/pallas_call | solution.py:204
  19.4 8.4 %all-to-all-done = f32[8,144,128]{2,1,0:T(8,128)S(1)} async-done(((f32[8,144,128]{2,1,0:T(8,128)}), f32[8,144,128]{2,1,0:T(8,128)S(1)}, u32[]{:S(2)}, u32[]{:S(2)}) %all-to-all-start) | async-done | bytes 589856 | tf_op jit(solution)/shard_map/all_to_all | solution.py:540
  27.8 3.6 %all-to-all-start.2 = ((f32[8,144,128]{2,1,0:T(8,128)}), f32[8,144,128]{2,1,0:T(8,128)S(1)}, u32[]{:S(2)}, u32[]{:S(2)}) async-start(f32[8,144,128]{2,1,0:T(8,128)} %bitcast.30), calls=%async_computation.2 | async-start | bytes 1179648 | tf_op jit(solution)/shard_map/all_to_all | solution.py:540
  32.0 4.0 %pack.5 = f32[1152,128]{1,0:T(8,128)} custom-call(f32[36,3,3,8,128]{4,3,2,1,0:T(8,128)} %field.7), custom_call_target="tpu_custom_call" | custom-call | flops 2500000000 | bytes 7500000 | tf_op jit(solution)/shard_map/pack/pallas_call | solution.py:204
  37.1 10.5 %all-to-all-done.2 = f32[8,144,128]{2,1,0:T(8,128)S(1)} async-done(((f32[8,144,128]{2,1,0:T(8,128)}), f32[8,144,128]{2,1,0:T(8,128)S(1)}, u32[]{:S(2)}, u32[]{:S(2)}) %all-to-all-start.2) | async-done | bytes 589856 | tf_op jit(solution)/shard_map/all_to_all | solution.py:540
  47.5 3.6 %all-to-all-start.3 = ((f32[8,144,128]{2,1,0:T(8,128)}), f32[8,144,128]{2,1,0:T(8,128)S(1)}, u32[]{:S(2)}, u32[]{:S(2)}) async-start(f32[8,144,128]{2,1,0:T(8,128)} %bitcast.8), calls=%async_computation.3 | async-start | bytes 1179648 | tf_op jit(solution)/shard_map/all_to_all | solution.py:540
  59.4 5.2 %collective-permute-start.4 = (f32[1152,128]{1,0:T(8,128)S(1)}, f32[1152,128]{1,0:T(8,128)}, u32[]{:S(2)}, u32[]{:S(2)}) collective-permute-start(f32[1152,128]{1,0:T(8,128)S(1)} %bitcast.24), channel_id=1, source_target_pairs={{0,1},{1,2},{2,3},{4,5},{5,6},{6,7},{8,9},{9,10},{10,11},{12,13},{... | collective-permute-start | bytes 1769480 | tf_op jit(solution)/shard_map/ppermute | solution.py:545
  67.2 3.0 %collective-permute-start.6 = (f32[1152,128]{1,0:T(8,128)S(1)}, f32[1152,128]{1,0:T(8,128)}, u32[]{:S(2)}, u32[]{:S(2)}) collective-permute-start(f32[1152,128]{1,0:T(8,128)S(1)} %bitcast.27), channel_id=1, source_target_pairs={{0,1},{1,2},{2,3},{4,5},{5,6},{6,7},{8,9},{9,10},{10,11},{12,13},{... | collective-permute-start | bytes 1769480 | tf_op jit(solution)/shard_map/ppermute | solution.py:545
  73.8 12.2 %apply_twice.3 = (f32[1728,128]{1,0:T(8,128)}, f32[8,128]{1,0:T(8,128)}) custom-call(s32[1]{0:T(128)} %bitcast.place, f32[1152,128]{1,0:T(8,128)} %bitcast.23, f32[1152,128]{1,0:T(8,128)} %copy-done.8, f32[1152,128]{1,0:T(8,128)} %copy-done.9, f32[288,128]{1,0:T(8,128)} %broadcast_in_dim.99.scale, f32[288,128]{1,0:T(8,128)} %broadcast_in_dim.100.unscale, ...), custom_call_target="tpu_custom_call" | custom-call | flops 15000000512 | bytes 45000000 | tf_op jit(solution)/shard_map/apply_twice/pallas_call | solution.py:423
  85.9 6.0 %all-to-all-start.1 = ((f32[8,216,128]{2,1,0:T(8,128)}), f32[8,216,128]{2,1,0:T(8,128)S(1)}, u32[]{:S(2)}, u32[]{:S(2)}) async-start(f32[8,216,128]{2,1,0:T(8,128)} %bitcast.20), calls=%async_computation.1 | async-start | bytes 1769472 | tf_op jit(solution)/shard_map/all_to_all | solution.py:540
  91.9 12.2 %apply_twice.4 = (f32[1728,128]{1,0:T(8,128)}, f32[8,128]{1,0:T(8,128)}) custom-call(s32[1]{0:T(128)} %bitcast.place, f32[1152,128]{1,0:T(8,128)} %bitcast.26, f32[1152,128]{1,0:T(8,128)} %collective-permute-done.4.before, f32[1152,128]{1,0:T(8,128)} %collective-permute-done.5.after, f32[288,128]{1,0:T(8,128)} %broadcast_in_dim.99.scale, ...), custom_call_target="tpu_custom_call" | custom-call | flops 15000000512 | bytes 45000000 | tf_op jit(solution)/shard_map/apply_twice/pallas_call | solution.py:423
  104.1 12.2 %apply_twice.5 = (f32[1728,128]{1,0:T(8,128)}, f32[8,128]{1,0:T(8,128)}) custom-call(s32[1]{0:T(128)} %bitcast.place, f32[1152,128]{1,0:T(8,128)} %bitcast.29, f32[1152,128]{1,0:T(8,128)} %collective-permute-done.6.before, f32[1152,128]{1,0:T(8,128)} %collective-permute-done.7.after, f32[288,128]{1,0:T(8,128)} %broadcast_in_dim.99.scale, ...), custom_call_target="tpu_custom_call" | custom-call | flops 15000000512 | bytes 45000000 | tf_op jit(solution)/shard_map/apply_twice/pallas_call | solution.py:423
  116.3 2.5 %pad_maximum_fusion = f32[8,432,128]{2,1,0:T(8,128)} fusion(f32[8,216,128]{2,1,0:T(8,128)} %bitcast.18, f32[8,216,128]{2,1,0:T(8,128)S(1)} %bitcast.17), kind=kLoop, calls=%fused_computation | loop fusion | flops 442368 | bytes 3538944 | tf_op jit(solution)/shard_map/concatenate | solution.py:560
  119.8 6.0 %all-to-all-start.4 = ((f32[8,432,128]{2,1,0:T(8,128)}), f32[8,432,128]{2,1,0:T(8,128)S(1)}, u32[]{:S(2)}, u32[]{:S(2)}) async-start(f32[8,432,128]{2,1,0:T(8,128)} %pad_maximum_fusion), calls=%async_computation.4 | async-start | bytes 3538944 | tf_op jit(solution)/shard_map/all_to_all | solution.py:540
  127.4 2.8 %collective-permute-start.9 = (f32[8,128]{1,0:T(8,128)S(1)}, f32[8,128]{1,0:T(8,128)S(1)}, u32[]{:S(2)}, u32[]{:S(2)}) collective-permute-start(f32[8,128]{1,0:T(8,128)S(1)} %add.69), channel_id=1, source_target_pairs={{0,2},{1,3},{2,0},{3,1},{4,6},{5,7},{6,4},{7,5},{8,10},{9,11},{10,... | collective-permute-start | bytes 12296 | tf_op jit(solution)/shard_map/ppermute | solution.py:530
  131.8 2.0 %collective-permute-start.10 = (f32[8,128]{1,0:T(8,128)S(1)}, f32[8,128]{1,0:T(8,128)S(1)}, u32[]{:S(2)}, u32[]{:S(2)}) collective-permute-start(f32[8,128]{1,0:T(8,128)S(1)} %add.70), channel_id=1, source_target_pairs={{0,4},{4,0},{8,12},{12,8},{16,20},{20,16},{24,28},{28,24},{1,5},{5... | collective-permute-start | bytes 12296 | tf_op jit(solution)/shard_map/ppermute | solution.py:530
  133.7 7.6 %collective-permute-done.10 = f32[8,128]{1,0:T(8,128)S(1)} collective-permute-done((f32[8,128]{1,0:T(8,128)S(1)}, f32[8,128]{1,0:T(8,128)S(1)}, u32[]{:S(2)}, u32[]{:S(2)}) %collective-permute-start.10) | collective-permute-done | bytes 4128 | tf_op jit(solution)/shard_map/ppermute | solution.py:530
  141.3 1.9 %collective-permute-start.11 = (f32[8,128]{1,0:T(8,128)S(1)}, f32[8,128]{1,0:T(8,128)S(1)}, u32[]{:S(2)}, u32[]{:S(2)}) collective-permute-start(f32[8,128]{1,0:T(8,128)S(1)} %add.71), channel_id=1, source_target_pairs={{0,8},{4,12},{8,0},{12,4},{16,24},{20,28},{24,16},{28,20},{1,9},{5... | collective-permute-start | bytes 12296 | tf_op jit(solution)/shard_map/ppermute | solution.py:530
  143.2 13.7 %collective-permute-done.11 = f32[8,128]{1,0:T(8,128)S(1)} collective-permute-done((f32[8,128]{1,0:T(8,128)S(1)}, f32[8,128]{1,0:T(8,128)S(1)}, u32[]{:S(2)}, u32[]{:S(2)}) %collective-permute-start.11) | collective-permute-done | bytes 4128 | tf_op jit(solution)/shard_map/ppermute | solution.py:530
  156.9 3.4 %collective-permute-start.12 = (f32[8,128]{1,0:T(8,128)S(1)}, f32[8,128]{1,0:T(8,128)S(1)}, u32[]{:S(2)}, u32[]{:S(2)}) collective-permute-start(f32[8,128]{1,0:T(8,128)S(1)} %add.72), channel_id=1, source_target_pairs={{0,16},{4,20},{8,24},{12,28},{16,0},{20,4},{24,8},{28,12},{1,17},{... | collective-permute-start | bytes 12296 | tf_op jit(solution)/shard_map/ppermute | solution.py:530
  160.3 8.0 %collective-permute-done.12 = f32[8,128]{1,0:T(8,128)S(1)} collective-permute-done((f32[8,128]{1,0:T(8,128)S(1)}, f32[8,128]{1,0:T(8,128)S(1)}, u32[]{:S(2)}, u32[]{:S(2)}) %collective-permute-start.12) | collective-permute-done | bytes 4128 | tf_op jit(solution)/shard_map/ppermute | solution.py:530
  177.5 6.8 %finish.1 = (f32[36,3,3,8,128]{4,3,2,1,0:T(8,128)}, f32[36,3,3,8,128]{4,3,2,1,0:T(8,128)}) custom-call(f32[36,3,3,8,128]{4,3,2,1,0:T(8,128)} %field.7, f32[1728,128]{1,0:T(8,128)} %bitcast.19, f32[3456,128]{1,0:T(8,128)} %bitcast.16, f32[4]{0:T(128)} %pad_maximum_fusion.3.coefs), custom_call_target="tpu_custom_call" | custom-call | flops 6000000000 | bytes 18000000 | tf_op jit(solution)/shard_map/finish/pallas_call | solution.py:475
  (71 shorter events, 26.0 us)
Async XLA Ops:
  4.7 23.1 %all-to-all-start = ((f32[8,144,128]{2,1,0:T(8,128)}), f32[8,144,128]{2,1,0:T(8,128)S(1)}, u32[]{:S(2)}, u32[]{:S(2)}) async-start(f32[8,144,128]{2,1,0:T(8,128)} %bitcast.31), calls=%async_computation | async-start | bytes 1179648 | tf_op jit(solution)/shard_map/all_to_all | solution.py:540
  11.9 6.8 %copy-start.6 = (s32[660,4]{0,1:T(4,128)S(1)}, s32[660,4]{0,1:T(4,128)}, u32[]{:S(2)}) copy-start(s32[660,4]{0,1:T(4,128)} %param.11) | copy-start | bytes 31684
  15.9 41.2 %collective-permute-start.2 = (f32[2,3,8,128]{3,2,1,0:T(8,128)}, f32[2,3,8,128]{3,2,1,0:T(8,128)S(1)}, u32[]{:S(2)}, u32[]{:S(2)}) collective-permute-start(f32[2,3,8,128]{3,2,1,0:T(8,128)} %get-tuple-element.10.both), channel_id=1, source_target_pairs={{0,1},{1,2},{2,3},{4,5},{5,6},{6,7},{8,9},{9,10},{10,11},{12,13},{... | collective-permute-start | bytes 73736 | tf_op jit(solution)/shard_map/ppermute | solution.py:549
  17.4 39.8 %collective-permute-start.3 = (f32[2,3,8,128]{3,2,1,0:T(8,128)}, f32[2,3,8,128]{3,2,1,0:T(8,128)S(1)}, u32[]{:S(2)}, u32[]{:S(2)}) collective-permute-start(f32[2,3,8,128]{3,2,1,0:T(8,128)} %get-tuple-element.10.both), channel_id=1, source_target_pairs={{1,0},{2,1},{3,2},{5,4},{6,5},{7,6},{9,8},{10,9},{11,10},{13,12},{... | collective-permute-start | bytes 73736 | tf_op jit(solution)/shard_map/ppermute | solution.py:550
  27.8 25.8 %copy-start.3 = (f32[8,144,128]{2,1,0:T(8,128)}, f32[8,144,128]{2,1,0:T(8,128)S(1)}, u32[]{:S(2)}) copy-start(f32[8,144,128]{2,1,0:T(8,128)S(1)} %all-to-all-done) | copy-start | bytes 1769476
  27.8 19.7 %all-to-all-start.2 = ((f32[8,144,128]{2,1,0:T(8,128)}), f32[8,144,128]{2,1,0:T(8,128)S(1)}, u32[]{:S(2)}, u32[]{:S(2)}) async-start(f32[8,144,128]{2,1,0:T(8,128)} %bitcast.30), calls=%async_computation.2 | async-start | bytes 1179648 | tf_op jit(solution)/shard_map/all_to_all | solution.py:540
  47.5 17.1 %copy-start.4 = (f32[8,144,128]{2,1,0:T(8,128)}, f32[8,144,128]{2,1,0:T(8,128)S(1)}, u32[]{:S(2)}) copy-start(f32[8,144,128]{2,1,0:T(8,128)S(1)} %all-to-all-done.2) | copy-start | bytes 1769476
  47.5 19.7 %all-to-all-start.3 = ((f32[8,144,128]{2,1,0:T(8,128)}), f32[8,144,128]{2,1,0:T(8,128)S(1)}, u32[]{:S(2)}, u32[]{:S(2)}) async-start(f32[8,144,128]{2,1,0:T(8,128)} %bitcast.8), calls=%async_computation.3 | async-start | bytes 1179648 | tf_op jit(solution)/shard_map/all_to_all | solution.py:540
  51.9 18.3 %collective-permute-start = (f32[1152,128]{1,0:T(8,128)S(1)}, f32[1152,128]{1,0:T(8,128)S(1)}, u32[]{:S(2)}, u32[]{:S(2)}) collective-permute-start(f32[1152,128]{1,0:T(8,128)S(1)} %bitcast.21), channel_id=1, source_target_pairs={{0,1},{1,2},{2,3},{4,5},{5,6},{6,7},{8,9},{9,10},{10,11},{12,13},{... | collective-permute-start | bytes 1769480 | tf_op jit(solution)/shard_map/ppermute | solution.py:545
  53.6 17.9 %collective-permute-start.1 = (f32[1152,128]{1,0:T(8,128)S(1)}, f32[1152,128]{1,0:T(8,128)S(1)}, u32[]{:S(2)}, u32[]{:S(2)}) collective-permute-start(f32[1152,128]{1,0:T(8,128)S(1)} %bitcast.22), channel_id=1, source_target_pairs={{1,0},{2,1},{3,2},{5,4},{6,5},{7,6},{9,8},{10,9},{11,10},{13,12},{... | collective-permute-start | bytes 1769480 | tf_op jit(solution)/shard_map/ppermute | solution.py:546
  59.4 32.5 %collective-permute-start.4 = (f32[1152,128]{1,0:T(8,128)S(1)}, f32[1152,128]{1,0:T(8,128)}, u32[]{:S(2)}, u32[]{:S(2)}) collective-permute-start(f32[1152,128]{1,0:T(8,128)S(1)} %bitcast.24), channel_id=1, source_target_pairs={{0,1},{1,2},{2,3},{4,5},{5,6},{6,7},{8,9},{9,10},{10,11},{12,13},{... | collective-permute-start | bytes 1769480 | tf_op jit(solution)/shard_map/ppermute | solution.py:545
  64.6 27.3 %collective-permute-start.5 = (f32[1152,128]{1,0:T(8,128)S(1)}, f32[1152,128]{1,0:T(8,128)}, u32[]{:S(2)}, u32[]{:S(2)}) collective-permute-start(f32[1152,128]{1,0:T(8,128)S(1)} %bitcast.25), channel_id=1, source_target_pairs={{1,0},{2,1},{3,2},{5,4},{6,5},{7,6},{9,8},{10,9},{11,10},{13,12},{... | collective-permute-start | bytes 1769480 | tf_op jit(solution)/shard_map/ppermute | solution.py:546
  67.2 18.7 %copy-start.5 = (f32[8,144,128]{2,1,0:T(8,128)}, f32[8,144,128]{2,1,0:T(8,128)S(1)}, u32[]{:S(2)}) copy-start(f32[8,144,128]{2,1,0:T(8,128)S(1)} %all-to-all-done.3) | copy-start | bytes 1769476
  67.2 36.9 %collective-permute-start.6 = (f32[1152,128]{1,0:T(8,128)S(1)}, f32[1152,128]{1,0:T(8,128)}, u32[]{:S(2)}, u32[]{:S(2)}) collective-permute-start(f32[1152,128]{1,0:T(8,128)S(1)} %bitcast.27), channel_id=1, source_target_pairs={{0,1},{1,2},{2,3},{4,5},{5,6},{6,7},{8,9},{9,10},{10,11},{12,13},{... | collective-permute-start | bytes 1769480 | tf_op jit(solution)/shard_map/ppermute | solution.py:545
  70.2 33.9 %collective-permute-start.7 = (f32[1152,128]{1,0:T(8,128)S(1)}, f32[1152,128]{1,0:T(8,128)}, u32[]{:S(2)}, u32[]{:S(2)}) collective-permute-start(f32[1152,128]{1,0:T(8,128)S(1)} %bitcast.28), channel_id=1, source_target_pairs={{1,0},{2,1},{3,2},{5,4},{6,5},{7,6},{9,8},{10,9},{11,10},{13,12},{... | collective-permute-start | bytes 1769480 | tf_op jit(solution)/shard_map/ppermute | solution.py:546
  85.9 32.9 %all-to-all-start.1 = ((f32[8,216,128]{2,1,0:T(8,128)}), f32[8,216,128]{2,1,0:T(8,128)S(1)}, u32[]{:S(2)}, u32[]{:S(2)}) async-start(f32[8,216,128]{2,1,0:T(8,128)} %bitcast.20), calls=%async_computation.1 | async-start | bytes 1769472 | tf_op jit(solution)/shard_map/all_to_all | solution.py:540
  104.1 12.2 %copy-start.1 = (f32[1728,128]{1,0:T(8,128)S(1)}, f32[1728,128]{1,0:T(8,128)}, u32[]{:S(2)}) copy-start(f32[1728,128]{1,0:T(8,128)} %get-tuple-element.14) | copy-start | bytes 2654212
  118.8 6.9 %copy-start.7 = (f32[8,128]{1,0:T(8,128)S(1)}, f32[8,128]{1,0:T(8,128)}, u32[]{:S(2)}) copy-start(f32[8,128]{1,0:T(8,128)} %get-tuple-element.17) | copy-start | bytes 12292
  119.8 56.5 %all-to-all-start.4 = ((f32[8,432,128]{2,1,0:T(8,128)}), f32[8,432,128]{2,1,0:T(8,128)S(1)}, u32[]{:S(2)}, u32[]{:S(2)}) async-start(f32[8,432,128]{2,1,0:T(8,128)} %pad_maximum_fusion), calls=%async_computation.4 | async-start | bytes 3538944 | tf_op jit(solution)/shard_map/all_to_all | solution.py:540
  125.8 1.6 collective-permute-start.8
  127.4 4.4 %collective-permute-start.9 = (f32[8,128]{1,0:T(8,128)S(1)}, f32[8,128]{1,0:T(8,128)S(1)}, u32[]{:S(2)}, u32[]{:S(2)}) collective-permute-start(f32[8,128]{1,0:T(8,128)S(1)} %add.69), channel_id=1, source_target_pairs={{0,2},{1,3},{2,0},{3,1},{4,6},{5,7},{6,4},{7,5},{8,10},{9,11},{10,... | collective-permute-start | bytes 12296 | tf_op jit(solution)/shard_map/ppermute | solution.py:530
  131.8 9.5 %collective-permute-start.10 = (f32[8,128]{1,0:T(8,128)S(1)}, f32[8,128]{1,0:T(8,128)S(1)}, u32[]{:S(2)}, u32[]{:S(2)}) collective-permute-start(f32[8,128]{1,0:T(8,128)S(1)} %add.70), channel_id=1, source_target_pairs={{0,4},{4,0},{8,12},{12,8},{16,20},{20,16},{24,28},{28,24},{1,5},{5... | collective-permute-start | bytes 12296 | tf_op jit(solution)/shard_map/ppermute | solution.py:530
  141.3 15.6 %collective-permute-start.11 = (f32[8,128]{1,0:T(8,128)S(1)}, f32[8,128]{1,0:T(8,128)S(1)}, u32[]{:S(2)}, u32[]{:S(2)}) collective-permute-start(f32[8,128]{1,0:T(8,128)S(1)} %add.71), channel_id=1, source_target_pairs={{0,8},{4,12},{8,0},{12,4},{16,24},{20,28},{24,16},{28,20},{1,9},{5... | collective-permute-start | bytes 12296 | tf_op jit(solution)/shard_map/ppermute | solution.py:530
  156.9 11.5 %collective-permute-start.12 = (f32[8,128]{1,0:T(8,128)S(1)}, f32[8,128]{1,0:T(8,128)S(1)}, u32[]{:S(2)}, u32[]{:S(2)}) collective-permute-start(f32[8,128]{1,0:T(8,128)S(1)} %add.72), channel_id=1, source_target_pairs={{0,16},{4,20},{8,24},{12,28},{16,0},{20,4},{24,8},{28,12},{1,17},{... | collective-permute-start | bytes 12296 | tf_op jit(solution)/shard_map/ppermute | solution.py:530
  (6 other events, 9.1 us)

commit v2 on v1

--- a/solution.py
+++ b/solution.py
@@ -167,14 +167,31 @@
     return halo
 
 
-UNROLL = 3
-
-
-def pack_kernel(field, *refs):
+UNROLL = 6
+
+
+GROUP = PARTS // 2
+
+
+def send_halves(half, block, scratch, keep, send, sems):
+    copies = []
+    for member in range(GROUP):
+        to = pl.ds(member * block, block)
+        for n, (goal, which) in enumerate(((keep, half), (send, 1 - half))):
+            start = pl.multiple_of((2 * member + which) * block, 8)
+            source = scratch.at[pl.ds(start, block), :]
+            copies.append(pltpu.make_async_copy(source, goal.at[to, :], sems.at[2 * member + n]))
+    for copy in copies:
+        copy.start()
+    for copy in copies:
+        copy.wait()
+
+
+def pack_kernel(half, field, *refs):
     modes = field.shape[0]
-    out = refs[-1]
-    if len(refs) > 1:
-        mean, ply, both, out = refs
+    keep, send, out, sems = refs[-4:]
+    if len(refs) > 4:
+        mean, ply, both = refs[:3]
         for x in range(SLAB):
             both[0, x] = mean[x]
             both[1, x] = (ply[x] + 1).astype(jnp.float32)
@@ -189,28 +206,35 @@
         return carry
 
     lax.fori_loop(0, modes // UNROLL, body, 0)
+    send_halves(half[0], ROWS * modes, out, keep, send, sems)
 
 
 def estimate(micros):
     return pl.CostEstimate(flops=int(micros * 1e9), bytes_accessed=int(micros * 3e6), transcendentals=0)
 
 
-def pack(field, comp, *stiffness):
+def pack(half, field, comp, *stiffness):
     modes = field.shape[0]
     block = (modes, 1) + field.shape[2:]
     vmem = pl.BlockSpec(memory_space=pltpu.VMEM)
     shapes = [jax.ShapeDtypeStruct((2,) + s.shape, jnp.float32) for s in stiffness[:1]]
-    shapes.append(jax.ShapeDtypeStruct((PARTS * modes * ROWS, LANES), jnp.float32))
+    out_specs = [vmem] * len(shapes) + [pl.BlockSpec(memory_space=pl.ANY)] * 2
+    shapes += [jax.ShapeDtypeStruct((GROUP * modes * ROWS, LANES), jnp.float32)] * 2
     return pl.pallas_call(
         pack_kernel,
         grid=(1,),
         out_shape=shapes,
-        in_specs=[pl.BlockSpec(block, lambda i: (0, comp, 0, 0, 0))] + [vmem] * len(stiffness),
-        out_specs=[vmem] * len(shapes),
+        in_specs=[pl.BlockSpec(memory_space=pltpu.SMEM), pl.BlockSpec(block, lambda i: (0, comp, 0, 0, 0))]
+        + [vmem] * len(stiffness),
+        out_specs=out_specs,
+        scratch_shapes=[
+            pltpu.VMEM((PARTS * modes * ROWS, LANES), jnp.float32),
+            pltpu.SemaphoreType.DMA((PARTS,)),
+        ],
         compiler_params=pltpu.CompilerParams(vmem_limit_bytes=VMEM),
         cost_estimate=estimate(2.5),
         name="pack",
-    )(field, *stiffness)
+    )(half, field, *stiffness)
 
 
 def stiffness_kernel(place, before, both, after, ply_stiffness, fields, wide):
@@ -376,8 +400,8 @@
 
 
 def apply_kernel(
-    place, own, before, after, scale, unscale, to_even, to_all, fields, fibre, so_far,
-    out, partial, field, first, second, mixed, flux, scaled, acc, faces, *, comp,
+    place, half, own, before, after, scale, unscale, to_even, to_all, fields, fibre, so_far,
+    keep, send, partial, out, field, first, second, mixed, flux, scaled, acc, faces, sems, *, comp,
 ):
     slots = scale.shape[0]
     here = place[0]
@@ -402,19 +426,21 @@
     scratch = (mixed, flux, scaled, acc, faces, inside, to_even, to_all, here)
     apply_operator(field, first, *scratch, TILES, INNER)
     apply_operator(first, second, *scratch, INNER, SLAB)
+    for p in range(SLAB):
+        out[pl.ds(p, slots, stride=2 * SLAB), :] = first[:, tile_cols(p)] * unscale[...]
+        out[pl.ds(p + SLAB, slots, stride=2 * SLAB), :] = second[:, tile_cols(p)] * unscale[...]
+    send_halves(half[0], slots // PARTS * 2 * SLAB, out, keep, send, sems)
     sums = [jnp.zeros((1, LANES), jnp.float32)] * 5
     for p in range(SLAB):
         b = load(own, p)
         q = first[:, tile_cols(p)] * unscale[...]
         w = second[:, tile_cols(p)] * unscale[...]
-        out[pl.ds(p, slots, stride=2 * SLAB), :] = q
-        out[pl.ds(p + SLAB, slots, stride=2 * SLAB), :] = w
         for n, (one, two) in enumerate(((b, b), (b, q), (q, q), (b, w), (q, w))):
             sums[n] = sums[n] + jnp.sum(one * two, axis=0, keepdims=True)
     partial[...] = so_far[...] + jnp.concatenate(sums + [jnp.zeros((3, LANES), jnp.float32)], axis=0)
 
 
-def apply_twice(comp, place, own, before, after, tables, fields, fibre, so_far):
+def apply_twice(comp, place, half, own, before, after, tables, fields, fibre, so_far):
     scale, unscale, to_even, to_all = tables
     slots = scale.shape[0]
     vmem = pl.BlockSpec(memory_space=pltpu.VMEM)
@@ -422,13 +448,12 @@
     f32 = lambda *shape: pltpu.VMEM(shape, jnp.float32)
     return pl.pallas_call(
         functools.partial(apply_kernel, comp=comp),
-        out_shape=[
-            jax.ShapeDtypeStruct((slots * 2 * SLAB, LANES), jnp.float32),
-            jax.ShapeDtypeStruct((8, LANES), jnp.float32),
-        ],
-        in_specs=[smem] + [vmem] * 8 + [smem, vmem],
-        out_specs=[vmem, vmem],
+        out_shape=[jax.ShapeDtypeStruct((slots * SLAB, LANES), jnp.float32)] * 2
+        + [jax.ShapeDtypeStruct((8, LANES), jnp.float32)],
+        in_specs=[smem, smem] + [vmem] * 8 + [smem, vmem],
+        out_specs=[pl.BlockSpec(memory_space=pl.ANY)] * 2 + [vmem],
         scratch_shapes=[
+            f32(slots * 2 * SLAB, LANES),
             f32(slots, TILES * LANES),
             f32(slots, INNER * LANES),
             f32(slots, SLAB * LANES),
@@ -437,38 +462,37 @@
             f32(FULL, INNER * LANES),
             f32(slots, INNER * LANES),
             f32(6 * FACE, TILES * LANES),
+            pltpu.SemaphoreType.DMA((PARTS,)),
         ],
         compiler_params=pltpu.CompilerParams(vmem_limit_bytes=VMEM),
         cost_estimate=estimate(15),
         name="apply_twice",
-    )(place, own, before, after, scale, unscale, to_even, to_all, fields, fibre, so_far)
+    )(place, half, own, before, after, scale, unscale, to_even, to_all, fields, fibre, so_far)
 
 
 def finish(field, images, coefs):
     modes = field.shape[0]
     per_part = modes * 2 * SLAB
-    steps = 4
-
-    def kernel(field, first_images, other_images, coefs, solution_field, residual):
+    steps = 2
+
+    def kernel(field, *refs):
+        images, coefs, solution_field, residual = refs[:COMPS], refs[COMPS], refs[-2], refs[-1]
         first = pl.program_id(0) * (modes // steps)
 
         def body(step, carry):
-            for inner in range(UNROLL):
-                mode = step * UNROLL + inner
+            for inner in range(SLAB):
+                mode = step * SLAB + inner
                 base = (first + mode) * 2 * SLAB
                 for comp in range(COMPS):
-                    source, stride, start = first_images, per_part, base
-                    if comp > 0:
-                        source, stride, start = other_images, 2 * per_part, base + (comp - 1) * per_part
                     for p in range(SLAB):
                         b = field[mode, comp, p]
-                        q = swap_back(source[pl.ds(start + p, PARTS, stride=stride), :])
-                        w = swap_back(source[pl.ds(start + p + SLAB, PARTS, stride=stride), :])
+                        q = swap_back(images[comp][pl.ds(base + p, PARTS, stride=per_part), :])
+                        w = swap_back(images[comp][pl.ds(base + p + SLAB, PARTS, stride=per_part), :])
                         solution_field[mode, comp, p] = coefs[0] * b + coefs[1] * q
                         residual[mode, comp, p] = b + coefs[2] * q + coefs[3] * w
             return carry
 
-        lax.fori_loop(0, modes // steps // UNROLL, body, 0)
+        lax.fori_loop(0, modes // steps // SLAB, body, 0)
 
     block = pl.BlockSpec((modes // steps,) + field.shape[1:], lambda i: (i, 0, 0, 0, 0))
     whole = pl.BlockSpec(memory_space=pltpu.VMEM)
@@ -476,7 +500,7 @@
         kernel,
         grid=(steps,),
         out_shape=[jax.ShapeDtypeStruct(field.shape, jnp.float32)] * 2,
-        in_specs=[block, whole, whole, pl.BlockSpec(memory_space=pltpu.SMEM)],
+        in_specs=[block] + [whole] * COMPS + [pl.BlockSpec(memory_space=pltpu.SMEM)],
         out_specs=[block, block],
         compiler_params=pltpu.CompilerParams(vmem_limit_bytes=VMEM),
         cost_estimate=estimate(6),
@@ -486,7 +510,8 @@
 
 def mode_tables(coupling_table, slots):
     lower, upper, variable, code = (coupling_table[:, n] for n in range(4))
-    slot = jnp.arange(slots, dtype=jnp.int32)
+    order = jnp.arange(slots, dtype=jnp.int32).reshape(2, GROUP, slots // PARTS)
+    slot = order.transpose(1, 0, 2).reshape(slots)
     is_lower = lower[:, None] == slot
     is_upper = upper[:, None] == slot
     degree = jnp.sum(jnp.where(is_upper, code[:, None], 0), axis=0)
@@ -537,27 +562,39 @@
     devices = lax.axis_size("space")
     up = [(i, i + 1) for i in range(devices - 1)]
     down = [(j, i) for i, j in up]
-    swap = lambda v: lax.all_to_all(v, "mode", 0, 0, tiled=True)
-    (first,) = pack(right_side, 0)
-    both, second = pack(right_side, 1, mean_stiffness, ply_map)
-    (third,) = pack(right_side, 2)
-    own = [swap(p) for p in (first, second, third)]
+    index = lax.axis_index("mode").astype(jnp.int32)
+    half = index // GROUP
+    place = (2 * (index % GROUP) + half).reshape(1)
+    groups = [list(range(GROUP)), list(range(GROUP, PARTS))]
+
+    def exchange(keep, send):
+        came = lax.ppermute(send, "mode", [(i, i ^ GROUP) for i in range(PARTS)])
+        keep, came = (v.reshape(GROUP, -1, LANES) for v in (keep, came))
+        both = jnp.where(
+            half == 0, jnp.concatenate([keep, came], axis=1), jnp.concatenate([came, keep], axis=1)
+        )
+        both = lax.all_to_all(both, "mode", 0, 0, axis_index_groups=groups, tiled=True)
+        return both.reshape(-1, LANES)
+
+    half_row = half.reshape(1)
+    first = pack(half_row, right_side, 0)
+    both, *second = pack(half_row, right_side, 1, mean_stiffness, ply_map)
+    third = pack(half_row, right_side, 2)
+    own = [exchange(*p) for p in (first, second, third)]
     before = [lax.ppermute(p, "space", up) for p in own]
     after = [lax.ppermute(p, "space", down) for p in own]
     tables = mode_tables(coupling_table, slots)
-    place = lax.axis_index("mode").astype(jnp.int32).reshape(1)
     both_before = lax.ppermute(both, "space", up)
     both_after = lax.ppermute(both, "space", down)
     fields = stiffness_fields(place, both_before, both, both_after, ply_stiffness)
     partial = jnp.zeros((8, LANES), jnp.float32)
-    outs = []
+    images = []
     for comp in range(COMPS):
-        out, partial = apply_twice(
-            comp, place, own[comp], before[comp], after[comp], tables, fields, fibre_weights, partial
+        keep, send, partial = apply_twice(
+            comp, place, half_row, own[comp], before[comp], after[comp], tables, fields, fibre_weights,
+            partial,
         )
-        outs.append(out)
-    halves = [o.reshape(PARTS, -1, LANES) for o in outs[1:]]
-    images = [swap(outs[0]), swap(jnp.concatenate(halves, axis=1).reshape(-1, LANES))]
+        images.append(exchange(keep, send))
     bb, bq, qq, bw, qw = (jnp.sum(all_sum(partial)[n]) for n in range(5))
     step_one = bb / bq
     norm = bb - 2.0 * step_one * bq + step_one * step_one * qq

time: 185 us -> 249 us (1.35)
  waiting for transfers between devices: 51.9 us -> 95.9 us
  starting transfers between devices: 53.9 us -> 66.7 us
  other arithmetic: 7.22 us -> 14.2 us
    ppermute x0 -> x6, waiting for transfers between devices: none -> 72.3 us  [exchange(): came = lax.ppermute(send, 'mode', [(i, i ^ GROUP) for i in range(PARTS)])]
    ppermute x5, waiting for transfers between devices: 31.7 us -> 11.2 us  [all_sum(): lax.ppermute(value, axis, [(i, i ^ bit) for i in range(devices)])]
    ppermute x0 -> x6, starting transfers between devices: none -> 15.5 us  [exchange(): came = lax.ppermute(send, 'mode', [(i, i ^ GROUP) for i in range(PARTS)])]
    select_n x0 -> x6, other arithmetic: none -> 9.07 us  [exchange(): jnp.where(half == 0, jnp.concatenate([keep, came], axis=1), jnp.concatena...]
    all_to_all x5 -> x6, waiting for transfers between devices: 20.1 us -> 12.4 us  [exchange(): lax.all_to_all(both, 'mode', 0, 0, axis_index_groups=groups, tiled=True)]
    all_to_all x5 -> x6, starting transfers between devices: 26.5 us -> 23.3 us  [exchange(): lax.all_to_all(both, 'mode', 0, 0, axis_index_groups=groups, tiled=True)]
    concatenate x1 -> x0, other arithmetic: 2.5 us -> none  [transposed(): jnp.concatenate(halves, axis=1).reshape(-1, LANES)]
  transfers between devices with their start and end apart: 18 -> 25, of which waited for: 8 -> 11; matrix products, arithmetic and copies ran while one was open for 6% -> 7% of each run, Pallas kernels for 25% -> 19%
where the time goes in v2:
time: 249 us; the launch traced here: 248 us
  waiting for transfers between devices  95.9 us (39%)
  starting transfers between devices  66.7 us (27%)
  Pallas kernels  57.3 us (23%)
  other arithmetic  14.2 us (6%)
  between operations  7.38 us (3%)
  local copies, waits for them, and re-layouts  4.99 us (2%)
    ppermute x6, waiting for transfers between devices, exchange(): came = lax.ppermute(send, 'mode', [(i, i ^ GROUP) for i in range(PARTS)])  72.3 us
    pallas_call x3, Pallas kernels, apply_twice(): pl.pallas_call(functools.partial(apply_kernel, comp=comp), out_shape=[jax...  38.8 us
    all_to_all x6, starting transfers between devices, exchange(): lax.all_to_all(both, 'mode', 0, 0, axis_index_groups=groups, tiled=True)  23.3 us
    ppermute x6, starting transfers between devices, exchange(): came = lax.ppermute(send, 'mode', [(i, i ^ GROUP) for i in range(PARTS)])  15.5 us
    all_to_all x6, waiting for transfers between devices, exchange(): lax.all_to_all(both, 'mode', 0, 0, axis_index_groups=groups, tiled=True)  12.4 us
    ppermute x5, waiting for transfers between devices, all_sum(): lax.ppermute(value, axis, [(i, i ^ bit) for i in range(devices)])  11.2 us
    ppermute x3, starting transfers between devices, transposed(): before = [lax.ppermute(p, 'space', up) for p in own]  11 us
    pallas_call x3, Pallas kernels, pack(): pl.pallas_call(pack_kernel, grid=(1,), out_shape=shapes, in_specs=[pl.Blo...  10.5 us
  transfers between devices with their start and end apart: 25, of which 11 were waited for; matrix products, arithmetic and copies ran while one was open for 7% of the time, Pallas kernels for 19%

profile of v2, /device:TPU:0, one launch (start us, length us, event | category | flops | bytes accessed | tf_op | source)
XLA Modules:
  0.0 248.2 jit_solution(13337931185699088912)
XLA Ops:
  0.6 3.9 %pack.4 = (f32[2,3,8,128]{3,2,1,0:T(8,128)}, f32[576,128]{1,0:T(8,128)}, f32[576,128]{1,0:T(8,128)}) custom-call(s32[1]{0:T(128)} %bitcast.1.half, f32[36,3,3,8,128]{4,3,2,1,0:T(8,128)} %field.7, f32[3,8,128]{2,1,0:T(8,128)} %refs_0_.1, s32[3,8,128]{2,1,0:T(8,128)} %refs_1_.1), custom_call_target="tpu_custom_call" | custom-call | flops 2500000000 | bytes 7500000 | tf_op jit(solution)/shard_map/pack/pallas_call | solution.py:223
  8.4 3.3 %pack.3 = (f32[576,128]{1,0:T(8,128)}, f32[576,128]{1,0:T(8,128)}) custom-call(s32[1]{0:T(128)} %bitcast.1.half, f32[36,3,3,8,128]{4,3,2,1,0:T(8,128)} %field.7), custom_call_target="tpu_custom_call" | custom-call | flops 2500000000 | bytes 7500000 | tf_op jit(solution)/shard_map/pack/pallas_call | solution.py:223
  11.7 3.5 %collective-permute-start = (f32[576,128]{1,0:T(8,128)}, f32[576,128]{1,0:T(8,128)S(1)}, u32[]{:S(2)}, u32[]{:S(2)}) collective-permute-start(f32[576,128]{1,0:T(8,128)} %get-tuple-element.19), channel_id=1, source_target_pairs={{0,16},{4,20},{8,24},{12,28},{16,0},{20,4},{24,8},{28,12},{1,17},{... | collective-permute-start | bytes 884744 | tf_op jit(solution)/shard_map/ppermute | solution.py:571
  15.3 3.3 %pack.5 = (f32[576,128]{1,0:T(8,128)}, f32[576,128]{1,0:T(8,128)}) custom-call(s32[1]{0:T(128)} %bitcast.1.half, f32[36,3,3,8,128]{4,3,2,1,0:T(8,128)} %field.7), custom_call_target="tpu_custom_call" | custom-call | flops 2500000000 | bytes 7500000 | tf_op jit(solution)/shard_map/pack/pallas_call | solution.py:223
  22.9 17.8 %collective-permute-done = f32[576,128]{1,0:T(8,128)S(1)} collective-permute-done((f32[576,128]{1,0:T(8,128)}, f32[576,128]{1,0:T(8,128)S(1)}, u32[]{:S(2)}, u32[]{:S(2)}) %collective-permute-start) | collective-permute-done | bytes 294944 | tf_op jit(solution)/shard_map/ppermute | solution.py:571
  41.6 4.7 %all-to-all-start = ((f32[4,288,128]{2,1,0:T(8,128)}), f32[4,288,128]{2,1,0:T(8,128)S(1)}, u32[]{:S(2)}, u32[]{:S(2)}) async-start(f32[4,288,128]{2,1,0:T(8,128)} %maximum_select_fusion.3), calls=%async_computation | async-start | bytes 1179648 | tf_op jit(solution)/shard_map/all_to_all | solution.py:576
  49.2 11.8 %all-to-all-done = f32[4,288,128]{2,1,0:T(8,128)S(1)} async-done(((f32[4,288,128]{2,1,0:T(8,128)}), f32[4,288,128]{2,1,0:T(8,128)S(1)}, u32[]{:S(2)}, u32[]{:S(2)}) %all-to-all-start) | async-done | bytes 589856 | tf_op jit(solution)/shard_map/all_to_all | solution.py:576
  61.1 3.5 %all-to-all-start.2 = ((f32[4,288,128]{2,1,0:T(8,128)}), f32[4,288,128]{2,1,0:T(8,128)S(1)}, u32[]{:S(2)}, u32[]{:S(2)}) async-start(f32[4,288,128]{2,1,0:T(8,128)} %maximum_select_fusion.4), calls=%async_computation.2 | async-start | bytes 1179648 | tf_op jit(solution)/shard_map/all_to_all | solution.py:576
  73.9 3.5 %all-to-all-start.4 = ((f32[4,288,128]{2,1,0:T(8,128)}), f32[4,288,128]{2,1,0:T(8,128)S(1)}, u32[]{:S(2)}, u32[]{:S(2)}) async-start(f32[4,288,128]{2,1,0:T(8,128)} %maximum_select_fusion.5), calls=%async_computation.4 | async-start | bytes 1179648 | tf_op jit(solution)/shard_map/all_to_all | solution.py:576
  77.3 5.4 %collective-permute-start.7 = (f32[1152,128]{1,0:T(8,128)S(1)}, f32[1152,128]{1,0:T(8,128)}, u32[]{:S(2)}, u32[]{:S(2)}) collective-permute-start(f32[1152,128]{1,0:T(8,128)S(1)} %bitcast.27), channel_id=1, source_target_pairs={{0,1},{1,2},{2,3},{4,5},{5,6},{6,7},{8,9},{9,10},{10,11},{12,13},{... | collective-permute-start | bytes 1769480 | tf_op jit(solution)/shard_map/ppermute | solution.py:584
  86.4 13.0 %apply_twice.3 = (f32[864,128]{1,0:T(8,128)}, f32[864,128]{1,0:T(8,128)}, f32[8,128]{1,0:T(8,128)}) custom-call(s32[1]{0:T(128)} %bitcast.place, s32[1]{0:T(128)} %bitcast.1.half, f32[1152,128]{1,0:T(8,128)} %bitcast.32, f32[1152,128]{1,0:T(8,128)} %copy-done.11, f32[1152,128]{1,0:T(8,128)} %copy-done.12, f32[288,128]{1,0:T(8,128)} %broadcast_in_dim.95.scale, ...), custom_call_target="tpu_custom_call" | custom-call | flops 15000000512 | bytes 45000000 | tf_op jit(solution)/shard_map/apply_twice/pallas_call | solution.py:449
  102.3 3.5 %collective-permute-start.11 = (f32[1152,128]{1,0:T(8,128)S(1)}, f32[1152,128]{1,0:T(8,128)S(1)}, u32[]{:S(2)}, u32[]{:S(2)}) collective-permute-start(f32[1152,128]{1,0:T(8,128)S(1)} %bitcast.33), channel_id=1, source_target_pairs={{0,1},{1,2},{2,3},{4,5},{5,6},{6,7},{8,9},{9,10},{10,11},{12,13},{... | collective-permute-start | bytes 1769480 | tf_op jit(solution)/shard_map/ppermute | solution.py:584
  107.2 14.8 %collective-permute-done.5 = f32[864,128]{1,0:T(8,128)S(1)} collective-permute-done((f32[864,128]{1,0:T(8,128)}, f32[864,128]{1,0:T(8,128)S(1)}, u32[]{:S(2)}, u32[]{:S(2)}) %collective-permute-start.5) | collective-permute-done | bytes 442400 | tf_op jit(solution)/shard_map/ppermute | solution.py:571
  124.2 4.3 %all-to-all-start.1 = ((f32[4,432,128]{2,1,0:T(8,128)}), f32[4,432,128]{2,1,0:T(8,128)S(1)}, u32[]{:S(2)}, u32[]{:S(2)}) async-start(f32[4,432,128]{2,1,0:T(8,128)} %maximum_select_fusion), calls=%async_computation.1 | async-start | bytes 1769472 | tf_op jit(solution)/shard_map/all_to_all | solution.py:576
  128.6 12.9 %apply_twice.4 = (f32[864,128]{1,0:T(8,128)}, f32[864,128]{1,0:T(8,128)}, f32[8,128]{1,0:T(8,128)}) custom-call(s32[1]{0:T(128)} %bitcast.place, s32[1]{0:T(128)} %bitcast.1.half, f32[1152,128]{1,0:T(8,128)} %bitcast.29, f32[1152,128]{1,0:T(8,128)} %collective-permute-done.7.before, f32[1152,128]{1,0:T(8,128)} %collective-permute-done.8.after, ...), custom_call_target="tpu_custom_call" | custom-call | flops 15000000512 | bytes 45000000 | tf_op jit(solution)/shard_map/apply_twice/pallas_call | solution.py:449
  141.5 3.3 %collective-permute-start.9 = (f32[864,128]{1,0:T(8,128)}, f32[864,128]{1,0:T(8,128)S(1)}, u32[]{:S(2)}, u32[]{:S(2)}) collective-permute-start(f32[864,128]{1,0:T(8,128)} %get-tuple-element.27), channel_id=1, source_target_pairs={{0,16},{4,20},{8,24},{12,28},{16,0},{20,4},{24,8},{28,12},{1,17},{... | collective-permute-start | bytes 1327112 | tf_op jit(solution)/shard_map/ppermute | solution.py:571
  144.9 19.9 %collective-permute-done.9 = f32[864,128]{1,0:T(8,128)S(1)} collective-permute-done((f32[864,128]{1,0:T(8,128)}, f32[864,128]{1,0:T(8,128)S(1)}, u32[]{:S(2)}, u32[]{:S(2)}) %collective-permute-start.9) | collective-permute-done | bytes 442400 | tf_op jit(solution)/shard_map/ppermute | solution.py:571
  166.9 3.7 %all-to-all-start.3 = ((f32[4,432,128]{2,1,0:T(8,128)}), f32[4,432,128]{2,1,0:T(8,128)S(1)}, u32[]{:S(2)}, u32[]{:S(2)}) async-start(f32[4,432,128]{2,1,0:T(8,128)} %maximum_select_fusion.1), calls=%async_computation.3 | async-start | bytes 1769472 | tf_op jit(solution)/shard_map/all_to_all | solution.py:576
  171.6 12.9 %apply_twice.5 = (f32[864,128]{1,0:T(8,128)}, f32[864,128]{1,0:T(8,128)}, f32[8,128]{1,0:T(8,128)}) custom-call(s32[1]{0:T(128)} %bitcast.place, s32[1]{0:T(128)} %bitcast.1.half, f32[1152,128]{1,0:T(8,128)} %bitcast.35, f32[1152,128]{1,0:T(8,128)} %copy-done.13, f32[1152,128]{1,0:T(8,128)} %copy-done.14, f32[288,128]{1,0:T(8,128)} %broadcast_in_dim.95.scale, ...), custom_call_target="tpu_custom_call" | custom-call | flops 15000000512 | bytes 45000000 | tf_op jit(solution)/shard_map/apply_twice/pallas_call | solution.py:449
  187.4 19.8 %collective-permute-done.13 = f32[864,128]{1,0:T(8,128)S(1)} collective-permute-done((f32[864,128]{1,0:T(8,128)}, f32[864,128]{1,0:T(8,128)S(1)}, u32[]{:S(2)}, u32[]{:S(2)}) %collective-permute-start.13) | collective-permute-done | bytes 442400 | tf_op jit(solution)/shard_map/ppermute | solution.py:571
  209.4 3.5 %all-to-all-start.5 = ((f32[4,432,128]{2,1,0:T(8,128)}), f32[4,432,128]{2,1,0:T(8,128)S(1)}, u32[]{:S(2)}, u32[]{:S(2)}) async-start(f32[4,432,128]{2,1,0:T(8,128)} %maximum_select_fusion.2), calls=%async_computation.5 | async-start | bytes 1769472 | tf_op jit(solution)/shard_map/all_to_all | solution.py:576
  220.0 4.7 %collective-permute-done.16 = f32[8,128]{1,0:T(8,128)S(1)} collective-permute-done((f32[8,128]{1,0:T(8,128)S(1)}, f32[8,128]{1,0:T(8,128)S(1)}, u32[]{:S(2)}, u32[]{:S(2)}) %collective-permute-start.16) | collective-permute-done | bytes 4128 | tf_op jit(solution)/shard_map/ppermute | solution.py:555
  228.4 3.3 %collective-permute-start.18 = (f32[8,128]{1,0:T(8,128)S(1)}, f32[8,128]{1,0:T(8,128)S(1)}, u32[]{:S(2)}, u32[]{:S(2)}) collective-permute-start(f32[8,128]{1,0:T(8,128)S(1)} %add.104), channel_id=1, source_target_pairs={{0,16},{4,20},{8,24},{12,28},{16,0},{20,4},{24,8},{28,12},{1,17},{... | collective-permute-start | bytes 12296 | tf_op jit(solution)/shard_map/ppermute | solution.py:555
  241.9 6.3 %finish.1 = (f32[36,3,3,8,128]{4,3,2,1,0:T(8,128)}, f32[36,3,3,8,128]{4,3,2,1,0:T(8,128)}) custom-call(f32[36,3,3,8,128]{4,3,2,1,0:T(8,128)} %field.7, f32[1728,128]{1,0:T(8,128)} %bitcast.24, f32[1728,128]{1,0:T(8,128)} %bitcast.25, f32[1728,128]{1,0:T(8,128)} %bitcast.26, f32[4]{0:T(128)} %pad_maximum_fusion.2.refs_3_), custom_call_target="tpu_custom_call" | custom-call | flops 6000000000 | bytes 18000000 | tf_op jit(solution)/shard_map/finish/pallas_call | solution.py:499
  (104 shorter events, 54.0 us)
Async XLA Ops:
  4.6 65.5 %collective-permute-start.3 = (f32[2,3,8,128]{3,2,1,0:T(8,128)}, f32[2,3,8,128]{3,2,1,0:T(8,128)S(1)}, u32[]{:S(2)}, u32[]{:S(2)}) collective-permute-start(f32[2,3,8,128]{3,2,1,0:T(8,128)} %get-tuple-element.20.both), channel_id=1, source_target_pairs={{0,1},{1,2},{2,3},{4,5},{5,6},{6,7},{8,9},{9,10},{10,11},{12,13},{... | collective-permute-start | bytes 73736 | tf_op jit(solution)/shard_map/ppermute | solution.py:587
  7.1 63.0 %collective-permute-start.4 = (f32[2,3,8,128]{3,2,1,0:T(8,128)}, f32[2,3,8,128]{3,2,1,0:T(8,128)S(1)}, u32[]{:S(2)}, u32[]{:S(2)}) collective-permute-start(f32[2,3,8,128]{3,2,1,0:T(8,128)} %get-tuple-element.20.both), channel_id=1, source_target_pairs={{1,0},{2,1},{3,2},{5,4},{6,5},{7,6},{9,8},{10,9},{11,10},{13,12},{... | collective-permute-start | bytes 73736 | tf_op jit(solution)/shard_map/ppermute | solution.py:588
  11.7 29.0 %collective-permute-start = (f32[576,128]{1,0:T(8,128)}, f32[576,128]{1,0:T(8,128)S(1)}, u32[]{:S(2)}, u32[]{:S(2)}) collective-permute-start(f32[576,128]{1,0:T(8,128)} %get-tuple-element.19), channel_id=1, source_target_pairs={{0,16},{4,20},{8,24},{12,28},{16,0},{20,4},{24,8},{28,12},{1,17},{... | collective-permute-start | bytes 884744 | tf_op jit(solution)/shard_map/ppermute | solution.py:571
  15.2 33.2 %collective-permute-start.6 = (f32[576,128]{1,0:T(8,128)S(1)}, f32[576,128]{1,0:T(8,128)S(1)}, u32[]{:S(2)}, u32[]{:S(2)}) collective-permute-start(f32[576,128]{1,0:T(8,128)S(1)} %copy-done.15), channel_id=1, source_target_pairs={{0,16},{4,20},{8,24},{12,28},{16,0},{20,4},{24,8},{28,12},{1,17},{... | collective-permute-start | bytes 884744 | tf_op jit(solution)/shard_map/ppermute | solution.py:571
  18.6 53.8 %collective-permute-start.10 = (f32[576,128]{1,0:T(8,128)}, f32[576,128]{1,0:T(8,128)S(1)}, u32[]{:S(2)}, u32[]{:S(2)}) collective-permute-start(f32[576,128]{1,0:T(8,128)} %get-tuple-element.29), channel_id=1, source_target_pairs={{0,16},{4,20},{8,24},{12,28},{16,0},{20,4},{24,8},{28,12},{1,17},{... | collective-permute-start | bytes 884744 | tf_op jit(solution)/shard_map/ppermute | solution.py:571
  41.6 19.5 %all-to-all-start = ((f32[4,288,128]{2,1,0:T(8,128)}), f32[4,288,128]{2,1,0:T(8,128)S(1)}, u32[]{:S(2)}, u32[]{:S(2)}) async-start(f32[4,288,128]{2,1,0:T(8,128)} %maximum_select_fusion.3), calls=%async_computation | async-start | bytes 1179648 | tf_op jit(solution)/shard_map/all_to_all | solution.py:576
  61.1 12.8 %all-to-all-start.2 = ((f32[4,288,128]{2,1,0:T(8,128)}), f32[4,288,128]{2,1,0:T(8,128)S(1)}, u32[]{:S(2)}, u32[]{:S(2)}) async-start(f32[4,288,128]{2,1,0:T(8,128)} %maximum_select_fusion.4), calls=%async_computation.2 | async-start | bytes 1179648 | tf_op jit(solution)/shard_map/all_to_all | solution.py:576
  65.6 18.5 %collective-permute-start.1 = (f32[1152,128]{1,0:T(8,128)S(1)}, f32[1152,128]{1,0:T(8,128)S(1)}, u32[]{:S(2)}, u32[]{:S(2)}) collective-permute-start(f32[1152,128]{1,0:T(8,128)S(1)} %bitcast.30), channel_id=1, source_target_pairs={{0,1},{1,2},{2,3},{4,5},{5,6},{6,7},{8,9},{9,10},{10,11},{12,13},{... | collective-permute-start | bytes 1769480 | tf_op jit(solution)/shard_map/ppermute | solution.py:584
  67.6 16.4 %collective-permute-start.2 = (f32[1152,128]{1,0:T(8,128)S(1)}, f32[1152,128]{1,0:T(8,128)S(1)}, u32[]{:S(2)}, u32[]{:S(2)}) collective-permute-start(f32[1152,128]{1,0:T(8,128)S(1)} %bitcast.31), channel_id=1, source_target_pairs={{1,0},{2,1},{3,2},{5,4},{6,5},{7,6},{9,8},{10,9},{11,10},{13,12},{... | collective-permute-start | bytes 1769480 | tf_op jit(solution)/shard_map/ppermute | solution.py:585
  73.9 28.4 %all-to-all-start.4 = ((f32[4,288,128]{2,1,0:T(8,128)}), f32[4,288,128]{2,1,0:T(8,128)S(1)}, u32[]{:S(2)}, u32[]{:S(2)}) async-start(f32[4,288,128]{2,1,0:T(8,128)} %maximum_select_fusion.5), calls=%async_computation.4 | async-start | bytes 1179648 | tf_op jit(solution)/shard_map/all_to_all | solution.py:576
  77.3 51.2 %collective-permute-start.7 = (f32[1152,128]{1,0:T(8,128)S(1)}, f32[1152,128]{1,0:T(8,128)}, u32[]{:S(2)}, u32[]{:S(2)}) collective-permute-start(f32[1152,128]{1,0:T(8,128)S(1)} %bitcast.27), channel_id=1, source_target_pairs={{0,1},{1,2},{2,3},{4,5},{5,6},{6,7},{8,9},{9,10},{10,11},{12,13},{... | collective-permute-start | bytes 1769480 | tf_op jit(solution)/shard_map/ppermute | solution.py:584
  82.8 45.8 %collective-permute-start.8 = (f32[1152,128]{1,0:T(8,128)S(1)}, f32[1152,128]{1,0:T(8,128)}, u32[]{:S(2)}, u32[]{:S(2)}) collective-permute-start(f32[1152,128]{1,0:T(8,128)S(1)} %bitcast.28), channel_id=1, source_target_pairs={{1,0},{2,1},{3,2},{5,4},{6,5},{7,6},{9,8},{10,9},{11,10},{13,12},{... | collective-permute-start | bytes 1769480 | tf_op jit(solution)/shard_map/ppermute | solution.py:585
  99.4 22.7 %collective-permute-start.5 = (f32[864,128]{1,0:T(8,128)}, f32[864,128]{1,0:T(8,128)S(1)}, u32[]{:S(2)}, u32[]{:S(2)}) collective-permute-start(f32[864,128]{1,0:T(8,128)} %get-tuple-element.22), channel_id=1, source_target_pairs={{0,16},{4,20},{8,24},{12,28},{16,0},{20,4},{24,8},{28,12},{1,17},{... | collective-permute-start | bytes 1327112 | tf_op jit(solution)/shard_map/ppermute | solution.py:571
  102.3 68.4 %collective-permute-start.11 = (f32[1152,128]{1,0:T(8,128)S(1)}, f32[1152,128]{1,0:T(8,128)S(1)}, u32[]{:S(2)}, u32[]{:S(2)}) collective-permute-start(f32[1152,128]{1,0:T(8,128)S(1)} %bitcast.33), channel_id=1, source_target_pairs={{0,1},{1,2},{2,3},{4,5},{5,6},{6,7},{8,9},{9,10},{10,11},{12,13},{... | collective-permute-start | bytes 1769480 | tf_op jit(solution)/shard_map/ppermute | solution.py:584
  105.8 64.9 %collective-permute-start.12 = (f32[1152,128]{1,0:T(8,128)S(1)}, f32[1152,128]{1,0:T(8,128)S(1)}, u32[]{:S(2)}, u32[]{:S(2)}) collective-permute-start(f32[1152,128]{1,0:T(8,128)S(1)} %bitcast.34), channel_id=1, source_target_pairs={{1,0},{2,1},{3,2},{5,4},{6,5},{7,6},{9,8},{10,9},{11,10},{13,12},{... | collective-permute-start | bytes 1769480 | tf_op jit(solution)/shard_map/ppermute | solution.py:585
  124.2 42.6 %all-to-all-start.1 = ((f32[4,432,128]{2,1,0:T(8,128)}), f32[4,432,128]{2,1,0:T(8,128)S(1)}, u32[]{:S(2)}, u32[]{:S(2)}) async-start(f32[4,432,128]{2,1,0:T(8,128)} %maximum_select_fusion), calls=%async_computation.1 | async-start | bytes 1769472 | tf_op jit(solution)/shard_map/all_to_all | solution.py:576
  141.5 23.2 %collective-permute-start.9 = (f32[864,128]{1,0:T(8,128)}, f32[864,128]{1,0:T(8,128)S(1)}, u32[]{:S(2)}, u32[]{:S(2)}) collective-permute-start(f32[864,128]{1,0:T(8,128)} %get-tuple-element.27), channel_id=1, source_target_pairs={{0,16},{4,20},{8,24},{12,28},{16,0},{20,4},{24,8},{28,12},{1,17},{... | collective-permute-start | bytes 1327112 | tf_op jit(solution)/shard_map/ppermute | solution.py:571
  166.9 42.5 %all-to-all-start.3 = ((f32[4,432,128]{2,1,0:T(8,128)}), f32[4,432,128]{2,1,0:T(8,128)S(1)}, u32[]{:S(2)}, u32[]{:S(2)}) async-start(f32[4,432,128]{2,1,0:T(8,128)} %maximum_select_fusion.1), calls=%async_computation.3 | async-start | bytes 1769472 | tf_op jit(solution)/shard_map/all_to_all | solution.py:576
  184.6 22.6 %collective-permute-start.13 = (f32[864,128]{1,0:T(8,128)}, f32[864,128]{1,0:T(8,128)S(1)}, u32[]{:S(2)}, u32[]{:S(2)}) collective-permute-start(f32[864,128]{1,0:T(8,128)} %get-tuple-element.32), channel_id=1, source_target_pairs={{0,16},{4,20},{8,24},{12,28},{16,0},{20,4},{24,8},{28,12},{1,17},{... | collective-permute-start | bytes 1327112 | tf_op jit(solution)/shard_map/ppermute | solution.py:571
  209.4 31.6 %all-to-all-start.5 = ((f32[4,432,128]{2,1,0:T(8,128)}), f32[4,432,128]{2,1,0:T(8,128)S(1)}, u32[]{:S(2)}, u32[]{:S(2)}) async-start(f32[4,432,128]{2,1,0:T(8,128)} %maximum_select_fusion.2), calls=%async_computation.5 | async-start | bytes 1769472 | tf_op jit(solution)/shard_map/all_to_all | solution.py:576
  214.2 4.0 %collective-permute-start.15 = (f32[8,128]{1,0:T(8,128)S(1)}, f32[8,128]{1,0:T(8,128)S(1)}, u32[]{:S(2)}, u32[]{:S(2)}) collective-permute-start(f32[8,128]{1,0:T(8,128)S(1)} %add.101), channel_id=1, source_target_pairs={{0,2},{1,3},{2,0},{3,1},{4,6},{5,7},{6,4},{7,5},{8,10},{9,11},{10,... | collective-permute-start | bytes 12296 | tf_op jit(solution)/shard_map/ppermute | solution.py:555
  218.1 6.7 %collective-permute-start.16 = (f32[8,128]{1,0:T(8,128)S(1)}, f32[8,128]{1,0:T(8,128)S(1)}, u32[]{:S(2)}, u32[]{:S(2)}) collective-permute-start(f32[8,128]{1,0:T(8,128)S(1)} %add.102), channel_id=1, source_target_pairs={{0,4},{4,0},{8,12},{12,8},{16,20},{20,16},{24,28},{28,24},{1,5},{5... | collective-permute-start | bytes 12296 | tf_op jit(solution)/shard_map/ppermute | solution.py:555
  224.8 3.6 %collective-permute-start.17 = (f32[8,128]{1,0:T(8,128)S(1)}, f32[8,128]{1,0:T(8,128)S(1)}, u32[]{:S(2)}, u32[]{:S(2)}) collective-permute-start(f32[8,128]{1,0:T(8,128)S(1)} %add.103), channel_id=1, source_target_pairs={{0,8},{4,12},{8,0},{12,4},{16,24},{20,28},{24,16},{28,20},{1,9},{5... | collective-permute-start | bytes 12296 | tf_op jit(solution)/shard_map/ppermute | solution.py:555
  228.4 4.9 %collective-permute-start.18 = (f32[8,128]{1,0:T(8,128)S(1)}, f32[8,128]{1,0:T(8,128)S(1)}, u32[]{:S(2)}, u32[]{:S(2)}) collective-permute-start(f32[8,128]{1,0:T(8,128)S(1)} %add.104), channel_id=1, source_target_pairs={{0,16},{4,20},{8,24},{12,28},{16,0},{20,4},{24,8},{28,12},{1,17},{... | collective-permute-start | bytes 12296 | tf_op jit(solution)/shard_map/ppermute | solution.py:555
  (19 other events, 162.2 us)

commit v3 on v1

--- a/solution.py
+++ b/solution.py
@@ -167,14 +167,17 @@
     return halo
 
 
-UNROLL = 3
+UNROLL = 6
+
+
+ORDER = (0, 2, 4, 6, 1, 3, 5, 7)
 
 
 def pack_kernel(field, *refs):
     modes = field.shape[0]
     out = refs[-1]
-    if len(refs) > 1:
-        mean, ply, both, out = refs
+    if len(refs) == 4:
+        mean, ply, both = refs[:3]
         for x in range(SLAB):
             both[0, x] = mean[x]
             both[1, x] = (ply[x] + 1).astype(jnp.float32)
@@ -195,7 +198,7 @@
     return pl.CostEstimate(flops=int(micros * 1e9), bytes_accessed=int(micros * 3e6), transcendentals=0)
 
 
-def pack(field, comp, *stiffness):
+def pack(field, comp, stiffness=(), after=()):
     modes = field.shape[0]
     block = (modes, 1) + field.shape[2:]
     vmem = pl.BlockSpec(memory_space=pltpu.VMEM)
@@ -205,12 +208,14 @@
         pack_kernel,
         grid=(1,),
         out_shape=shapes,
-        in_specs=[pl.BlockSpec(block, lambda i: (0, comp, 0, 0, 0))] + [vmem] * len(stiffness),
+        in_specs=[pl.BlockSpec(block, lambda i: (0, comp, 0, 0, 0))]
+        + [vmem] * len(stiffness)
+        + [pl.BlockSpec(memory_space=pl.ANY)] * len(after),
         out_specs=[vmem] * len(shapes),
         compiler_params=pltpu.CompilerParams(vmem_limit_bytes=VMEM),
         cost_estimate=estimate(2.5),
         name="pack",
-    )(field, *stiffness)
+    )(field, *stiffness, *after)
 
 
 def stiffness_kernel(place, before, both, after, ply_stiffness, fields, wide):
@@ -444,49 +449,48 @@
     )(place, own, before, after, scale, unscale, to_even, to_all, fields, fibre, so_far)
 
 
-def finish(field, images, coefs):
+def finish_kernel(field, image, coefs, *refs):
     modes = field.shape[0]
+    solution_field, residual = refs[-2:]
     per_part = modes * 2 * SLAB
-    steps = 4
-
-    def kernel(field, first_images, other_images, coefs, solution_field, residual):
-        first = pl.program_id(0) * (modes // steps)
-
-        def body(step, carry):
-            for inner in range(UNROLL):
-                mode = step * UNROLL + inner
-                base = (first + mode) * 2 * SLAB
-                for comp in range(COMPS):
-                    source, stride, start = first_images, per_part, base
-                    if comp > 0:
-                        source, stride, start = other_images, 2 * per_part, base + (comp - 1) * per_part
-                    for p in range(SLAB):
-                        b = field[mode, comp, p]
-                        q = swap_back(source[pl.ds(start + p, PARTS, stride=stride), :])
-                        w = swap_back(source[pl.ds(start + p + SLAB, PARTS, stride=stride), :])
-                        solution_field[mode, comp, p] = coefs[0] * b + coefs[1] * q
-                        residual[mode, comp, p] = b + coefs[2] * q + coefs[3] * w
-            return carry
-
-        lax.fori_loop(0, modes // steps // UNROLL, body, 0)
-
-    block = pl.BlockSpec((modes // steps,) + field.shape[1:], lambda i: (i, 0, 0, 0, 0))
-    whole = pl.BlockSpec(memory_space=pltpu.VMEM)
+
+    def body(step, carry):
+        for inner in range(UNROLL):
+            mode = step * UNROLL + inner
+            for p in range(SLAB):
+                row = mode * 2 * SLAB + p
+                b = field[mode, 0, p]
+                q = swap_back(image[pl.ds(row, PARTS, stride=per_part), :])
+                w = swap_back(image[pl.ds(row + SLAB, PARTS, stride=per_part), :])
+                solution_field[mode, 0, p] = coefs[0] * b + coefs[1] * q
+                residual[mode, 0, p] = b + coefs[2] * q + coefs[3] * w
+        return carry
+
+    lax.fori_loop(0, modes // UNROLL, body, 0)
+
+
+def finish(field, comp, image, coefs, so_far):
+    block = pl.BlockSpec((field.shape[0], 1) + field.shape[2:], lambda i: (0, comp, 0, 0, 0))
+    vmem = pl.BlockSpec(memory_space=pltpu.VMEM)
     return pl.pallas_call(
-        kernel,
-        grid=(steps,),
+        finish_kernel,
+        grid=(1,),
         out_shape=[jax.ShapeDtypeStruct(field.shape, jnp.float32)] * 2,
-        in_specs=[block, whole, whole, pl.BlockSpec(memory_space=pltpu.SMEM)],
+        in_specs=[block, vmem, pl.BlockSpec(memory_space=pltpu.SMEM)]
+        + [pl.BlockSpec(memory_space=pl.ANY)] * len(so_far),
         out_specs=[block, block],
+        input_output_aliases={3 + n: n for n in range(len(so_far))},
         compiler_params=pltpu.CompilerParams(vmem_limit_bytes=VMEM),
-        cost_estimate=estimate(6),
+        cost_estimate=estimate(2.5),
         name="finish",
-    )(field, *images, coefs)
+    )(field, image, coefs, *so_far)
 
 
 def mode_tables(coupling_table, slots):
     lower, upper, variable, code = (coupling_table[:, n] for n in range(4))
-    slot = jnp.arange(slots, dtype=jnp.int32)
+    within = jnp.arange(slots // PARTS, dtype=jnp.int32)
+    first_modes = jnp.array(ORDER, jnp.int32) * (slots // PARTS)
+    slot = (first_modes[:, None] + within).reshape(slots)
     is_lower = lower[:, None] == slot
     is_upper = upper[:, None] == slot
     degree = jnp.sum(jnp.where(is_upper, code[:, None], 0), axis=0)
@@ -537,27 +541,33 @@
     devices = lax.axis_size("space")
     up = [(i, i + 1) for i in range(devices - 1)]
     down = [(j, i) for i, j in up]
-    swap = lambda v: lax.all_to_all(v, "mode", 0, 0, tiled=True)
+    index = lax.axis_index("mode").astype(jnp.int32)
+    place = jnp.sum(jnp.where(jnp.array(ORDER) == index, jnp.arange(PARTS, dtype=jnp.int32), 0)).reshape(1)
+
+    def swap(rows):
+        return lax.all_to_all(rows, "mode", 0, 0, axis_index_groups=[list(ORDER)], tiled=True)
+
+    def halo(rows):
+        return lax.ppermute(rows, "space", up), lax.ppermute(rows, "space", down)
+
     (first,) = pack(right_side, 0)
-    both, second = pack(right_side, 1, mean_stiffness, ply_map)
-    (third,) = pack(right_side, 2)
-    own = [swap(p) for p in (first, second, third)]
-    before = [lax.ppermute(p, "space", up) for p in own]
-    after = [lax.ppermute(p, "space", down) for p in own]
+    both, second = pack(right_side, 1, (mean_stiffness, ply_map))
+    own = [swap(first), swap(second)]
+    halos = [halo(rows) for rows in own]
+    (third,) = pack(right_side, 2, (), halos[0])
+    own.append(swap(third))
+    halos.append(halo(own[2]))
     tables = mode_tables(coupling_table, slots)
-    place = lax.axis_index("mode").astype(jnp.int32).reshape(1)
     both_before = lax.ppermute(both, "space", up)
     both_after = lax.ppermute(both, "space", down)
     fields = stiffness_fields(place, both_before, both, both_after, ply_stiffness)
     partial = jnp.zeros((8, LANES), jnp.float32)
-    outs = []
+    images = []
     for comp in range(COMPS):
         out, partial = apply_twice(
-            comp, place, own[comp], before[comp], after[comp], tables, fields, fibre_weights, partial
+            comp, place, own[comp], *halos[comp], tables, fields, fibre_weights, partial
         )
-        outs.append(out)
-    halves = [o.reshape(PARTS, -1, LANES) for o in outs[1:]]
-    images = [swap(outs[0]), swap(jnp.concatenate(halves, axis=1).reshape(-1, LANES))]
+        images.append(swap(out))
     bb, bq, qq, bw, qw = (jnp.sum(all_sum(partial)[n]) for n in range(5))
     step_one = bb / bq
     norm = bb - 2.0 * step_one * bq + step_one * step_one * qq
@@ -573,7 +583,10 @@
             step_one * step_two,
         ]
     )
-    return tuple(finish(right_side, images, coefs))
+    outputs = ()
+    for comp in range(COMPS):
+        outputs = finish(right_side, comp, images[comp], coefs, outputs)
+    return tuple(outputs)
 
 
 def on_device(right_side, mean_stiffness, ply_stiffness, fibre_weights, ply_map, coupling_table):

time: 185 us -> 185 us (level)
  starting transfers between devices: 53.9 us -> 48.7 us
  Pallas kernels: 57.1 us -> 61.7 us
    all_to_all x5 -> x6, waiting for transfers between devices: 20.1 us -> 40.2 us  [swap(): lax.all_to_all(rows, 'mode', 0, 0, axis_index_groups=[list(ORDER)], tiled...]
    ppermute x5, waiting for transfers between devices: 31.7 us -> 12.1 us  [all_sum(): lax.ppermute(value, axis, [(i, i ^ bit) for i in range(devices)])]
    pallas_call x1 -> x3, Pallas kernels: 6.81 us -> 11.3 us  [finish(): pl.pallas_call(finish_kernel, grid=(1,), out_shape=[jax.ShapeDtypeStruct(...]
    concatenate x1 -> x0, other arithmetic: 2.5 us -> none  [transposed(): jnp.concatenate(halves, axis=1).reshape(-1, LANES)]
    pallas_call x3, Pallas kernels: 12.1 us -> 9.75 us  [pack(): pl.pallas_call(pack_kernel, grid=(1,), out_shape=shapes, in_specs=[pl.Blo...]
    ppermute x5, starting transfers between devices: 10.9 us -> 8.7 us  [all_sum(): lax.ppermute(value, axis, [(i, i ^ bit) for i in range(devices)])]
    all_to_all x5 -> x6, starting transfers between devices: 26.5 us -> 24.4 us  [swap(): lax.all_to_all(rows, 'mode', 0, 0, axis_index_groups=[list(ORDER)], tiled...]
    ppermute x6, starting transfers between devices: 13.8 us -> 11.9 us  [halo(): return (lax.ppermute(rows, 'space', up), lax.ppermute(rows, 'space', down))]
  transfers between devices with their start and end apart: 18 -> 19, of which waited for: 8 -> 10; matrix products, arithmetic and copies ran while one was open for 6% -> 5% of each run, Pallas kernels for 25% -> 30%
where the time goes in v3:
time: 185 us; the launch traced here: 184 us
  Pallas kernels  61.7 us (33%)
  waiting for transfers between devices  52.3 us (28%)
  starting transfers between devices  48.7 us (26%)
  between operations  7.55 us (4%)
  local copies, waits for them, and re-layouts  6.26 us (3%)
  other arithmetic  5.74 us (3%)
    all_to_all x6, waiting for transfers between devices, swap(): lax.all_to_all(rows, 'mode', 0, 0, axis_index_groups=[list(ORDER)], tiled...  40.2 us
    pallas_call x3, Pallas kernels, apply_twice(): pl.pallas_call(functools.partial(apply_kernel, comp=comp), out_shape=[jax...  38.4 us
    all_to_all x6, starting transfers between devices, swap(): lax.all_to_all(rows, 'mode', 0, 0, axis_index_groups=[list(ORDER)], tiled...  24.4 us
    ppermute x5, waiting for transfers between devices, all_sum(): lax.ppermute(value, axis, [(i, i ^ bit) for i in range(devices)])  12.1 us
    ppermute x6, starting transfers between devices, halo(): return (lax.ppermute(rows, 'space', up), lax.ppermute(rows, 'space', down))  11.9 us
    pallas_call x3, Pallas kernels, finish(): pl.pallas_call(finish_kernel, grid=(1,), out_shape=[jax.ShapeDtypeStruct(...  11.3 us
    pallas_call x3, Pallas kernels, pack(): pl.pallas_call(pack_kernel, grid=(1,), out_shape=shapes, in_specs=[pl.Blo...  9.75 us
    ppermute x5, starting transfers between devices, all_sum(): lax.ppermute(value, axis, [(i, i ^ bit) for i in range(devices)])  8.7 us
  transfers between devices with their start and end apart: 19, of which 10 were waited for; matrix products, arithmetic and copies ran while one was open for 5% of the time, Pallas kernels for 30%

profile of v3, /device:TPU:0, one launch (start us, length us, event | category | flops | bytes accessed | tf_op | source)
XLA Modules:
  0.0 184.0 jit_solution(12071793021829824157)
XLA Ops:
  0.6 3.3 %pack.5 = (f32[2,3,8,128]{3,2,1,0:T(8,128)}, f32[1152,128]{1,0:T(8,128)}) custom-call(f32[36,3,3,8,128]{4,3,2,1,0:T(8,128)} %field.11, f32[3,8,128]{2,1,0:T(8,128)} %refs_0_.1, s32[3,8,128]{2,1,0:T(8,128)} %refs_1_.1), custom_call_target="tpu_custom_call" | custom-call | flops 2500000000 | bytes 7500000 | tf_op jit(solution)/shard_map/pack/pallas_call | solution.py:207
  7.7 3.2 %pack.3 = f32[1152,128]{1,0:T(8,128)} custom-call(f32[36,3,3,8,128]{4,3,2,1,0:T(8,128)} %field.11), custom_call_target="tpu_custom_call" | custom-call | flops 2500000000 | bytes 7500000 | tf_op jit(solution)/shard_map/pack/pallas_call | solution.py:207
  10.9 6.6 %all-to-all-start = ((f32[8,144,128]{2,1,0:T(8,128)}), f32[8,144,128]{2,1,0:T(8,128)S(1)}, u32[]{:S(2)}, u32[]{:S(2)}) async-start(f32[8,144,128]{2,1,0:T(8,128)} %bitcast.32), calls=%async_computation | async-start | bytes 1179648 | tf_op jit(solution)/shard_map/all_to_all | solution.py:548
  20.0 14.5 %all-to-all-done = f32[8,144,128]{2,1,0:T(8,128)S(1)} async-done(((f32[8,144,128]{2,1,0:T(8,128)}), f32[8,144,128]{2,1,0:T(8,128)S(1)}, u32[]{:S(2)}, u32[]{:S(2)}) %all-to-all-start) | async-done | bytes 589856 | tf_op jit(solution)/shard_map/all_to_all | solution.py:548
  34.6 3.5 %all-to-all-start.2 = ((f32[8,144,128]{2,1,0:T(8,128)}), f32[8,144,128]{2,1,0:T(8,128)S(1)}, u32[]{:S(2)}, u32[]{:S(2)}) async-start(f32[8,144,128]{2,1,0:T(8,128)} %bitcast.5), calls=%async_computation.2 | async-start | bytes 1179648 | tf_op jit(solution)/shard_map/all_to_all | solution.py:548
  39.1 3.0 %collective-permute-start = (f32[1152,128]{1,0:T(8,128)S(1)}, f32[1152,128]{1,0:T(8,128)S(1)}, u32[]{:S(2)}, u32[]{:S(2)}) collective-permute-start(f32[1152,128]{1,0:T(8,128)S(1)} %bitcast.23), channel_id=1, source_target_pairs={{0,1},{1,2},{2,3},{4,5},{5,6},{6,7},{8,9},{9,10},{10,11},{12,13},{... | collective-permute-start | bytes 1769480 | tf_op jit(solution)/shard_map/ppermute | solution.py:551
  49.1 7.0 %all-to-all-done.2 = f32[8,144,128]{2,1,0:T(8,128)S(1)} async-done(((f32[8,144,128]{2,1,0:T(8,128)}), f32[8,144,128]{2,1,0:T(8,128)S(1)}, u32[]{:S(2)}, u32[]{:S(2)}) %all-to-all-start.2) | async-done | bytes 589856 | tf_op jit(solution)/shard_map/all_to_all | solution.py:548
  61.2 3.3 %pack.4 = f32[1152,128]{1,0:T(8,128)} custom-call(f32[36,3,3,8,128]{4,3,2,1,0:T(8,128)} %field.11, f32[1152,128]{1,0:T(8,128)} %copy-done.9, f32[1152,128]{1,0:T(8,128)} %copy-done.10), custom_call_target="tpu_custom_call" | custom-call | flops 2500000000 | bytes 7500000 | tf_op jit(solution)/shard_map/pack/pallas_call | solution.py:207
  64.4 3.5 %all-to-all-start.1 = ((f32[8,144,128]{2,1,0:T(8,128)}), f32[8,144,128]{2,1,0:T(8,128)S(1)}, u32[]{:S(2)}, u32[]{:S(2)}) async-start(f32[8,144,128]{2,1,0:T(8,128)} %bitcast.33), calls=%async_computation.1 | async-start | bytes 1179648 | tf_op jit(solution)/shard_map/all_to_all | solution.py:548
  70.1 12.8 %apply_twice.3 = (f32[1728,128]{1,0:T(8,128)}, f32[8,128]{1,0:T(8,128)}) custom-call(s32[1]{0:T(128)} %bitcast.place, f32[1152,128]{1,0:T(8,128)} %bitcast.25, f32[1152,128]{1,0:T(8,128)} %copy-done.9, f32[1152,128]{1,0:T(8,128)} %copy-done.10, f32[288,128]{1,0:T(8,128)} %broadcast_in_dim.102.scale, f32[288,128]{1,0:T(8,128)} %broadcast_in_dim.103.unscale, ...), custom_call_target="tpu_custom_call" | custom-call | flops 15000000512 | bytes 45000000 | tf_op jit(solution)/shard_map/apply_twice/pallas_call | solution.py:428
  82.9 3.1 %all-to-all-done.1 = f32[8,144,128]{2,1,0:T(8,128)S(1)} async-done(((f32[8,144,128]{2,1,0:T(8,128)}), f32[8,144,128]{2,1,0:T(8,128)S(1)}, u32[]{:S(2)}, u32[]{:S(2)}) %all-to-all-start.1) | async-done | bytes 589856 | tf_op jit(solution)/shard_map/all_to_all | solution.py:548
  86.0 3.6 %all-to-all-start.5 = ((f32[8,216,128]{2,1,0:T(8,128)}), f32[8,216,128]{2,1,0:T(8,128)S(1)}, u32[]{:S(2)}, u32[]{:S(2)}) async-start(f32[8,216,128]{2,1,0:T(8,128)} %bitcast.21), calls=%async_computation.5 | async-start | bytes 1769472 | tf_op jit(solution)/shard_map/all_to_all | solution.py:548
  94.7 12.8 %apply_twice.4 = (f32[1728,128]{1,0:T(8,128)}, f32[8,128]{1,0:T(8,128)}) custom-call(s32[1]{0:T(128)} %bitcast.place, f32[1152,128]{1,0:T(8,128)} %bitcast.28, f32[1152,128]{1,0:T(8,128)} %copy-done.11, f32[1152,128]{1,0:T(8,128)} %collective-permute-done.7.after, f32[288,128]{1,0:T(8,128)} %broadcast_in_dim.102.scale, ...), custom_call_target="tpu_custom_call" | custom-call | flops 15000000512 | bytes 45000000 | tf_op jit(solution)/shard_map/apply_twice/pallas_call | solution.py:428
  107.5 5.6 %all-to-all-done.5 = f32[8,216,128]{2,1,0:T(8,128)S(1)} async-done(((f32[8,216,128]{2,1,0:T(8,128)}), f32[8,216,128]{2,1,0:T(8,128)S(1)}, u32[]{:S(2)}, u32[]{:S(2)}) %all-to-all-start.5) | async-done | bytes 884768 | tf_op jit(solution)/shard_map/all_to_all | solution.py:548
  113.1 3.6 %all-to-all-start.4 = ((f32[8,216,128]{2,1,0:T(8,128)}), f32[8,216,128]{2,1,0:T(8,128)S(1)}, u32[]{:S(2)}, u32[]{:S(2)}) async-start(f32[8,216,128]{2,1,0:T(8,128)} %bitcast.22), calls=%async_computation.4 | async-start | bytes 1769472 | tf_op jit(solution)/shard_map/all_to_all | solution.py:548
  116.7 12.8 %apply_twice.5 = (f32[1728,128]{1,0:T(8,128)}, f32[8,128]{1,0:T(8,128)}) custom-call(s32[1]{0:T(128)} %bitcast.place, f32[1152,128]{1,0:T(8,128)} %bitcast.31, f32[1152,128]{1,0:T(8,128)} %collective-permute-done.2.before, f32[1152,128]{1,0:T(8,128)} %collective-permute-done.3.after, f32[288,128]{1,0:T(8,128)} %broadcast_in_dim.102.scale, ...), custom_call_target="tpu_custom_call" | custom-call | flops 15000000512 | bytes 45000000 | tf_op jit(solution)/shard_map/apply_twice/pallas_call | solution.py:428
  129.5 9.9 %all-to-all-done.4 = f32[8,216,128]{2,1,0:T(8,128)S(1)} async-done(((f32[8,216,128]{2,1,0:T(8,128)}), f32[8,216,128]{2,1,0:T(8,128)S(1)}, u32[]{:S(2)}, u32[]{:S(2)}) %all-to-all-start.4) | async-done | bytes 884768 | tf_op jit(solution)/shard_map/all_to_all | solution.py:548
  139.5 3.6 %all-to-all-start.3 = ((f32[8,216,128]{2,1,0:T(8,128)}), f32[8,216,128]{2,1,0:T(8,128)S(1)}, u32[]{:S(2)}, u32[]{:S(2)}) async-start(f32[8,216,128]{2,1,0:T(8,128)} %bitcast.19), calls=%async_computation.3 | async-start | bytes 1769472 | tf_op jit(solution)/shard_map/all_to_all | solution.py:548
  144.3 3.6 %collective-permute-done.9 = f32[8,128]{1,0:T(8,128)S(1)} collective-permute-done((f32[8,128]{1,0:T(8,128)S(1)}, f32[8,128]{1,0:T(8,128)S(1)}, u32[]{:S(2)}, u32[]{:S(2)}) %collective-permute-start.9) | collective-permute-done | bytes 4128 | tf_op jit(solution)/shard_map/ppermute | solution.py:534
  156.1 4.5 %collective-permute-start.12 = (f32[8,128]{1,0:T(8,128)S(1)}, f32[8,128]{1,0:T(8,128)S(1)}, u32[]{:S(2)}, u32[]{:S(2)}) collective-permute-start(f32[8,128]{1,0:T(8,128)S(1)} %add.100), channel_id=1, source_target_pairs={{0,16},{4,20},{8,24},{12,28},{16,0},{20,4},{24,8},{28,12},{1,17},{... | collective-permute-start | bytes 12296 | tf_op jit(solution)/shard_map/ppermute | solution.py:534
  160.6 3.2 %collective-permute-done.12 = f32[8,128]{1,0:T(8,128)S(1)} collective-permute-done((f32[8,128]{1,0:T(8,128)S(1)}, f32[8,128]{1,0:T(8,128)S(1)}, u32[]{:S(2)}, u32[]{:S(2)}) %collective-permute-start.12) | collective-permute-done | bytes 4128 | tf_op jit(solution)/shard_map/ppermute | solution.py:534
  171.8 3.8 %finish.3 = (f32[36,3,3,8,128]{4,3,2,1,0:T(8,128)}, f32[36,3,3,8,128]{4,3,2,1,0:T(8,128)}) custom-call(f32[36,3,3,8,128]{4,3,2,1,0:T(8,128)} %field.11, f32[1728,128]{1,0:T(8,128)} %bitcast.17, f32[4]{0:T(128)} %pad_maximum_fusion.2.coefs), custom_call_target="tpu_custom_call" | custom-call | flops 2500000000 | bytes 7500000 | tf_op jit(solution)/shard_map/finish/pallas_call | solution.py:475
  175.6 3.8 %finish.4 = (f32[36,3,3,8,128]{4,3,2,1,0:T(8,128)}, f32[36,3,3,8,128]{4,3,2,1,0:T(8,128)}) custom-call(f32[36,3,3,8,128]{4,3,2,1,0:T(8,128)} %field.11, f32[1728,128]{1,0:T(8,128)} %bitcast.18, f32[4]{0:T(128)} %pad_maximum_fusion.2.coefs, f32[36,3,3,8,128]{4,3,2,1,0:T(8,128)} %get-tuple-element.22.refs_0_, ...), custom_call_target="tpu_custom_call", output_to_operand_aliasing={{0}: (3, {}), {1}: (4, {})} | custom-call | flops 2500000000 | bytes 7500000 | tf_op jit(solution)/shard_map/finish/pallas_call | solution.py:475
  180.3 3.8 %finish.5 = (f32[36,3,3,8,128]{4,3,2,1,0:T(8,128)}, f32[36,3,3,8,128]{4,3,2,1,0:T(8,128)}) custom-call(f32[36,3,3,8,128]{4,3,2,1,0:T(8,128)} %field.11, f32[1728,128]{1,0:T(8,128)} %bitcast.20, f32[4]{0:T(128)} %pad_maximum_fusion.2.coefs, f32[36,3,3,8,128]{4,3,2,1,0:T(8,128)} %get-tuple-element.24.refs_0_, ...), custom_call_target="tpu_custom_call", output_to_operand_aliasing={{0}: (3, {}), {1}: (4, {})} | custom-call | flops 2500000000 | bytes 7500000 | tf_op jit(solution)/shard_map/finish/pallas_call | solution.py:475
  (83 shorter events, 38.2 us)
Async XLA Ops:
  3.9 13.7 %copy-start.8 = (s32[8]{0:T(128)S(1)}, s32[8]{0:T(128)}, u32[]{:S(2)}) copy-start(s32[8]{0:T(128)} %constant.42) | copy-start | bytes 100
  3.9 13.8 %copy-start.6 = (s32[660,4]{0,1:T(4,128)S(1)}, s32[660,4]{0,1:T(4,128)}, u32[]{:S(2)}) copy-start(s32[660,4]{0,1:T(4,128)} %param.13) | copy-start | bytes 31684
  3.9 42.4 %collective-permute-start.4 = (f32[2,3,8,128]{3,2,1,0:T(8,128)}, f32[2,3,8,128]{3,2,1,0:T(8,128)S(1)}, u32[]{:S(2)}, u32[]{:S(2)}) collective-permute-start(f32[2,3,8,128]{3,2,1,0:T(8,128)} %get-tuple-element.14.both), channel_id=1, source_target_pairs={{0,1},{1,2},{2,3},{4,5},{5,6},{6,7},{8,9},{9,10},{10,11},{12,13},{... | collective-permute-start | bytes 73736 | tf_op jit(solution)/shard_map/ppermute | solution.py:561
  6.4 39.9 %collective-permute-start.5 = (f32[2,3,8,128]{3,2,1,0:T(8,128)}, f32[2,3,8,128]{3,2,1,0:T(8,128)S(1)}, u32[]{:S(2)}, u32[]{:S(2)}) collective-permute-start(f32[2,3,8,128]{3,2,1,0:T(8,128)} %get-tuple-element.14.both), channel_id=1, source_target_pairs={{1,0},{2,1},{3,2},{5,4},{6,5},{7,6},{9,8},{10,9},{11,10},{13,12},{... | collective-permute-start | bytes 73736 | tf_op jit(solution)/shard_map/ppermute | solution.py:562
  10.9 23.6 %all-to-all-start = ((f32[8,144,128]{2,1,0:T(8,128)}), f32[8,144,128]{2,1,0:T(8,128)S(1)}, u32[]{:S(2)}, u32[]{:S(2)}) async-start(f32[8,144,128]{2,1,0:T(8,128)} %bitcast.32), calls=%async_computation | async-start | bytes 1179648 | tf_op jit(solution)/shard_map/all_to_all | solution.py:548
  34.6 21.6 %all-to-all-start.2 = ((f32[8,144,128]{2,1,0:T(8,128)}), f32[8,144,128]{2,1,0:T(8,128)S(1)}, u32[]{:S(2)}, u32[]{:S(2)}) async-start(f32[8,144,128]{2,1,0:T(8,128)} %bitcast.5), calls=%async_computation.2 | async-start | bytes 1179648 | tf_op jit(solution)/shard_map/all_to_all | solution.py:548
  39.1 20.4 %collective-permute-start = (f32[1152,128]{1,0:T(8,128)S(1)}, f32[1152,128]{1,0:T(8,128)S(1)}, u32[]{:S(2)}, u32[]{:S(2)}) collective-permute-start(f32[1152,128]{1,0:T(8,128)S(1)} %bitcast.23), channel_id=1, source_target_pairs={{0,1},{1,2},{2,3},{4,5},{5,6},{6,7},{8,9},{9,10},{10,11},{12,13},{... | collective-permute-start | bytes 1769480 | tf_op jit(solution)/shard_map/ppermute | solution.py:551
  42.1 17.4 %collective-permute-start.1 = (f32[1152,128]{1,0:T(8,128)S(1)}, f32[1152,128]{1,0:T(8,128)S(1)}, u32[]{:S(2)}, u32[]{:S(2)}) collective-permute-start(f32[1152,128]{1,0:T(8,128)S(1)} %bitcast.24), channel_id=1, source_target_pairs={{1,0},{2,1},{3,2},{5,4},{6,5},{7,6},{9,8},{10,9},{11,10},{13,12},{... | collective-permute-start | bytes 1769480 | tf_op jit(solution)/shard_map/ppermute | solution.py:551
  56.2 37.7 %collective-permute-start.6 = (f32[1152,128]{1,0:T(8,128)S(1)}, f32[1152,128]{1,0:T(8,128)S(1)}, u32[]{:S(2)}, u32[]{:S(2)}) collective-permute-start(f32[1152,128]{1,0:T(8,128)S(1)} %bitcast.26), channel_id=1, source_target_pairs={{0,1},{1,2},{2,3},{4,5},{5,6},{6,7},{8,9},{9,10},{10,11},{12,13},{... | collective-permute-start | bytes 1769480 | tf_op jit(solution)/shard_map/ppermute | solution.py:551
  58.2 35.6 %collective-permute-start.7 = (f32[1152,128]{1,0:T(8,128)S(1)}, f32[1152,128]{1,0:T(8,128)}, u32[]{:S(2)}, u32[]{:S(2)}) collective-permute-start(f32[1152,128]{1,0:T(8,128)S(1)} %bitcast.27), channel_id=1, source_target_pairs={{1,0},{2,1},{3,2},{5,4},{6,5},{7,6},{9,8},{10,9},{11,10},{13,12},{... | collective-permute-start | bytes 1769480 | tf_op jit(solution)/shard_map/ppermute | solution.py:551
  64.4 21.5 %all-to-all-start.1 = ((f32[8,144,128]{2,1,0:T(8,128)}), f32[8,144,128]{2,1,0:T(8,128)S(1)}, u32[]{:S(2)}, u32[]{:S(2)}) async-start(f32[8,144,128]{2,1,0:T(8,128)} %bitcast.33), calls=%async_computation.1 | async-start | bytes 1179648 | tf_op jit(solution)/shard_map/all_to_all | solution.py:548
  86.0 21.5 %copy-start.5 = (f32[8,144,128]{2,1,0:T(8,128)}, f32[8,144,128]{2,1,0:T(8,128)S(1)}, u32[]{:S(2)}) copy-start(f32[8,144,128]{2,1,0:T(8,128)S(1)} %all-to-all-done.1) | copy-start | bytes 1769476
  86.0 27.2 %all-to-all-start.5 = ((f32[8,216,128]{2,1,0:T(8,128)}), f32[8,216,128]{2,1,0:T(8,128)S(1)}, u32[]{:S(2)}, u32[]{:S(2)}) async-start(f32[8,216,128]{2,1,0:T(8,128)} %bitcast.21), calls=%async_computation.5 | async-start | bytes 1769472 | tf_op jit(solution)/shard_map/all_to_all | solution.py:548
  89.5 27.2 %collective-permute-start.2 = (f32[1152,128]{1,0:T(8,128)S(1)}, f32[1152,128]{1,0:T(8,128)}, u32[]{:S(2)}, u32[]{:S(2)}) collective-permute-start(f32[1152,128]{1,0:T(8,128)S(1)} %bitcast.29), channel_id=1, source_target_pairs={{0,1},{1,2},{2,3},{4,5},{5,6},{6,7},{8,9},{9,10},{10,11},{12,13},{... | collective-permute-start | bytes 1769480 | tf_op jit(solution)/shard_map/ppermute | solution.py:551
  92.4 24.3 %collective-permute-start.3 = (f32[1152,128]{1,0:T(8,128)S(1)}, f32[1152,128]{1,0:T(8,128)}, u32[]{:S(2)}, u32[]{:S(2)}) collective-permute-start(f32[1152,128]{1,0:T(8,128)S(1)} %bitcast.30), channel_id=1, source_target_pairs={{1,0},{2,1},{3,2},{5,4},{6,5},{7,6},{9,8},{10,9},{11,10},{13,12},{... | collective-permute-start | bytes 1769480 | tf_op jit(solution)/shard_map/ppermute | solution.py:551
  113.1 16.4 %copy-start = (f32[8,216,128]{2,1,0:T(8,128)}, f32[8,216,128]{2,1,0:T(8,128)S(1)}, u32[]{:S(2)}) copy-start(f32[8,216,128]{2,1,0:T(8,128)S(1)} %all-to-all-done.5) | copy-start | bytes 2654212
  113.1 26.3 %all-to-all-start.4 = ((f32[8,216,128]{2,1,0:T(8,128)}), f32[8,216,128]{2,1,0:T(8,128)S(1)}, u32[]{:S(2)}, u32[]{:S(2)}) async-start(f32[8,216,128]{2,1,0:T(8,128)} %bitcast.22), calls=%async_computation.4 | async-start | bytes 1769472 | tf_op jit(solution)/shard_map/all_to_all | solution.py:548
  139.5 36.1 %copy-start.1 = (f32[8,216,128]{2,1,0:T(8,128)}, f32[8,216,128]{2,1,0:T(8,128)S(1)}, u32[]{:S(2)}) copy-start(f32[8,216,128]{2,1,0:T(8,128)S(1)} %all-to-all-done.4) | copy-start | bytes 2654212
  139.5 39.9 %all-to-all-start.3 = ((f32[8,216,128]{2,1,0:T(8,128)}), f32[8,216,128]{2,1,0:T(8,128)S(1)}, u32[]{:S(2)}, u32[]{:S(2)}) async-start(f32[8,216,128]{2,1,0:T(8,128)} %bitcast.19), calls=%async_computation.3 | async-start | bytes 1769472 | tf_op jit(solution)/shard_map/all_to_all | solution.py:548
  143.0 1.2 collective-permute-start.8
  144.3 3.6 %collective-permute-start.9 = (f32[8,128]{1,0:T(8,128)S(1)}, f32[8,128]{1,0:T(8,128)S(1)}, u32[]{:S(2)}, u32[]{:S(2)}) collective-permute-start(f32[8,128]{1,0:T(8,128)S(1)} %add.97), channel_id=1, source_target_pairs={{0,2},{1,3},{2,0},{3,1},{4,6},{5,7},{6,4},{7,5},{8,10},{9,11},{10,... | collective-permute-start | bytes 12296 | tf_op jit(solution)/shard_map/ppermute | solution.py:534
  147.9 3.6 %collective-permute-start.10 = (f32[8,128]{1,0:T(8,128)S(1)}, f32[8,128]{1,0:T(8,128)S(1)}, u32[]{:S(2)}, u32[]{:S(2)}) collective-permute-start(f32[8,128]{1,0:T(8,128)S(1)} %add.98), channel_id=1, source_target_pairs={{0,4},{4,0},{8,12},{12,8},{16,20},{20,16},{24,28},{28,24},{1,5},{5... | collective-permute-start | bytes 12296 | tf_op jit(solution)/shard_map/ppermute | solution.py:534
  151.5 4.6 %collective-permute-start.11 = (f32[8,128]{1,0:T(8,128)S(1)}, f32[8,128]{1,0:T(8,128)S(1)}, u32[]{:S(2)}, u32[]{:S(2)}) collective-permute-start(f32[8,128]{1,0:T(8,128)S(1)} %add.99), channel_id=1, source_target_pairs={{0,8},{4,12},{8,0},{12,4},{16,24},{20,28},{24,16},{28,20},{1,9},{5... | collective-permute-start | bytes 12296 | tf_op jit(solution)/shard_map/ppermute | solution.py:534
  156.1 7.8 %collective-permute-start.12 = (f32[8,128]{1,0:T(8,128)S(1)}, f32[8,128]{1,0:T(8,128)S(1)}, u32[]{:S(2)}, u32[]{:S(2)}) collective-permute-start(f32[8,128]{1,0:T(8,128)S(1)} %add.100), channel_id=1, source_target_pairs={{0,16},{4,20},{8,24},{12,28},{16,0},{20,4},{24,8},{28,12},{1,17},{... | collective-permute-start | bytes 12296 | tf_op jit(solution)/shard_map/ppermute | solution.py:534
  (10 other events, 40.4 us)

commit v4 on v3

--- a/solution.py
+++ b/solution.py
@@ -170,14 +170,14 @@
 UNROLL = 6
 
 
-ORDER = (0, 2, 4, 6, 1, 3, 5, 7)
+ORDER = tuple(range(PARTS))
 
 
 def pack_kernel(field, *refs):
     modes = field.shape[0]
     out = refs[-1]
-    if len(refs) == 4:
-        mean, ply, both = refs[:3]
+    if len(refs) > 1:
+        mean, ply, both = refs[0], refs[1], refs[-2]
         for x in range(SLAB):
             both[0, x] = mean[x]
             both[1, x] = (ply[x] + 1).astype(jnp.float32)
@@ -257,11 +257,13 @@
 HALO = 5
 
 
-def neighbour(tiles, index, side, place, full=False):
+def neighbour(tiles, index, side, place, full=False, wrap=False):
     t = tiles[index]
     lane = lax.broadcasted_iota(jnp.int32, t.shape, 1)
     slot = lane % WIDE
     roll = lambda v, s: pltpu.roll(v, s % LANES, 1)
+    if side in (2, 3) and wrap:
+        return roll(t, WIDE if side == 2 else -WIDE)
     if side in (2, 3):
         y = (place + lane // WIDE) & 7
         if side == 2:
@@ -299,8 +301,9 @@
     return jnp.concatenate([high, low], axis=0)
 
 
-STEP = 32
+STEP = 16
 FACE = 16
+CENTRE = 6 * FACE
 EVEN_BLOCKS = ((0, 32), (32, EVEN))
 
 
@@ -314,6 +317,16 @@
         for side in sides_of(t, INNER):
             value = (0.5 * weights[side // 2]) * (tiles[t] + neighbour(tiles, t, side, place, True))
             faces[side * FACE : (side + 1) * FACE, tile_cols(t)] = value
+        if t < INNER:
+            centre = 1.0 + sum(faces[side * FACE + VARS : side * FACE + VARS + 1, tile_cols(t)] for side in range(6))
+            faces[CENTRE : CENTRE + 1, tile_cols(t)] = centre
+            lane = lax.broadcasted_iota(jnp.int32, (1, LANES), 1)
+            y = (place + lane // WIDE) & 7
+            for side, edge in ((2, 0), (3, 7)):
+                row = side * FACE + VARS
+                faces[row + 1 : row + 2, tile_cols(t)] = jnp.where(
+                    y == edge, 0.0, faces[row : row + 1, tile_cols(t)]
+                )
 
 
 def apply_operator(src, dst, mixed, flux, scaled, acc, faces, inside, to_even, to_all, place, inner, outer):
@@ -361,9 +374,10 @@
         rows = pl.ds(pl.multiple_of(step * STEP, STEP), STEP)
         tiles = [src[rows, tile_cols(t)] for t in range(inner)]
         for t in range(outer):
-            result = tiles[t] + acc[rows, tile_cols(t)]
+            result = acc[rows, tile_cols(t)] + faces[CENTRE : CENTRE + 1, tile_cols(t)] * tiles[t]
             for side in range(6):
-                result = result + face(side, VARS, t) * (tiles[t] - neighbour(tiles, t, side, place))
+                row = VARS + 1 if side in (2, 3) else VARS
+                result = result - face(side, row, t) * neighbour(tiles, t, side, place, wrap=True)
             if t >= SLAB:
                 result = inside[t] * result
             dst[rows, tile_cols(t)] = result
@@ -381,9 +395,9 @@
 
 
 def apply_kernel(
-    place, own, before, after, scale, unscale, to_even, to_all, fields, fibre, so_far,
-    out, partial, field, first, second, mixed, flux, scaled, acc, faces, *, comp,
+    place, own, before, after, scale, unscale, to_even, to_all, fields, fibre, so_far, *refs, comp, block, offset,
 ):
+    rows_out, partial, out, field, first, second, mixed, flux, scaled, acc, faces, sems = refs[-12:]
     slots = scale.shape[0]
     here = place[0]
     face_stiffness(fields, faces, [fibre[comp, d] for d in range(3)], here)
@@ -407,33 +421,48 @@
     scratch = (mixed, flux, scaled, acc, faces, inside, to_even, to_all, here)
     apply_operator(field, first, *scratch, TILES, INNER)
     apply_operator(first, second, *scratch, INNER, SLAB)
+    for p in range(SLAB):
+        out[pl.ds(p, slots, stride=2 * SLAB), :] = first[:, tile_cols(p)] * unscale[...]
+        out[pl.ds(p + SLAB, slots, stride=2 * SLAB), :] = second[:, tile_cols(p)] * unscale[...]
+    part = slots // PARTS * 2 * SLAB
+    copies = [
+        pltpu.make_async_copy(
+            out.at[pl.ds(n * part, part), :], rows_out.at[pl.ds(n * block + offset, part), :], sems.at[n]
+        )
+        for n in range(PARTS)
+    ]
+    for copy in copies:
+        copy.start()
     sums = [jnp.zeros((1, LANES), jnp.float32)] * 5
     for p in range(SLAB):
         b = load(own, p)
         q = first[:, tile_cols(p)] * unscale[...]
         w = second[:, tile_cols(p)] * unscale[...]
-        out[pl.ds(p, slots, stride=2 * SLAB), :] = q
-        out[pl.ds(p + SLAB, slots, stride=2 * SLAB), :] = w
         for n, (one, two) in enumerate(((b, b), (b, q), (q, q), (b, w), (q, w))):
             sums[n] = sums[n] + jnp.sum(one * two, axis=0, keepdims=True)
     partial[...] = so_far[...] + jnp.concatenate(sums + [jnp.zeros((3, LANES), jnp.float32)], axis=0)
-
-
-def apply_twice(comp, place, own, before, after, tables, fields, fibre, so_far):
+    for copy in copies:
+        copy.wait()
+
+
+def apply_twice(comp, place, own, before, after, tables, fields, fibre, so_far, block, offset, rows_out=()):
     scale, unscale, to_even, to_all = tables
     slots = scale.shape[0]
     vmem = pl.BlockSpec(memory_space=pltpu.VMEM)
     smem = pl.BlockSpec(memory_space=pltpu.SMEM)
+    whole = pl.BlockSpec(memory_space=pl.ANY)
     f32 = lambda *shape: pltpu.VMEM(shape, jnp.float32)
     return pl.pallas_call(
-        functools.partial(apply_kernel, comp=comp),
+        functools.partial(apply_kernel, comp=comp, block=block, offset=offset),
         out_shape=[
-            jax.ShapeDtypeStruct((slots * 2 * SLAB, LANES), jnp.float32),
+            jax.ShapeDtypeStruct((PARTS * block, LANES), jnp.float32),
             jax.ShapeDtypeStruct((8, LANES), jnp.float32),
         ],
-        in_specs=[smem] + [vmem] * 8 + [smem, vmem],
-        out_specs=[vmem, vmem],
+        in_specs=[smem] + [vmem] * 8 + [smem, vmem] + [whole] * len(rows_out),
+        out_specs=[whole, vmem],
+        input_output_aliases={11: 0} if rows_out else {},
         scratch_shapes=[
+            f32(slots * 2 * SLAB, LANES),
             f32(slots, TILES * LANES),
             f32(slots, INNER * LANES),
             f32(slots, SLAB * LANES),
@@ -441,49 +470,66 @@
             f32(6, EVEN, TILES * LANES),
             f32(FULL, INNER * LANES),
             f32(slots, INNER * LANES),
-            f32(6 * FACE, TILES * LANES),
+            f32(6 * FACE + 8, TILES * LANES),
+            pltpu.SemaphoreType.DMA((PARTS,)),
         ],
         compiler_params=pltpu.CompilerParams(vmem_limit_bytes=VMEM),
         cost_estimate=estimate(15),
         name="apply_twice",
-    )(place, own, before, after, scale, unscale, to_even, to_all, fields, fibre, so_far)
-
-
-def finish_kernel(field, image, coefs, *refs):
+    )(place, own, before, after, scale, unscale, to_even, to_all, fields, fibre, so_far, *rows_out)
+
+
+def combination(total):
+    bb, bq, qq, bw, qw = (jnp.sum(total[n : n + 1, :], axis=1, keepdims=True) for n in range(5))
+    step_one = bb / bq
+    norm = bb - 2.0 * step_one * bq + step_one * step_one * qq
+    grown = 1.0 + norm / bb
+    curve = grown * grown * bq - step_one * grown * (bw + qq) + step_one * step_one * qw
+    step_two = norm / curve
+    spread = lambda v: jnp.broadcast_to(v, (8, LANES))
+    sole = spread(step_one + step_two * grown)
+    cross = spread(step_one * step_two)
+    return sole, cross
+
+
+STEPS = 3
+
+
+def finish_kernel(field, image, images, total, solution_field, residual):
     modes = field.shape[0]
-    solution_field, residual = refs[-2:]
-    per_part = modes * 2 * SLAB
+    part = STEPS * modes * 2 * SLAB
+    sole, cross = combination(total)
 
     def body(step, carry):
-        for inner in range(UNROLL):
-            mode = step * UNROLL + inner
-            for p in range(SLAB):
-                row = mode * 2 * SLAB + p
-                b = field[mode, 0, p]
-                q = swap_back(image[pl.ds(row, PARTS, stride=per_part), :])
-                w = swap_back(image[pl.ds(row + SLAB, PARTS, stride=per_part), :])
-                solution_field[mode, 0, p] = coefs[0] * b + coefs[1] * q
-                residual[mode, 0, p] = b + coefs[2] * q + coefs[3] * w
+        for inner in range(SLAB):
+            mode = step * SLAB + inner
+            for comp in range(COMPS):
+                source, block, offset = (image, part, 0) if comp == 0 else (images, 2 * part, (comp - 1) * part)
+                for p in range(SLAB):
+                    row = offset + (pl.program_id(0) * modes + mode) * 2 * SLAB + p
+                    b = field[mode, comp, p]
+                    q = swap_back(source[pl.ds(row, PARTS, stride=block), :])
+                    w = swap_back(source[pl.ds(row + SLAB, PARTS, stride=block), :])
+                    solution_field[mode, comp, p] = sole * b - cross * q
+                    residual[mode, comp, p] = b - sole * q + cross * w
         return carry
 
-    lax.fori_loop(0, modes // UNROLL, body, 0)
-
-
-def finish(field, comp, image, coefs, so_far):
-    block = pl.BlockSpec((field.shape[0], 1) + field.shape[2:], lambda i: (0, comp, 0, 0, 0))
+    lax.fori_loop(0, modes // SLAB, body, 0)
+
+
+def finish(field, image, images, total):
+    block = pl.BlockSpec((field.shape[0] // STEPS,) + field.shape[1:], lambda i: (i, 0, 0, 0, 0))
     vmem = pl.BlockSpec(memory_space=pltpu.VMEM)
     return pl.pallas_call(
         finish_kernel,
-        grid=(1,),
+        grid=(STEPS,),
         out_shape=[jax.ShapeDtypeStruct(field.shape, jnp.float32)] * 2,
-        in_specs=[block, vmem, pl.BlockSpec(memory_space=pltpu.SMEM)]
-        + [pl.BlockSpec(memory_space=pl.ANY)] * len(so_far),
+        in_specs=[block, vmem, vmem, vmem],
         out_specs=[block, block],
-        input_output_aliases={3 + n: n for n in range(len(so_far))},
         compiler_params=pltpu.CompilerParams(vmem_limit_bytes=VMEM),
-        cost_estimate=estimate(2.5),
+        cost_estimate=estimate(6),
         name="finish",
-    )(field, image, coefs, *so_far)
+    )(field, image, images, total)
 
 
 def mode_tables(coupling_table, slots):
@@ -551,42 +597,25 @@
         return lax.ppermute(rows, "space", up), lax.ppermute(rows, "space", down)
 
     (first,) = pack(right_side, 0)
-    both, second = pack(right_side, 1, (mean_stiffness, ply_map))
+    (second,) = pack(right_side, 1)
     own = [swap(first), swap(second)]
+    both, third = pack(right_side, 2, (mean_stiffness, ply_map), own[:1])
+    own.append(swap(third))
     halos = [halo(rows) for rows in own]
-    (third,) = pack(right_side, 2, (), halos[0])
-    own.append(swap(third))
-    halos.append(halo(own[2]))
     tables = mode_tables(coupling_table, slots)
     both_before = lax.ppermute(both, "space", up)
     both_after = lax.ppermute(both, "space", down)
     fields = stiffness_fields(place, both_before, both, both_after, ply_stiffness)
     partial = jnp.zeros((8, LANES), jnp.float32)
-    images = []
-    for comp in range(COMPS):
-        out, partial = apply_twice(
-            comp, place, own[comp], *halos[comp], tables, fields, fibre_weights, partial
-        )
-        images.append(swap(out))
-    bb, bq, qq, bw, qw = (jnp.sum(all_sum(partial)[n]) for n in range(5))
-    step_one = bb / bq
-    norm = bb - 2.0 * step_one * bq + step_one * step_one * qq
-    beta = norm / bb
-    grown = 1.0 + beta
-    curve = grown * grown * bq - step_one * grown * (bw + qq) + step_one * step_one * qw
-    step_two = norm / curve
-    coefs = jnp.stack(
-        [
-            step_one + step_two * grown,
-            -step_one * step_two,
-            -step_one - step_two * grown,
-            step_one * step_two,
-        ]
+    part = slots // PARTS * 2 * SLAB
+    tables_and_fields = (tables, fields, fibre_weights)
+    image, partial = apply_twice(0, place, own[0], *halos[0], *tables_and_fields, partial, part, 0)
+    image = swap(image)
+    images, partial = apply_twice(1, place, own[1], *halos[1], *tables_and_fields, partial, 2 * part, 0)
+    images, partial = apply_twice(
+        2, place, own[2], *halos[2], *tables_and_fields, partial, 2 * part, part, (images,)
     )
-    outputs = ()
-    for comp in range(COMPS):
-        outputs = finish(right_side, comp, images[comp], coefs, outputs)
-    return tuple(outputs)
+    return tuple(finish(right_side, image, swap(images), all_sum(partial)))
 
 
 def on_device(right_side, mean_stiffness, ply_stiffness, fibre_weights, ply_map, coupling_table):

time: 185 us -> 180 us (0.973)
  starting transfers between devices: 48.7 us -> 63.5 us
  waiting for transfers between devices: 52.3 us -> 38.1 us
  between operations: 7.55 us -> 0.93 us
    all_to_all x6 -> x5, waiting for transfers between devices: 40.2 us -> 9.87 us  [swap(): lax.all_to_all(rows, 'mode', 0, 0, axis_index_groups=[list(ORDER)], tiled...]
    ppermute x5, waiting for transfers between devices: 12.1 us -> 28.2 us  [all_sum(): lax.ppermute(value, axis, [(i, i ^ bit) for i in range(devices)])]
    ppermute x5, starting transfers between devices: 8.7 us -> 14.6 us  [all_sum(): lax.ppermute(value, axis, [(i, i ^ bit) for i in range(devices)])]
    all_to_all x6 -> x5, starting transfers between devices: 24.4 us -> 28.3 us  [swap(): lax.all_to_all(rows, 'mode', 0, 0, axis_index_groups=[list(ORDER)], tiled...]
    ppermute x6, starting transfers between devices: 11.9 us -> 15.1 us  [halo(): return (lax.ppermute(rows, 'space', up), lax.ppermute(rows, 'space', down))]
    pallas_call x6 -> x4, Pallas kernels: 49.6 us -> 50.8 us  [the longest x3 44 us: apply_twice(): pl.pallas_call(functools.partial(apply_kernel, comp=comp, block=block, of...]
    unnamed x30 -> x24, local copies, waits for them, and re-layouts: 4.02 us -> 3.96 us
  transfers between devices with their start and end apart: 19 -> 18, of which waited for: 10 -> 6; matrix products, arithmetic and copies ran while one was open for 5% -> 5% of each run, Pallas kernels for 30% -> 30%
where the time goes in v4:
time: 180 us; the launch traced here: 179 us
  starting transfers between devices  63.5 us (35%)
  Pallas kernels  62.9 us (35%)
  waiting for transfers between devices  38.1 us (21%)
  local copies, waits for them, and re-layouts  6.3 us (4%)
  other arithmetic  5.11 us (3%)
    pallas_call x3, Pallas kernels, apply_twice(): pl.pallas_call(functools.partial(apply_kernel, comp=comp, block=block, of...  44 us
    all_to_all x5, starting transfers between devices, swap(): lax.all_to_all(rows, 'mode', 0, 0, axis_index_groups=[list(ORDER)], tiled...  28.3 us
    ppermute x5, waiting for transfers between devices, all_sum(): lax.ppermute(value, axis, [(i, i ^ bit) for i in range(devices)])  28.2 us
    ppermute x6, starting transfers between devices, halo(): return (lax.ppermute(rows, 'space', up), lax.ppermute(rows, 'space', down))  15.1 us
    ppermute x5, starting transfers between devices, all_sum(): lax.ppermute(value, axis, [(i, i ^ bit) for i in range(devices)])  14.6 us
    all_to_all x5, waiting for transfers between devices, swap(): lax.all_to_all(rows, 'mode', 0, 0, axis_index_groups=[list(ORDER)], tiled...  9.87 us
    pallas_call x3, Pallas kernels, pack(): pl.pallas_call(pack_kernel, grid=(1,), out_shape=shapes, in_specs=[pl.Blo...  9.77 us
    pallas_call x1, Pallas kernels, finish(): pl.pallas_call(finish_kernel, grid=(STEPS,), out_shape=[jax.ShapeDtypeStr...  6.85 us
  transfers between devices with their start and end apart: 18, of which 6 were waited for; matrix products, arithmetic and copies ran while one was open for 5% of the time, Pallas kernels for 30%

profile of v4, /device:TPU:0, one launch (start us, length us, event | category | flops | bytes accessed | tf_op | source)
XLA Modules:
  0.0 178.6 jit_solution(7602087149690426330)
XLA Ops:
  0.6 3.2 %pack.3 = f32[1152,128]{1,0:T(8,128)} custom-call(f32[36,3,3,8,128]{4,3,2,1,0:T(8,128)} %field.7), custom_call_target="tpu_custom_call" | custom-call | flops 2500000000 | bytes 7500000 | tf_op jit(solution)/shard_map/pack/pallas_call | solution.py:207
  3.9 7.3 %all-to-all-start = ((f32[8,144,128]{2,1,0:T(8,128)}), f32[8,144,128]{2,1,0:T(8,128)S(1)}, u32[]{:S(2)}, u32[]{:S(2)}) async-start(f32[8,144,128]{2,1,0:T(8,128)} %bitcast.26), calls=%async_computation | async-start | bytes 1179648 | tf_op jit(solution)/shard_map/all_to_all | solution.py:594
  12.9 3.3 %pack.5 = f32[1152,128]{1,0:T(8,128)} custom-call(f32[36,3,3,8,128]{4,3,2,1,0:T(8,128)} %field.7), custom_call_target="tpu_custom_call" | custom-call | flops 2500000000 | bytes 7500000 | tf_op jit(solution)/shard_map/pack/pallas_call | solution.py:207
  17.2 9.9 %all-to-all-done = f32[8,144,128]{2,1,0:T(8,128)S(1)} async-done(((f32[8,144,128]{2,1,0:T(8,128)}), f32[8,144,128]{2,1,0:T(8,128)S(1)}, u32[]{:S(2)}, u32[]{:S(2)}) %all-to-all-start) | async-done | bytes 589856 | tf_op jit(solution)/shard_map/all_to_all | solution.py:594
  27.0 3.6 %all-to-all-start.3 = ((f32[8,144,128]{2,1,0:T(8,128)}), f32[8,144,128]{2,1,0:T(8,128)S(1)}, u32[]{:S(2)}, u32[]{:S(2)}) async-start(f32[8,144,128]{2,1,0:T(8,128)} %bitcast.7), calls=%async_computation.3 | async-start | bytes 1179648 | tf_op jit(solution)/shard_map/all_to_all | solution.py:594
  33.8 3.1 %collective-permute-start = (f32[1152,128]{1,0:T(8,128)S(1)}, f32[1152,128]{1,0:T(8,128)S(1)}, u32[]{:S(2)}, u32[]{:S(2)}) collective-permute-start(f32[1152,128]{1,0:T(8,128)S(1)} %bitcast.16), channel_id=1, source_target_pairs={{0,1},{1,2},{2,3},{4,5},{5,6},{6,7},{8,9},{9,10},{10,11},{12,13},{... | collective-permute-start | bytes 1769480 | tf_op jit(solution)/shard_map/ppermute | solution.py:597
  36.8 3.3 %pack.4 = (f32[2,3,8,128]{3,2,1,0:T(8,128)}, f32[1152,128]{1,0:T(8,128)}) custom-call(f32[36,3,3,8,128]{4,3,2,1,0:T(8,128)} %field.7, f32[3,8,128]{2,1,0:T(8,128)} %refs_0_.1, s32[3,8,128]{2,1,0:T(8,128)} %refs_1_.1, f32[1152,128]{1,0:T(8,128)} %bitcast.17), custom_call_target="tpu_custom_call" | custom-call | flops 2500000000 | bytes 7500000 | tf_op jit(solution)/shard_map/pack/pallas_call | solution.py:207
  41.4 4.2 %collective-permute-start.2 = (f32[2,3,8,128]{3,2,1,0:T(8,128)}, f32[2,3,8,128]{3,2,1,0:T(8,128)}, u32[]{:S(2)}, u32[]{:S(2)}) collective-permute-start(f32[2,3,8,128]{3,2,1,0:T(8,128)} %get-tuple-element.10.both), channel_id=1, source_target_pairs={{0,1},{1,2},{2,3},{4,5},{5,6},{6,7},{8,9},{9,10},{10,11},{12,13},{... | collective-permute-start | bytes 73736 | tf_op jit(solution)/shard_map/ppermute | solution.py:606
  48.8 6.0 %all-to-all-start.2 = ((f32[8,144,128]{2,1,0:T(8,128)}), f32[8,144,128]{2,1,0:T(8,128)S(1)}, u32[]{:S(2)}, u32[]{:S(2)}) async-start(f32[8,144,128]{2,1,0:T(8,128)} %bitcast.25), calls=%async_computation.2 | async-start | bytes 1179648 | tf_op jit(solution)/shard_map/all_to_all | solution.py:594
  54.8 4.2 %collective-permute-start.6 = (f32[1152,128]{1,0:T(8,128)S(1)}, f32[1152,128]{1,0:T(8,128)}, u32[]{:S(2)}, u32[]{:S(2)}) collective-permute-start(f32[1152,128]{1,0:T(8,128)S(1)} %bitcast.20), channel_id=1, source_target_pairs={{0,1},{1,2},{2,3},{4,5},{5,6},{6,7},{8,9},{9,10},{10,11},{12,13},{... | collective-permute-start | bytes 1769480 | tf_op jit(solution)/shard_map/ppermute | solution.py:597
  59.0 2.3 %stiffness_fields.1.fields = f32[16,1024]{1,0:T(8,128)} custom-call(s32[1]{0:T(128)} %bitcast.place, f32[2,3,8,128]{3,2,1,0:T(8,128)} %collective-permute-done.2.before, f32[2,3,8,128]{3,2,1,0:T(8,128)} %get-tuple-element.10.both, f32[2,3,8,128]{3,2,1,0:T(8,128)} %collective-permute-done.3.after, f32[10]{0:T(128)} %ply_stiffness.1), custom_call_target="tpu_custom_call" | custom-call | flops 2000000000 | bytes 6000000 | tf_op jit(solution)/shard_map/stiffness_fields/pallas_call | solution.py:244
  63.6 14.6 %apply_twice.3 = (f32[1728,128]{1,0:T(8,128)}, f32[8,128]{1,0:T(8,128)}) custom-call(s32[1]{0:T(128)} %bitcast.place, f32[1152,128]{1,0:T(8,128)} %bitcast.18, f32[1152,128]{1,0:T(8,128)} %copy-done.8, f32[1152,128]{1,0:T(8,128)} %copy-done.7, f32[288,128]{1,0:T(8,128)} %broadcast_in_dim.102.scale, f32[288,128]{1,0:T(8,128)} %broadcast_in_dim.103.unscale, ...), custom_call_target="tpu_custom_call" | custom-call | flops 15000000512 | bytes 45000000 | tf_op jit(solution)/shard_map/apply_twice/pallas_call | solution.py:455
  78.3 5.7 %all-to-all-start.1 = ((f32[8,216,128]{2,1,0:T(8,128)}), f32[8,216,128]{2,1,0:T(8,128)S(1)}, u32[]{:S(2)}, u32[]{:S(2)}) async-start(f32[8,216,128]{2,1,0:T(8,128)} %bitcast.14), calls=%async_computation.1 | async-start | bytes 1769472 | tf_op jit(solution)/shard_map/all_to_all | solution.py:594
  85.3 4.0 %collective-permute-start.4 = (f32[1152,128]{1,0:T(8,128)S(1)}, f32[1152,128]{1,0:T(8,128)S(1)}, u32[]{:S(2)}, u32[]{:S(2)}) collective-permute-start(f32[1152,128]{1,0:T(8,128)S(1)} %bitcast.23), channel_id=1, source_target_pairs={{0,1},{1,2},{2,3},{4,5},{5,6},{6,7},{8,9},{9,10},{10,11},{12,13},{... | collective-permute-start | bytes 1769480 | tf_op jit(solution)/shard_map/ppermute | solution.py:597
  90.1 14.7 %apply_twice.4 = (f32[3456,128]{1,0:T(8,128)}, f32[8,128]{1,0:T(8,128)}) custom-call(s32[1]{0:T(128)} %bitcast.place, f32[1152,128]{1,0:T(8,128)} %bitcast.21, f32[1152,128]{1,0:T(8,128)} %collective-permute-done.6.before, f32[1152,128]{1,0:T(8,128)} %copy-done.9, f32[288,128]{1,0:T(8,128)} %broadcast_in_dim.102.scale, ...), custom_call_target="tpu_custom_call" | custom-call | flops 15000000512 | bytes 45000000 | tf_op jit(solution)/shard_map/apply_twice/pallas_call | solution.py:455
  105.8 14.7 %apply_twice.5 = (f32[3456,128]{1,0:T(8,128)}, f32[8,128]{1,0:T(8,128)}) custom-call(s32[1]{0:T(128)} %bitcast.place, f32[1152,128]{1,0:T(8,128)} %bitcast.24, f32[1152,128]{1,0:T(8,128)} %copy-done.11, f32[1152,128]{1,0:T(8,128)} %copy-done.10, f32[288,128]{1,0:T(8,128)} %broadcast_in_dim.102.scale, ...), custom_call_target="tpu_custom_call", output_to_operand_aliasing={{0}: (11, {})} | custom-call | flops 15000000512 | bytes 45000000 | tf_op jit(solution)/shard_map/apply_twice/pallas_call | solution.py:455
  121.4 5.7 %all-to-all-start.4 = ((f32[8,432,128]{2,1,0:T(8,128)}), f32[8,432,128]{2,1,0:T(8,128)S(1)}, u32[]{:S(2)}, u32[]{:S(2)}) async-start(f32[8,432,128]{2,1,0:T(8,128)} %bitcast.12), calls=%async_computation.4 | async-start | bytes 3538944 | tf_op jit(solution)/shard_map/all_to_all | solution.py:594
  130.0 3.1 %collective-permute-done.9 = f32[8,128]{1,0:T(8,128)S(1)} collective-permute-done((f32[8,128]{1,0:T(8,128)S(1)}, f32[8,128]{1,0:T(8,128)S(1)}, u32[]{:S(2)}, u32[]{:S(2)}) %collective-permute-start.9) | collective-permute-done | bytes 4128 | tf_op jit(solution)/shard_map/ppermute | solution.py:580
  134.7 2.8 %collective-permute-done.10 = f32[8,128]{1,0:T(8,128)S(1)} collective-permute-done((f32[8,128]{1,0:T(8,128)S(1)}, f32[8,128]{1,0:T(8,128)S(1)}, u32[]{:S(2)}, u32[]{:S(2)}) %collective-permute-start.10) | collective-permute-done | bytes 4128 | tf_op jit(solution)/shard_map/ppermute | solution.py:580
  137.5 6.8 %collective-permute-start.11 = (f32[8,128]{1,0:T(8,128)S(1)}, f32[8,128]{1,0:T(8,128)S(1)}, u32[]{:S(2)}, u32[]{:S(2)}) collective-permute-start(f32[8,128]{1,0:T(8,128)S(1)} %add.64), channel_id=1, source_target_pairs={{0,8},{4,12},{8,0},{12,4},{16,24},{20,28},{24,16},{28,20},{1,9},{5... | collective-permute-start | bytes 12296 | tf_op jit(solution)/shard_map/ppermute | solution.py:580
  144.4 13.5 %collective-permute-done.11 = f32[8,128]{1,0:T(8,128)S(1)} collective-permute-done((f32[8,128]{1,0:T(8,128)S(1)}, f32[8,128]{1,0:T(8,128)S(1)}, u32[]{:S(2)}, u32[]{:S(2)}) %collective-permute-start.11) | collective-permute-done | bytes 4128 | tf_op jit(solution)/shard_map/ppermute | solution.py:580
  157.8 4.1 %collective-permute-start.12 = (f32[8,128]{1,0:T(8,128)S(1)}, f32[8,128]{1,0:T(8,128)S(1)}, u32[]{:S(2)}, u32[]{:S(2)}) collective-permute-start(f32[8,128]{1,0:T(8,128)S(1)} %add.65), channel_id=1, source_target_pairs={{0,16},{4,20},{8,24},{12,28},{16,0},{20,4},{24,8},{28,12},{1,17},{... | collective-permute-start | bytes 12296 | tf_op jit(solution)/shard_map/ppermute | solution.py:580
  161.9 8.0 %collective-permute-done.12 = f32[8,128]{1,0:T(8,128)S(1)} collective-permute-done((f32[8,128]{1,0:T(8,128)S(1)}, f32[8,128]{1,0:T(8,128)S(1)}, u32[]{:S(2)}, u32[]{:S(2)}) %collective-permute-start.12) | collective-permute-done | bytes 4128 | tf_op jit(solution)/shard_map/ppermute | solution.py:580
  171.8 6.9 %finish.1 = (f32[36,3,3,8,128]{4,3,2,1,0:T(8,128)}, f32[36,3,3,8,128]{4,3,2,1,0:T(8,128)}) custom-call(f32[36,3,3,8,128]{4,3,2,1,0:T(8,128)} %field.7, f32[1728,128]{1,0:T(8,128)} %bitcast.13, f32[3456,128]{1,0:T(8,128)} %bitcast.11, f32[8,128]{1,0:T(8,128)} %add.66.total), custom_call_target="tpu_custom_call" | custom-call | flops 6000000000 | bytes 18000000 | tf_op jit(solution)/shard_map/finish/pallas_call | solution.py:523
  (72 shorter events, 22.8 us)
Async XLA Ops:
  0.6 10.7 %copy-start.5 = (s32[660,4]{0,1:T(4,128)S(1)}, s32[660,4]{0,1:T(4,128)}, u32[]{:S(2)}) copy-start(s32[660,4]{0,1:T(4,128)} %param.13) | copy-start | bytes 31684
  3.9 23.1 %all-to-all-start = ((f32[8,144,128]{2,1,0:T(8,128)}), f32[8,144,128]{2,1,0:T(8,128)S(1)}, u32[]{:S(2)}, u32[]{:S(2)}) async-start(f32[8,144,128]{2,1,0:T(8,128)} %bitcast.26), calls=%async_computation | async-start | bytes 1179648 | tf_op jit(solution)/shard_map/all_to_all | solution.py:594
  27.0 6.7 %copy-start.2 = (f32[8,144,128]{2,1,0:T(8,128)}, f32[8,144,128]{2,1,0:T(8,128)S(1)}, u32[]{:S(2)}) copy-start(f32[8,144,128]{2,1,0:T(8,128)S(1)} %all-to-all-done) | copy-start | bytes 1769476
  27.0 20.4 %all-to-all-start.3 = ((f32[8,144,128]{2,1,0:T(8,128)}), f32[8,144,128]{2,1,0:T(8,128)S(1)}, u32[]{:S(2)}, u32[]{:S(2)}) async-start(f32[8,144,128]{2,1,0:T(8,128)} %bitcast.7), calls=%async_computation.3 | async-start | bytes 1179648 | tf_op jit(solution)/shard_map/all_to_all | solution.py:594
  32.5 28.9 %collective-permute-start.1 = (f32[1152,128]{1,0:T(8,128)S(1)}, f32[1152,128]{1,0:T(8,128)S(1)}, u32[]{:S(2)}, u32[]{:S(2)}) collective-permute-start(f32[1152,128]{1,0:T(8,128)S(1)} %bitcast.15), channel_id=1, source_target_pairs={{1,0},{2,1},{3,2},{5,4},{6,5},{7,6},{9,8},{10,9},{11,10},{13,12},{... | collective-permute-start | bytes 1769480 | tf_op jit(solution)/shard_map/ppermute | solution.py:597
  33.8 27.6 %collective-permute-start = (f32[1152,128]{1,0:T(8,128)S(1)}, f32[1152,128]{1,0:T(8,128)S(1)}, u32[]{:S(2)}, u32[]{:S(2)}) collective-permute-start(f32[1152,128]{1,0:T(8,128)S(1)} %bitcast.16), channel_id=1, source_target_pairs={{0,1},{1,2},{2,3},{4,5},{5,6},{6,7},{8,9},{9,10},{10,11},{12,13},{... | collective-permute-start | bytes 1769480 | tf_op jit(solution)/shard_map/ppermute | solution.py:597
  40.1 14.7 %collective-permute-start.3 = (f32[2,3,8,128]{3,2,1,0:T(8,128)}, f32[2,3,8,128]{3,2,1,0:T(8,128)}, u32[]{:S(2)}, u32[]{:S(2)}) collective-permute-start(f32[2,3,8,128]{3,2,1,0:T(8,128)} %get-tuple-element.10.both), channel_id=1, source_target_pairs={{1,0},{2,1},{3,2},{5,4},{6,5},{7,6},{9,8},{10,9},{11,10},{13,12},{... | collective-permute-start | bytes 73736 | tf_op jit(solution)/shard_map/ppermute | solution.py:607
  41.4 17.6 %collective-permute-start.2 = (f32[2,3,8,128]{3,2,1,0:T(8,128)}, f32[2,3,8,128]{3,2,1,0:T(8,128)}, u32[]{:S(2)}, u32[]{:S(2)}) collective-permute-start(f32[2,3,8,128]{3,2,1,0:T(8,128)} %get-tuple-element.10.both), channel_id=1, source_target_pairs={{0,1},{1,2},{2,3},{4,5},{5,6},{6,7},{8,9},{9,10},{10,11},{12,13},{... | collective-permute-start | bytes 73736 | tf_op jit(solution)/shard_map/ppermute | solution.py:606
  47.5 13.9 %copy-start.3 = (f32[8,144,128]{2,1,0:T(8,128)}, f32[8,144,128]{2,1,0:T(8,128)S(1)}, u32[]{:S(2)}) copy-start(f32[8,144,128]{2,1,0:T(8,128)S(1)} %all-to-all-done.3) | copy-start | bytes 1769476
  47.5 41.8 %collective-permute-start.7 = (f32[1152,128]{1,0:T(8,128)S(1)}, f32[1152,128]{1,0:T(8,128)S(1)}, u32[]{:S(2)}, u32[]{:S(2)}) collective-permute-start(f32[1152,128]{1,0:T(8,128)S(1)} %bitcast.19), channel_id=1, source_target_pairs={{1,0},{2,1},{3,2},{5,4},{6,5},{7,6},{9,8},{10,9},{11,10},{13,12},{... | collective-permute-start | bytes 1769480 | tf_op jit(solution)/shard_map/ppermute | solution.py:597
  48.8 29.5 %all-to-all-start.2 = ((f32[8,144,128]{2,1,0:T(8,128)}), f32[8,144,128]{2,1,0:T(8,128)S(1)}, u32[]{:S(2)}, u32[]{:S(2)}) async-start(f32[8,144,128]{2,1,0:T(8,128)} %bitcast.25), calls=%async_computation.2 | async-start | bytes 1179648 | tf_op jit(solution)/shard_map/all_to_all | solution.py:594
  54.8 34.5 %collective-permute-start.6 = (f32[1152,128]{1,0:T(8,128)S(1)}, f32[1152,128]{1,0:T(8,128)}, u32[]{:S(2)}, u32[]{:S(2)}) collective-permute-start(f32[1152,128]{1,0:T(8,128)S(1)} %bitcast.20), channel_id=1, source_target_pairs={{0,1},{1,2},{2,3},{4,5},{5,6},{6,7},{8,9},{9,10},{10,11},{12,13},{... | collective-permute-start | bytes 1769480 | tf_op jit(solution)/shard_map/ppermute | solution.py:597
  61.3 2.2 %copy-start.7 = (f32[1152,128]{1,0:T(8,128)}, f32[1152,128]{1,0:T(8,128)S(1)}, u32[]{:S(2)}) copy-start(f32[1152,128]{1,0:T(8,128)S(1)} %collective-permute-done.1.after) | copy-start | bytes 1769476
  78.2 26.5 %copy-start.4 = (f32[8,144,128]{2,1,0:T(8,128)}, f32[8,144,128]{2,1,0:T(8,128)S(1)}, u32[]{:S(2)}) copy-start(f32[8,144,128]{2,1,0:T(8,128)S(1)} %all-to-all-done.2) | copy-start | bytes 1769476
  78.3 42.2 %all-to-all-start.1 = ((f32[8,216,128]{2,1,0:T(8,128)}), f32[8,216,128]{2,1,0:T(8,128)S(1)}, u32[]{:S(2)}, u32[]{:S(2)}) async-start(f32[8,216,128]{2,1,0:T(8,128)} %bitcast.14), calls=%async_computation.1 | async-start | bytes 1769472 | tf_op jit(solution)/shard_map/all_to_all | solution.py:594
  84.0 20.8 %collective-permute-start.5 = (f32[1152,128]{1,0:T(8,128)S(1)}, f32[1152,128]{1,0:T(8,128)S(1)}, u32[]{:S(2)}, u32[]{:S(2)}) collective-permute-start(f32[1152,128]{1,0:T(8,128)S(1)} %bitcast.22), channel_id=1, source_target_pairs={{1,0},{2,1},{3,2},{5,4},{6,5},{7,6},{9,8},{10,9},{11,10},{13,12},{... | collective-permute-start | bytes 1769480 | tf_op jit(solution)/shard_map/ppermute | solution.py:597
  85.3 19.5 %collective-permute-start.4 = (f32[1152,128]{1,0:T(8,128)S(1)}, f32[1152,128]{1,0:T(8,128)S(1)}, u32[]{:S(2)}, u32[]{:S(2)}) collective-permute-start(f32[1152,128]{1,0:T(8,128)S(1)} %bitcast.23), channel_id=1, source_target_pairs={{0,1},{1,2},{2,3},{4,5},{5,6},{6,7},{8,9},{9,10},{10,11},{12,13},{... | collective-permute-start | bytes 1769480 | tf_op jit(solution)/shard_map/ppermute | solution.py:597
  120.5 6.6 %copy-start.6 = (f32[8,128]{1,0:T(8,128)S(1)}, f32[8,128]{1,0:T(8,128)}, u32[]{:S(2)}) copy-start(f32[8,128]{1,0:T(8,128)} %get-tuple-element.17) | copy-start | bytes 12292
  121.4 49.1 %all-to-all-start.4 = ((f32[8,432,128]{2,1,0:T(8,128)}), f32[8,432,128]{2,1,0:T(8,128)S(1)}, u32[]{:S(2)}, u32[]{:S(2)}) async-start(f32[8,432,128]{2,1,0:T(8,128)} %bitcast.12), calls=%async_computation.4 | async-start | bytes 3538944 | tf_op jit(solution)/shard_map/all_to_all | solution.py:594
  127.1 2.3 %collective-permute-start.8 = (f32[8,128]{1,0:T(8,128)S(1)}, f32[8,128]{1,0:T(8,128)S(1)}, u32[]{:S(2)}, u32[]{:S(2)}) collective-permute-start(f32[8,128]{1,0:T(8,128)S(1)} %copy-done.6), channel_id=1, source_target_pairs={{0,1},{1,0},{2,3},{3,2},{4,5},{5,4},{6,7},{7,6},{8,9},{9,8},{10,11... | collective-permute-start | bytes 12296 | tf_op jit(solution)/shard_map/ppermute | solution.py:580
  129.4 3.6 %collective-permute-start.9 = (f32[8,128]{1,0:T(8,128)S(1)}, f32[8,128]{1,0:T(8,128)S(1)}, u32[]{:S(2)}, u32[]{:S(2)}) collective-permute-start(f32[8,128]{1,0:T(8,128)S(1)} %add.62), channel_id=1, source_target_pairs={{0,2},{1,3},{2,0},{3,1},{4,6},{5,7},{6,4},{7,5},{8,10},{9,11},{10,... | collective-permute-start | bytes 12296 | tf_op jit(solution)/shard_map/ppermute | solution.py:580
  133.0 4.5 %collective-permute-start.10 = (f32[8,128]{1,0:T(8,128)S(1)}, f32[8,128]{1,0:T(8,128)S(1)}, u32[]{:S(2)}, u32[]{:S(2)}) collective-permute-start(f32[8,128]{1,0:T(8,128)S(1)} %add.63), channel_id=1, source_target_pairs={{0,4},{4,0},{8,12},{12,8},{16,20},{20,16},{24,28},{28,24},{1,5},{5... | collective-permute-start | bytes 12296 | tf_op jit(solution)/shard_map/ppermute | solution.py:580
  137.5 20.3 %collective-permute-start.11 = (f32[8,128]{1,0:T(8,128)S(1)}, f32[8,128]{1,0:T(8,128)S(1)}, u32[]{:S(2)}, u32[]{:S(2)}) collective-permute-start(f32[8,128]{1,0:T(8,128)S(1)} %add.64), channel_id=1, source_target_pairs={{0,8},{4,12},{8,0},{12,4},{16,24},{20,28},{24,16},{28,20},{1,9},{5... | collective-permute-start | bytes 12296 | tf_op jit(solution)/shard_map/ppermute | solution.py:580
  157.8 12.1 %collective-permute-start.12 = (f32[8,128]{1,0:T(8,128)S(1)}, f32[8,128]{1,0:T(8,128)S(1)}, u32[]{:S(2)}, u32[]{:S(2)}) collective-permute-start(f32[8,128]{1,0:T(8,128)S(1)} %add.65), channel_id=1, source_target_pairs={{0,16},{4,20},{8,24},{12,28},{16,0},{20,4},{24,8},{28,12},{1,17},{... | collective-permute-start | bytes 12296 | tf_op jit(solution)/shard_map/ppermute | solution.py:580
  (6 other events, 7.0 us)

commit v5 on v4

--- a/solution.py
+++ b/solution.py
@@ -167,13 +167,10 @@
     return halo
 
 
-UNROLL = 6
-
-
-ORDER = tuple(range(PARTS))
-
-
-def pack_kernel(field, *refs):
+UNROLL = 3
+
+
+def pack_kernel(field, *refs, comps):
     modes = field.shape[0]
     out = refs[-1]
     if len(refs) > 1:
@@ -181,39 +178,41 @@
         for x in range(SLAB):
             both[0, x] = mean[x]
             both[1, x] = (ply[x] + 1).astype(jnp.float32)
+    rows = ROWS * len(comps)
+    unroll = 2 * UNROLL // len(comps)
 
     def body(step, carry):
-        for inner in range(UNROLL):
-            mode = step * UNROLL + inner
-            planes = [field[mode, 0, x] for x in range(SLAB)]
-            halo = halo_row(dict(enumerate(planes)))
-            for p, tile in enumerate(planes + [halo]):
-                out[pl.ds(mode * ROWS + p, PARTS, stride=ROWS * modes), :] = swap_out(tile)
+        for inner in range(unroll):
+            mode = step * unroll + inner
+            for n, comp in enumerate(comps):
+                planes = [field[mode, comp, x] for x in range(SLAB)]
+                halo = halo_row(dict(enumerate(planes)))
+                for p, tile in enumerate(planes + [halo]):
+                    out[pl.ds(mode * rows + n * ROWS + p, PARTS, stride=rows * modes), :] = swap_out(tile)
         return carry
 
-    lax.fori_loop(0, modes // UNROLL, body, 0)
+    lax.fori_loop(0, modes // unroll, body, 0)
 
 
 def estimate(micros):
     return pl.CostEstimate(flops=int(micros * 1e9), bytes_accessed=int(micros * 3e6), transcendentals=0)
 
 
-def pack(field, comp, stiffness=(), after=()):
+def pack(field, comps, stiffness=(), after=()):
     modes = field.shape[0]
-    block = (modes, 1) + field.shape[2:]
     vmem = pl.BlockSpec(memory_space=pltpu.VMEM)
     shapes = [jax.ShapeDtypeStruct((2,) + s.shape, jnp.float32) for s in stiffness[:1]]
-    shapes.append(jax.ShapeDtypeStruct((PARTS * modes * ROWS, LANES), jnp.float32))
+    shapes.append(jax.ShapeDtypeStruct((PARTS * modes * ROWS * len(comps), LANES), jnp.float32))
     return pl.pallas_call(
-        pack_kernel,
+        functools.partial(pack_kernel, comps=comps),
         grid=(1,),
         out_shape=shapes,
-        in_specs=[pl.BlockSpec(block, lambda i: (0, comp, 0, 0, 0))]
+        in_specs=[pl.BlockSpec((modes, max(comps) + 1) + field.shape[2:], lambda i: (0, 0, 0, 0, 0))]
         + [vmem] * len(stiffness)
         + [pl.BlockSpec(memory_space=pl.ANY)] * len(after),
         out_specs=[vmem] * len(shapes),
         compiler_params=pltpu.CompilerParams(vmem_limit_bytes=VMEM),
-        cost_estimate=estimate(2.5),
+        cost_estimate=estimate(2.5 * len(comps)),
         name="pack",
     )(field, *stiffness, *after)
 
@@ -301,7 +300,7 @@
     return jnp.concatenate([high, low], axis=0)
 
 
-STEP = 16
+STEP = 32
 FACE = 16
 CENTRE = 6 * FACE
 EVEN_BLOCKS = ((0, 32), (32, EVEN))
@@ -329,46 +328,75 @@
                 )
 
 
+CHUNK = 2
+
+
+def chunks(count):
+    return [range(start, min(start + CHUNK, count)) for start in range(0, count, CHUNK)]
+
+
+def chunk_cols(tiles):
+    return slice(LANES * tiles[0], LANES * (tiles[-1] + 1))
+
+
 def apply_operator(src, dst, mixed, flux, scaled, acc, faces, inside, to_even, to_all, place, inner, outer):
     slots = src.shape[0]
-    for start in range(0, inner * LANES, 512):
-        cols = slice(start, min(start + 512, inner * LANES))
-        mixed[:, cols] = jnp.dot(to_even[...], split(src[:, cols]), preferred_element_type=jnp.float32)
 
     def face(side, k, t):
         return faces[side * FACE + k : side * FACE + k + 1, tile_cols(t)]
 
-    for low, high in EVEN_BLOCKS:
-        flows = {}
-        for t in range(inner):
-            sides = sides_of(t, outer)
+    def mix(tiles):
+        cols = chunk_cols(tiles)
+        mixed[:, cols] = jnp.dot(to_even[...], split(src[:, cols]), preferred_element_type=jnp.float32)
+
+    def flows(t):
+        for low, high in EVEN_BLOCKS:
             total = {}
             for k in range(VARS):
                 value = mixed[k * EVEN + low : k * EVEN + high, tile_cols(t)]
-                for side in sides:
+                for side in sides_of(t, outer):
                     term = face(side, k, t) * value
                     total[side] = term if k == 0 else total[side] + term
-            for side in sides:
-                flux[side, low:high, tile_cols(t)] = total[side]
-        even = [mixed[SPAN + low : SPAN + high, tile_cols(t)] for t in range(inner)]
-        for t in range(outer):
+            for side, value in total.items():
+                flux[side, low:high, tile_cols(t)] = value
+
+    def scale_even(t):
+        for low, high in EVEN_BLOCKS:
+            even = EvenTiles(mixed, low, high)
             steps = [even[t] - neighbour(even, t, side, place) for side in range(6)]
             for k in range(VARS):
                 total = face(0, k, t) * steps[0]
                 for side in range(1, 6):
                     total = total + face(side, k, t) * steps[side]
                 scaled[k * EVEN + low : k * EVEN + high, tile_cols(t)] = total
-        for t in range(outer):
             total = None
             for side in range(6):
                 opposite = FluxTiles(flux, side ^ 1, low, high)
                 term = flux[side, low:high, tile_cols(t)] - neighbour(opposite, t, side, place)
                 total = term if total is None else total + term
             scaled[SPAN + low : SPAN + high, tile_cols(t)] = total
-    scaled[SPAN + EVEN : FULL, : outer * LANES] = jnp.zeros((FULL - SPAN - EVEN, outer * LANES), jnp.float32)
-    for start in range(0, outer * LANES, 512):
-        cols = slice(start, min(start + 512, outer * LANES))
+        scaled[SPAN + EVEN : FULL, tile_cols(t)] = jnp.zeros((FULL - SPAN - EVEN, LANES), jnp.float32)
+
+    def spread(tiles):
+        cols = chunk_cols(tiles)
         acc[:, cols] = jnp.dot(to_all[...], split(scaled[:, cols]), preferred_element_type=jnp.float32)
+
+    before = ()
+    for tiles in chunks(inner):
+        mix(tiles)
+        for t in before:
+            flows(t)
+        before = tiles
+    for t in before:
+        flows(t)
+    before = ()
+    for tiles in chunks(outer):
+        for t in tiles:
+            scale_even(t)
+        if before:
+            spread(before)
+        before = tiles
+    spread(before)
 
     def last(step, carry):
         rows = pl.ds(pl.multiple_of(step * STEP, STEP), STEP)
@@ -386,6 +414,14 @@
     lax.fori_loop(0, slots // STEP, last, 0)
 
 
+class EvenTiles:
+    def __init__(self, mixed, low, high):
+        self.mixed, self.low, self.high = mixed, low, high
+
+    def __getitem__(self, t):
+        return self.mixed[SPAN + self.low : SPAN + self.high, tile_cols(t)]
+
+
 class FluxTiles:
     def __init__(self, flux, side, low, high):
         self.flux, self.side, self.low, self.high = flux, side, low, high
@@ -395,15 +431,15 @@
 
 
 def apply_kernel(
-    place, own, before, after, scale, unscale, to_even, to_all, fields, fibre, so_far, *refs, comp, block, offset,
+    place, own, before, after, scale, to_even, to_all, fields, fibre, *refs, comp, row, rows, block, offset,
 ):
-    rows_out, partial, out, field, first, second, mixed, flux, scaled, acc, faces, sems = refs[-12:]
+    out_rows, partial, out, field, first, second, mixed, flux, scaled, acc, faces, sems = refs[-12:]
     slots = scale.shape[0]
     here = place[0]
     face_stiffness(fields, faces, [fibre[comp, d] for d in range(3)], here)
     lane = lax.broadcasted_iota(jnp.int32, (slots, LANES), 1)
     slot = lane % WIDE
-    load = lambda ref, p: ref[pl.ds(p, slots, stride=ROWS), :]
+    load = lambda ref, p: ref[pl.ds(row + p, slots, stride=rows), :]
     left = pltpu.roll(load(before, 3), LANES - 3, 1)
     right = pltpu.roll(load(after, 3), 3, 1)
     halo = jnp.where((slot == 0) | (slot == 5), left, load(own, 3))
@@ -421,46 +457,55 @@
     scratch = (mixed, flux, scaled, acc, faces, inside, to_even, to_all, here)
     apply_operator(field, first, *scratch, TILES, INNER)
     apply_operator(first, second, *scratch, INNER, SLAB)
+    sums = [jnp.zeros((1, LANES), jnp.float32)] * 5
+    unscale = 1.0 / scale[...]
     for p in range(SLAB):
-        out[pl.ds(p, slots, stride=2 * SLAB), :] = first[:, tile_cols(p)] * unscale[...]
-        out[pl.ds(p + SLAB, slots, stride=2 * SLAB), :] = second[:, tile_cols(p)] * unscale[...]
+        b = load(own, p)
+        q = first[:, tile_cols(p)] * unscale
+        w = second[:, tile_cols(p)] * unscale
+        out[pl.ds(p, slots, stride=2 * SLAB), :] = q
+        out[pl.ds(p + SLAB, slots, stride=2 * SLAB), :] = w
+        for n, (one, two) in enumerate(((b, b), (b, q), (q, q), (b, w), (q, w))):
+            sums[n] = sums[n] + jnp.sum(one * two, axis=0, keepdims=True)
     part = slots // PARTS * 2 * SLAB
     copies = [
         pltpu.make_async_copy(
-            out.at[pl.ds(n * part, part), :], rows_out.at[pl.ds(n * block + offset, part), :], sems.at[n]
+            out.at[pl.ds(n * part, part), :], out_rows.at[pl.ds(n * block + offset, part), :], sems.at[n]
         )
         for n in range(PARTS)
     ]
     for copy in copies:
         copy.start()
-    sums = [jnp.zeros((1, LANES), jnp.float32)] * 5
-    for p in range(SLAB):
-        b = load(own, p)
-        q = first[:, tile_cols(p)] * unscale[...]
-        w = second[:, tile_cols(p)] * unscale[...]
-        for n, (one, two) in enumerate(((b, b), (b, q), (q, q), (b, w), (q, w))):
-            sums[n] = sums[n] + jnp.sum(one * two, axis=0, keepdims=True)
-    partial[...] = so_far[...] + jnp.concatenate(sums + [jnp.zeros((3, LANES), jnp.float32)], axis=0)
+    total = jnp.concatenate(sums + [jnp.zeros((3, LANES), jnp.float32)], axis=0)
+    partial[...] = total + refs[0][...] if comp > 0 else total
     for copy in copies:
         copy.wait()
 
 
-def apply_twice(comp, place, own, before, after, tables, fields, fibre, so_far, block, offset, rows_out=()):
-    scale, unscale, to_even, to_all = tables
+def apply_twice(comp, place, own, before, after, tables, fields, fibre, so_far=None, out_rows=None):
+    scale, to_even, to_all = tables
     slots = scale.shape[0]
+    part = slots // PARTS * 2 * SLAB
     vmem = pl.BlockSpec(memory_space=pltpu.VMEM)
     smem = pl.BlockSpec(memory_space=pltpu.SMEM)
     whole = pl.BlockSpec(memory_space=pl.ANY)
     f32 = lambda *shape: pltpu.VMEM(shape, jnp.float32)
+    alone = comp == 0
+    block = part if alone else 2 * part
+    extra = [v for v in (so_far, out_rows) if v is not None]
+    kernel = functools.partial(
+        apply_kernel, comp=comp, row=0 if alone else ROWS * (comp - 1), rows=ROWS if alone else 2 * ROWS,
+        block=block, offset=part if comp == 2 else 0,
+    )
     return pl.pallas_call(
-        functools.partial(apply_kernel, comp=comp, block=block, offset=offset),
+        kernel,
         out_shape=[
             jax.ShapeDtypeStruct((PARTS * block, LANES), jnp.float32),
             jax.ShapeDtypeStruct((8, LANES), jnp.float32),
         ],
-        in_specs=[smem] + [vmem] * 8 + [smem, vmem] + [whole] * len(rows_out),
+        in_specs=[smem] + [vmem] * 7 + [smem] + [vmem, whole][: len(extra)],
         out_specs=[whole, vmem],
-        input_output_aliases={11: 0} if rows_out else {},
+        input_output_aliases={10: 0} if comp == 2 else {},
         scratch_shapes=[
             f32(slots * 2 * SLAB, LANES),
             f32(slots, TILES * LANES),
@@ -476,7 +521,7 @@
         compiler_params=pltpu.CompilerParams(vmem_limit_bytes=VMEM),
         cost_estimate=estimate(15),
         name="apply_twice",
-    )(place, own, before, after, scale, unscale, to_even, to_all, fields, fibre, so_far, *rows_out)
+    )(place, own, before, after, scale, to_even, to_all, fields, fibre, *extra)
 
 
 def combination(total):
@@ -495,48 +540,56 @@
 STEPS = 3
 
 
-def finish_kernel(field, image, images, total, solution_field, residual):
+def finish_kernel(field, image, total, *refs, comps):
+    solution_field, residual = refs[-2:]
     modes = field.shape[0]
     part = STEPS * modes * 2 * SLAB
+    block = part * len(comps)
     sole, cross = combination(total)
 
     def body(step, carry):
         for inner in range(SLAB):
             mode = step * SLAB + inner
-            for comp in range(COMPS):
-                source, block, offset = (image, part, 0) if comp == 0 else (images, 2 * part, (comp - 1) * part)
+            for n in range(len(comps)):
                 for p in range(SLAB):
-                    row = offset + (pl.program_id(0) * modes + mode) * 2 * SLAB + p
-                    b = field[mode, comp, p]
-                    q = swap_back(source[pl.ds(row, PARTS, stride=block), :])
-                    w = swap_back(source[pl.ds(row + SLAB, PARTS, stride=block), :])
-                    solution_field[mode, comp, p] = sole * b - cross * q
-                    residual[mode, comp, p] = b - sole * q + cross * w
+                    row = n * part + (pl.program_id(0) * modes + mode) * 2 * SLAB + p
+                    b = field[mode, comps[n], p]
+                    q = swap_back(image[pl.ds(row, PARTS, stride=block), :])
+                    w = swap_back(image[pl.ds(row + SLAB, PARTS, stride=block), :])
+                    solution_field[mode, comps[n], p] = sole * b - cross * q
+                    residual[mode, comps[n], p] = b - sole * q + cross * w
+        if len(refs) > 2:
+            for inner in range(SLAB):
+                mode = step * SLAB + inner
+                solution_field[mode, 0] = refs[0][mode, 0]
+                residual[mode, 0] = refs[1][mode, 0]
         return carry
 
     lax.fori_loop(0, modes // SLAB, body, 0)
 
 
-def finish(field, image, images, total):
-    block = pl.BlockSpec((field.shape[0] // STEPS,) + field.shape[1:], lambda i: (i, 0, 0, 0, 0))
+def finish(field, comps, image, total, so_far=()):
+    whole = field.shape[2:]
+    rows = field.shape[0] // STEPS
+    index = lambda i: (i, 0, 0, 0, 0)
+    block = pl.BlockSpec((rows, max(comps) + 1) + whole, index)
     vmem = pl.BlockSpec(memory_space=pltpu.VMEM)
+    count = 1 if max(comps) == 0 else COMPS
     return pl.pallas_call(
-        finish_kernel,
+        functools.partial(finish_kernel, comps=comps),
         grid=(STEPS,),
-        out_shape=[jax.ShapeDtypeStruct(field.shape, jnp.float32)] * 2,
-        in_specs=[block, vmem, vmem, vmem],
+        out_shape=[jax.ShapeDtypeStruct((field.shape[0], count) + whole, jnp.float32)] * 2,
+        in_specs=[block, vmem, vmem] + [pl.BlockSpec((rows, 1) + whole, index)] * len(so_far),
         out_specs=[block, block],
         compiler_params=pltpu.CompilerParams(vmem_limit_bytes=VMEM),
-        cost_estimate=estimate(6),
+        cost_estimate=estimate(2.5 * len(comps)),
         name="finish",
-    )(field, image, images, total)
+    )(field, image, total, *so_far)
 
 
 def mode_tables(coupling_table, slots):
     lower, upper, variable, code = (coupling_table[:, n] for n in range(4))
-    within = jnp.arange(slots // PARTS, dtype=jnp.int32)
-    first_modes = jnp.array(ORDER, jnp.int32) * (slots // PARTS)
-    slot = (first_modes[:, None] + within).reshape(slots)
+    slot = jnp.arange(slots, dtype=jnp.int32)
     is_lower = lower[:, None] == slot
     is_upper = upper[:, None] == slot
     degree = jnp.sum(jnp.where(is_upper, code[:, None], 0), axis=0)
@@ -569,17 +622,17 @@
     scale = jnp.sqrt(factorial)
     wide = lambda v: jnp.broadcast_to(v[:, None], (slots, LANES))
     twice = lambda v: jnp.concatenate([v, v], axis=1)
-    return wide(scale), wide(1.0 / scale), twice(to_even), twice(to_all)
+    return wide(scale), twice(to_even), twice(to_all)
 
 
 def all_sum(value):
-    for axis in ("space", "mode"):
+    for axis, bit in (("space", 1), ("space", 2), ("mode", 1)):
         devices = lax.axis_size(axis)
-        bit = 1
-        while bit < devices:
-            value = value + lax.ppermute(value, axis, [(i, i ^ bit) for i in range(devices)])
-            bit *= 2
-    return value
+        value = value + lax.ppermute(value, axis, [(i, i ^ bit) for i in range(devices)])
+    others = [
+        lax.ppermute(value, "mode", [(i, i ^ bit) for i in range(PARTS)]) for bit in range(2, PARTS, 2)
+    ]
+    return (value + others[0]) + (others[1] + others[2])
 
 
 def transposed(right_side, mean_stiffness, ply_stiffness, fibre_weights, ply_map, coupling_table):
@@ -587,40 +640,33 @@
     devices = lax.axis_size("space")
     up = [(i, i + 1) for i in range(devices - 1)]
     down = [(j, i) for i, j in up]
-    index = lax.axis_index("mode").astype(jnp.int32)
-    place = jnp.sum(jnp.where(jnp.array(ORDER) == index, jnp.arange(PARTS, dtype=jnp.int32), 0)).reshape(1)
+    place = lax.axis_index("mode").astype(jnp.int32).reshape(1)
 
     def swap(rows):
-        return lax.all_to_all(rows, "mode", 0, 0, axis_index_groups=[list(ORDER)], tiled=True)
+        return lax.all_to_all(rows, "mode", 0, 0, tiled=True)
 
     def halo(rows):
-        return lax.ppermute(rows, "space", up), lax.ppermute(rows, "space", down)
-
-    (first,) = pack(right_side, 0)
-    (second,) = pack(right_side, 1)
-    own = [swap(first), swap(second)]
-    both, third = pack(right_side, 2, (mean_stiffness, ply_map), own[:1])
-    own.append(swap(third))
-    halos = [halo(rows) for rows in own]
+        return rows, lax.ppermute(rows, "space", up), lax.ppermute(rows, "space", down)
+
+    (first,) = pack(right_side, (0,))
+    both, others = pack(right_side, (1, 2), (mean_stiffness, ply_map), (first,))
+    first, others = halo(swap(first)), halo(swap(others))
     tables = mode_tables(coupling_table, slots)
     both_before = lax.ppermute(both, "space", up)
     both_after = lax.ppermute(both, "space", down)
     fields = stiffness_fields(place, both_before, both, both_after, ply_stiffness)
-    partial = jnp.zeros((8, LANES), jnp.float32)
-    part = slots // PARTS * 2 * SLAB
-    tables_and_fields = (tables, fields, fibre_weights)
-    image, partial = apply_twice(0, place, own[0], *halos[0], *tables_and_fields, partial, part, 0)
+    image, partial = apply_twice(0, place, *first, tables, fields, fibre_weights)
     image = swap(image)
-    images, partial = apply_twice(1, place, own[1], *halos[1], *tables_and_fields, partial, 2 * part, 0)
-    images, partial = apply_twice(
-        2, place, own[2], *halos[2], *tables_and_fields, partial, 2 * part, part, (images,)
-    )
-    return tuple(finish(right_side, image, swap(images), all_sum(partial)))
+    images, partial = apply_twice(1, place, *others, tables, fields, fibre_weights, partial)
+    images, partial = apply_twice(2, place, *others, tables, fields, fibre_weights, partial, images)
+    total = all_sum(partial)
+    done = finish(right_side, (0,), image, total)
+    return tuple(finish(right_side, (1, 2), swap(images), total, tuple(done)))
 
 
 def on_device(right_side, mean_stiffness, ply_stiffness, fibre_weights, ply_map, coupling_table):
     args = (right_side, mean_stiffness, ply_stiffness, fibre_weights, ply_map, coupling_table)
-    fits = right_side.shape[1:] == (COMPS, SLAB, 8, 128) and lax.axis_size("mode") == PARTS
+    fits = right_side.shape[1:] == (COMPS, SLAB, 8, 128) and (lax.axis_size("mode"), lax.axis_size("space")) == (PARTS, 4)
     return transposed(*args) if fits else plain(*args)
 
 

time: 180 us -> 172 us (0.956)
  starting transfers between devices: 63.5 us -> 42.5 us
  waiting for transfers between devices: 38.1 us -> 56.5 us
  local copies, waits for them, and re-layouts: 6.3 us -> 3.8 us
    ppermute x6 -> x7, waiting for transfers between devices: 0.02 us -> 22.7 us  [the longest x3 22.7 us: all_sum(): lax.ppermute(value, 'mode', [(i, i ^ bit) for i in range(PARTS)])]
    ppermute x5 -> x3, waiting for transfers between devices: 28.2 us -> 10.8 us  [all_sum(): lax.ppermute(value, axis, [(i, i ^ bit) for i in range(devices)])]
    all_to_all x5 -> x4, waiting for transfers between devices: 9.87 us -> 23 us  [swap(): return lax.all_to_all(rows, 'mode', 0, 0, tiled=True)]
    ppermute x5 -> x3, starting transfers between devices: 14.6 us -> 3.54 us  [all_sum(): lax.ppermute(value, axis, [(i, i ^ bit) for i in range(devices)])]
    all_to_all x5 -> x4, starting transfers between devices: 28.3 us -> 20.5 us  [swap(): return lax.all_to_all(rows, 'mode', 0, 0, tiled=True)]
    unnamed x24 -> x20, local copies, waits for them, and re-layouts: 3.96 us -> 2.88 us
    ppermute x6 -> x7, starting transfers between devices: 15.1 us -> 14.1 us  [the longest x2 7.14 us: halo(): lax.ppermute(rows, 'space', up)]
  transfers between devices with their start and end apart: 18 -> 16, of which waited for: 6 -> 7; matrix products, arithmetic and copies ran while one was open for 5% -> 4% of each run, Pallas kernels for 30% -> 30%
where the time goes in v5:
time: 172 us; the launch traced here: 171 us
  Pallas kernels  61.4 us (36%)
  waiting for transfers between devices  56.5 us (33%)
  starting transfers between devices  42.5 us (25%)
  other arithmetic  4.05 us (2%)
  local copies, waits for them, and re-layouts  3.8 us (2%)
  matrix products  1.8 us (1%)
    pallas_call x3, Pallas kernels, apply_twice(): pl.pallas_call(kernel, out_shape=[jax.ShapeDtypeStruct((PARTS * block, LA...  39.5 us
    all_to_all x4, waiting for transfers between devices, swap(): return lax.all_to_all(rows, 'mode', 0, 0, tiled=True)  23 us
    ppermute x3, waiting for transfers between devices, all_sum(): lax.ppermute(value, 'mode', [(i, i ^ bit) for i in range(PARTS)])  22.7 us
    all_to_all x4, starting transfers between devices, swap(): return lax.all_to_all(rows, 'mode', 0, 0, tiled=True)  20.5 us
    pallas_call x2, Pallas kernels, finish(): pl.pallas_call(functools.partial(finish_kernel, comps=comps), grid=(STEPS...  11.7 us
    ppermute x3, waiting for transfers between devices, all_sum(): lax.ppermute(value, axis, [(i, i ^ bit) for i in range(devices)])  10.8 us
    pallas_call x2, Pallas kernels, pack(): pl.pallas_call(functools.partial(pack_kernel, comps=comps), grid=(1,), ou...  8.52 us
    ppermute x2, starting transfers between devices, halo(): lax.ppermute(rows, 'space', up)  7.14 us
  transfers between devices with their start and end apart: 16, of which 7 were waited for; matrix products, arithmetic and copies ran while one was open for 4% of the time, Pallas kernels for 30%

profile of v5, /device:TPU:0, one launch (start us, length us, event | category | flops | bytes accessed | tf_op | source)
XLA Modules:
  0.0 170.9 jit_solution(16804610649405582049)
XLA Ops:
  0.6 3.2 %pack.2.refs_2_ = f32[1152,128]{1,0:T(8,128)} custom-call(f32[36,3,3,8,128]{4,3,2,1,0:T(8,128)} %field.7), custom_call_target="tpu_custom_call" | custom-call | flops 2500000000 | bytes 7500000 | tf_op jit(solution)/shard_map/pack/pallas_call | solution.py:206
  3.9 7.3 %all-to-all-start.1 = ((f32[8,144,128]{2,1,0:T(8,128)}), f32[8,144,128]{2,1,0:T(8,128)S(1)}, u32[]{:S(2)}, u32[]{:S(2)}) async-start(f32[8,144,128]{2,1,0:T(8,128)} %bitcast.21), calls=%async_computation.1 | async-start | bytes 1179648 | tf_op jit(solution)/shard_map/all_to_all | solution.py:646
  11.1 5.3 %pack.3 = (f32[2,3,8,128]{3,2,1,0:T(8,128)}, f32[2304,128]{1,0:T(8,128)}) custom-call(f32[36,3,3,8,128]{4,3,2,1,0:T(8,128)} %field.7, f32[3,8,128]{2,1,0:T(8,128)} %refs_0_.1, s32[3,8,128]{2,1,0:T(8,128)} %refs_1_.1, f32[1152,128]{1,0:T(8,128)} %pack.2.refs_2_), custom_call_target="tpu_custom_call" | custom-call | flops 5000000000 | bytes 15000000 | tf_op jit(solution)/shard_map/pack/pallas_call | solution.py:206
  17.7 3.0 %collective-permute-start.2 = (f32[2,3,8,128]{3,2,1,0:T(8,128)}, f32[2,3,8,128]{3,2,1,0:T(8,128)S(1)}, u32[]{:S(2)}, u32[]{:S(2)}) collective-permute-start(f32[2,3,8,128]{3,2,1,0:T(8,128)} %get-tuple-element.13.both), channel_id=1, source_target_pairs={{0,1},{1,2},{2,3},{4,5},{5,6},{6,7},{8,9},{9,10},{10,11},{12,13},{... | collective-permute-start | bytes 73736 | tf_op jit(solution)/shard_map/ppermute | solution.py:655
  21.2 5.9 %all-to-all-done.1 = f32[8,144,128]{2,1,0:T(8,128)S(1)} async-done(((f32[8,144,128]{2,1,0:T(8,128)}), f32[8,144,128]{2,1,0:T(8,128)S(1)}, u32[]{:S(2)}, u32[]{:S(2)}) %all-to-all-start.1) | async-done | bytes 589856 | tf_op jit(solution)/shard_map/all_to_all | solution.py:646
  27.0 3.6 %all-to-all-start = ((f32[8,288,128]{2,1,0:T(8,128)}), f32[8,288,128]{2,1,0:T(8,128)S(1)}, u32[]{:S(2)}, u32[]{:S(2)}) async-start(f32[8,288,128]{2,1,0:T(8,128)} %bitcast.15), calls=%async_computation | async-start | bytes 2359296 | tf_op jit(solution)/shard_map/all_to_all | solution.py:646
  34.4 3.1 %collective-permute-start.4 = (f32[1152,128]{1,0:T(8,128)S(1)}, f32[1152,128]{1,0:T(8,128)S(1)}, u32[]{:S(2)}, u32[]{:S(2)}) collective-permute-start(f32[1152,128]{1,0:T(8,128)S(1)} %bitcast.19), channel_id=1, source_target_pairs={{0,1},{1,2},{2,3},{4,5},{5,6},{6,7},{8,9},{9,10},{10,11},{12,13},{... | collective-permute-start | bytes 1769480 | tf_op jit(solution)/shard_map/ppermute | solution.py:649
  40.6 1.7 stiffness_fields.1.fields
  42.2 17.2 %all-to-all-done = f32[8,288,128]{2,1,0:T(8,128)S(1)} async-done(((f32[8,288,128]{2,1,0:T(8,128)}), f32[8,288,128]{2,1,0:T(8,128)S(1)}, u32[]{:S(2)}, u32[]{:S(2)}) %all-to-all-start) | async-done | bytes 1179680 | tf_op jit(solution)/shard_map/all_to_all | solution.py:646
  60.7 4.1 %collective-permute-start = (f32[2304,128]{1,0:T(8,128)S(1)}, f32[2304,128]{1,0:T(8,128)}, u32[]{:S(2)}, u32[]{:S(2)}) collective-permute-start(f32[2304,128]{1,0:T(8,128)S(1)} %bitcast.12), channel_id=1, source_target_pairs={{0,1},{1,2},{2,3},{4,5},{5,6},{6,7},{8,9},{9,10},{10,11},{12,13},{... | collective-permute-start | bytes 3538952 | tf_op jit(solution)/shard_map/ppermute | solution.py:649
  65.8 12.7 %apply_twice.3 = (f32[1728,128]{1,0:T(8,128)}, f32[8,128]{1,0:T(8,128)}) custom-call(s32[1]{0:T(128)} %bitcast.place, f32[1152,128]{1,0:T(8,128)} %bitcast.20, f32[1152,128]{1,0:T(8,128)} %copy-done.7, f32[1152,128]{1,0:T(8,128)} %copy-done.6, f32[288,128]{1,0:T(8,128)} %broadcast_in_dim.90.scale, bf16[624,576]{1,0:T(8,128)(2,1)} %pad_maximum_fusion.to_even, ...), custom_call_target="tpu_custom_call" | custom-call | flops 15000000512 | bytes 45000000 | tf_op jit(solution)/shard_map/apply_twice/pallas_call | solution.py:500
  78.6 3.7 %all-to-all-start.3 = ((f32[8,216,128]{2,1,0:T(8,128)}), f32[8,216,128]{2,1,0:T(8,128)S(1)}, u32[]{:S(2)}, u32[]{:S(2)}) async-start(f32[8,216,128]{2,1,0:T(8,128)} %bitcast.17), calls=%async_computation.3 | async-start | bytes 1769472 | tf_op jit(solution)/shard_map/all_to_all | solution.py:646
  82.3 13.4 %apply_twice.4 = (f32[3456,128]{1,0:T(8,128)}, f32[8,128]{1,0:T(8,128)}) custom-call(s32[1]{0:T(128)} %bitcast.place, f32[2304,128]{1,0:T(8,128)} %bitcast.13, f32[2304,128]{1,0:T(8,128)} %collective-permute-done.before, f32[2304,128]{1,0:T(8,128)} %collective-permute-done.1.after, f32[288,128]{1,0:T(8,128)} %broadcast_in_dim.90.scale, ...), custom_call_target="tpu_custom_call" | custom-call | flops 15000000512 | bytes 45000000 | tf_op jit(solution)/shard_map/apply_twice/pallas_call | solution.py:500
  95.7 13.4 %apply_twice.5 = (f32[3456,128]{1,0:T(8,128)}, f32[8,128]{1,0:T(8,128)}) custom-call(s32[1]{0:T(128)} %bitcast.place, f32[2304,128]{1,0:T(8,128)} %bitcast.14, f32[2304,128]{1,0:T(8,128)} %collective-permute-done.before, f32[2304,128]{1,0:T(8,128)} %collective-permute-done.1.after, ...), custom_call_target="tpu_custom_call", output_to_operand_aliasing={{0}: (10, {})} | custom-call | flops 15000000512 | bytes 45000000 | tf_op jit(solution)/shard_map/apply_twice/pallas_call | solution.py:500
  110.1 5.9 %all-to-all-start.2 = ((f32[8,432,128]{2,1,0:T(8,128)}), f32[8,432,128]{2,1,0:T(8,128)S(1)}, u32[]{:S(2)}, u32[]{:S(2)}) async-start(f32[8,432,128]{2,1,0:T(8,128)} %bitcast.10), calls=%async_computation.2 | async-start | bytes 3538944 | tf_op jit(solution)/shard_map/all_to_all | solution.py:646
  117.2 1.5 collective-permute-start.7
  118.7 2.1 %collective-permute-done.7 = f32[8,128]{1,0:T(8,128)S(1)} collective-permute-done((f32[8,128]{1,0:T(8,128)S(1)}, f32[8,128]{1,0:T(8,128)S(1)}, u32[]{:S(2)}, u32[]{:S(2)}) %collective-permute-start.7) | collective-permute-done | bytes 4128 | tf_op jit(solution)/shard_map/ppermute | solution.py:631
  120.8 2.0 %collective-permute-start.8 = (f32[8,128]{1,0:T(8,128)S(1)}, f32[8,128]{1,0:T(8,128)S(1)}, u32[]{:S(2)}, u32[]{:S(2)}) collective-permute-start(f32[8,128]{1,0:T(8,128)S(1)} %add.38), channel_id=1, source_target_pairs={{0,4},{4,0},{8,12},{12,8},{16,20},{20,16},{24,28},{28,24},{1,5},{5... | collective-permute-start | bytes 12296 | tf_op jit(solution)/shard_map/ppermute | solution.py:631
  122.8 7.6 %collective-permute-done.8 = f32[8,128]{1,0:T(8,128)S(1)} collective-permute-done((f32[8,128]{1,0:T(8,128)S(1)}, f32[8,128]{1,0:T(8,128)S(1)}, u32[]{:S(2)}, u32[]{:S(2)}) %collective-permute-start.8) | collective-permute-done | bytes 4128 | tf_op jit(solution)/shard_map/ppermute | solution.py:631
  130.4 3.3 %collective-permute-start.11 = (f32[8,128]{1,0:T(8,128)S(1)}, f32[8,128]{1,0:T(8,128)S(1)}, u32[]{:S(2)}, u32[]{:S(2)}) collective-permute-start(f32[8,128]{1,0:T(8,128)S(1)} %add.39), channel_id=1, source_target_pairs={{0,24},{4,28},{8,16},{12,20},{16,8},{20,12},{24,0},{28,4},{1,25},{... | collective-permute-start | bytes 12296 | tf_op jit(solution)/shard_map/ppermute | solution.py:633
  134.8 14.0 %collective-permute-done.11 = f32[8,128]{1,0:T(8,128)S(1)} collective-permute-done((f32[8,128]{1,0:T(8,128)S(1)}, f32[8,128]{1,0:T(8,128)S(1)}, u32[]{:S(2)}, u32[]{:S(2)}) %collective-permute-start.11) | collective-permute-done | bytes 4128 | tf_op jit(solution)/shard_map/ppermute | solution.py:633
  148.8 8.6 %collective-permute-done.10 = f32[8,128]{1,0:T(8,128)S(1)} collective-permute-done((f32[8,128]{1,0:T(8,128)S(1)}, f32[8,128]{1,0:T(8,128)S(1)}, u32[]{:S(2)}, u32[]{:S(2)}) %collective-permute-start.10) | collective-permute-done | bytes 4128 | tf_op jit(solution)/shard_map/ppermute | solution.py:633
  158.0 5.2 %finish.2 = (f32[36,1,3,8,128]{4,3,2,1,0:T(8,128)}, f32[36,1,3,8,128]{4,3,2,1,0:T(8,128)}) custom-call(f32[36,3,3,8,128]{4,3,2,1,0:T(8,128)} %field.7, f32[1728,128]{1,0:T(8,128)} %bitcast.16, f32[8,128]{1,0:T(8,128)} %add_add_fusion.total), custom_call_target="tpu_custom_call" | custom-call | flops 2500000000 | bytes 7500000 | tf_op jit(solution)/shard_map/finish/pallas_call | solution.py:578
  164.4 6.5 %finish.3 = (f32[36,3,3,8,128]{4,3,2,1,0:T(8,128)}, f32[36,3,3,8,128]{4,3,2,1,0:T(8,128)}) custom-call(f32[36,3,3,8,128]{4,3,2,1,0:T(8,128)} %field.7, f32[3456,128]{1,0:T(8,128)} %bitcast.9, f32[8,128]{1,0:T(8,128)} %add_add_fusion.total, f32[36,1,3,8,128]{4,3,2,1,0:T(8,128)} %get-tuple-element.20.refs_0_, f32[36,1,3,8,128]{4,3,2,1,0:T(8,128)} %get-tuple-element.21.refs_1_), custom_call_target="tpu_custom_call" | custom-call | flops 5000000000 | bytes 15000000 | tf_op jit(solution)/shard_map/finish/pallas_call | solution.py:578
  (57 shorter events, 15.9 us)
Async XLA Ops:
  3.9 23.1 %all-to-all-start.1 = ((f32[8,144,128]{2,1,0:T(8,128)}), f32[8,144,128]{2,1,0:T(8,128)S(1)}, u32[]{:S(2)}, u32[]{:S(2)}) async-start(f32[8,144,128]{2,1,0:T(8,128)} %bitcast.21), calls=%async_computation.1 | async-start | bytes 1179648 | tf_op jit(solution)/shard_map/all_to_all | solution.py:646
  11.1 9.6 %copy-start.4 = (s32[660,4]{0,1:T(4,128)S(1)}, s32[660,4]{0,1:T(4,128)}, u32[]{:S(2)}) copy-start(s32[660,4]{0,1:T(4,128)} %param.11) | copy-start | bytes 31684
  16.4 23.6 %collective-permute-start.3 = (f32[2,3,8,128]{3,2,1,0:T(8,128)}, f32[2,3,8,128]{3,2,1,0:T(8,128)S(1)}, u32[]{:S(2)}, u32[]{:S(2)}) collective-permute-start(f32[2,3,8,128]{3,2,1,0:T(8,128)} %get-tuple-element.13.both), channel_id=1, source_target_pairs={{1,0},{2,1},{3,2},{5,4},{6,5},{7,6},{9,8},{10,9},{11,10},{13,12},{... | collective-permute-start | bytes 73736 | tf_op jit(solution)/shard_map/ppermute | solution.py:656
  17.7 22.3 %collective-permute-start.2 = (f32[2,3,8,128]{3,2,1,0:T(8,128)}, f32[2,3,8,128]{3,2,1,0:T(8,128)S(1)}, u32[]{:S(2)}, u32[]{:S(2)}) collective-permute-start(f32[2,3,8,128]{3,2,1,0:T(8,128)} %get-tuple-element.13.both), channel_id=1, source_target_pairs={{0,1},{1,2},{2,3},{4,5},{5,6},{6,7},{8,9},{9,10},{10,11},{12,13},{... | collective-permute-start | bytes 73736 | tf_op jit(solution)/shard_map/ppermute | solution.py:655
  27.0 7.4 %copy-start.3 = (f32[8,144,128]{2,1,0:T(8,128)}, f32[8,144,128]{2,1,0:T(8,128)S(1)}, u32[]{:S(2)}) copy-start(f32[8,144,128]{2,1,0:T(8,128)S(1)} %all-to-all-done.1) | copy-start | bytes 1769476
  27.0 32.4 %all-to-all-start = ((f32[8,288,128]{2,1,0:T(8,128)}), f32[8,288,128]{2,1,0:T(8,128)S(1)}, u32[]{:S(2)}, u32[]{:S(2)}) async-start(f32[8,288,128]{2,1,0:T(8,128)} %bitcast.15), calls=%async_computation | async-start | bytes 2359296 | tf_op jit(solution)/shard_map/all_to_all | solution.py:646
  33.1 31.6 %collective-permute-start.5 = (f32[1152,128]{1,0:T(8,128)S(1)}, f32[1152,128]{1,0:T(8,128)S(1)}, u32[]{:S(2)}, u32[]{:S(2)}) collective-permute-start(f32[1152,128]{1,0:T(8,128)S(1)} %bitcast.18), channel_id=1, source_target_pairs={{1,0},{2,1},{3,2},{5,4},{6,5},{7,6},{9,8},{10,9},{11,10},{13,12},{... | collective-permute-start | bytes 1769480 | tf_op jit(solution)/shard_map/ppermute | solution.py:649
  34.4 30.3 %collective-permute-start.4 = (f32[1152,128]{1,0:T(8,128)S(1)}, f32[1152,128]{1,0:T(8,128)S(1)}, u32[]{:S(2)}, u32[]{:S(2)}) collective-permute-start(f32[1152,128]{1,0:T(8,128)S(1)} %bitcast.19), channel_id=1, source_target_pairs={{0,1},{1,2},{2,3},{4,5},{5,6},{6,7},{8,9},{9,10},{10,11},{12,13},{... | collective-permute-start | bytes 1769480 | tf_op jit(solution)/shard_map/ppermute | solution.py:649
  59.4 19.1 %copy-start.1 = (f32[8,288,128]{2,1,0:T(8,128)}, f32[8,288,128]{2,1,0:T(8,128)S(1)}, u32[]{:S(2)}) copy-start(f32[8,288,128]{2,1,0:T(8,128)S(1)} %all-to-all-done) | copy-start | bytes 3538948
  59.4 22.9 %collective-permute-start.1 = (f32[2304,128]{1,0:T(8,128)S(1)}, f32[2304,128]{1,0:T(8,128)}, u32[]{:S(2)}, u32[]{:S(2)}) collective-permute-start(f32[2304,128]{1,0:T(8,128)S(1)} %bitcast.11), channel_id=1, source_target_pairs={{1,0},{2,1},{3,2},{5,4},{6,5},{7,6},{9,8},{10,9},{11,10},{13,12},{... | collective-permute-start | bytes 3538952 | tf_op jit(solution)/shard_map/ppermute | solution.py:649
  60.7 21.6 %collective-permute-start = (f32[2304,128]{1,0:T(8,128)S(1)}, f32[2304,128]{1,0:T(8,128)}, u32[]{:S(2)}, u32[]{:S(2)}) collective-permute-start(f32[2304,128]{1,0:T(8,128)S(1)} %bitcast.12), channel_id=1, source_target_pairs={{0,1},{1,2},{2,3},{4,5},{5,6},{6,7},{8,9},{9,10},{10,11},{12,13},{... | collective-permute-start | bytes 3538952 | tf_op jit(solution)/shard_map/ppermute | solution.py:649
  64.8 0.9 copy-start.6
  64.8 1.0 copy-start.7
  78.6 30.6 %all-to-all-start.3 = ((f32[8,216,128]{2,1,0:T(8,128)}), f32[8,216,128]{2,1,0:T(8,128)S(1)}, u32[]{:S(2)}, u32[]{:S(2)}) async-start(f32[8,216,128]{2,1,0:T(8,128)} %bitcast.17), calls=%async_computation.3 | async-start | bytes 1769472 | tf_op jit(solution)/shard_map/all_to_all | solution.py:646
  109.2 0.9 copy-start.2
  109.2 6.8 %copy-start.5 = (f32[8,128]{1,0:T(8,128)S(1)}, f32[8,128]{1,0:T(8,128)}, u32[]{:S(2)}) copy-start(f32[8,128]{1,0:T(8,128)} %get-tuple-element.18) | copy-start | bytes 12292
  110.1 53.1 %all-to-all-start.2 = ((f32[8,432,128]{2,1,0:T(8,128)}), f32[8,432,128]{2,1,0:T(8,128)S(1)}, u32[]{:S(2)}, u32[]{:S(2)}) async-start(f32[8,432,128]{2,1,0:T(8,128)} %bitcast.10), calls=%async_computation.2 | async-start | bytes 3538944 | tf_op jit(solution)/shard_map/all_to_all | solution.py:646
  116.0 1.2 collective-permute-start.6
  117.2 3.6 %collective-permute-start.7 = (f32[8,128]{1,0:T(8,128)S(1)}, f32[8,128]{1,0:T(8,128)S(1)}, u32[]{:S(2)}, u32[]{:S(2)}) collective-permute-start(f32[8,128]{1,0:T(8,128)S(1)} %add.37), channel_id=1, source_target_pairs={{0,2},{1,3},{2,0},{3,1},{4,6},{5,7},{6,4},{7,5},{8,10},{9,11},{10,... | collective-permute-start | bytes 12296 | tf_op jit(solution)/shard_map/ppermute | solution.py:631
  120.8 9.5 %collective-permute-start.8 = (f32[8,128]{1,0:T(8,128)S(1)}, f32[8,128]{1,0:T(8,128)S(1)}, u32[]{:S(2)}, u32[]{:S(2)}) collective-permute-start(f32[8,128]{1,0:T(8,128)S(1)} %add.38), channel_id=1, source_target_pairs={{0,4},{4,0},{8,12},{12,8},{16,20},{20,16},{24,28},{28,24},{1,5},{5... | collective-permute-start | bytes 12296 | tf_op jit(solution)/shard_map/ppermute | solution.py:631
  130.4 18.4 %collective-permute-start.11 = (f32[8,128]{1,0:T(8,128)S(1)}, f32[8,128]{1,0:T(8,128)S(1)}, u32[]{:S(2)}, u32[]{:S(2)}) collective-permute-start(f32[8,128]{1,0:T(8,128)S(1)} %add.39), channel_id=1, source_target_pairs={{0,24},{4,28},{8,16},{12,20},{16,8},{20,12},{24,0},{28,4},{1,25},{... | collective-permute-start | bytes 12296 | tf_op jit(solution)/shard_map/ppermute | solution.py:633
  133.6 23.8 %collective-permute-start.10 = (f32[8,128]{1,0:T(8,128)S(1)}, f32[8,128]{1,0:T(8,128)S(1)}, u32[]{:S(2)}, u32[]{:S(2)}) collective-permute-start(f32[8,128]{1,0:T(8,128)S(1)} %add.39), channel_id=1, source_target_pairs={{0,16},{4,20},{8,24},{12,28},{16,0},{20,4},{24,8},{28,12},{1,17},{... | collective-permute-start | bytes 12296 | tf_op jit(solution)/shard_map/ppermute | solution.py:633
  133.6 23.8 %collective-permute-start.9 = (f32[8,128]{1,0:T(8,128)S(1)}, f32[8,128]{1,0:T(8,128)S(1)}, u32[]{:S(2)}, u32[]{:S(2)}) collective-permute-start(f32[8,128]{1,0:T(8,128)S(1)} %add.39), channel_id=1, source_target_pairs={{0,8},{4,12},{8,0},{12,4},{16,24},{20,28},{24,16},{28,20},{1,9},{5... | collective-permute-start | bytes 12296 | tf_op jit(solution)/shard_map/ppermute | solution.py:633
  163.2 1.2 copy-start
  (2 other events, 1.2 us)

commit v6 on v5

--- a/solution.py
+++ b/solution.py
@@ -188,7 +188,7 @@
                 planes = [field[mode, comp, x] for x in range(SLAB)]
                 halo = halo_row(dict(enumerate(planes)))
                 for p, tile in enumerate(planes + [halo]):
-                    out[pl.ds(mode * rows + n * ROWS + p, PARTS, stride=rows * modes), :] = swap_out(tile)
+                    out[pl.ds((n * modes + mode) * ROWS + p, PARTS, stride=rows * modes), :] = swap_out(tile)
         return carry
 
     lax.fori_loop(0, modes // unroll, body, 0)
@@ -215,6 +215,34 @@
         cost_estimate=estimate(2.5 * len(comps)),
         name="pack",
     )(field, *stiffness, *after)
+
+
+def part_kernel(rows, ready, *refs):
+    *outs, sems = refs
+    size = outs[0].shape[0] // PARTS
+    copies = []
+    for n, out in enumerate(outs):
+        for device in range(PARTS):
+            source = rows.at[pl.ds((device * len(outs) + n) * size, size), :]
+            goal = out.at[pl.ds(device * size, size), :]
+            copies.append(pltpu.make_async_copy(source, goal, sems.at[n * PARTS + device]))
+    for copy in copies:
+        copy.start()
+    for copy in copies:
+        copy.wait()
+
+
+def part_components(rows, ready, count):
+    whole = pl.BlockSpec(memory_space=pl.ANY)
+    return pl.pallas_call(
+        part_kernel,
+        out_shape=[jax.ShapeDtypeStruct((rows.shape[0] // count, LANES), jnp.float32)] * count,
+        in_specs=[whole, whole],
+        out_specs=[whole] * count,
+        scratch_shapes=[pltpu.SemaphoreType.DMA((count * PARTS,))],
+        cost_estimate=estimate(1),
+        name="part_components",
+    )(rows, ready)
 
 
 def stiffness_kernel(place, before, both, after, ply_stiffness, fields, wide):
@@ -328,7 +356,7 @@
                 )
 
 
-CHUNK = 2
+CHUNK = 4
 
 
 def chunks(count):
@@ -431,15 +459,15 @@
 
 
 def apply_kernel(
-    place, own, before, after, scale, to_even, to_all, fields, fibre, *refs, comp, row, rows, block, offset,
+    place, own, before, after, scale, to_even, to_all, fields, fibre, *refs, comp,
 ):
-    out_rows, partial, out, field, first, second, mixed, flux, scaled, acc, faces, sems = refs[-12:]
+    out, partial, field, first, second, mixed, flux, scaled, acc, faces = refs[-10:]
     slots = scale.shape[0]
     here = place[0]
     face_stiffness(fields, faces, [fibre[comp, d] for d in range(3)], here)
     lane = lax.broadcasted_iota(jnp.int32, (slots, LANES), 1)
     slot = lane % WIDE
-    load = lambda ref, p: ref[pl.ds(row + p, slots, stride=rows), :]
+    load = lambda ref, p: ref[pl.ds(p, slots, stride=ROWS), :]
     left = pltpu.roll(load(before, 3), LANES - 3, 1)
     right = pltpu.roll(load(after, 3), 3, 1)
     halo = jnp.where((slot == 0) | (slot == 5), left, load(own, 3))
@@ -467,47 +495,25 @@
         out[pl.ds(p + SLAB, slots, stride=2 * SLAB), :] = w
         for n, (one, two) in enumerate(((b, b), (b, q), (q, q), (b, w), (q, w))):
             sums[n] = sums[n] + jnp.sum(one * two, axis=0, keepdims=True)
-    part = slots // PARTS * 2 * SLAB
-    copies = [
-        pltpu.make_async_copy(
-            out.at[pl.ds(n * part, part), :], out_rows.at[pl.ds(n * block + offset, part), :], sems.at[n]
-        )
-        for n in range(PARTS)
-    ]
-    for copy in copies:
-        copy.start()
     total = jnp.concatenate(sums + [jnp.zeros((3, LANES), jnp.float32)], axis=0)
     partial[...] = total + refs[0][...] if comp > 0 else total
-    for copy in copies:
-        copy.wait()
-
-
-def apply_twice(comp, place, own, before, after, tables, fields, fibre, so_far=None, out_rows=None):
+
+
+def apply_twice(comp, place, own, before, after, tables, fields, fibre, *so_far):
     scale, to_even, to_all = tables
     slots = scale.shape[0]
-    part = slots // PARTS * 2 * SLAB
     vmem = pl.BlockSpec(memory_space=pltpu.VMEM)
     smem = pl.BlockSpec(memory_space=pltpu.SMEM)
-    whole = pl.BlockSpec(memory_space=pl.ANY)
     f32 = lambda *shape: pltpu.VMEM(shape, jnp.float32)
-    alone = comp == 0
-    block = part if alone else 2 * part
-    extra = [v for v in (so_far, out_rows) if v is not None]
-    kernel = functools.partial(
-        apply_kernel, comp=comp, row=0 if alone else ROWS * (comp - 1), rows=ROWS if alone else 2 * ROWS,
-        block=block, offset=part if comp == 2 else 0,
-    )
     return pl.pallas_call(
-        kernel,
+        functools.partial(apply_kernel, comp=comp),
         out_shape=[
-            jax.ShapeDtypeStruct((PARTS * block, LANES), jnp.float32),
+            jax.ShapeDtypeStruct((slots * 2 * SLAB, LANES), jnp.float32),
             jax.ShapeDtypeStruct((8, LANES), jnp.float32),
         ],
-        in_specs=[smem] + [vmem] * 7 + [smem] + [vmem, whole][: len(extra)],
-        out_specs=[whole, vmem],
-        input_output_aliases={10: 0} if comp == 2 else {},
+        in_specs=[smem] + [vmem] * 7 + [smem] + [vmem] * len(so_far),
+        out_specs=[vmem, vmem],
         scratch_shapes=[
-            f32(slots * 2 * SLAB, LANES),
             f32(slots, TILES * LANES),
             f32(slots, INNER * LANES),
             f32(slots, SLAB * LANES),
@@ -516,75 +522,68 @@
             f32(FULL, INNER * LANES),
             f32(slots, INNER * LANES),
             f32(6 * FACE + 8, TILES * LANES),
-            pltpu.SemaphoreType.DMA((PARTS,)),
         ],
         compiler_params=pltpu.CompilerParams(vmem_limit_bytes=VMEM),
         cost_estimate=estimate(15),
         name="apply_twice",
-    )(place, own, before, after, scale, to_even, to_all, fields, fibre, *extra)
-
-
-def combination(total):
+    )(place, own, before, after, scale, to_even, to_all, fields, fibre, *so_far)
+
+
+def factor_kernel(total, factors):
     bb, bq, qq, bw, qw = (jnp.sum(total[n : n + 1, :], axis=1, keepdims=True) for n in range(5))
     step_one = bb / bq
     norm = bb - 2.0 * step_one * bq + step_one * step_one * qq
     grown = 1.0 + norm / bb
     curve = grown * grown * bq - step_one * grown * (bw + qq) + step_one * step_one * qw
     step_two = norm / curve
-    spread = lambda v: jnp.broadcast_to(v, (8, LANES))
-    sole = spread(step_one + step_two * grown)
-    cross = spread(step_one * step_two)
-    return sole, cross
-
-
-STEPS = 3
-
-
-def finish_kernel(field, image, total, *refs, comps):
+    factors[0:8, :] = jnp.broadcast_to(step_one + step_two * grown, (8, LANES))
+    factors[8:16, :] = jnp.broadcast_to(step_one * step_two, (8, LANES))
+
+
+def combination(total):
+    return pl.pallas_call(
+        factor_kernel,
+        out_shape=jax.ShapeDtypeStruct((16, LANES), jnp.float32),
+        cost_estimate=estimate(1),
+        name="combination",
+    )(total)
+
+
+def finish_kernel(field, image, factors, *refs):
+    modes = field.shape[0]
     solution_field, residual = refs[-2:]
-    modes = field.shape[0]
-    part = STEPS * modes * 2 * SLAB
-    block = part * len(comps)
-    sole, cross = combination(total)
+    per_part = modes * 2 * SLAB
+    sole, cross = factors[0:8, :], factors[8:16, :]
 
     def body(step, carry):
-        for inner in range(SLAB):
-            mode = step * SLAB + inner
-            for n in range(len(comps)):
-                for p in range(SLAB):
-                    row = n * part + (pl.program_id(0) * modes + mode) * 2 * SLAB + p
-                    b = field[mode, comps[n], p]
-                    q = swap_back(image[pl.ds(row, PARTS, stride=block), :])
-                    w = swap_back(image[pl.ds(row + SLAB, PARTS, stride=block), :])
-                    solution_field[mode, comps[n], p] = sole * b - cross * q
-                    residual[mode, comps[n], p] = b - sole * q + cross * w
-        if len(refs) > 2:
-            for inner in range(SLAB):
-                mode = step * SLAB + inner
-                solution_field[mode, 0] = refs[0][mode, 0]
-                residual[mode, 0] = refs[1][mode, 0]
+        for inner in range(2 * UNROLL):
+            mode = step * 2 * UNROLL + inner
+            for p in range(SLAB):
+                row = mode * 2 * SLAB + p
+                b = field[mode, 0, p]
+                q = swap_back(image[pl.ds(row, PARTS, stride=per_part), :])
+                w = swap_back(image[pl.ds(row + SLAB, PARTS, stride=per_part), :])
+                solution_field[mode, 0, p] = sole * b - cross * q
+                residual[mode, 0, p] = b - sole * q + cross * w
         return carry
 
-    lax.fori_loop(0, modes // SLAB, body, 0)
-
-
-def finish(field, comps, image, total, so_far=()):
-    whole = field.shape[2:]
-    rows = field.shape[0] // STEPS
-    index = lambda i: (i, 0, 0, 0, 0)
-    block = pl.BlockSpec((rows, max(comps) + 1) + whole, index)
+    lax.fori_loop(0, modes // (2 * UNROLL), body, 0)
+
+
+def finish(field, comp, image, factors, so_far):
+    block = pl.BlockSpec((field.shape[0], 1) + field.shape[2:], lambda i: (0, comp, 0, 0, 0))
     vmem = pl.BlockSpec(memory_space=pltpu.VMEM)
-    count = 1 if max(comps) == 0 else COMPS
     return pl.pallas_call(
-        functools.partial(finish_kernel, comps=comps),
-        grid=(STEPS,),
-        out_shape=[jax.ShapeDtypeStruct((field.shape[0], count) + whole, jnp.float32)] * 2,
-        in_specs=[block, vmem, vmem] + [pl.BlockSpec((rows, 1) + whole, index)] * len(so_far),
+        finish_kernel,
+        grid=(1,),
+        out_shape=[jax.ShapeDtypeStruct(field.shape, jnp.float32)] * 2,
+        in_specs=[block, vmem, vmem] + [pl.BlockSpec(memory_space=pl.ANY)] * len(so_far),
         out_specs=[block, block],
+        input_output_aliases={3 + n: n for n in range(len(so_far))},
         compiler_params=pltpu.CompilerParams(vmem_limit_bytes=VMEM),
-        cost_estimate=estimate(2.5 * len(comps)),
+        cost_estimate=estimate(3),
         name="finish",
-    )(field, image, total, *so_far)
+    )(field, image, factors, *so_far)
 
 
 def mode_tables(coupling_table, slots):
@@ -650,18 +649,23 @@
 
     (first,) = pack(right_side, (0,))
     both, others = pack(right_side, (1, 2), (mean_stiffness, ply_map), (first,))
-    first, others = halo(swap(first)), halo(swap(others))
+    first = halo(swap(first))
+    others = swap(others)
     tables = mode_tables(coupling_table, slots)
     both_before = lax.ppermute(both, "space", up)
     both_after = lax.ppermute(both, "space", down)
     fields = stiffness_fields(place, both_before, both, both_after, ply_stiffness)
     image, partial = apply_twice(0, place, *first, tables, fields, fibre_weights)
-    image = swap(image)
-    images, partial = apply_twice(1, place, *others, tables, fields, fibre_weights, partial)
-    images, partial = apply_twice(2, place, *others, tables, fields, fibre_weights, partial, images)
-    total = all_sum(partial)
-    done = finish(right_side, (0,), image, total)
-    return tuple(finish(right_side, (1, 2), swap(images), total, tuple(done)))
+    images = [swap(image)]
+    parts = part_components(others, partial, COMPS - 1)
+    for comp, rows in enumerate(parts, 1):
+        image, partial = apply_twice(comp, place, *halo(rows), tables, fields, fibre_weights, partial)
+        images.append(swap(image))
+    factors = combination(all_sum(partial))
+    outputs = ()
+    for comp in range(COMPS):
+        outputs = finish(right_side, comp, images[comp], factors, outputs)
+    return tuple(outputs)
 
 
 def on_device(right_side, mean_stiffness, ply_stiffness, fibre_weights, ply_map, coupling_table):

time: 172 us -> 208 us (1.21)
  Pallas kernels: 61.4 us -> 96 us
  starting transfers between devices: 42.5 us -> 47.5 us
  waiting for transfers between devices: 56.5 us -> 51.7 us
    pallas_call x5 -> x8, Pallas kernels: 51.2 us -> 85.9 us  [the longest x1 37 us: part_components(): pl.pallas_call(part_kernel, out_shape=[jax.ShapeDtypeStruct((rows.shape[0...]
    ppermute x3, waiting for transfers between devices: 22.7 us -> 9.6 us  [all_sum(): lax.ppermute(value, 'mode', [(i, i ^ bit) for i in range(PARTS)])]
    all_to_all x4 -> x5, waiting for transfers between devices: 23 us -> 35.4 us  [swap(): return lax.all_to_all(rows, 'mode', 0, 0, tiled=True)]
    ppermute x3, waiting for transfers between devices: 10.8 us -> 6.6 us  [all_sum(): lax.ppermute(value, axis, [(i, i ^ bit) for i in range(devices)])]
    ppermute x2 -> x3, starting transfers between devices: 7.14 us -> 11 us  [halo(): lax.ppermute(rows, 'space', up)]
    unnamed x20 -> x28, local copies, waits for them, and re-layouts: 2.88 us -> 4.39 us
    all_to_all x4 -> x5, starting transfers between devices: 20.5 us -> 21.7 us  [swap(): return lax.all_to_all(rows, 'mode', 0, 0, tiled=True)]
  transfers between devices with their start and end apart: 16 -> 19, of which waited for: 7 -> 9; matrix products, arithmetic and copies ran while one was open for 4% -> 3% of each run, Pallas kernels for 30% -> 23%
where the time goes in v6:
time: 208 us; the launch traced here: 207 us
  Pallas kernels  96 us (46%)
  waiting for transfers between devices  51.7 us (25%)
  starting transfers between devices  47.5 us (23%)
  local copies, waits for them, and re-layouts  5.33 us (3%)
  other arithmetic  4.01 us (2%)
    pallas_call x1, Pallas kernels, part_components(): pl.pallas_call(part_kernel, out_shape=[jax.ShapeDtypeStruct((rows.shape[0...  37 us
    pallas_call x3, Pallas kernels, apply_twice(): pl.pallas_call(functools.partial(apply_kernel, comp=comp), out_shape=[jax...  36.3 us
    all_to_all x5, waiting for transfers between devices, swap(): return lax.all_to_all(rows, 'mode', 0, 0, tiled=True)  35.4 us
    all_to_all x5, starting transfers between devices, swap(): return lax.all_to_all(rows, 'mode', 0, 0, tiled=True)  21.7 us
    pallas_call x3, Pallas kernels, finish(): pl.pallas_call(finish_kernel, grid=(1,), out_shape=[jax.ShapeDtypeStruct(...  11.2 us
    ppermute x3, starting transfers between devices, halo(): lax.ppermute(rows, 'space', up)  11 us
    ppermute x3, waiting for transfers between devices, all_sum(): lax.ppermute(value, 'mode', [(i, i ^ bit) for i in range(PARTS)])  9.6 us
    pallas_call x2, Pallas kernels, pack(): pl.pallas_call(functools.partial(pack_kernel, comps=comps), grid=(1,), ou...  8.52 us
  transfers between devices with their start and end apart: 19, of which 9 were waited for; matrix products, arithmetic and copies ran while one was open for 3% of the time, Pallas kernels for 23%

profile of v6, /device:TPU:0, one launch (start us, length us, event | category | flops | bytes accessed | tf_op | source)
XLA Modules:
  0.0 207.2 jit_solution(1338231091554240189)
XLA Ops:
  3.9 5.3 %pack.3 = (f32[2,3,8,128]{3,2,1,0:T(8,128)}, f32[2304,128]{1,0:T(8,128)}) custom-call(f32[36,3,3,8,128]{4,3,2,1,0:T(8,128)} %field.9, f32[3,8,128]{2,1,0:T(8,128)} %refs_0_.1, s32[3,8,128]{2,1,0:T(8,128)} %refs_1_.1, f32[1152,128]{1,0:T(8,128)} %pack.2.refs_2_), custom_call_target="tpu_custom_call" | custom-call | flops 5000000000 | bytes 15000000 | tf_op jit(solution)/shard_map/pack/pallas_call | solution.py:206
  13.5 7.3 %all-to-all-start.1 = ((f32[8,144,128]{2,1,0:T(8,128)}), f32[8,144,128]{2,1,0:T(8,128)S(1)}, u32[]{:S(2)}, u32[]{:S(2)}) async-start(f32[8,144,128]{2,1,0:T(8,128)} %bitcast.3), calls=%async_computation.1 | async-start | bytes 1179648 | tf_op jit(solution)/shard_map/all_to_all | solution.py:645
  23.6 14.6 %all-to-all-done.1 = f32[8,144,128]{2,1,0:T(8,128)S(1)} async-done(((f32[8,144,128]{2,1,0:T(8,128)}), f32[8,144,128]{2,1,0:T(8,128)S(1)}, u32[]{:S(2)}, u32[]{:S(2)}) %all-to-all-start.1) | async-done | bytes 589856 | tf_op jit(solution)/shard_map/all_to_all | solution.py:645
  38.3 3.6 %all-to-all-start = ((f32[8,288,128]{2,1,0:T(8,128)}), f32[8,288,128]{2,1,0:T(8,128)S(1)}, u32[]{:S(2)}, u32[]{:S(2)}) async-start(f32[8,288,128]{2,1,0:T(8,128)} %bitcast.1), calls=%async_computation | async-start | bytes 2359296 | tf_op jit(solution)/shard_map/all_to_all | solution.py:645
  43.1 3.9 %collective-permute-start = (f32[1152,128]{1,0:T(8,128)S(1)}, f32[1152,128]{1,0:T(8,128)}, u32[]{:S(2)}, u32[]{:S(2)}) collective-permute-start(f32[1152,128]{1,0:T(8,128)S(1)} %bitcast.18), channel_id=1, source_target_pairs={{0,1},{1,2},{2,3},{4,5},{5,6},{6,7},{8,9},{9,10},{10,11},{12,13},{... | collective-permute-start | bytes 1769480 | tf_op jit(solution)/shard_map/ppermute | solution.py:648
  52.6 12.1 %apply_twice.3 = (f32[1728,128]{1,0:T(8,128)}, f32[8,128]{1,0:T(8,128)}) custom-call(s32[1]{0:T(128)} %bitcast.place, f32[1152,128]{1,0:T(8,128)} %bitcast.19, f32[1152,128]{1,0:T(8,128)} %collective-permute-done.before, f32[1152,128]{1,0:T(8,128)} %copy-done.8, f32[288,128]{1,0:T(8,128)} %broadcast_in_dim.90.scale, ...), custom_call_target="tpu_custom_call" | custom-call | flops 15000000512 | bytes 45000000 | tf_op jit(solution)/shard_map/apply_twice/pallas_call | solution.py:508
  64.7 6.1 %all-to-all-done = f32[8,288,128]{2,1,0:T(8,128)S(1)} async-done(((f32[8,288,128]{2,1,0:T(8,128)}), f32[8,288,128]{2,1,0:T(8,128)S(1)}, u32[]{:S(2)}, u32[]{:S(2)}) %all-to-all-start) | async-done | bytes 1179680 | tf_op jit(solution)/shard_map/all_to_all | solution.py:645
  71.8 37.0 %part_components.1 = (f32[1152,128]{1,0:T(8,128)}, f32[1152,128]{1,0:T(8,128)}) custom-call(f32[2304,128]{1,0:T(8,128)} %bitcast.11, f32[8,128]{1,0:T(8,128)} %get-tuple-element.18.ready.refs_0_), custom_call_target="tpu_custom_call" | custom-call | flops 1000000000 | bytes 3000000 | tf_op jit(solution)/shard_map/part_components/pallas_call | solution.py:237
  110.2 3.9 %collective-permute-start.6 = (f32[1152,128]{1,0:T(8,128)}, f32[1152,128]{1,0:T(8,128)}, u32[]{:S(2)}, u32[]{:S(2)}) collective-permute-start(f32[1152,128]{1,0:T(8,128)} %get-tuple-element.20.own), channel_id=1, source_target_pairs={{0,1},{1,2},{2,3},{4,5},{5,6},{6,7},{8,9},{9,10},{10,11},{12,13},{... | collective-permute-start | bytes 1769480 | tf_op jit(solution)/shard_map/ppermute | solution.py:648
  114.1 3.6 %all-to-all-start.4 = ((f32[8,216,128]{2,1,0:T(8,128)}), f32[8,216,128]{2,1,0:T(8,128)S(1)}, u32[]{:S(2)}, u32[]{:S(2)}) async-start(f32[8,216,128]{2,1,0:T(8,128)} %bitcast.9), calls=%async_computation.4 | async-start | bytes 1769472 | tf_op jit(solution)/shard_map/all_to_all | solution.py:645
  119.0 3.2 %collective-permute-start.4 = (f32[1152,128]{1,0:T(8,128)S(1)}, f32[1152,128]{1,0:T(8,128)S(1)}, u32[]{:S(2)}, u32[]{:S(2)}) collective-permute-start(f32[1152,128]{1,0:T(8,128)S(1)} %copy-done.7), channel_id=1, source_target_pairs={{0,1},{1,2},{2,3},{4,5},{5,6},{6,7},{8,9},{9,10},{10,11},{12,13},{... | collective-permute-start | bytes 1769480 | tf_op jit(solution)/shard_map/ppermute | solution.py:648
  123.1 12.1 %apply_twice.4 = (f32[1728,128]{1,0:T(8,128)}, f32[8,128]{1,0:T(8,128)}) custom-call(s32[1]{0:T(128)} %bitcast.place, f32[1152,128]{1,0:T(8,128)} %get-tuple-element.20.own, f32[1152,128]{1,0:T(8,128)} %collective-permute-done.6.before, f32[1152,128]{1,0:T(8,128)} %copy-done.11, f32[288,128]{1,0:T(8,128)} %broadcast_in_dim.90.scale, ...), custom_call_target="tpu_custom_call" | custom-call | flops 15000000512 | bytes 45000000 | tf_op jit(solution)/shard_map/apply_twice/pallas_call | solution.py:508
  135.2 5.4 %all-to-all-done.4 = f32[8,216,128]{2,1,0:T(8,128)S(1)} async-done(((f32[8,216,128]{2,1,0:T(8,128)}), f32[8,216,128]{2,1,0:T(8,128)S(1)}, u32[]{:S(2)}, u32[]{:S(2)}) %all-to-all-start.4) | async-done | bytes 884768 | tf_op jit(solution)/shard_map/all_to_all | solution.py:645
  140.6 3.6 %all-to-all-start.3 = ((f32[8,216,128]{2,1,0:T(8,128)}), f32[8,216,128]{2,1,0:T(8,128)S(1)}, u32[]{:S(2)}, u32[]{:S(2)}) async-start(f32[8,216,128]{2,1,0:T(8,128)} %bitcast.16), calls=%async_computation.3 | async-start | bytes 1769472 | tf_op jit(solution)/shard_map/all_to_all | solution.py:645
  145.2 12.1 %apply_twice.5 = (f32[1728,128]{1,0:T(8,128)}, f32[8,128]{1,0:T(8,128)}) custom-call(s32[1]{0:T(128)} %bitcast.place, f32[1152,128]{1,0:T(8,128)} %get-tuple-element.19.own, f32[1152,128]{1,0:T(8,128)} %copy-done.10, f32[1152,128]{1,0:T(8,128)} %copy-done.9, f32[288,128]{1,0:T(8,128)} %broadcast_in_dim.90.scale, bf16[624,576]{1,0:T(8,128)(2,1)} %pad_maximum_fusion.to_even, ...), custom_call_target="tpu_custom_call" | custom-call | flops 15000000512 | bytes 45000000 | tf_op jit(solution)/shard_map/apply_twice/pallas_call | solution.py:508
  157.3 9.3 %all-to-all-done.3 = f32[8,216,128]{2,1,0:T(8,128)S(1)} async-done(((f32[8,216,128]{2,1,0:T(8,128)}), f32[8,216,128]{2,1,0:T(8,128)S(1)}, u32[]{:S(2)}, u32[]{:S(2)}) %all-to-all-start.3) | async-done | bytes 884768 | tf_op jit(solution)/shard_map/all_to_all | solution.py:645
  166.7 3.6 %all-to-all-start.2 = ((f32[8,216,128]{2,1,0:T(8,128)}), f32[8,216,128]{2,1,0:T(8,128)S(1)}, u32[]{:S(2)}, u32[]{:S(2)}) async-start(f32[8,216,128]{2,1,0:T(8,128)} %bitcast.14), calls=%async_computation.2 | async-start | bytes 1769472 | tf_op jit(solution)/shard_map/all_to_all | solution.py:645
  171.5 3.6 %collective-permute-done.9 = f32[8,128]{1,0:T(8,128)S(1)} collective-permute-done((f32[8,128]{1,0:T(8,128)S(1)}, f32[8,128]{1,0:T(8,128)S(1)}, u32[]{:S(2)}, u32[]{:S(2)}) %collective-permute-start.9) | collective-permute-done | bytes 4128 | tf_op jit(solution)/shard_map/ppermute | solution.py:630
  178.9 4.0 %collective-permute-start.13 = (f32[8,128]{1,0:T(8,128)S(1)}, f32[8,128]{1,0:T(8,128)S(1)}, u32[]{:S(2)}, u32[]{:S(2)}) collective-permute-start(f32[8,128]{1,0:T(8,128)S(1)} %add.39), channel_id=1, source_target_pairs={{0,24},{4,28},{8,16},{12,20},{16,8},{20,12},{24,0},{28,4},{1,25},{... | collective-permute-start | bytes 12296 | tf_op jit(solution)/shard_map/ppermute | solution.py:632
  183.5 5.6 %collective-permute-done.13 = f32[8,128]{1,0:T(8,128)S(1)} collective-permute-done((f32[8,128]{1,0:T(8,128)S(1)}, f32[8,128]{1,0:T(8,128)S(1)}, u32[]{:S(2)}, u32[]{:S(2)}) %collective-permute-start.13) | collective-permute-done | bytes 4128 | tf_op jit(solution)/shard_map/ppermute | solution.py:632
  189.1 4.0 %collective-permute-done.12 = f32[8,128]{1,0:T(8,128)S(1)} collective-permute-done((f32[8,128]{1,0:T(8,128)S(1)}, f32[8,128]{1,0:T(8,128)S(1)}, u32[]{:S(2)}, u32[]{:S(2)}) %collective-permute-start.12) | collective-permute-done | bytes 4128 | tf_op jit(solution)/shard_map/ppermute | solution.py:632
  195.0 3.7 %finish.3 = (f32[36,3,3,8,128]{4,3,2,1,0:T(8,128)}, f32[36,3,3,8,128]{4,3,2,1,0:T(8,128)}) custom-call(f32[36,3,3,8,128]{4,3,2,1,0:T(8,128)} %field.9, f32[1728,128]{1,0:T(8,128)} %bitcast.12, f32[16,128]{1,0:T(8,128)} %combination.1.factors), custom_call_target="tpu_custom_call" | custom-call | flops 3000000000 | bytes 9000000 | tf_op jit(solution)/shard_map/finish/pallas_call | solution.py:576
  198.8 3.7 %finish.4 = (f32[36,3,3,8,128]{4,3,2,1,0:T(8,128)}, f32[36,3,3,8,128]{4,3,2,1,0:T(8,128)}) custom-call(f32[36,3,3,8,128]{4,3,2,1,0:T(8,128)} %field.9, f32[1728,128]{1,0:T(8,128)} %bitcast.13, f32[16,128]{1,0:T(8,128)} %combination.1.factors, f32[36,3,3,8,128]{4,3,2,1,0:T(8,128)} %get-tuple-element.26.refs_0_, ...), custom_call_target="tpu_custom_call", output_to_operand_aliasing={{0}: (3, {}), {1}: (4, {})} | custom-call | flops 3000000000 | bytes 9000000 | tf_op jit(solution)/shard_map/finish/pallas_call | solution.py:576
  203.5 3.7 %finish.5 = (f32[36,3,3,8,128]{4,3,2,1,0:T(8,128)}, f32[36,3,3,8,128]{4,3,2,1,0:T(8,128)}) custom-call(f32[36,3,3,8,128]{4,3,2,1,0:T(8,128)} %field.9, f32[1728,128]{1,0:T(8,128)} %bitcast.15, f32[16,128]{1,0:T(8,128)} %combination.1.factors, f32[36,3,3,8,128]{4,3,2,1,0:T(8,128)} %get-tuple-element.28.refs_0_, ...), custom_call_target="tpu_custom_call", output_to_operand_aliasing={{0}: (3, {}), {1}: (4, {})} | custom-call | flops 3000000000 | bytes 9000000 | tf_op jit(solution)/shard_map/finish/pallas_call | solution.py:576
  (74 shorter events, 31.3 us)
Async XLA Ops:
  3.9 16.9 %copy-start.5 = (s32[660,4]{0,1:T(4,128)S(1)}, s32[660,4]{0,1:T(4,128)}, u32[]{:S(2)}) copy-start(s32[660,4]{0,1:T(4,128)} %param.11) | copy-start | bytes 31684
  9.2 40.2 %collective-permute-start.3 = (f32[2,3,8,128]{3,2,1,0:T(8,128)}, f32[2,3,8,128]{3,2,1,0:T(8,128)S(1)}, u32[]{:S(2)}, u32[]{:S(2)}) collective-permute-start(f32[2,3,8,128]{3,2,1,0:T(8,128)} %get-tuple-element.17.both), channel_id=1, source_target_pairs={{1,0},{2,1},{3,2},{5,4},{6,5},{7,6},{9,8},{10,9},{11,10},{13,12},{... | collective-permute-start | bytes 73736 | tf_op jit(solution)/shard_map/ppermute | solution.py:656
  10.4 39.0 %collective-permute-start.2 = (f32[2,3,8,128]{3,2,1,0:T(8,128)}, f32[2,3,8,128]{3,2,1,0:T(8,128)S(1)}, u32[]{:S(2)}, u32[]{:S(2)}) collective-permute-start(f32[2,3,8,128]{3,2,1,0:T(8,128)} %get-tuple-element.17.both), channel_id=1, source_target_pairs={{0,1},{1,2},{2,3},{4,5},{5,6},{6,7},{8,9},{9,10},{10,11},{12,13},{... | collective-permute-start | bytes 73736 | tf_op jit(solution)/shard_map/ppermute | solution.py:655
  13.5 24.8 %all-to-all-start.1 = ((f32[8,144,128]{2,1,0:T(8,128)}), f32[8,144,128]{2,1,0:T(8,128)S(1)}, u32[]{:S(2)}, u32[]{:S(2)}) async-start(f32[8,144,128]{2,1,0:T(8,128)} %bitcast.3), calls=%async_computation.1 | async-start | bytes 1179648 | tf_op jit(solution)/shard_map/all_to_all | solution.py:645
  38.3 10.0 %copy-start.4 = (f32[8,144,128]{2,1,0:T(8,128)}, f32[8,144,128]{2,1,0:T(8,128)S(1)}, u32[]{:S(2)}) copy-start(f32[8,144,128]{2,1,0:T(8,128)S(1)} %all-to-all-done.1) | copy-start | bytes 1769476
  38.3 32.5 %all-to-all-start = ((f32[8,288,128]{2,1,0:T(8,128)}), f32[8,288,128]{2,1,0:T(8,128)S(1)}, u32[]{:S(2)}, u32[]{:S(2)}) async-start(f32[8,288,128]{2,1,0:T(8,128)} %bitcast.1), calls=%async_computation | async-start | bytes 2359296 | tf_op jit(solution)/shard_map/all_to_all | solution.py:645
  41.8 9.8 %collective-permute-start.1 = (f32[1152,128]{1,0:T(8,128)S(1)}, f32[1152,128]{1,0:T(8,128)S(1)}, u32[]{:S(2)}, u32[]{:S(2)}) collective-permute-start(f32[1152,128]{1,0:T(8,128)S(1)} %bitcast.17), channel_id=1, source_target_pairs={{1,0},{2,1},{3,2},{5,4},{6,5},{7,6},{9,8},{10,9},{11,10},{13,12},{... | collective-permute-start | bytes 1769480 | tf_op jit(solution)/shard_map/ppermute | solution.py:648
  43.1 8.5 %collective-permute-start = (f32[1152,128]{1,0:T(8,128)S(1)}, f32[1152,128]{1,0:T(8,128)}, u32[]{:S(2)}, u32[]{:S(2)}) collective-permute-start(f32[1152,128]{1,0:T(8,128)S(1)} %bitcast.18), channel_id=1, source_target_pairs={{0,1},{1,2},{2,3},{4,5},{5,6},{6,7},{8,9},{9,10},{10,11},{12,13},{... | collective-permute-start | bytes 1769480 | tf_op jit(solution)/shard_map/ppermute | solution.py:648
  108.8 13.5 %collective-permute-start.7 = (f32[1152,128]{1,0:T(8,128)}, f32[1152,128]{1,0:T(8,128)S(1)}, u32[]{:S(2)}, u32[]{:S(2)}) collective-permute-start(f32[1152,128]{1,0:T(8,128)} %get-tuple-element.20.own), channel_id=1, source_target_pairs={{1,0},{2,1},{3,2},{5,4},{6,5},{7,6},{9,8},{10,9},{11,10},{13,12},{... | collective-permute-start | bytes 1769480 | tf_op jit(solution)/shard_map/ppermute | solution.py:648
  110.2 12.1 %collective-permute-start.6 = (f32[1152,128]{1,0:T(8,128)}, f32[1152,128]{1,0:T(8,128)}, u32[]{:S(2)}, u32[]{:S(2)}) collective-permute-start(f32[1152,128]{1,0:T(8,128)} %get-tuple-element.20.own), channel_id=1, source_target_pairs={{0,1},{1,2},{2,3},{4,5},{5,6},{6,7},{8,9},{9,10},{10,11},{12,13},{... | collective-permute-start | bytes 1769480 | tf_op jit(solution)/shard_map/ppermute | solution.py:648
  114.1 26.5 %all-to-all-start.4 = ((f32[8,216,128]{2,1,0:T(8,128)}), f32[8,216,128]{2,1,0:T(8,128)S(1)}, u32[]{:S(2)}, u32[]{:S(2)}) async-start(f32[8,216,128]{2,1,0:T(8,128)} %bitcast.9), calls=%async_computation.4 | async-start | bytes 1769472 | tf_op jit(solution)/shard_map/all_to_all | solution.py:645
  117.7 26.5 %collective-permute-start.5 = (f32[1152,128]{1,0:T(8,128)S(1)}, f32[1152,128]{1,0:T(8,128)S(1)}, u32[]{:S(2)}, u32[]{:S(2)}) collective-permute-start(f32[1152,128]{1,0:T(8,128)S(1)} %copy-done.7), channel_id=1, source_target_pairs={{1,0},{2,1},{3,2},{5,4},{6,5},{7,6},{9,8},{10,9},{11,10},{13,12},{... | collective-permute-start | bytes 1769480 | tf_op jit(solution)/shard_map/ppermute | solution.py:648
  119.0 25.2 %collective-permute-start.4 = (f32[1152,128]{1,0:T(8,128)S(1)}, f32[1152,128]{1,0:T(8,128)S(1)}, u32[]{:S(2)}, u32[]{:S(2)}) collective-permute-start(f32[1152,128]{1,0:T(8,128)S(1)} %copy-done.7), channel_id=1, source_target_pairs={{0,1},{1,2},{2,3},{4,5},{5,6},{6,7},{8,9},{9,10},{10,11},{12,13},{... | collective-permute-start | bytes 1769480 | tf_op jit(solution)/shard_map/ppermute | solution.py:648
  140.6 16.8 %copy-start.1 = (f32[8,216,128]{2,1,0:T(8,128)}, f32[8,216,128]{2,1,0:T(8,128)S(1)}, u32[]{:S(2)}) copy-start(f32[8,216,128]{2,1,0:T(8,128)S(1)} %all-to-all-done.4) | copy-start | bytes 2654212
  140.6 26.1 %all-to-all-start.3 = ((f32[8,216,128]{2,1,0:T(8,128)}), f32[8,216,128]{2,1,0:T(8,128)S(1)}, u32[]{:S(2)}, u32[]{:S(2)}) async-start(f32[8,216,128]{2,1,0:T(8,128)} %bitcast.16), calls=%async_computation.3 | async-start | bytes 1769472 | tf_op jit(solution)/shard_map/all_to_all | solution.py:645
  157.3 12.9 %copy-start.6 = (f32[8,128]{1,0:T(8,128)S(1)}, f32[8,128]{1,0:T(8,128)}, u32[]{:S(2)}) copy-start(f32[8,128]{1,0:T(8,128)} %get-tuple-element.23) | copy-start | bytes 12292
  166.7 28.4 %copy-start.2 = (f32[8,216,128]{2,1,0:T(8,128)}, f32[8,216,128]{2,1,0:T(8,128)S(1)}, u32[]{:S(2)}) copy-start(f32[8,216,128]{2,1,0:T(8,128)S(1)} %all-to-all-done.3) | copy-start | bytes 2654212
  166.7 35.9 %all-to-all-start.2 = ((f32[8,216,128]{2,1,0:T(8,128)}), f32[8,216,128]{2,1,0:T(8,128)S(1)}, u32[]{:S(2)}, u32[]{:S(2)}) async-start(f32[8,216,128]{2,1,0:T(8,128)} %bitcast.14), calls=%async_computation.2 | async-start | bytes 1769472 | tf_op jit(solution)/shard_map/all_to_all | solution.py:645
  170.3 1.2 collective-permute-start.8
  171.5 3.6 %collective-permute-start.9 = (f32[8,128]{1,0:T(8,128)S(1)}, f32[8,128]{1,0:T(8,128)S(1)}, u32[]{:S(2)}, u32[]{:S(2)}) collective-permute-start(f32[8,128]{1,0:T(8,128)S(1)} %add.37), channel_id=1, source_target_pairs={{0,2},{1,3},{2,0},{3,1},{4,6},{5,7},{6,4},{7,5},{8,10},{9,11},{10,... | collective-permute-start | bytes 12296 | tf_op jit(solution)/shard_map/ppermute | solution.py:630
  175.1 3.8 %collective-permute-start.10 = (f32[8,128]{1,0:T(8,128)S(1)}, f32[8,128]{1,0:T(8,128)S(1)}, u32[]{:S(2)}, u32[]{:S(2)}) collective-permute-start(f32[8,128]{1,0:T(8,128)S(1)} %add.38), channel_id=1, source_target_pairs={{0,4},{4,0},{8,12},{12,8},{16,20},{20,16},{24,28},{28,24},{1,5},{5... | collective-permute-start | bytes 12296 | tf_op jit(solution)/shard_map/ppermute | solution.py:630
  178.9 10.1 %collective-permute-start.13 = (f32[8,128]{1,0:T(8,128)S(1)}, f32[8,128]{1,0:T(8,128)S(1)}, u32[]{:S(2)}, u32[]{:S(2)}) collective-permute-start(f32[8,128]{1,0:T(8,128)S(1)} %add.39), channel_id=1, source_target_pairs={{0,24},{4,28},{8,16},{12,20},{16,8},{20,12},{24,0},{28,4},{1,25},{... | collective-permute-start | bytes 12296 | tf_op jit(solution)/shard_map/ppermute | solution.py:632
  182.9 10.2 %collective-permute-start.12 = (f32[8,128]{1,0:T(8,128)S(1)}, f32[8,128]{1,0:T(8,128)S(1)}, u32[]{:S(2)}, u32[]{:S(2)}) collective-permute-start(f32[8,128]{1,0:T(8,128)S(1)} %add.39), channel_id=1, source_target_pairs={{0,16},{4,20},{8,24},{12,28},{16,0},{20,4},{24,8},{28,12},{1,17},{... | collective-permute-start | bytes 12296 | tf_op jit(solution)/shard_map/ppermute | solution.py:632
  182.9 10.2 %collective-permute-start.11 = (f32[8,128]{1,0:T(8,128)S(1)}, f32[8,128]{1,0:T(8,128)S(1)}, u32[]{:S(2)}, u32[]{:S(2)}) collective-permute-start(f32[8,128]{1,0:T(8,128)S(1)} %add.39), channel_id=1, source_target_pairs={{0,8},{4,12},{8,0},{12,4},{16,24},{20,28},{24,16},{28,20},{1,9},{5... | collective-permute-start | bytes 12296 | tf_op jit(solution)/shard_map/ppermute | solution.py:632
  (9 other events, 15.7 us)

commit v7 on v6

--- a/solution.py
+++ b/solution.py
@@ -212,37 +212,41 @@
         + [pl.BlockSpec(memory_space=pl.ANY)] * len(after),
         out_specs=[vmem] * len(shapes),
         compiler_params=pltpu.CompilerParams(vmem_limit_bytes=VMEM),
-        cost_estimate=estimate(2.5 * len(comps)),
+        cost_estimate=estimate(0.5),
         name="pack",
     )(field, *stiffness, *after)
 
 
-def part_kernel(rows, ready, *refs):
-    *outs, sems = refs
-    size = outs[0].shape[0] // PARTS
-    copies = []
-    for n, out in enumerate(outs):
-        for device in range(PARTS):
-            source = rows.at[pl.ds((device * len(outs) + n) * size, size), :]
-            goal = out.at[pl.ds(device * size, size), :]
-            copies.append(pltpu.make_async_copy(source, goal, sems.at[n * PARTS + device]))
-    for copy in copies:
-        copy.start()
-    for copy in copies:
-        copy.wait()
-
-
-def part_components(rows, ready, count):
+def copy_kernel(source, ready, goal):
+    goal[...] = source[...]
+
+
+def part_component(rows, n, ready):
+    blocks = rows.reshape(PARTS, -1, LANES)
+    part = (PARTS, blocks.shape[1] // (COMPS - 1), LANES)
     whole = pl.BlockSpec(memory_space=pl.ANY)
     return pl.pallas_call(
-        part_kernel,
-        out_shape=[jax.ShapeDtypeStruct((rows.shape[0] // count, LANES), jnp.float32)] * count,
-        in_specs=[whole, whole],
-        out_specs=[whole] * count,
-        scratch_shapes=[pltpu.SemaphoreType.DMA((count * PARTS,))],
-        cost_estimate=estimate(1),
-        name="part_components",
-    )(rows, ready)
+        copy_kernel,
+        grid=(1,),
+        out_shape=jax.ShapeDtypeStruct(part, jnp.float32),
+        in_specs=[pl.BlockSpec(part, lambda i: (0, n, 0)), whole],
+        out_specs=pl.BlockSpec(part, lambda i: (0, 0, 0)),
+        compiler_params=pltpu.CompilerParams(vmem_limit_bytes=VMEM),
+        cost_estimate=estimate(0.5),
+        name="part_component",
+    )(blocks, ready).reshape(-1, LANES)
+
+
+def after_rows(table, ready):
+    vmem = pl.BlockSpec(memory_space=pltpu.VMEM)
+    return pl.pallas_call(
+        copy_kernel,
+        out_shape=jax.ShapeDtypeStruct(table.shape, table.dtype),
+        in_specs=[vmem, pl.BlockSpec(memory_space=pl.ANY)],
+        out_specs=vmem,
+        cost_estimate=estimate(0.5),
+        name="after_rows",
+    )(table, ready)
 
 
 def stiffness_kernel(place, before, both, after, ply_stiffness, fields, wide):
@@ -274,7 +278,7 @@
         in_specs=[smem, vmem, vmem, vmem, smem],
         out_specs=vmem,
         scratch_shapes=[pltpu.VMEM((8, LANES), jnp.float32)],
-        cost_estimate=estimate(2),
+        cost_estimate=estimate(0.5),
         name="stiffness_fields",
     )(place, before, both, after, ply_stiffness)
 
@@ -651,15 +655,15 @@
     both, others = pack(right_side, (1, 2), (mean_stiffness, ply_map), (first,))
     first = halo(swap(first))
     others = swap(others)
-    tables = mode_tables(coupling_table, slots)
+    tables = mode_tables(after_rows(coupling_table, first[0]), slots)
     both_before = lax.ppermute(both, "space", up)
     both_after = lax.ppermute(both, "space", down)
     fields = stiffness_fields(place, both_before, both, both_after, ply_stiffness)
     image, partial = apply_twice(0, place, *first, tables, fields, fibre_weights)
     images = [swap(image)]
-    parts = part_components(others, partial, COMPS - 1)
-    for comp, rows in enumerate(parts, 1):
-        image, partial = apply_twice(comp, place, *halo(rows), tables, fields, fibre_weights, partial)
+    for comp in range(1, COMPS):
+        rows = halo(part_component(others, comp - 1, partial))
+        image, partial = apply_twice(comp, place, *rows, tables, fields, fibre_weights, partial)
         images.append(swap(image))
     factors = combination(all_sum(partial))
     outputs = ()

time: 208 us -> 168 us (0.81)
  Pallas kernels: 96 us -> 64.6 us
  waiting for transfers between devices: 51.7 us -> 29 us
  starting transfers between devices: 47.5 us -> 55.4 us
  local copies, waits for them, and re-layouts: 5.33 us -> 9.64 us
    pallas_call x1 -> x3, Pallas kernels: 37 us -> 5.57 us  [the longest x2 3.84 us: part_component(): pl.pallas_call(copy_kernel, grid=(1,), out_shape=jax.ShapeDtypeStruct(par...]
    all_to_all x5, waiting for transfers between devices: 35.4 us -> 13.8 us  [swap(): return lax.all_to_all(rows, 'mode', 0, 0, tiled=True)]
    all_to_all x5, starting transfers between devices: 21.7 us -> 26.8 us  [swap(): return lax.all_to_all(rows, 'mode', 0, 0, tiled=True)]
    unnamed x28 -> x33, local copies, waits for them, and re-layouts: 4.39 us -> 6.86 us
  transfers between devices with their start and end apart: 19 -> 19, of which waited for: 9 -> 10; matrix products, arithmetic and copies ran while one was open for 3% -> 7% of each run, Pallas kernels for 23% -> 33%
where the time goes in v7:
time: 168 us; the launch traced here: 167 us
  Pallas kernels  64.6 us (38%)
  starting transfers between devices  55.4 us (33%)
  waiting for transfers between devices  29 us (17%)
  local copies, waits for them, and re-layouts  9.64 us (6%)
  other arithmetic  5.91 us (4%)
  matrix products  1.8 us (1%)
    pallas_call x3, Pallas kernels, apply_twice(): pl.pallas_call(functools.partial(apply_kernel, comp=comp), out_shape=[jax...  36.3 us
    all_to_all x5, starting transfers between devices, swap(): return lax.all_to_all(rows, 'mode', 0, 0, tiled=True)  26.8 us
    all_to_all x5, waiting for transfers between devices, swap(): return lax.all_to_all(rows, 'mode', 0, 0, tiled=True)  13.8 us
    ppermute x3, starting transfers between devices, halo(): lax.ppermute(rows, 'space', up)  12.6 us
    pallas_call x3, Pallas kernels, finish(): pl.pallas_call(finish_kernel, grid=(1,), out_shape=[jax.ShapeDtypeStruct(...  11.2 us
    ppermute x3, waiting for transfers between devices, all_sum(): lax.ppermute(value, 'mode', [(i, i ^ bit) for i in range(PARTS)])  9.79 us
    pallas_call x2, Pallas kernels, pack(): pl.pallas_call(functools.partial(pack_kernel, comps=comps), grid=(1,), ou...  8.51 us
    unnamed x33, local copies, waits for them, and re-layouts  6.86 us
  transfers between devices with their start and end apart: 19, of which 10 were waited for; matrix products, arithmetic and copies ran while one was open for 7% of the time, Pallas kernels for 33%

profile of v7, /device:TPU:0, one launch (start us, length us, event | category | flops | bytes accessed | tf_op | source)
XLA Modules:
  0.0 167.3 jit_solution(18098049347568699325)
XLA Ops:
  0.6 3.2 %pack.2.refs_2_ = f32[1152,128]{1,0:T(8,128)} custom-call(f32[36,3,3,8,128]{4,3,2,1,0:T(8,128)} %field.9), custom_call_target="tpu_custom_call" | custom-call | flops 500000000 | bytes 1500000 | tf_op jit(solution)/shard_map/pack/pallas_call | solution.py:206
  3.9 7.4 %all-to-all-start.1 = ((f32[8,144,128]{2,1,0:T(8,128)}), f32[8,144,128]{2,1,0:T(8,128)S(1)}, u32[]{:S(2)}, u32[]{:S(2)}) async-start(f32[8,144,128]{2,1,0:T(8,128)} %bitcast.12), calls=%async_computation.1 | async-start | bytes 1179648 | tf_op jit(solution)/shard_map/all_to_all | solution.py:649
  11.3 5.3 %pack.3 = (f32[2,3,8,128]{3,2,1,0:T(8,128)}, f32[2304,128]{1,0:T(8,128)}) custom-call(f32[36,3,3,8,128]{4,3,2,1,0:T(8,128)} %field.9, f32[3,8,128]{2,1,0:T(8,128)} %refs_0_.1, s32[3,8,128]{2,1,0:T(8,128)} %refs_1_.1, f32[1152,128]{1,0:T(8,128)} %pack.2.refs_2_), custom_call_target="tpu_custom_call" | custom-call | flops 500000000 | bytes 1500000 | tf_op jit(solution)/shard_map/pack/pallas_call | solution.py:206
  17.8 3.0 %collective-permute-start.2 = (f32[2,3,8,128]{3,2,1,0:T(8,128)}, f32[2,3,8,128]{3,2,1,0:T(8,128)S(1)}, u32[]{:S(2)}, u32[]{:S(2)}) collective-permute-start(f32[2,3,8,128]{3,2,1,0:T(8,128)} %get-tuple-element.15.both), channel_id=1, source_target_pairs={{0,1},{1,2},{2,3},{4,5},{5,6},{6,7},{8,9},{9,10},{10,11},{12,13},{... | collective-permute-start | bytes 73736 | tf_op jit(solution)/shard_map/ppermute | solution.py:659
  24.1 3.0 %all-to-all-done.1 = f32[8,144,128]{2,1,0:T(8,128)S(1)} async-done(((f32[8,144,128]{2,1,0:T(8,128)}), f32[8,144,128]{2,1,0:T(8,128)S(1)}, u32[]{:S(2)}, u32[]{:S(2)}) %all-to-all-start.1) | async-done | bytes 589856 | tf_op jit(solution)/shard_map/all_to_all | solution.py:649
  27.2 3.6 %all-to-all-start = ((f32[8,288,128]{2,1,0:T(8,128)}), f32[8,288,128]{2,1,0:T(8,128)S(1)}, u32[]{:S(2)}, u32[]{:S(2)}) async-start(f32[8,288,128]{2,1,0:T(8,128)} %bitcast.1), calls=%async_computation | async-start | bytes 2359296 | tf_op jit(solution)/shard_map/all_to_all | solution.py:649
  36.4 3.1 %collective-permute-start = (f32[1152,128]{1,0:T(8,128)}, f32[1152,128]{1,0:T(8,128)S(1)}, u32[]{:S(2)}, u32[]{:S(2)}) collective-permute-start(f32[1152,128]{1,0:T(8,128)} %bitcast.19), channel_id=1, source_target_pairs={{0,1},{1,2},{2,3},{4,5},{5,6},{6,7},{8,9},{9,10},{10,11},{12,13},{... | collective-permute-start | bytes 1769480 | tf_op jit(solution)/shard_map/ppermute | solution.py:652
  47.0 12.1 %apply_twice.3 = (f32[1728,128]{1,0:T(8,128)}, f32[8,128]{1,0:T(8,128)}) custom-call(s32[1]{0:T(128)} %bitcast.place, f32[1152,128]{1,0:T(8,128)} %bitcast.20, f32[1152,128]{1,0:T(8,128)} %copy-done.9, f32[1152,128]{1,0:T(8,128)} %copy-done.8, f32[288,128]{1,0:T(8,128)} %broadcast_in_dim.90.scale, bf16[624,576]{1,0:T(8,128)(2,1)} %pad_maximum_fusion.to_even, ...), custom_call_target="tpu_custom_call" | custom-call | flops 15000000512 | bytes 45000000 | tf_op jit(solution)/shard_map/apply_twice/pallas_call | solution.py:512
  64.4 4.4 %collective-permute-start.4 = (f32[1152,128]{1,0:T(8,128)}, f32[1152,128]{1,0:T(8,128)S(1)}, u32[]{:S(2)}, u32[]{:S(2)}) collective-permute-start(f32[1152,128]{1,0:T(8,128)} %bitcast.25), channel_id=1, source_target_pairs={{0,1},{1,2},{2,3},{4,5},{5,6},{6,7},{8,9},{9,10},{10,11},{12,13},{... | collective-permute-start | bytes 1769480 | tf_op jit(solution)/shard_map/ppermute | solution.py:652
  68.7 6.0 %all-to-all-start.4 = ((f32[8,216,128]{2,1,0:T(8,128)}), f32[8,216,128]{2,1,0:T(8,128)S(1)}, u32[]{:S(2)}, u32[]{:S(2)}) async-start(f32[8,216,128]{2,1,0:T(8,128)} %bitcast.10), calls=%async_computation.4 | async-start | bytes 1769472 | tf_op jit(solution)/shard_map/all_to_all | solution.py:649
  76.4 12.1 %apply_twice.4 = (f32[1728,128]{1,0:T(8,128)}, f32[8,128]{1,0:T(8,128)}) custom-call(s32[1]{0:T(128)} %bitcast.place, f32[1152,128]{1,0:T(8,128)} %bitcast.26, f32[1152,128]{1,0:T(8,128)} %copy-done.13, f32[1152,128]{1,0:T(8,128)} %copy-done.12, f32[288,128]{1,0:T(8,128)} %broadcast_in_dim.90.scale, bf16[624,576]{1,0:T(8,128)(2,1)} %pad_maximum_fusion.to_even, ...), custom_call_target="tpu_custom_call" | custom-call | flops 15000000512 | bytes 45000000 | tf_op jit(solution)/shard_map/apply_twice/pallas_call | solution.py:512
  91.7 5.2 %collective-permute-start.6 = (f32[1152,128]{1,0:T(8,128)}, f32[1152,128]{1,0:T(8,128)S(1)}, u32[]{:S(2)}, u32[]{:S(2)}) collective-permute-start(f32[1152,128]{1,0:T(8,128)} %bitcast.22), channel_id=1, source_target_pairs={{0,1},{1,2},{2,3},{4,5},{5,6},{6,7},{8,9},{9,10},{10,11},{12,13},{... | collective-permute-start | bytes 1769480 | tf_op jit(solution)/shard_map/ppermute | solution.py:652
  97.5 5.4 %all-to-all-start.3 = ((f32[8,216,128]{2,1,0:T(8,128)}), f32[8,216,128]{2,1,0:T(8,128)S(1)}, u32[]{:S(2)}, u32[]{:S(2)}) async-start(f32[8,216,128]{2,1,0:T(8,128)} %bitcast.8), calls=%async_computation.3 | async-start | bytes 1769472 | tf_op jit(solution)/shard_map/all_to_all | solution.py:649
  104.6 12.1 %apply_twice.5 = (f32[1728,128]{1,0:T(8,128)}, f32[8,128]{1,0:T(8,128)}) custom-call(s32[1]{0:T(128)} %bitcast.place, f32[1152,128]{1,0:T(8,128)} %bitcast.23, f32[1152,128]{1,0:T(8,128)} %copy-done.11, f32[1152,128]{1,0:T(8,128)} %copy-done.10, f32[288,128]{1,0:T(8,128)} %broadcast_in_dim.90.scale, bf16[624,576]{1,0:T(8,128)(2,1)} %pad_maximum_fusion.to_even, ...), custom_call_target="tpu_custom_call" | custom-call | flops 15000000512 | bytes 45000000 | tf_op jit(solution)/shard_map/apply_twice/pallas_call | solution.py:512
  116.7 9.1 %all-to-all-done.3 = f32[8,216,128]{2,1,0:T(8,128)S(1)} async-done(((f32[8,216,128]{2,1,0:T(8,128)}), f32[8,216,128]{2,1,0:T(8,128)S(1)}, u32[]{:S(2)}, u32[]{:S(2)}) %all-to-all-start.3) | async-done | bytes 884768 | tf_op jit(solution)/shard_map/all_to_all | solution.py:649
  125.7 4.4 %all-to-all-start.2 = ((f32[8,216,128]{2,1,0:T(8,128)}), f32[8,216,128]{2,1,0:T(8,128)S(1)}, u32[]{:S(2)}, u32[]{:S(2)}) async-start(f32[8,216,128]{2,1,0:T(8,128)} %bitcast.15), calls=%async_computation.2 | async-start | bytes 1769472 | tf_op jit(solution)/shard_map/all_to_all | solution.py:649
  132.5 2.5 %collective-permute-done.9 = f32[8,128]{1,0:T(8,128)S(1)} collective-permute-done((f32[8,128]{1,0:T(8,128)S(1)}, f32[8,128]{1,0:T(8,128)S(1)}, u32[]{:S(2)}, u32[]{:S(2)}) %collective-permute-start.9) | collective-permute-done | bytes 4128 | tf_op jit(solution)/shard_map/ppermute | solution.py:634
  135.0 2.0 %collective-permute-start.10 = (f32[8,128]{1,0:T(8,128)S(1)}, f32[8,128]{1,0:T(8,128)S(1)}, u32[]{:S(2)}, u32[]{:S(2)}) collective-permute-start(f32[8,128]{1,0:T(8,128)S(1)} %add.38), channel_id=1, source_target_pairs={{0,4},{4,0},{8,12},{12,8},{16,20},{20,16},{24,28},{28,24},{1,5},{5... | collective-permute-start | bytes 12296 | tf_op jit(solution)/shard_map/ppermute | solution.py:634
  138.7 4.1 %collective-permute-start.13 = (f32[8,128]{1,0:T(8,128)S(1)}, f32[8,128]{1,0:T(8,128)S(1)}, u32[]{:S(2)}, u32[]{:S(2)}) collective-permute-start(f32[8,128]{1,0:T(8,128)S(1)} %add.39), channel_id=1, source_target_pairs={{0,24},{4,28},{8,16},{12,20},{16,8},{20,12},{24,0},{28,4},{1,25},{... | collective-permute-start | bytes 12296 | tf_op jit(solution)/shard_map/ppermute | solution.py:636
  143.3 5.8 %collective-permute-done.13 = f32[8,128]{1,0:T(8,128)S(1)} collective-permute-done((f32[8,128]{1,0:T(8,128)S(1)}, f32[8,128]{1,0:T(8,128)S(1)}, u32[]{:S(2)}, u32[]{:S(2)}) %collective-permute-start.13) | collective-permute-done | bytes 4128 | tf_op jit(solution)/shard_map/ppermute | solution.py:636
  149.1 4.0 %collective-permute-done.12 = f32[8,128]{1,0:T(8,128)S(1)} collective-permute-done((f32[8,128]{1,0:T(8,128)S(1)}, f32[8,128]{1,0:T(8,128)S(1)}, u32[]{:S(2)}, u32[]{:S(2)}) %collective-permute-start.12) | collective-permute-done | bytes 4128 | tf_op jit(solution)/shard_map/ppermute | solution.py:636
  155.1 3.7 %finish.3 = (f32[36,3,3,8,128]{4,3,2,1,0:T(8,128)}, f32[36,3,3,8,128]{4,3,2,1,0:T(8,128)}) custom-call(f32[36,3,3,8,128]{4,3,2,1,0:T(8,128)} %field.9, f32[1728,128]{1,0:T(8,128)} %bitcast.13, f32[16,128]{1,0:T(8,128)} %combination.1.factors), custom_call_target="tpu_custom_call" | custom-call | flops 3000000000 | bytes 9000000 | tf_op jit(solution)/shard_map/finish/pallas_call | solution.py:580
  158.8 3.7 %finish.4 = (f32[36,3,3,8,128]{4,3,2,1,0:T(8,128)}, f32[36,3,3,8,128]{4,3,2,1,0:T(8,128)}) custom-call(f32[36,3,3,8,128]{4,3,2,1,0:T(8,128)} %field.9, f32[1728,128]{1,0:T(8,128)} %bitcast.14, f32[16,128]{1,0:T(8,128)} %combination.1.factors, f32[36,3,3,8,128]{4,3,2,1,0:T(8,128)} %get-tuple-element.22.refs_0_, ...), custom_call_target="tpu_custom_call", output_to_operand_aliasing={{0}: (3, {}), {1}: (4, {})} | custom-call | flops 3000000000 | bytes 9000000 | tf_op jit(solution)/shard_map/finish/pallas_call | solution.py:580
  163.5 3.7 %finish.5 = (f32[36,3,3,8,128]{4,3,2,1,0:T(8,128)}, f32[36,3,3,8,128]{4,3,2,1,0:T(8,128)}) custom-call(f32[36,3,3,8,128]{4,3,2,1,0:T(8,128)} %field.9, f32[1728,128]{1,0:T(8,128)} %bitcast.16, f32[16,128]{1,0:T(8,128)} %combination.1.factors, f32[36,3,3,8,128]{4,3,2,1,0:T(8,128)} %get-tuple-element.24.refs_0_, ...), custom_call_target="tpu_custom_call", output_to_operand_aliasing={{0}: (3, {}), {1}: (4, {})} | custom-call | flops 3000000000 | bytes 9000000 | tf_op jit(solution)/shard_map/finish/pallas_call | solution.py:580
  (81 shorter events, 37.6 us)
Async XLA Ops:
  3.9 17.0 %copy-start.6 = (s32[660,4]{0,1:T(4,128)S(1)}, s32[660,4]{0,1:T(4,128)}, u32[]{:S(2)}) copy-start(s32[660,4]{0,1:T(4,128)} %param.11) | copy-start | bytes 31684
  3.9 23.3 %all-to-all-start.1 = ((f32[8,144,128]{2,1,0:T(8,128)}), f32[8,144,128]{2,1,0:T(8,128)S(1)}, u32[]{:S(2)}, u32[]{:S(2)}) async-start(f32[8,144,128]{2,1,0:T(8,128)} %bitcast.12), calls=%async_computation.1 | async-start | bytes 1179648 | tf_op jit(solution)/shard_map/all_to_all | solution.py:649
  16.5 5.3 %collective-permute-start.3 = (f32[2,3,8,128]{3,2,1,0:T(8,128)}, f32[2,3,8,128]{3,2,1,0:T(8,128)S(1)}, u32[]{:S(2)}, u32[]{:S(2)}) collective-permute-start(f32[2,3,8,128]{3,2,1,0:T(8,128)} %get-tuple-element.15.both), channel_id=1, source_target_pairs={{1,0},{2,1},{3,2},{5,4},{6,5},{7,6},{9,8},{10,9},{11,10},{13,12},{... | collective-permute-start | bytes 73736 | tf_op jit(solution)/shard_map/ppermute | solution.py:660
  17.8 4.1 %collective-permute-start.2 = (f32[2,3,8,128]{3,2,1,0:T(8,128)}, f32[2,3,8,128]{3,2,1,0:T(8,128)S(1)}, u32[]{:S(2)}, u32[]{:S(2)}) collective-permute-start(f32[2,3,8,128]{3,2,1,0:T(8,128)} %get-tuple-element.15.both), channel_id=1, source_target_pairs={{0,1},{1,2},{2,3},{4,5},{5,6},{6,7},{8,9},{9,10},{10,11},{12,13},{... | collective-permute-start | bytes 73736 | tf_op jit(solution)/shard_map/ppermute | solution.py:659
  27.2 33.0 %all-to-all-start = ((f32[8,288,128]{2,1,0:T(8,128)}), f32[8,288,128]{2,1,0:T(8,128)S(1)}, u32[]{:S(2)}, u32[]{:S(2)}) async-start(f32[8,288,128]{2,1,0:T(8,128)} %bitcast.1), calls=%async_computation | async-start | bytes 2359296 | tf_op jit(solution)/shard_map/all_to_all | solution.py:649
  32.5 8.8 %copy-start = (s32[660,4]{1,0:T(8,128)S(1)}, s32[660,4]{1,0:T(8,128)}, u32[]{:S(2)}) copy-start(s32[660,4]{1,0:T(8,128)} %after_rows.1) | copy-start | bytes 31684
  35.1 10.8 %collective-permute-start.1 = (f32[1152,128]{1,0:T(8,128)}, f32[1152,128]{1,0:T(8,128)S(1)}, u32[]{:S(2)}, u32[]{:S(2)}) collective-permute-start(f32[1152,128]{1,0:T(8,128)} %bitcast.18), channel_id=1, source_target_pairs={{1,0},{2,1},{3,2},{5,4},{6,5},{7,6},{9,8},{10,9},{11,10},{13,12},{... | collective-permute-start | bytes 1769480 | tf_op jit(solution)/shard_map/ppermute | solution.py:652
  36.4 9.6 %collective-permute-start = (f32[1152,128]{1,0:T(8,128)}, f32[1152,128]{1,0:T(8,128)S(1)}, u32[]{:S(2)}, u32[]{:S(2)}) collective-permute-start(f32[1152,128]{1,0:T(8,128)} %bitcast.19), channel_id=1, source_target_pairs={{0,1},{1,2},{2,3},{4,5},{5,6},{6,7},{8,9},{9,10},{10,11},{12,13},{... | collective-permute-start | bytes 1769480 | tf_op jit(solution)/shard_map/ppermute | solution.py:652
  63.1 11.7 %collective-permute-start.5 = (f32[1152,128]{1,0:T(8,128)}, f32[1152,128]{1,0:T(8,128)S(1)}, u32[]{:S(2)}, u32[]{:S(2)}) collective-permute-start(f32[1152,128]{1,0:T(8,128)} %bitcast.24), channel_id=1, source_target_pairs={{1,0},{2,1},{3,2},{5,4},{6,5},{7,6},{9,8},{10,9},{11,10},{13,12},{... | collective-permute-start | bytes 1769480 | tf_op jit(solution)/shard_map/ppermute | solution.py:652
  64.4 10.4 %collective-permute-start.4 = (f32[1152,128]{1,0:T(8,128)}, f32[1152,128]{1,0:T(8,128)S(1)}, u32[]{:S(2)}, u32[]{:S(2)}) collective-permute-start(f32[1152,128]{1,0:T(8,128)} %bitcast.25), channel_id=1, source_target_pairs={{0,1},{1,2},{2,3},{4,5},{5,6},{6,7},{8,9},{9,10},{10,11},{12,13},{... | collective-permute-start | bytes 1769480 | tf_op jit(solution)/shard_map/ppermute | solution.py:652
  68.7 28.8 %all-to-all-start.4 = ((f32[8,216,128]{2,1,0:T(8,128)}), f32[8,216,128]{2,1,0:T(8,128)S(1)}, u32[]{:S(2)}, u32[]{:S(2)}) async-start(f32[8,216,128]{2,1,0:T(8,128)} %bitcast.10), calls=%async_computation.4 | async-start | bytes 1769472 | tf_op jit(solution)/shard_map/all_to_all | solution.py:649
  90.4 12.5 %collective-permute-start.7 = (f32[1152,128]{1,0:T(8,128)}, f32[1152,128]{1,0:T(8,128)S(1)}, u32[]{:S(2)}, u32[]{:S(2)}) collective-permute-start(f32[1152,128]{1,0:T(8,128)} %bitcast.21), channel_id=1, source_target_pairs={{1,0},{2,1},{3,2},{5,4},{6,5},{7,6},{9,8},{10,9},{11,10},{13,12},{... | collective-permute-start | bytes 1769480 | tf_op jit(solution)/shard_map/ppermute | solution.py:652
  91.7 11.3 %collective-permute-start.6 = (f32[1152,128]{1,0:T(8,128)}, f32[1152,128]{1,0:T(8,128)S(1)}, u32[]{:S(2)}, u32[]{:S(2)}) collective-permute-start(f32[1152,128]{1,0:T(8,128)} %bitcast.22), channel_id=1, source_target_pairs={{0,1},{1,2},{2,3},{4,5},{5,6},{6,7},{8,9},{9,10},{10,11},{12,13},{... | collective-permute-start | bytes 1769480 | tf_op jit(solution)/shard_map/ppermute | solution.py:652
  97.5 19.1 %copy-start.2 = (f32[8,216,128]{2,1,0:T(8,128)}, f32[8,216,128]{2,1,0:T(8,128)S(1)}, u32[]{:S(2)}) copy-start(f32[8,216,128]{2,1,0:T(8,128)S(1)} %all-to-all-done.4) | copy-start | bytes 2654212
  97.5 28.2 %all-to-all-start.3 = ((f32[8,216,128]{2,1,0:T(8,128)}), f32[8,216,128]{2,1,0:T(8,128)S(1)}, u32[]{:S(2)}, u32[]{:S(2)}) async-start(f32[8,216,128]{2,1,0:T(8,128)} %bitcast.8), calls=%async_computation.3 | async-start | bytes 1769472 | tf_op jit(solution)/shard_map/all_to_all | solution.py:649
  116.7 13.5 %copy-start.7 = (f32[8,128]{1,0:T(8,128)S(1)}, f32[8,128]{1,0:T(8,128)}, u32[]{:S(2)}) copy-start(f32[8,128]{1,0:T(8,128)} %get-tuple-element.19) | copy-start | bytes 12292
  125.7 29.4 %copy-start.3 = (f32[8,216,128]{2,1,0:T(8,128)}, f32[8,216,128]{2,1,0:T(8,128)S(1)}, u32[]{:S(2)}) copy-start(f32[8,216,128]{2,1,0:T(8,128)S(1)} %all-to-all-done.3) | copy-start | bytes 2654212
  125.7 36.9 %all-to-all-start.2 = ((f32[8,216,128]{2,1,0:T(8,128)}), f32[8,216,128]{2,1,0:T(8,128)S(1)}, u32[]{:S(2)}, u32[]{:S(2)}) async-start(f32[8,216,128]{2,1,0:T(8,128)} %bitcast.15), calls=%async_computation.2 | async-start | bytes 1769472 | tf_op jit(solution)/shard_map/all_to_all | solution.py:649
  130.1 1.2 collective-permute-start.8
  131.4 3.6 %collective-permute-start.9 = (f32[8,128]{1,0:T(8,128)S(1)}, f32[8,128]{1,0:T(8,128)S(1)}, u32[]{:S(2)}, u32[]{:S(2)}) collective-permute-start(f32[8,128]{1,0:T(8,128)S(1)} %add.37), channel_id=1, source_target_pairs={{0,2},{1,3},{2,0},{3,1},{4,6},{5,7},{6,4},{7,5},{8,10},{9,11},{10,... | collective-permute-start | bytes 12296 | tf_op jit(solution)/shard_map/ppermute | solution.py:634
  135.0 3.7 %collective-permute-start.10 = (f32[8,128]{1,0:T(8,128)S(1)}, f32[8,128]{1,0:T(8,128)S(1)}, u32[]{:S(2)}, u32[]{:S(2)}) collective-permute-start(f32[8,128]{1,0:T(8,128)S(1)} %add.38), channel_id=1, source_target_pairs={{0,4},{4,0},{8,12},{12,8},{16,20},{20,16},{24,28},{28,24},{1,5},{5... | collective-permute-start | bytes 12296 | tf_op jit(solution)/shard_map/ppermute | solution.py:634
  138.7 10.5 %collective-permute-start.13 = (f32[8,128]{1,0:T(8,128)S(1)}, f32[8,128]{1,0:T(8,128)S(1)}, u32[]{:S(2)}, u32[]{:S(2)}) collective-permute-start(f32[8,128]{1,0:T(8,128)S(1)} %add.39), channel_id=1, source_target_pairs={{0,24},{4,28},{8,16},{12,20},{16,8},{20,12},{24,0},{28,4},{1,25},{... | collective-permute-start | bytes 12296 | tf_op jit(solution)/shard_map/ppermute | solution.py:636
  142.8 10.4 %collective-permute-start.12 = (f32[8,128]{1,0:T(8,128)S(1)}, f32[8,128]{1,0:T(8,128)S(1)}, u32[]{:S(2)}, u32[]{:S(2)}) collective-permute-start(f32[8,128]{1,0:T(8,128)S(1)} %add.39), channel_id=1, source_target_pairs={{0,16},{4,20},{8,24},{12,28},{16,0},{20,4},{24,8},{28,12},{1,17},{... | collective-permute-start | bytes 12296 | tf_op jit(solution)/shard_map/ppermute | solution.py:636
  142.8 10.4 %collective-permute-start.11 = (f32[8,128]{1,0:T(8,128)S(1)}, f32[8,128]{1,0:T(8,128)S(1)}, u32[]{:S(2)}, u32[]{:S(2)}) collective-permute-start(f32[8,128]{1,0:T(8,128)S(1)} %add.39), channel_id=1, source_target_pairs={{0,8},{4,12},{8,0},{12,4},{16,24},{20,28},{24,16},{28,20},{1,9},{5... | collective-permute-start | bytes 12296 | tf_op jit(solution)/shard_map/ppermute | solution.py:636
  (11 other events, 12.0 us)

commit v8 on v7

--- a/solution.py
+++ b/solution.py
@@ -528,66 +528,102 @@
             f32(6 * FACE + 8, TILES * LANES),
         ],
         compiler_params=pltpu.CompilerParams(vmem_limit_bytes=VMEM),
-        cost_estimate=estimate(15),
+        cost_estimate=estimate(2),
         name="apply_twice",
     )(place, own, before, after, scale, to_even, to_all, fields, fibre, *so_far)
 
 
-def factor_kernel(total, factors):
+def combination(total):
     bb, bq, qq, bw, qw = (jnp.sum(total[n : n + 1, :], axis=1, keepdims=True) for n in range(5))
     step_one = bb / bq
     norm = bb - 2.0 * step_one * bq + step_one * step_one * qq
     grown = 1.0 + norm / bb
     curve = grown * grown * bq - step_one * grown * (bw + qq) + step_one * step_one * qw
     step_two = norm / curve
-    factors[0:8, :] = jnp.broadcast_to(step_one + step_two * grown, (8, LANES))
-    factors[8:16, :] = jnp.broadcast_to(step_one * step_two, (8, LANES))
-
-
-def combination(total):
-    return pl.pallas_call(
-        factor_kernel,
-        out_shape=jax.ShapeDtypeStruct((16, LANES), jnp.float32),
-        cost_estimate=estimate(1),
-        name="combination",
-    )(total)
-
-
-def finish_kernel(field, image, factors, *refs):
-    modes = field.shape[0]
-    solution_field, residual = refs[-2:]
+    return step_one + step_two * grown, step_one * step_two
+
+
+def unpack_kernel(image, natural):
+    modes = natural.shape[1]
     per_part = modes * 2 * SLAB
-    sole, cross = factors[0:8, :], factors[8:16, :]
 
     def body(step, carry):
         for inner in range(2 * UNROLL):
             mode = step * 2 * UNROLL + inner
-            for p in range(SLAB):
-                row = mode * 2 * SLAB + p
-                b = field[mode, 0, p]
-                q = swap_back(image[pl.ds(row, PARTS, stride=per_part), :])
-                w = swap_back(image[pl.ds(row + SLAB, PARTS, stride=per_part), :])
-                solution_field[mode, 0, p] = sole * b - cross * q
-                residual[mode, 0, p] = b - sole * q + cross * w
+            for power in range(2):
+                for p in range(SLAB):
+                    row = (mode * 2 + power) * SLAB + p
+                    natural[power, mode, p] = swap_back(image[pl.ds(row, PARTS, stride=per_part), :])
         return carry
 
     lax.fori_loop(0, modes // (2 * UNROLL), body, 0)
 
 
-def finish(field, comp, image, factors, so_far):
-    block = pl.BlockSpec((field.shape[0], 1) + field.shape[2:], lambda i: (0, comp, 0, 0, 0))
+def unpack(image, modes):
+    vmem = pl.BlockSpec(memory_space=pltpu.VMEM)
+    return pl.pallas_call(
+        unpack_kernel,
+        out_shape=jax.ShapeDtypeStruct((2, modes, SLAB, 8, LANES), jnp.float32),
+        in_specs=[vmem],
+        out_specs=vmem,
+        compiler_params=pltpu.CompilerParams(vmem_limit_bytes=VMEM),
+        cost_estimate=estimate(3),
+        name="unpack",
+    )(image)
+
+
+STEPS = 2
+
+
+def finish_kernel(field, total, image, *refs):
+    *natural, solution_field, residual, factors = refs
+    modes = field.shape[0]
+    per_part = STEPS * modes * 2 * SLAB
+
+    @pl.when(pl.program_id(0) == 0)
+    def _():
+        sole, cross = combination(total)
+        factors[0:8, :] = jnp.broadcast_to(sole, (8, LANES))
+        factors[8:16, :] = jnp.broadcast_to(cross, (8, LANES))
+
+    sole, cross = factors[0:8, :], factors[8:16, :]
+    first = pl.program_id(0) * modes
+
+    def body(step, carry):
+        for inner in range(2 * UNROLL):
+            mode = step * 2 * UNROLL + inner
+            for comp in range(COMPS):
+                for p in range(SLAB):
+                    b = field[mode, comp, p]
+                    if comp < len(natural):
+                        q, w = natural[comp][0, mode, p], natural[comp][1, mode, p]
+                    else:
+                        row = (first + mode) * 2 * SLAB + p
+                        q = swap_back(image[pl.ds(row, PARTS, stride=per_part), :])
+                        w = swap_back(image[pl.ds(row + SLAB, PARTS, stride=per_part), :])
+                    solution_field[mode, comp, p] = sole * b - cross * q
+                    residual[mode, comp, p] = b - sole * q + cross * w
+        return carry
+
+    lax.fori_loop(0, modes // (2 * UNROLL), body, 0)
+
+
+def finish(field, total, image, *natural):
+    rows = field.shape[0] // STEPS
+    block = pl.BlockSpec((rows,) + field.shape[1:], lambda i: (i, 0, 0, 0, 0))
     vmem = pl.BlockSpec(memory_space=pltpu.VMEM)
     return pl.pallas_call(
         finish_kernel,
-        grid=(1,),
+        grid=(STEPS,),
         out_shape=[jax.ShapeDtypeStruct(field.shape, jnp.float32)] * 2,
-        in_specs=[block, vmem, vmem] + [pl.BlockSpec(memory_space=pl.ANY)] * len(so_far),
+        in_specs=[block, vmem, vmem]
+        + [pl.BlockSpec((2, rows) + field.shape[2:], lambda i: (0, i, 0, 0, 0))] * len(natural),
         out_specs=[block, block],
-        input_output_aliases={3 + n: n for n in range(len(so_far))},
+        scratch_shapes=[pltpu.VMEM((16, LANES), jnp.float32)],
         compiler_params=pltpu.CompilerParams(vmem_limit_bytes=VMEM),
-        cost_estimate=estimate(3),
+        cost_estimate=estimate(6),
         name="finish",
-    )(field, image, factors, *so_far)
+    )(field, total, image, *natural)
 
 
 def mode_tables(coupling_table, slots):
@@ -665,11 +701,8 @@
         rows = halo(part_component(others, comp - 1, partial))
         image, partial = apply_twice(comp, place, *rows, tables, fields, fibre_weights, partial)
         images.append(swap(image))
-    factors = combination(all_sum(partial))
-    outputs = ()
-    for comp in range(COMPS):
-        outputs = finish(right_side, comp, images[comp], factors, outputs)
-    return tuple(outputs)
+    natural = [unpack(image, right_side.shape[0]) for image in images[:-1]]
+    return tuple(finish(right_side, all_sum(partial), images[-1], *natural))
 
 
 def on_device(right_side, mean_stiffness, ply_stiffness, fibre_weights, ply_map, coupling_table):

time: 168 us -> 162 us (0.964)
  waiting for transfers between devices: 29 us -> 12 us
  starting transfers between devices: 55.4 us -> 69.9 us
  local copies, waits for them, and re-layouts: 9.64 us -> 7.07 us
    all_to_all x5, waiting for transfers between devices: 13.8 us -> 4.04 us  [swap(): return lax.all_to_all(rows, 'mode', 0, 0, tiled=True)]
    ppermute x3, starting transfers between devices: 3.15 us -> 12.9 us  [all_sum(): lax.ppermute(value, axis, [(i, i ^ bit) for i in range(devices)])]
    ppermute x3, waiting for transfers between devices: 9.79 us -> 0.26 us  [all_sum(): lax.ppermute(value, 'mode', [(i, i ^ bit) for i in range(PARTS)])]
    ppermute x3, starting transfers between devices: 12.6 us -> 16.9 us  [halo(): lax.ppermute(rows, 'space', up)]
    ppermute x3, waiting for transfers between devices: 0.01 us -> 3.53 us  [halo(): lax.ppermute(rows, 'space', up)]
    unnamed x33, local copies, waits for them, and re-layouts: 6.86 us -> 4.26 us
    pallas_call x4 -> x3, Pallas kernels: 12.6 us -> 11.6 us  [the longest x2 7.21 us: unpack(): pl.pallas_call(unpack_kernel, out_shape=jax.ShapeDtypeStruct((2, modes, S...]
  transfers between devices with their start and end apart: 19 -> 19, of which waited for: 10 -> 9; matrix products, arithmetic and copies ran while one was open for 7% -> 7% of each run, Pallas kernels for 33% -> 35%
where the time goes in v8:
time: 162 us; the launch traced here: 161 us
  starting transfers between devices  69.9 us (43%)
  Pallas kernels  63.7 us (39%)
  waiting for transfers between devices  12 us (7%)
  local copies, waits for them, and re-layouts  7.07 us (4%)
  other arithmetic  5.92 us (4%)
  matrix products  1.8 us (1%)
    pallas_call x3, Pallas kernels, apply_twice(): pl.pallas_call(functools.partial(apply_kernel, comp=comp), out_shape=[jax...  36.2 us
    all_to_all x5, starting transfers between devices, swap(): return lax.all_to_all(rows, 'mode', 0, 0, tiled=True)  27.5 us
    ppermute x3, starting transfers between devices, halo(): lax.ppermute(rows, 'space', up)  16.9 us
    ppermute x3, starting transfers between devices, all_sum(): lax.ppermute(value, axis, [(i, i ^ bit) for i in range(devices)])  12.9 us
    pallas_call x2, Pallas kernels, pack(): pl.pallas_call(functools.partial(pack_kernel, comps=comps), grid=(1,), ou...  8.51 us
    pallas_call x2, Pallas kernels, unpack(): pl.pallas_call(unpack_kernel, out_shape=jax.ShapeDtypeStruct((2, modes, S...  7.21 us
    pallas_call x1, Pallas kernels, finish(): pl.pallas_call(finish_kernel, grid=(STEPS,), out_shape=[jax.ShapeDtypeStr...  4.43 us
    ppermute x3, starting transfers between devices, all_sum(): lax.ppermute(value, 'mode', [(i, i ^ bit) for i in range(PARTS)])  4.39 us
  transfers between devices with their start and end apart: 19, of which 9 were waited for; matrix products, arithmetic and copies ran while one was open for 7% of the time, Pallas kernels for 35%

profile of v8, /device:TPU:0, one launch (start us, length us, event | category | flops | bytes accessed | tf_op | source)
XLA Modules:
  0.0 161.2 jit_solution(6425462983522075648)
XLA Ops:
  0.6 3.2 %pack.2.refs_2_ = f32[1152,128]{1,0:T(8,128)} custom-call(f32[36,3,3,8,128]{4,3,2,1,0:T(8,128)} %field.5), custom_call_target="tpu_custom_call" | custom-call | flops 500000000 | bytes 1500000 | tf_op jit(solution)/shard_map/pack/pallas_call | solution.py:206
  3.9 7.4 %all-to-all-start.1 = ((f32[8,144,128]{2,1,0:T(8,128)}), f32[8,144,128]{2,1,0:T(8,128)S(1)}, u32[]{:S(2)}, u32[]{:S(2)}) async-start(f32[8,144,128]{2,1,0:T(8,128)} %bitcast.12), calls=%async_computation.1 | async-start | bytes 1179648 | tf_op jit(solution)/shard_map/all_to_all | solution.py:685
  11.3 5.3 %pack.3 = (f32[2,3,8,128]{3,2,1,0:T(8,128)}, f32[2304,128]{1,0:T(8,128)}) custom-call(f32[36,3,3,8,128]{4,3,2,1,0:T(8,128)} %field.5, f32[3,8,128]{2,1,0:T(8,128)} %refs_0_.1, s32[3,8,128]{2,1,0:T(8,128)} %refs_1_.1, f32[1152,128]{1,0:T(8,128)} %pack.2.refs_2_), custom_call_target="tpu_custom_call" | custom-call | flops 500000000 | bytes 1500000 | tf_op jit(solution)/shard_map/pack/pallas_call | solution.py:206
  17.8 3.0 %collective-permute-start.2 = (f32[2,3,8,128]{3,2,1,0:T(8,128)}, f32[2,3,8,128]{3,2,1,0:T(8,128)S(1)}, u32[]{:S(2)}, u32[]{:S(2)}) collective-permute-start(f32[2,3,8,128]{3,2,1,0:T(8,128)} %get-tuple-element.11.both), channel_id=1, source_target_pairs={{0,1},{1,2},{2,3},{4,5},{5,6},{6,7},{8,9},{9,10},{10,11},{12,13},{... | collective-permute-start | bytes 73736 | tf_op jit(solution)/shard_map/ppermute | solution.py:695
  24.1 3.0 %all-to-all-done.1 = f32[8,144,128]{2,1,0:T(8,128)S(1)} async-done(((f32[8,144,128]{2,1,0:T(8,128)}), f32[8,144,128]{2,1,0:T(8,128)S(1)}, u32[]{:S(2)}, u32[]{:S(2)}) %all-to-all-start.1) | async-done | bytes 589856 | tf_op jit(solution)/shard_map/all_to_all | solution.py:685
  27.2 3.6 %all-to-all-start = ((f32[8,288,128]{2,1,0:T(8,128)}), f32[8,288,128]{2,1,0:T(8,128)S(1)}, u32[]{:S(2)}, u32[]{:S(2)}) async-start(f32[8,288,128]{2,1,0:T(8,128)} %bitcast.1), calls=%async_computation | async-start | bytes 2359296 | tf_op jit(solution)/shard_map/all_to_all | solution.py:685
  32.1 3.1 %collective-permute-start = (f32[1152,128]{1,0:T(8,128)S(1)}, f32[1152,128]{1,0:T(8,128)S(1)}, u32[]{:S(2)}, u32[]{:S(2)}) collective-permute-start(f32[1152,128]{1,0:T(8,128)S(1)} %bitcast.20), channel_id=1, source_target_pairs={{0,1},{1,2},{2,3},{4,5},{5,6},{6,7},{8,9},{9,10},{10,11},{12,13},{... | collective-permute-start | bytes 1769480 | tf_op jit(solution)/shard_map/ppermute | solution.py:688
  47.0 12.1 %apply_twice.3 = (f32[1728,128]{1,0:T(8,128)}, f32[8,128]{1,0:T(8,128)}) custom-call(s32[1]{0:T(128)} %bitcast.place, f32[1152,128]{1,0:T(8,128)} %bitcast.22, f32[1152,128]{1,0:T(8,128)} %copy-done.9, f32[1152,128]{1,0:T(8,128)} %copy-done.8, f32[288,128]{1,0:T(8,128)} %broadcast_in_dim.90.scale, bf16[624,576]{1,0:T(8,128)(2,1)} %pad_maximum_fusion.to_even, ...), custom_call_target="tpu_custom_call" | custom-call | flops 2000000000 | bytes 6000000 | tf_op jit(solution)/shard_map/apply_twice/pallas_call | solution.py:512
  60.1 5.0 %all-to-all-start.3 = ((f32[8,216,128]{2,1,0:T(8,128)}), f32[8,216,128]{2,1,0:T(8,128)S(1)}, u32[]{:S(2)}, u32[]{:S(2)}) async-start(f32[8,216,128]{2,1,0:T(8,128)} %bitcast.18), calls=%async_computation.3 | async-start | bytes 1769472 | tf_op jit(solution)/shard_map/all_to_all | solution.py:685
  65.2 1.9 %part_component.2 = f32[8,144,128]{2,1,0:T(8,128)} custom-call(f32[8,288,128]{2,1,0:T(8,128)} %copy-done.1, f32[8,128]{1,0:T(8,128)} %get-tuple-element.12.ready.refs_0_), custom_call_target="tpu_custom_call" | custom-call | flops 500000000 | bytes 1500000 | tf_op jit(solution)/shard_map/part_component/pallas_call | solution.py:228
  68.6 4.7 %collective-permute-start.4 = (f32[1152,128]{1,0:T(8,128)}, f32[1152,128]{1,0:T(8,128)S(1)}, u32[]{:S(2)}, u32[]{:S(2)}) collective-permute-start(f32[1152,128]{1,0:T(8,128)} %bitcast.27), channel_id=1, source_target_pairs={{0,1},{1,2},{2,3},{4,5},{5,6},{6,7},{8,9},{9,10},{10,11},{12,13},{... | collective-permute-start | bytes 1769480 | tf_op jit(solution)/shard_map/ppermute | solution.py:688
  75.8 12.1 %apply_twice.4 = (f32[1728,128]{1,0:T(8,128)}, f32[8,128]{1,0:T(8,128)}) custom-call(s32[1]{0:T(128)} %bitcast.place, f32[1152,128]{1,0:T(8,128)} %bitcast.28, f32[1152,128]{1,0:T(8,128)} %copy-done.13, f32[1152,128]{1,0:T(8,128)} %copy-done.12, f32[288,128]{1,0:T(8,128)} %broadcast_in_dim.90.scale, bf16[624,576]{1,0:T(8,128)(2,1)} %pad_maximum_fusion.to_even, ...), custom_call_target="tpu_custom_call" | custom-call | flops 2000000000 | bytes 6000000 | tf_op jit(solution)/shard_map/apply_twice/pallas_call | solution.py:512
  87.9 5.7 %all-to-all-start.4 = ((f32[8,216,128]{2,1,0:T(8,128)}), f32[8,216,128]{2,1,0:T(8,128)S(1)}, u32[]{:S(2)}, u32[]{:S(2)}) async-start(f32[8,216,128]{2,1,0:T(8,128)} %bitcast.17), calls=%async_computation.4 | async-start | bytes 1769472 | tf_op jit(solution)/shard_map/all_to_all | solution.py:685
  93.6 1.9 %part_component.3 = f32[8,144,128]{2,1,0:T(8,128)} custom-call(f32[8,288,128]{2,1,0:T(8,128)} %copy-done.1, f32[8,128]{1,0:T(8,128)} %get-tuple-element.13.ready.refs_0_), custom_call_target="tpu_custom_call" | custom-call | flops 500000000 | bytes 1500000 | tf_op jit(solution)/shard_map/part_component/pallas_call | solution.py:228
  96.9 9.1 %collective-permute-start.6 = (f32[1152,128]{1,0:T(8,128)}, f32[1152,128]{1,0:T(8,128)S(1)}, u32[]{:S(2)}, u32[]{:S(2)}) collective-permute-start(f32[1152,128]{1,0:T(8,128)} %bitcast.24), channel_id=1, source_target_pairs={{0,1},{1,2},{2,3},{4,5},{5,6},{6,7},{8,9},{9,10},{10,11},{12,13},{... | collective-permute-start | bytes 1769480 | tf_op jit(solution)/shard_map/ppermute | solution.py:688
  108.6 12.1 %apply_twice.5 = (f32[1728,128]{1,0:T(8,128)}, f32[8,128]{1,0:T(8,128)}) custom-call(s32[1]{0:T(128)} %bitcast.place, f32[1152,128]{1,0:T(8,128)} %bitcast.25, f32[1152,128]{1,0:T(8,128)} %copy-done.11, f32[1152,128]{1,0:T(8,128)} %copy-done.10, f32[288,128]{1,0:T(8,128)} %broadcast_in_dim.90.scale, bf16[624,576]{1,0:T(8,128)(2,1)} %pad_maximum_fusion.to_even, ...), custom_call_target="tpu_custom_call" | custom-call | flops 2000000000 | bytes 6000000 | tf_op jit(solution)/shard_map/apply_twice/pallas_call | solution.py:512
  120.7 5.7 %all-to-all-start.2 = ((f32[8,216,128]{2,1,0:T(8,128)}), f32[8,216,128]{2,1,0:T(8,128)S(1)}, u32[]{:S(2)}, u32[]{:S(2)}) async-start(f32[8,216,128]{2,1,0:T(8,128)} %bitcast.15), calls=%async_computation.2 | async-start | bytes 1769472 | tf_op jit(solution)/shard_map/all_to_all | solution.py:685
  126.5 8.0 %collective-permute-start.8 = (f32[8,128]{1,0:T(8,128)S(1)}, f32[8,128]{1,0:T(8,128)S(1)}, u32[]{:S(2)}, u32[]{:S(2)}) collective-permute-start(f32[8,128]{1,0:T(8,128)S(1)} %copy-done.7), channel_id=1, source_target_pairs={{0,1},{1,0},{2,3},{3,2},{4,5},{5,4},{6,7},{7,6},{8,9},{9,8},{10,11... | collective-permute-start | bytes 12296 | tf_op jit(solution)/shard_map/ppermute | solution.py:670
  135.3 2.9 %collective-permute-start.9 = (f32[8,128]{1,0:T(8,128)S(1)}, f32[8,128]{1,0:T(8,128)S(1)}, u32[]{:S(2)}, u32[]{:S(2)}) collective-permute-start(f32[8,128]{1,0:T(8,128)S(1)} %add.37), channel_id=1, source_target_pairs={{0,2},{1,3},{2,0},{3,1},{4,6},{5,7},{6,4},{7,5},{8,10},{9,11},{10,... | collective-permute-start | bytes 12296 | tf_op jit(solution)/shard_map/ppermute | solution.py:670
  139.8 2.0 %collective-permute-start.10 = (f32[8,128]{1,0:T(8,128)S(1)}, f32[8,128]{1,0:T(8,128)S(1)}, u32[]{:S(2)}, u32[]{:S(2)}) collective-permute-start(f32[8,128]{1,0:T(8,128)S(1)} %add.38), channel_id=1, source_target_pairs={{0,4},{4,0},{8,12},{12,8},{16,20},{20,16},{24,28},{28,24},{1,5},{5... | collective-permute-start | bytes 12296 | tf_op jit(solution)/shard_map/ppermute | solution.py:670
  143.4 3.8 %collective-permute-start.13 = (f32[8,128]{1,0:T(8,128)S(1)}, f32[8,128]{1,0:T(8,128)S(1)}, u32[]{:S(2)}, u32[]{:S(2)}) collective-permute-start(f32[8,128]{1,0:T(8,128)S(1)} %add.39), channel_id=1, source_target_pairs={{0,24},{4,28},{8,16},{12,20},{16,8},{20,12},{24,0},{28,4},{1,25},{... | collective-permute-start | bytes 12296 | tf_op jit(solution)/shard_map/ppermute | solution.py:672
  147.8 3.6 %unpack.2.refs_0_ = f32[2,36,3,8,128]{4,3,2,1,0:T(8,128)} custom-call(f32[1728,128]{1,0:T(8,128)} %bitcast.13), custom_call_target="tpu_custom_call" | custom-call | flops 3000000000 | bytes 9000000 | tf_op jit(solution)/shard_map/unpack/pallas_call | solution.py:564
  152.3 3.6 %unpack.3.refs_1_ = f32[2,36,3,8,128]{4,3,2,1,0:T(8,128)} custom-call(f32[1728,128]{1,0:T(8,128)} %bitcast.14), custom_call_target="tpu_custom_call" | custom-call | flops 3000000000 | bytes 9000000 | tf_op jit(solution)/shard_map/unpack/pallas_call | solution.py:564
  156.8 4.4 %finish.1 = (f32[36,3,3,8,128]{4,3,2,1,0:T(8,128)}, f32[36,3,3,8,128]{4,3,2,1,0:T(8,128)}) custom-call(f32[36,3,3,8,128]{4,3,2,1,0:T(8,128)} %field.5, f32[8,128]{1,0:T(8,128)} %add_add_fusion.total, f32[1728,128]{1,0:T(8,128)} %bitcast.16, f32[2,36,3,8,128]{4,3,2,1,0:T(8,128)} %unpack.2.refs_0_, f32[2,36,3,8,128]{4,3,2,1,0:T(8,128)} %unpack.3.refs_1_), custom_call_target="tpu_custom_call" | custom-call | flops 6000000000 | bytes 18000000 | tf_op jit(solution)/shard_map/finish/pallas_call | solution.py:615
  (80 shorter events, 33.1 us)
Async XLA Ops:
  3.9 17.0 %copy-start.6 = (s32[660,4]{0,1:T(4,128)S(1)}, s32[660,4]{0,1:T(4,128)}, u32[]{:S(2)}) copy-start(s32[660,4]{0,1:T(4,128)} %param.11) | copy-start | bytes 31684
  3.9 23.3 %all-to-all-start.1 = ((f32[8,144,128]{2,1,0:T(8,128)}), f32[8,144,128]{2,1,0:T(8,128)S(1)}, u32[]{:S(2)}, u32[]{:S(2)}) async-start(f32[8,144,128]{2,1,0:T(8,128)} %bitcast.12), calls=%async_computation.1 | async-start | bytes 1179648 | tf_op jit(solution)/shard_map/all_to_all | solution.py:685
  16.5 5.3 %collective-permute-start.3 = (f32[2,3,8,128]{3,2,1,0:T(8,128)}, f32[2,3,8,128]{3,2,1,0:T(8,128)S(1)}, u32[]{:S(2)}, u32[]{:S(2)}) collective-permute-start(f32[2,3,8,128]{3,2,1,0:T(8,128)} %get-tuple-element.11.both), channel_id=1, source_target_pairs={{1,0},{2,1},{3,2},{5,4},{6,5},{7,6},{9,8},{10,9},{11,10},{13,12},{... | collective-permute-start | bytes 73736 | tf_op jit(solution)/shard_map/ppermute | solution.py:696
  17.8 4.1 %collective-permute-start.2 = (f32[2,3,8,128]{3,2,1,0:T(8,128)}, f32[2,3,8,128]{3,2,1,0:T(8,128)S(1)}, u32[]{:S(2)}, u32[]{:S(2)}) collective-permute-start(f32[2,3,8,128]{3,2,1,0:T(8,128)} %get-tuple-element.11.both), channel_id=1, source_target_pairs={{0,1},{1,2},{2,3},{4,5},{5,6},{6,7},{8,9},{9,10},{10,11},{12,13},{... | collective-permute-start | bytes 73736 | tf_op jit(solution)/shard_map/ppermute | solution.py:695
  27.1 8.0 %copy-start.5 = (f32[8,144,128]{2,1,0:T(8,128)}, f32[8,144,128]{2,1,0:T(8,128)S(1)}, u32[]{:S(2)}) copy-start(f32[8,144,128]{2,1,0:T(8,128)S(1)} %all-to-all-done.1) | copy-start | bytes 1769476
  27.2 33.0 %all-to-all-start = ((f32[8,288,128]{2,1,0:T(8,128)}), f32[8,288,128]{2,1,0:T(8,128)S(1)}, u32[]{:S(2)}, u32[]{:S(2)}) async-start(f32[8,288,128]{2,1,0:T(8,128)} %bitcast.1), calls=%async_computation | async-start | bytes 2359296 | tf_op jit(solution)/shard_map/all_to_all | solution.py:685
  30.8 15.2 %collective-permute-start.1 = (f32[1152,128]{1,0:T(8,128)S(1)}, f32[1152,128]{1,0:T(8,128)S(1)}, u32[]{:S(2)}, u32[]{:S(2)}) collective-permute-start(f32[1152,128]{1,0:T(8,128)S(1)} %bitcast.19), channel_id=1, source_target_pairs={{1,0},{2,1},{3,2},{5,4},{6,5},{7,6},{9,8},{10,9},{11,10},{13,12},{... | collective-permute-start | bytes 1769480 | tf_op jit(solution)/shard_map/ppermute | solution.py:688
  32.1 13.9 %collective-permute-start = (f32[1152,128]{1,0:T(8,128)S(1)}, f32[1152,128]{1,0:T(8,128)S(1)}, u32[]{:S(2)}, u32[]{:S(2)}) collective-permute-start(f32[1152,128]{1,0:T(8,128)S(1)} %bitcast.20), channel_id=1, source_target_pairs={{0,1},{1,2},{2,3},{4,5},{5,6},{6,7},{8,9},{9,10},{10,11},{12,13},{... | collective-permute-start | bytes 1769480 | tf_op jit(solution)/shard_map/ppermute | solution.py:688
  60.1 27.8 %all-to-all-start.3 = ((f32[8,216,128]{2,1,0:T(8,128)}), f32[8,216,128]{2,1,0:T(8,128)S(1)}, u32[]{:S(2)}, u32[]{:S(2)}) async-start(f32[8,216,128]{2,1,0:T(8,128)} %bitcast.18), calls=%async_computation.3 | async-start | bytes 1769472 | tf_op jit(solution)/shard_map/all_to_all | solution.py:685
  67.1 6.1 %collective-permute-start.5 = (f32[1152,128]{1,0:T(8,128)}, f32[1152,128]{1,0:T(8,128)S(1)}, u32[]{:S(2)}, u32[]{:S(2)}) collective-permute-start(f32[1152,128]{1,0:T(8,128)} %bitcast.26), channel_id=1, source_target_pairs={{1,0},{2,1},{3,2},{5,4},{6,5},{7,6},{9,8},{10,9},{11,10},{13,12},{... | collective-permute-start | bytes 1769480 | tf_op jit(solution)/shard_map/ppermute | solution.py:688
  68.6 6.4 %collective-permute-start.4 = (f32[1152,128]{1,0:T(8,128)}, f32[1152,128]{1,0:T(8,128)S(1)}, u32[]{:S(2)}, u32[]{:S(2)}) collective-permute-start(f32[1152,128]{1,0:T(8,128)} %bitcast.27), channel_id=1, source_target_pairs={{0,1},{1,2},{2,3},{4,5},{5,6},{6,7},{8,9},{9,10},{10,11},{12,13},{... | collective-permute-start | bytes 1769480 | tf_op jit(solution)/shard_map/ppermute | solution.py:688
  87.9 7.6 %copy-start.2 = (f32[8,216,128]{2,1,0:T(8,128)}, f32[8,216,128]{2,1,0:T(8,128)S(1)}, u32[]{:S(2)}) copy-start(f32[8,216,128]{2,1,0:T(8,128)S(1)} %all-to-all-done.3) | copy-start | bytes 2654212
  87.9 32.8 %all-to-all-start.4 = ((f32[8,216,128]{2,1,0:T(8,128)}), f32[8,216,128]{2,1,0:T(8,128)S(1)}, u32[]{:S(2)}, u32[]{:S(2)}) async-start(f32[8,216,128]{2,1,0:T(8,128)} %bitcast.17), calls=%async_computation.4 | async-start | bytes 1769472 | tf_op jit(solution)/shard_map/all_to_all | solution.py:685
  95.6 10.4 %collective-permute-start.7 = (f32[1152,128]{1,0:T(8,128)}, f32[1152,128]{1,0:T(8,128)S(1)}, u32[]{:S(2)}, u32[]{:S(2)}) collective-permute-start(f32[1152,128]{1,0:T(8,128)} %bitcast.23), channel_id=1, source_target_pairs={{1,0},{2,1},{3,2},{5,4},{6,5},{7,6},{9,8},{10,9},{11,10},{13,12},{... | collective-permute-start | bytes 1769480 | tf_op jit(solution)/shard_map/ppermute | solution.py:688
  96.9 10.9 %collective-permute-start.6 = (f32[1152,128]{1,0:T(8,128)}, f32[1152,128]{1,0:T(8,128)S(1)}, u32[]{:S(2)}, u32[]{:S(2)}) collective-permute-start(f32[1152,128]{1,0:T(8,128)} %bitcast.24), channel_id=1, source_target_pairs={{0,1},{1,2},{2,3},{4,5},{5,6},{6,7},{8,9},{9,10},{10,11},{12,13},{... | collective-permute-start | bytes 1769480 | tf_op jit(solution)/shard_map/ppermute | solution.py:688
  120.7 5.8 %copy-start.7 = (f32[8,128]{1,0:T(8,128)S(1)}, f32[8,128]{1,0:T(8,128)}, u32[]{:S(2)}) copy-start(f32[8,128]{1,0:T(8,128)} %get-tuple-element.14) | copy-start | bytes 12292
  120.7 30.7 %copy-start.3 = (f32[8,216,128]{2,1,0:T(8,128)}, f32[8,216,128]{2,1,0:T(8,128)S(1)}, u32[]{:S(2)}) copy-start(f32[8,216,128]{2,1,0:T(8,128)S(1)} %all-to-all-done.4) | copy-start | bytes 2654212
  120.7 35.1 %all-to-all-start.2 = ((f32[8,216,128]{2,1,0:T(8,128)}), f32[8,216,128]{2,1,0:T(8,128)S(1)}, u32[]{:S(2)}, u32[]{:S(2)}) async-start(f32[8,216,128]{2,1,0:T(8,128)} %bitcast.15), calls=%async_computation.2 | async-start | bytes 1769472 | tf_op jit(solution)/shard_map/all_to_all | solution.py:685
  126.5 8.9 %collective-permute-start.8 = (f32[8,128]{1,0:T(8,128)S(1)}, f32[8,128]{1,0:T(8,128)S(1)}, u32[]{:S(2)}, u32[]{:S(2)}) collective-permute-start(f32[8,128]{1,0:T(8,128)S(1)} %copy-done.7), channel_id=1, source_target_pairs={{0,1},{1,0},{2,3},{3,2},{4,5},{5,4},{6,7},{7,6},{8,9},{9,8},{10,11... | collective-permute-start | bytes 12296 | tf_op jit(solution)/shard_map/ppermute | solution.py:670
  135.3 4.5 %collective-permute-start.9 = (f32[8,128]{1,0:T(8,128)S(1)}, f32[8,128]{1,0:T(8,128)S(1)}, u32[]{:S(2)}, u32[]{:S(2)}) collective-permute-start(f32[8,128]{1,0:T(8,128)S(1)} %add.37), channel_id=1, source_target_pairs={{0,2},{1,3},{2,0},{3,1},{4,6},{5,7},{6,4},{7,5},{8,10},{9,11},{10,... | collective-permute-start | bytes 12296 | tf_op jit(solution)/shard_map/ppermute | solution.py:670
  139.8 3.6 %collective-permute-start.10 = (f32[8,128]{1,0:T(8,128)S(1)}, f32[8,128]{1,0:T(8,128)S(1)}, u32[]{:S(2)}, u32[]{:S(2)}) collective-permute-start(f32[8,128]{1,0:T(8,128)S(1)} %add.38), channel_id=1, source_target_pairs={{0,4},{4,0},{8,12},{12,8},{16,20},{20,16},{24,28},{28,24},{1,5},{5... | collective-permute-start | bytes 12296 | tf_op jit(solution)/shard_map/ppermute | solution.py:670
  143.4 8.0 %collective-permute-start.13 = (f32[8,128]{1,0:T(8,128)S(1)}, f32[8,128]{1,0:T(8,128)S(1)}, u32[]{:S(2)}, u32[]{:S(2)}) collective-permute-start(f32[8,128]{1,0:T(8,128)S(1)} %add.39), channel_id=1, source_target_pairs={{0,24},{4,28},{8,16},{12,20},{16,8},{20,12},{24,0},{28,4},{1,25},{... | collective-permute-start | bytes 12296 | tf_op jit(solution)/shard_map/ppermute | solution.py:672
  147.1 4.5 %collective-permute-start.12 = (f32[8,128]{1,0:T(8,128)S(1)}, f32[8,128]{1,0:T(8,128)S(1)}, u32[]{:S(2)}, u32[]{:S(2)}) collective-permute-start(f32[8,128]{1,0:T(8,128)S(1)} %add.39), channel_id=1, source_target_pairs={{0,16},{4,20},{8,24},{12,28},{16,0},{20,4},{24,8},{28,12},{1,17},{... | collective-permute-start | bytes 12296 | tf_op jit(solution)/shard_map/ppermute | solution.py:672
  147.2 4.5 %collective-permute-start.11 = (f32[8,128]{1,0:T(8,128)S(1)}, f32[8,128]{1,0:T(8,128)S(1)}, u32[]{:S(2)}, u32[]{:S(2)}) collective-permute-start(f32[8,128]{1,0:T(8,128)S(1)} %add.39), channel_id=1, source_target_pairs={{0,8},{4,12},{8,0},{12,4},{16,24},{20,28},{24,16},{28,20},{1,9},{5... | collective-permute-start | bytes 12296 | tf_op jit(solution)/shard_map/ppermute | solution.py:672
  (11 other events, 19.0 us)

commit v9 on v8

--- a/solution.py
+++ b/solution.py
@@ -697,9 +697,9 @@
     fields = stiffness_fields(place, both_before, both, both_after, ply_stiffness)
     image, partial = apply_twice(0, place, *first, tables, fields, fibre_weights)
     images = [swap(image)]
+    parts = [halo(part_component(others, n, partial)) for n in range(COMPS - 1)]
     for comp in range(1, COMPS):
-        rows = halo(part_component(others, comp - 1, partial))
-        image, partial = apply_twice(comp, place, *rows, tables, fields, fibre_weights, partial)
+        image, partial = apply_twice(comp, place, *parts[comp - 1], tables, fields, fibre_weights, partial)
         images.append(swap(image))
     natural = [unpack(image, right_side.shape[0]) for image in images[:-1]]
     return tuple(finish(right_side, all_sum(partial), images[-1], *natural))

time: 162 us -> 166 us (1.025)
  waiting for transfers between devices: 12 us -> 15.6 us
    ppermute x3, waiting for transfers between devices: 0.26 us -> 3.87 us  [all_sum(): lax.ppermute(value, 'mode', [(i, i ^ bit) for i in range(PARTS)])]
  transfers between devices with their start and end apart: 19 -> 19, of which waited for: 9 -> 10; matrix products, arithmetic and copies ran while one was open for 7% -> 7% of each run, Pallas kernels for 35% -> 34%
where the time goes in v9:
time: 166 us; the launch traced here: 165 us
  starting transfers between devices  69.9 us (42%)
  Pallas kernels  63.7 us (38%)
  waiting for transfers between devices  15.6 us (9%)
  local copies, waits for them, and re-layouts  7.07 us (4%)
  other arithmetic  5.92 us (4%)
  matrix products  1.8 us (1%)
    pallas_call x3, Pallas kernels, apply_twice(): pl.pallas_call(functools.partial(apply_kernel, comp=comp), out_shape=[jax...  36.2 us
    all_to_all x5, starting transfers between devices, swap(): return lax.all_to_all(rows, 'mode', 0, 0, tiled=True)  27.5 us
    ppermute x3, starting transfers between devices, halo(): lax.ppermute(rows, 'space', up)  16.9 us
    ppermute x3, starting transfers between devices, all_sum(): lax.ppermute(value, axis, [(i, i ^ bit) for i in range(devices)])  12.9 us
    pallas_call x2, Pallas kernels, pack(): pl.pallas_call(functools.partial(pack_kernel, comps=comps), grid=(1,), ou...  8.51 us
    pallas_call x2, Pallas kernels, unpack(): pl.pallas_call(unpack_kernel, out_shape=jax.ShapeDtypeStruct((2, modes, S...  7.21 us
    pallas_call x1, Pallas kernels, finish(): pl.pallas_call(finish_kernel, grid=(STEPS,), out_shape=[jax.ShapeDtypeStr...  4.43 us
    ppermute x3, starting transfers between devices, all_sum(): lax.ppermute(value, 'mode', [(i, i ^ bit) for i in range(PARTS)])  4.39 us
  transfers between devices with their start and end apart: 19, of which 10 were waited for; matrix products, arithmetic and copies ran while one was open for 7% of the time, Pallas kernels for 34%

profile of v9, /device:TPU:0, one launch (start us, length us, event | category | flops | bytes accessed | tf_op | source)
XLA Modules:
  0.0 164.8 jit_solution(3281523172082085001)
XLA Ops:
  0.6 3.2 %pack.2.refs_2_ = f32[1152,128]{1,0:T(8,128)} custom-call(f32[36,3,3,8,128]{4,3,2,1,0:T(8,128)} %field.5), custom_call_target="tpu_custom_call" | custom-call | flops 500000000 | bytes 1500000 | tf_op jit(solution)/shard_map/pack/pallas_call | solution.py:206
  3.9 7.4 %all-to-all-start.1 = ((f32[8,144,128]{2,1,0:T(8,128)}), f32[8,144,128]{2,1,0:T(8,128)S(1)}, u32[]{:S(2)}, u32[]{:S(2)}) async-start(f32[8,144,128]{2,1,0:T(8,128)} %bitcast.12), calls=%async_computation.1 | async-start | bytes 1179648 | tf_op jit(solution)/shard_map/all_to_all | solution.py:685
  11.3 5.3 %pack.3 = (f32[2,3,8,128]{3,2,1,0:T(8,128)}, f32[2304,128]{1,0:T(8,128)}) custom-call(f32[36,3,3,8,128]{4,3,2,1,0:T(8,128)} %field.5, f32[3,8,128]{2,1,0:T(8,128)} %refs_0_.1, s32[3,8,128]{2,1,0:T(8,128)} %refs_1_.1, f32[1152,128]{1,0:T(8,128)} %pack.2.refs_2_), custom_call_target="tpu_custom_call" | custom-call | flops 500000000 | bytes 1500000 | tf_op jit(solution)/shard_map/pack/pallas_call | solution.py:206
  17.8 3.0 %collective-permute-start.2 = (f32[2,3,8,128]{3,2,1,0:T(8,128)}, f32[2,3,8,128]{3,2,1,0:T(8,128)S(1)}, u32[]{:S(2)}, u32[]{:S(2)}) collective-permute-start(f32[2,3,8,128]{3,2,1,0:T(8,128)} %get-tuple-element.11.both), channel_id=1, source_target_pairs={{0,1},{1,2},{2,3},{4,5},{5,6},{6,7},{8,9},{9,10},{10,11},{12,13},{... | collective-permute-start | bytes 73736 | tf_op jit(solution)/shard_map/ppermute | solution.py:695
  24.1 3.0 %all-to-all-done.1 = f32[8,144,128]{2,1,0:T(8,128)S(1)} async-done(((f32[8,144,128]{2,1,0:T(8,128)}), f32[8,144,128]{2,1,0:T(8,128)S(1)}, u32[]{:S(2)}, u32[]{:S(2)}) %all-to-all-start.1) | async-done | bytes 589856 | tf_op jit(solution)/shard_map/all_to_all | solution.py:685
  27.2 3.6 %all-to-all-start = ((f32[8,288,128]{2,1,0:T(8,128)}), f32[8,288,128]{2,1,0:T(8,128)S(1)}, u32[]{:S(2)}, u32[]{:S(2)}) async-start(f32[8,288,128]{2,1,0:T(8,128)} %bitcast.1), calls=%async_computation | async-start | bytes 2359296 | tf_op jit(solution)/shard_map/all_to_all | solution.py:685
  32.1 3.1 %collective-permute-start = (f32[1152,128]{1,0:T(8,128)S(1)}, f32[1152,128]{1,0:T(8,128)S(1)}, u32[]{:S(2)}, u32[]{:S(2)}) collective-permute-start(f32[1152,128]{1,0:T(8,128)S(1)} %bitcast.20), channel_id=1, source_target_pairs={{0,1},{1,2},{2,3},{4,5},{5,6},{6,7},{8,9},{9,10},{10,11},{12,13},{... | collective-permute-start | bytes 1769480 | tf_op jit(solution)/shard_map/ppermute | solution.py:688
  47.0 12.1 %apply_twice.3 = (f32[1728,128]{1,0:T(8,128)}, f32[8,128]{1,0:T(8,128)}) custom-call(s32[1]{0:T(128)} %bitcast.place, f32[1152,128]{1,0:T(8,128)} %bitcast.22, f32[1152,128]{1,0:T(8,128)} %copy-done.9, f32[1152,128]{1,0:T(8,128)} %copy-done.8, f32[288,128]{1,0:T(8,128)} %broadcast_in_dim.90.scale, bf16[624,576]{1,0:T(8,128)(2,1)} %pad_maximum_fusion.to_even, ...), custom_call_target="tpu_custom_call" | custom-call | flops 2000000000 | bytes 6000000 | tf_op jit(solution)/shard_map/apply_twice/pallas_call | solution.py:512
  60.1 5.0 %all-to-all-start.3 = ((f32[8,216,128]{2,1,0:T(8,128)}), f32[8,216,128]{2,1,0:T(8,128)S(1)}, u32[]{:S(2)}, u32[]{:S(2)}) async-start(f32[8,216,128]{2,1,0:T(8,128)} %bitcast.18), calls=%async_computation.3 | async-start | bytes 1769472 | tf_op jit(solution)/shard_map/all_to_all | solution.py:685
  65.2 1.9 %part_component.3 = f32[8,144,128]{2,1,0:T(8,128)} custom-call(f32[8,288,128]{2,1,0:T(8,128)} %copy-done.1, f32[8,128]{1,0:T(8,128)} %get-tuple-element.12.ready.refs_0_), custom_call_target="tpu_custom_call" | custom-call | flops 500000000 | bytes 1500000 | tf_op jit(solution)/shard_map/part_component/pallas_call | solution.py:228
  68.6 4.7 %collective-permute-start.6 = (f32[1152,128]{1,0:T(8,128)}, f32[1152,128]{1,0:T(8,128)S(1)}, u32[]{:S(2)}, u32[]{:S(2)}) collective-permute-start(f32[1152,128]{1,0:T(8,128)} %bitcast.27), channel_id=1, source_target_pairs={{0,1},{1,2},{2,3},{4,5},{5,6},{6,7},{8,9},{9,10},{10,11},{12,13},{... | collective-permute-start | bytes 1769480 | tf_op jit(solution)/shard_map/ppermute | solution.py:688
  75.8 12.1 %apply_twice.4 = (f32[1728,128]{1,0:T(8,128)}, f32[8,128]{1,0:T(8,128)}) custom-call(s32[1]{0:T(128)} %bitcast.place, f32[1152,128]{1,0:T(8,128)} %bitcast.28, f32[1152,128]{1,0:T(8,128)} %copy-done.13, f32[1152,128]{1,0:T(8,128)} %copy-done.12, f32[288,128]{1,0:T(8,128)} %broadcast_in_dim.90.scale, bf16[624,576]{1,0:T(8,128)(2,1)} %pad_maximum_fusion.to_even, ...), custom_call_target="tpu_custom_call" | custom-call | flops 2000000000 | bytes 6000000 | tf_op jit(solution)/shard_map/apply_twice/pallas_call | solution.py:512
  87.9 5.7 %all-to-all-start.4 = ((f32[8,216,128]{2,1,0:T(8,128)}), f32[8,216,128]{2,1,0:T(8,128)S(1)}, u32[]{:S(2)}, u32[]{:S(2)}) async-start(f32[8,216,128]{2,1,0:T(8,128)} %bitcast.17), calls=%async_computation.4 | async-start | bytes 1769472 | tf_op jit(solution)/shard_map/all_to_all | solution.py:685
  96.9 9.1 %collective-permute-start.4 = (f32[1152,128]{1,0:T(8,128)}, f32[1152,128]{1,0:T(8,128)S(1)}, u32[]{:S(2)}, u32[]{:S(2)}) collective-permute-start(f32[1152,128]{1,0:T(8,128)} %bitcast.24), channel_id=1, source_target_pairs={{0,1},{1,2},{2,3},{4,5},{5,6},{6,7},{8,9},{9,10},{10,11},{12,13},{... | collective-permute-start | bytes 1769480 | tf_op jit(solution)/shard_map/ppermute | solution.py:688
  108.6 12.1 %apply_twice.5 = (f32[1728,128]{1,0:T(8,128)}, f32[8,128]{1,0:T(8,128)}) custom-call(s32[1]{0:T(128)} %bitcast.place, f32[1152,128]{1,0:T(8,128)} %bitcast.25, f32[1152,128]{1,0:T(8,128)} %copy-done.11, f32[1152,128]{1,0:T(8,128)} %copy-done.10, f32[288,128]{1,0:T(8,128)} %broadcast_in_dim.90.scale, bf16[624,576]{1,0:T(8,128)(2,1)} %pad_maximum_fusion.to_even, ...), custom_call_target="tpu_custom_call" | custom-call | flops 2000000000 | bytes 6000000 | tf_op jit(solution)/shard_map/apply_twice/pallas_call | solution.py:512
  120.7 5.7 %all-to-all-start.2 = ((f32[8,216,128]{2,1,0:T(8,128)}), f32[8,216,128]{2,1,0:T(8,128)S(1)}, u32[]{:S(2)}, u32[]{:S(2)}) async-start(f32[8,216,128]{2,1,0:T(8,128)} %bitcast.15), calls=%async_computation.2 | async-start | bytes 1769472 | tf_op jit(solution)/shard_map/all_to_all | solution.py:685
  126.4 8.0 %collective-permute-start.8 = (f32[8,128]{1,0:T(8,128)S(1)}, f32[8,128]{1,0:T(8,128)S(1)}, u32[]{:S(2)}, u32[]{:S(2)}) collective-permute-start(f32[8,128]{1,0:T(8,128)S(1)} %copy-done.7), channel_id=1, source_target_pairs={{0,1},{1,0},{2,3},{3,2},{4,5},{5,4},{6,7},{7,6},{8,9},{9,8},{10,11... | collective-permute-start | bytes 12296 | tf_op jit(solution)/shard_map/ppermute | solution.py:670
  135.3 2.9 %collective-permute-start.9 = (f32[8,128]{1,0:T(8,128)S(1)}, f32[8,128]{1,0:T(8,128)S(1)}, u32[]{:S(2)}, u32[]{:S(2)}) collective-permute-start(f32[8,128]{1,0:T(8,128)S(1)} %add.37), channel_id=1, source_target_pairs={{0,2},{1,3},{2,0},{3,1},{4,6},{5,7},{6,4},{7,5},{8,10},{9,11},{10,... | collective-permute-start | bytes 12296 | tf_op jit(solution)/shard_map/ppermute | solution.py:670
  139.8 2.0 %collective-permute-start.10 = (f32[8,128]{1,0:T(8,128)S(1)}, f32[8,128]{1,0:T(8,128)S(1)}, u32[]{:S(2)}, u32[]{:S(2)}) collective-permute-start(f32[8,128]{1,0:T(8,128)S(1)} %add.38), channel_id=1, source_target_pairs={{0,4},{4,0},{8,12},{12,8},{16,20},{20,16},{24,28},{28,24},{1,5},{5... | collective-permute-start | bytes 12296 | tf_op jit(solution)/shard_map/ppermute | solution.py:670
  143.4 3.8 %collective-permute-start.13 = (f32[8,128]{1,0:T(8,128)S(1)}, f32[8,128]{1,0:T(8,128)S(1)}, u32[]{:S(2)}, u32[]{:S(2)}) collective-permute-start(f32[8,128]{1,0:T(8,128)S(1)} %add.39), channel_id=1, source_target_pairs={{0,24},{4,28},{8,16},{12,20},{16,8},{20,12},{24,0},{28,4},{1,25},{... | collective-permute-start | bytes 12296 | tf_op jit(solution)/shard_map/ppermute | solution.py:672
  148.8 2.9 %collective-permute-done.12 = f32[8,128]{1,0:T(8,128)S(1)} collective-permute-done((f32[8,128]{1,0:T(8,128)S(1)}, f32[8,128]{1,0:T(8,128)S(1)}, u32[]{:S(2)}, u32[]{:S(2)}) %collective-permute-start.12) | collective-permute-done | bytes 4128 | tf_op jit(solution)/shard_map/ppermute | solution.py:672
  152.3 3.6 %unpack.2.refs_0_ = f32[2,36,3,8,128]{4,3,2,1,0:T(8,128)} custom-call(f32[1728,128]{1,0:T(8,128)} %bitcast.13), custom_call_target="tpu_custom_call" | custom-call | flops 3000000000 | bytes 9000000 | tf_op jit(solution)/shard_map/unpack/pallas_call | solution.py:564
  155.9 3.6 %unpack.3.refs_1_ = f32[2,36,3,8,128]{4,3,2,1,0:T(8,128)} custom-call(f32[1728,128]{1,0:T(8,128)} %bitcast.14), custom_call_target="tpu_custom_call" | custom-call | flops 3000000000 | bytes 9000000 | tf_op jit(solution)/shard_map/unpack/pallas_call | solution.py:564
  160.4 4.4 %finish.1 = (f32[36,3,3,8,128]{4,3,2,1,0:T(8,128)}, f32[36,3,3,8,128]{4,3,2,1,0:T(8,128)}) custom-call(f32[36,3,3,8,128]{4,3,2,1,0:T(8,128)} %field.5, f32[8,128]{1,0:T(8,128)} %add_add_fusion.total, f32[1728,128]{1,0:T(8,128)} %bitcast.16, f32[2,36,3,8,128]{4,3,2,1,0:T(8,128)} %unpack.2.refs_0_, f32[2,36,3,8,128]{4,3,2,1,0:T(8,128)} %unpack.3.refs_1_), custom_call_target="tpu_custom_call" | custom-call | flops 6000000000 | bytes 18000000 | tf_op jit(solution)/shard_map/finish/pallas_call | solution.py:615
  (80 shorter events, 35.8 us)
Async XLA Ops:
  3.9 17.0 %copy-start.6 = (s32[660,4]{0,1:T(4,128)S(1)}, s32[660,4]{0,1:T(4,128)}, u32[]{:S(2)}) copy-start(s32[660,4]{0,1:T(4,128)} %param.11) | copy-start | bytes 31684
  3.9 23.3 %all-to-all-start.1 = ((f32[8,144,128]{2,1,0:T(8,128)}), f32[8,144,128]{2,1,0:T(8,128)S(1)}, u32[]{:S(2)}, u32[]{:S(2)}) async-start(f32[8,144,128]{2,1,0:T(8,128)} %bitcast.12), calls=%async_computation.1 | async-start | bytes 1179648 | tf_op jit(solution)/shard_map/all_to_all | solution.py:685
  16.5 5.3 %collective-permute-start.3 = (f32[2,3,8,128]{3,2,1,0:T(8,128)}, f32[2,3,8,128]{3,2,1,0:T(8,128)S(1)}, u32[]{:S(2)}, u32[]{:S(2)}) collective-permute-start(f32[2,3,8,128]{3,2,1,0:T(8,128)} %get-tuple-element.11.both), channel_id=1, source_target_pairs={{1,0},{2,1},{3,2},{5,4},{6,5},{7,6},{9,8},{10,9},{11,10},{13,12},{... | collective-permute-start | bytes 73736 | tf_op jit(solution)/shard_map/ppermute | solution.py:696
  17.8 4.1 %collective-permute-start.2 = (f32[2,3,8,128]{3,2,1,0:T(8,128)}, f32[2,3,8,128]{3,2,1,0:T(8,128)S(1)}, u32[]{:S(2)}, u32[]{:S(2)}) collective-permute-start(f32[2,3,8,128]{3,2,1,0:T(8,128)} %get-tuple-element.11.both), channel_id=1, source_target_pairs={{0,1},{1,2},{2,3},{4,5},{5,6},{6,7},{8,9},{9,10},{10,11},{12,13},{... | collective-permute-start | bytes 73736 | tf_op jit(solution)/shard_map/ppermute | solution.py:695
  27.1 8.0 %copy-start.5 = (f32[8,144,128]{2,1,0:T(8,128)}, f32[8,144,128]{2,1,0:T(8,128)S(1)}, u32[]{:S(2)}) copy-start(f32[8,144,128]{2,1,0:T(8,128)S(1)} %all-to-all-done.1) | copy-start | bytes 1769476
  27.2 33.0 %all-to-all-start = ((f32[8,288,128]{2,1,0:T(8,128)}), f32[8,288,128]{2,1,0:T(8,128)S(1)}, u32[]{:S(2)}, u32[]{:S(2)}) async-start(f32[8,288,128]{2,1,0:T(8,128)} %bitcast.1), calls=%async_computation | async-start | bytes 2359296 | tf_op jit(solution)/shard_map/all_to_all | solution.py:685
  30.8 15.2 %collective-permute-start.1 = (f32[1152,128]{1,0:T(8,128)S(1)}, f32[1152,128]{1,0:T(8,128)S(1)}, u32[]{:S(2)}, u32[]{:S(2)}) collective-permute-start(f32[1152,128]{1,0:T(8,128)S(1)} %bitcast.19), channel_id=1, source_target_pairs={{1,0},{2,1},{3,2},{5,4},{6,5},{7,6},{9,8},{10,9},{11,10},{13,12},{... | collective-permute-start | bytes 1769480 | tf_op jit(solution)/shard_map/ppermute | solution.py:688
  32.1 13.9 %collective-permute-start = (f32[1152,128]{1,0:T(8,128)S(1)}, f32[1152,128]{1,0:T(8,128)S(1)}, u32[]{:S(2)}, u32[]{:S(2)}) collective-permute-start(f32[1152,128]{1,0:T(8,128)S(1)} %bitcast.20), channel_id=1, source_target_pairs={{0,1},{1,2},{2,3},{4,5},{5,6},{6,7},{8,9},{9,10},{10,11},{12,13},{... | collective-permute-start | bytes 1769480 | tf_op jit(solution)/shard_map/ppermute | solution.py:688
  60.1 27.8 %all-to-all-start.3 = ((f32[8,216,128]{2,1,0:T(8,128)}), f32[8,216,128]{2,1,0:T(8,128)S(1)}, u32[]{:S(2)}, u32[]{:S(2)}) async-start(f32[8,216,128]{2,1,0:T(8,128)} %bitcast.18), calls=%async_computation.3 | async-start | bytes 1769472 | tf_op jit(solution)/shard_map/all_to_all | solution.py:685
  67.1 6.1 %collective-permute-start.7 = (f32[1152,128]{1,0:T(8,128)}, f32[1152,128]{1,0:T(8,128)S(1)}, u32[]{:S(2)}, u32[]{:S(2)}) collective-permute-start(f32[1152,128]{1,0:T(8,128)} %bitcast.26), channel_id=1, source_target_pairs={{1,0},{2,1},{3,2},{5,4},{6,5},{7,6},{9,8},{10,9},{11,10},{13,12},{... | collective-permute-start | bytes 1769480 | tf_op jit(solution)/shard_map/ppermute | solution.py:688
  68.6 6.4 %collective-permute-start.6 = (f32[1152,128]{1,0:T(8,128)}, f32[1152,128]{1,0:T(8,128)S(1)}, u32[]{:S(2)}, u32[]{:S(2)}) collective-permute-start(f32[1152,128]{1,0:T(8,128)} %bitcast.27), channel_id=1, source_target_pairs={{0,1},{1,2},{2,3},{4,5},{5,6},{6,7},{8,9},{9,10},{10,11},{12,13},{... | collective-permute-start | bytes 1769480 | tf_op jit(solution)/shard_map/ppermute | solution.py:688
  87.9 7.6 %copy-start.2 = (f32[8,216,128]{2,1,0:T(8,128)}, f32[8,216,128]{2,1,0:T(8,128)S(1)}, u32[]{:S(2)}) copy-start(f32[8,216,128]{2,1,0:T(8,128)S(1)} %all-to-all-done.3) | copy-start | bytes 2654212
  87.9 32.7 %all-to-all-start.4 = ((f32[8,216,128]{2,1,0:T(8,128)}), f32[8,216,128]{2,1,0:T(8,128)S(1)}, u32[]{:S(2)}, u32[]{:S(2)}) async-start(f32[8,216,128]{2,1,0:T(8,128)} %bitcast.17), calls=%async_computation.4 | async-start | bytes 1769472 | tf_op jit(solution)/shard_map/all_to_all | solution.py:685
  95.6 10.4 %collective-permute-start.5 = (f32[1152,128]{1,0:T(8,128)}, f32[1152,128]{1,0:T(8,128)S(1)}, u32[]{:S(2)}, u32[]{:S(2)}) collective-permute-start(f32[1152,128]{1,0:T(8,128)} %bitcast.23), channel_id=1, source_target_pairs={{1,0},{2,1},{3,2},{5,4},{6,5},{7,6},{9,8},{10,9},{11,10},{13,12},{... | collective-permute-start | bytes 1769480 | tf_op jit(solution)/shard_map/ppermute | solution.py:688
  96.9 10.9 %collective-permute-start.4 = (f32[1152,128]{1,0:T(8,128)}, f32[1152,128]{1,0:T(8,128)S(1)}, u32[]{:S(2)}, u32[]{:S(2)}) collective-permute-start(f32[1152,128]{1,0:T(8,128)} %bitcast.24), channel_id=1, source_target_pairs={{0,1},{1,2},{2,3},{4,5},{5,6},{6,7},{8,9},{9,10},{10,11},{12,13},{... | collective-permute-start | bytes 1769480 | tf_op jit(solution)/shard_map/ppermute | solution.py:688
  120.7 5.8 %copy-start.7 = (f32[8,128]{1,0:T(8,128)S(1)}, f32[8,128]{1,0:T(8,128)}, u32[]{:S(2)}) copy-start(f32[8,128]{1,0:T(8,128)} %get-tuple-element.14) | copy-start | bytes 12292
  120.7 35.2 %copy-start.3 = (f32[8,216,128]{2,1,0:T(8,128)}, f32[8,216,128]{2,1,0:T(8,128)S(1)}, u32[]{:S(2)}) copy-start(f32[8,216,128]{2,1,0:T(8,128)S(1)} %all-to-all-done.4) | copy-start | bytes 2654212
  120.7 38.8 %all-to-all-start.2 = ((f32[8,216,128]{2,1,0:T(8,128)}), f32[8,216,128]{2,1,0:T(8,128)S(1)}, u32[]{:S(2)}, u32[]{:S(2)}) async-start(f32[8,216,128]{2,1,0:T(8,128)} %bitcast.15), calls=%async_computation.2 | async-start | bytes 1769472 | tf_op jit(solution)/shard_map/all_to_all | solution.py:685
  126.4 8.9 %collective-permute-start.8 = (f32[8,128]{1,0:T(8,128)S(1)}, f32[8,128]{1,0:T(8,128)S(1)}, u32[]{:S(2)}, u32[]{:S(2)}) collective-permute-start(f32[8,128]{1,0:T(8,128)S(1)} %copy-done.7), channel_id=1, source_target_pairs={{0,1},{1,0},{2,3},{3,2},{4,5},{5,4},{6,7},{7,6},{8,9},{9,8},{10,11... | collective-permute-start | bytes 12296 | tf_op jit(solution)/shard_map/ppermute | solution.py:670
  135.3 4.5 %collective-permute-start.9 = (f32[8,128]{1,0:T(8,128)S(1)}, f32[8,128]{1,0:T(8,128)S(1)}, u32[]{:S(2)}, u32[]{:S(2)}) collective-permute-start(f32[8,128]{1,0:T(8,128)S(1)} %add.37), channel_id=1, source_target_pairs={{0,2},{1,3},{2,0},{3,1},{4,6},{5,7},{6,4},{7,5},{8,10},{9,11},{10,... | collective-permute-start | bytes 12296 | tf_op jit(solution)/shard_map/ppermute | solution.py:670
  139.8 3.6 %collective-permute-start.10 = (f32[8,128]{1,0:T(8,128)S(1)}, f32[8,128]{1,0:T(8,128)S(1)}, u32[]{:S(2)}, u32[]{:S(2)}) collective-permute-start(f32[8,128]{1,0:T(8,128)S(1)} %add.38), channel_id=1, source_target_pairs={{0,4},{4,0},{8,12},{12,8},{16,20},{20,16},{24,28},{28,24},{1,5},{5... | collective-permute-start | bytes 12296 | tf_op jit(solution)/shard_map/ppermute | solution.py:670
  143.4 5.4 %collective-permute-start.13 = (f32[8,128]{1,0:T(8,128)S(1)}, f32[8,128]{1,0:T(8,128)S(1)}, u32[]{:S(2)}, u32[]{:S(2)}) collective-permute-start(f32[8,128]{1,0:T(8,128)S(1)} %add.39), channel_id=1, source_target_pairs={{0,24},{4,28},{8,16},{12,20},{16,8},{20,12},{24,0},{28,4},{1,25},{... | collective-permute-start | bytes 12296 | tf_op jit(solution)/shard_map/ppermute | solution.py:672
  147.2 4.5 %collective-permute-start.12 = (f32[8,128]{1,0:T(8,128)S(1)}, f32[8,128]{1,0:T(8,128)S(1)}, u32[]{:S(2)}, u32[]{:S(2)}) collective-permute-start(f32[8,128]{1,0:T(8,128)S(1)} %add.39), channel_id=1, source_target_pairs={{0,16},{4,20},{8,24},{12,28},{16,0},{20,4},{24,8},{28,12},{1,17},{... | collective-permute-start | bytes 12296 | tf_op jit(solution)/shard_map/ppermute | solution.py:672
  147.2 4.5 %collective-permute-start.11 = (f32[8,128]{1,0:T(8,128)S(1)}, f32[8,128]{1,0:T(8,128)S(1)}, u32[]{:S(2)}, u32[]{:S(2)}) collective-permute-start(f32[8,128]{1,0:T(8,128)S(1)} %add.39), channel_id=1, source_target_pairs={{0,8},{4,12},{8,0},{12,4},{16,24},{20,28},{24,16},{28,20},{1,9},{5... | collective-permute-start | bytes 12296 | tf_op jit(solution)/shard_map/ppermute | solution.py:672
  (11 other events, 19.0 us)

commit v10 on v9

--- a/solution.py
+++ b/solution.py
@@ -503,7 +503,7 @@
     partial[...] = total + refs[0][...] if comp > 0 else total
 
 
-def apply_twice(comp, place, own, before, after, tables, fields, fibre, *so_far):
+def apply_twice(comp, place, own, before, after, tables, fields, fibre, so_far=(), ready=()):
     scale, to_even, to_all = tables
     slots = scale.shape[0]
     vmem = pl.BlockSpec(memory_space=pltpu.VMEM)
@@ -515,7 +515,7 @@
             jax.ShapeDtypeStruct((slots * 2 * SLAB, LANES), jnp.float32),
             jax.ShapeDtypeStruct((8, LANES), jnp.float32),
         ],
-        in_specs=[smem] + [vmem] * 7 + [smem] + [vmem] * len(so_far),
+        in_specs=[smem] + [vmem] * 7 + [smem] + [vmem] * len(so_far) + [pl.BlockSpec(memory_space=pl.ANY)] * len(ready),
         out_specs=[vmem, vmem],
         scratch_shapes=[
             f32(slots, TILES * LANES),
@@ -530,7 +530,7 @@
         compiler_params=pltpu.CompilerParams(vmem_limit_bytes=VMEM),
         cost_estimate=estimate(2),
         name="apply_twice",
-    )(place, own, before, after, scale, to_even, to_all, fields, fibre, *so_far)
+    )(place, own, before, after, scale, to_even, to_all, fields, fibre, *so_far, *ready)
 
 
 def combination(total):
@@ -697,12 +697,16 @@
     fields = stiffness_fields(place, both_before, both, both_after, ply_stiffness)
     image, partial = apply_twice(0, place, *first, tables, fields, fibre_weights)
     images = [swap(image)]
-    parts = [halo(part_component(others, n, partial)) for n in range(COMPS - 1)]
-    for comp in range(1, COMPS):
-        image, partial = apply_twice(comp, place, *parts[comp - 1], tables, fields, fibre_weights, partial)
-        images.append(swap(image))
-    natural = [unpack(image, right_side.shape[0]) for image in images[:-1]]
-    return tuple(finish(right_side, all_sum(partial), images[-1], *natural))
+    parts = [part_component(others, n, partial) for n in range(COMPS - 1)]
+    halos = [halo(rows) for rows in parts]
+    modes = right_side.shape[0]
+    image, partial = apply_twice(1, place, *halos[0], tables, fields, fibre_weights, (partial,), parts[1:])
+    images.append(swap(image))
+    natural = [unpack(images[0], modes)]
+    image, partial = apply_twice(2, place, *halos[1], tables, fields, fibre_weights, (partial,), natural)
+    images.append(swap(image))
+    natural.append(unpack(images[1], modes))
+    return tuple(finish(right_side, all_sum(partial), images[2], *natural))
 
 
 def on_device(right_side, mean_stiffness, ply_stiffness, fibre_weights, ply_map, coupling_table):

time: 166 us -> 161 us (0.970)
  waiting for transfers between devices: 15.6 us -> 12.6 us
  starting transfers between devices: 69.9 us -> 67.5 us
    ppermute x3, waiting for transfers between devices: 3.53 us -> 0.01 us  [halo(): lax.ppermute(rows, 'space', up)]
    ppermute x3, starting transfers between devices: 12.9 us -> 10.4 us  [all_sum(): lax.ppermute(value, axis, [(i, i ^ bit) for i in range(devices)])]
    unnamed x33 -> x35, local copies, waits for them, and re-layouts: 4.26 us -> 4.65 us
  transfers between devices with their start and end apart: 19 -> 19, of which waited for: 10 -> 8; matrix products, arithmetic and copies ran while one was open for 7% -> 7% of each run, Pallas kernels for 34% -> 35%
where the time goes in v10:
time: 161 us; the launch traced here: 160 us
  starting transfers between devices  67.5 us (42%)
  Pallas kernels  63.6 us (40%)
  waiting for transfers between devices  12.6 us (8%)
  local copies, waits for them, and re-layouts  7.47 us (5%)
  other arithmetic  5.92 us (4%)
  matrix products  1.8 us (1%)
    pallas_call x3, Pallas kernels, apply_twice(): pl.pallas_call(functools.partial(apply_kernel, comp=comp), out_shape=[jax...  36.2 us
    all_to_all x5, starting transfers between devices, swap(): return lax.all_to_all(rows, 'mode', 0, 0, tiled=True)  27.6 us
    ppermute x3, starting transfers between devices, halo(): lax.ppermute(rows, 'space', up)  16.7 us
    ppermute x3, starting transfers between devices, all_sum(): lax.ppermute(value, axis, [(i, i ^ bit) for i in range(devices)])  10.4 us
    pallas_call x2, Pallas kernels, pack(): pl.pallas_call(functools.partial(pack_kernel, comps=comps), grid=(1,), ou...  8.51 us
    pallas_call x2, Pallas kernels, unpack(): pl.pallas_call(unpack_kernel, out_shape=jax.ShapeDtypeStruct((2, modes, S...  7.22 us
    unnamed x35, local copies, waits for them, and re-layouts  4.65 us
    pallas_call x1, Pallas kernels, finish(): pl.pallas_call(finish_kernel, grid=(STEPS,), out_shape=[jax.ShapeDtypeStr...  4.43 us
  transfers between devices with their start and end apart: 19, of which 8 were waited for; matrix products, arithmetic and copies ran while one was open for 7% of the time, Pallas kernels for 35%

profile of v10, /device:TPU:0, one launch (start us, length us, event | category | flops | bytes accessed | tf_op | source)
XLA Modules:
  0.0 159.7 jit_solution(9375111086532532977)
XLA Ops:
  0.6 3.2 %pack.2.refs_2_ = f32[1152,128]{1,0:T(8,128)} custom-call(f32[36,3,3,8,128]{4,3,2,1,0:T(8,128)} %field.5), custom_call_target="tpu_custom_call" | custom-call | flops 500000000 | bytes 1500000 | tf_op jit(solution)/shard_map/pack/pallas_call | solution.py:206
  3.9 7.4 %all-to-all-start.1 = ((f32[8,144,128]{2,1,0:T(8,128)}), f32[8,144,128]{2,1,0:T(8,128)S(1)}, u32[]{:S(2)}, u32[]{:S(2)}) async-start(f32[8,144,128]{2,1,0:T(8,128)} %bitcast.12), calls=%async_computation.1 | async-start | bytes 1179648 | tf_op jit(solution)/shard_map/all_to_all | solution.py:685
  11.3 5.3 %pack.3 = (f32[2,3,8,128]{3,2,1,0:T(8,128)}, f32[2304,128]{1,0:T(8,128)}) custom-call(f32[36,3,3,8,128]{4,3,2,1,0:T(8,128)} %field.5, f32[3,8,128]{2,1,0:T(8,128)} %refs_0_.1, s32[3,8,128]{2,1,0:T(8,128)} %refs_1_.1, f32[1152,128]{1,0:T(8,128)} %pack.2.refs_2_), custom_call_target="tpu_custom_call" | custom-call | flops 500000000 | bytes 1500000 | tf_op jit(solution)/shard_map/pack/pallas_call | solution.py:206
  17.8 3.0 %collective-permute-start.2 = (f32[2,3,8,128]{3,2,1,0:T(8,128)}, f32[2,3,8,128]{3,2,1,0:T(8,128)S(1)}, u32[]{:S(2)}, u32[]{:S(2)}) collective-permute-start(f32[2,3,8,128]{3,2,1,0:T(8,128)} %get-tuple-element.11.both), channel_id=1, source_target_pairs={{0,1},{1,2},{2,3},{4,5},{5,6},{6,7},{8,9},{9,10},{10,11},{12,13},{... | collective-permute-start | bytes 73736 | tf_op jit(solution)/shard_map/ppermute | solution.py:695
  24.1 3.0 %all-to-all-done.1 = f32[8,144,128]{2,1,0:T(8,128)S(1)} async-done(((f32[8,144,128]{2,1,0:T(8,128)}), f32[8,144,128]{2,1,0:T(8,128)S(1)}, u32[]{:S(2)}, u32[]{:S(2)}) %all-to-all-start.1) | async-done | bytes 589856 | tf_op jit(solution)/shard_map/all_to_all | solution.py:685
  27.2 3.6 %all-to-all-start = ((f32[8,288,128]{2,1,0:T(8,128)}), f32[8,288,128]{2,1,0:T(8,128)S(1)}, u32[]{:S(2)}, u32[]{:S(2)}) async-start(f32[8,288,128]{2,1,0:T(8,128)} %bitcast.1), calls=%async_computation | async-start | bytes 2359296 | tf_op jit(solution)/shard_map/all_to_all | solution.py:685
  32.1 3.1 %collective-permute-start = (f32[1152,128]{1,0:T(8,128)S(1)}, f32[1152,128]{1,0:T(8,128)S(1)}, u32[]{:S(2)}, u32[]{:S(2)}) collective-permute-start(f32[1152,128]{1,0:T(8,128)S(1)} %bitcast.20), channel_id=1, source_target_pairs={{0,1},{1,2},{2,3},{4,5},{5,6},{6,7},{8,9},{9,10},{10,11},{12,13},{... | collective-permute-start | bytes 1769480 | tf_op jit(solution)/shard_map/ppermute | solution.py:688
  47.0 12.1 %apply_twice.3 = (f32[1728,128]{1,0:T(8,128)}, f32[8,128]{1,0:T(8,128)}) custom-call(s32[1]{0:T(128)} %bitcast.place, f32[1152,128]{1,0:T(8,128)} %bitcast.22, f32[1152,128]{1,0:T(8,128)} %copy-done.9, f32[1152,128]{1,0:T(8,128)} %copy-done.8, f32[288,128]{1,0:T(8,128)} %broadcast_in_dim.90.scale, bf16[624,576]{1,0:T(8,128)(2,1)} %pad_maximum_fusion.to_even, ...), custom_call_target="tpu_custom_call" | custom-call | flops 2000000000 | bytes 6000000 | tf_op jit(solution)/shard_map/apply_twice/pallas_call | solution.py:512
  60.1 5.0 %all-to-all-start.2 = ((f32[8,216,128]{2,1,0:T(8,128)}), f32[8,216,128]{2,1,0:T(8,128)S(1)}, u32[]{:S(2)}, u32[]{:S(2)}) async-start(f32[8,216,128]{2,1,0:T(8,128)} %bitcast.18), calls=%async_computation.2 | async-start | bytes 1769472 | tf_op jit(solution)/shard_map/all_to_all | solution.py:685
  68.6 4.7 %collective-permute-start.6 = (f32[1152,128]{1,0:T(8,128)}, f32[1152,128]{1,0:T(8,128)S(1)}, u32[]{:S(2)}, u32[]{:S(2)}) collective-permute-start(f32[1152,128]{1,0:T(8,128)} %bitcast.28), channel_id=1, source_target_pairs={{0,1},{1,2},{2,3},{4,5},{5,6},{6,7},{8,9},{9,10},{10,11},{12,13},{... | collective-permute-start | bytes 1769480 | tf_op jit(solution)/shard_map/ppermute | solution.py:688
  73.2 1.9 %part_component.2 = f32[8,144,128]{2,1,0:T(8,128)} custom-call(f32[8,288,128]{2,1,0:T(8,128)} %copy-done.1, f32[8,128]{1,0:T(8,128)} %get-tuple-element.12.ready.refs_0_), custom_call_target="tpu_custom_call" | custom-call | flops 500000000 | bytes 1500000 | tf_op jit(solution)/shard_map/part_component/pallas_call | solution.py:228
  76.2 12.1 %apply_twice.4 = (f32[1728,128]{1,0:T(8,128)}, f32[8,128]{1,0:T(8,128)}) custom-call(s32[1]{0:T(128)} %bitcast.place, f32[1152,128]{1,0:T(8,128)} %bitcast.29, f32[1152,128]{1,0:T(8,128)} %copy-done.14, f32[1152,128]{1,0:T(8,128)} %copy-done.13, f32[288,128]{1,0:T(8,128)} %broadcast_in_dim.90.scale, bf16[624,576]{1,0:T(8,128)(2,1)} %pad_maximum_fusion.to_even, ...), custom_call_target="tpu_custom_call" | custom-call | flops 2000000000 | bytes 6000000 | tf_op jit(solution)/shard_map/apply_twice/pallas_call | solution.py:512
  88.3 5.8 %all-to-all-start.4 = ((f32[8,216,128]{2,1,0:T(8,128)}), f32[8,216,128]{2,1,0:T(8,128)S(1)}, u32[]{:S(2)}, u32[]{:S(2)}) async-start(f32[8,216,128]{2,1,0:T(8,128)} %bitcast.17), calls=%async_computation.4 | async-start | bytes 1769472 | tf_op jit(solution)/shard_map/all_to_all | solution.py:685
  95.4 9.0 %collective-permute-start.4 = (f32[1152,128]{1,0:T(8,128)S(1)}, f32[1152,128]{1,0:T(8,128)S(1)}, u32[]{:S(2)}, u32[]{:S(2)}) collective-permute-start(f32[1152,128]{1,0:T(8,128)S(1)} %bitcast.26), channel_id=1, source_target_pairs={{0,1},{1,2},{2,3},{4,5},{5,6},{6,7},{8,9},{9,10},{10,11},{12,13},{... | collective-permute-start | bytes 1769480 | tf_op jit(solution)/shard_map/ppermute | solution.py:688
  104.5 3.6 %unpack.2.refs_1_.refs_0_ = f32[2,36,3,8,128]{4,3,2,1,0:T(8,128)} custom-call(f32[1728,128]{1,0:T(8,128)} %bitcast.16), custom_call_target="tpu_custom_call" | custom-call | flops 3000000000 | bytes 9000000 | tf_op jit(solution)/shard_map/unpack/pallas_call | solution.py:564
  109.1 12.1 %apply_twice.5 = (f32[1728,128]{1,0:T(8,128)}, f32[8,128]{1,0:T(8,128)}) custom-call(s32[1]{0:T(128)} %bitcast.place, f32[1152,128]{1,0:T(8,128)} %bitcast.24, f32[1152,128]{1,0:T(8,128)} %copy-done.12, f32[1152,128]{1,0:T(8,128)} %copy-done.11, f32[288,128]{1,0:T(8,128)} %broadcast_in_dim.90.scale, bf16[624,576]{1,0:T(8,128)(2,1)} %pad_maximum_fusion.to_even, ...), custom_call_target="tpu_custom_call" | custom-call | flops 2000000000 | bytes 6000000 | tf_op jit(solution)/shard_map/apply_twice/pallas_call | solution.py:512
  121.2 5.7 %all-to-all-start.3 = ((f32[8,216,128]{2,1,0:T(8,128)}), f32[8,216,128]{2,1,0:T(8,128)S(1)}, u32[]{:S(2)}, u32[]{:S(2)}) async-start(f32[8,216,128]{2,1,0:T(8,128)} %bitcast.14), calls=%async_computation.3 | async-start | bytes 1769472 | tf_op jit(solution)/shard_map/all_to_all | solution.py:685
  126.9 5.4 %collective-permute-start.8 = (f32[8,128]{1,0:T(8,128)S(1)}, f32[8,128]{1,0:T(8,128)S(1)}, u32[]{:S(2)}, u32[]{:S(2)}) collective-permute-start(f32[8,128]{1,0:T(8,128)S(1)} %copy-done.7), channel_id=1, source_target_pairs={{0,1},{1,0},{2,3},{3,2},{4,5},{5,4},{6,7},{7,6},{8,9},{9,8},{10,11... | collective-permute-start | bytes 12296 | tf_op jit(solution)/shard_map/ppermute | solution.py:670
  133.2 3.0 %collective-permute-start.9 = (f32[8,128]{1,0:T(8,128)S(1)}, f32[8,128]{1,0:T(8,128)S(1)}, u32[]{:S(2)}, u32[]{:S(2)}) collective-permute-start(f32[8,128]{1,0:T(8,128)S(1)} %add.37), channel_id=1, source_target_pairs={{0,2},{1,3},{2,0},{3,1},{4,6},{5,7},{6,4},{7,5},{8,10},{9,11},{10,... | collective-permute-start | bytes 12296 | tf_op jit(solution)/shard_map/ppermute | solution.py:670
  137.7 2.0 %collective-permute-start.10 = (f32[8,128]{1,0:T(8,128)S(1)}, f32[8,128]{1,0:T(8,128)S(1)}, u32[]{:S(2)}, u32[]{:S(2)}) collective-permute-start(f32[8,128]{1,0:T(8,128)S(1)} %add.38), channel_id=1, source_target_pairs={{0,4},{4,0},{8,12},{12,8},{16,20},{20,16},{24,28},{28,24},{1,5},{5... | collective-permute-start | bytes 12296 | tf_op jit(solution)/shard_map/ppermute | solution.py:670
  141.6 3.9 %collective-permute-start.13 = (f32[8,128]{1,0:T(8,128)S(1)}, f32[8,128]{1,0:T(8,128)S(1)}, u32[]{:S(2)}, u32[]{:S(2)}) collective-permute-start(f32[8,128]{1,0:T(8,128)S(1)} %add.39), channel_id=1, source_target_pairs={{0,24},{4,28},{8,16},{12,20},{16,8},{20,12},{24,0},{28,4},{1,25},{... | collective-permute-start | bytes 12296 | tf_op jit(solution)/shard_map/ppermute | solution.py:672
  147.2 2.9 %collective-permute-done.12 = f32[8,128]{1,0:T(8,128)S(1)} collective-permute-done((f32[8,128]{1,0:T(8,128)S(1)}, f32[8,128]{1,0:T(8,128)S(1)}, u32[]{:S(2)}, u32[]{:S(2)}) %collective-permute-start.12) | collective-permute-done | bytes 4128 | tf_op jit(solution)/shard_map/ppermute | solution.py:672
  150.7 3.6 %unpack.3.refs_1_ = f32[2,36,3,8,128]{4,3,2,1,0:T(8,128)} custom-call(f32[1728,128]{1,0:T(8,128)} %bitcast.13), custom_call_target="tpu_custom_call" | custom-call | flops 3000000000 | bytes 9000000 | tf_op jit(solution)/shard_map/unpack/pallas_call | solution.py:564
  155.3 4.4 %finish.1 = (f32[36,3,3,8,128]{4,3,2,1,0:T(8,128)}, f32[36,3,3,8,128]{4,3,2,1,0:T(8,128)}) custom-call(f32[36,3,3,8,128]{4,3,2,1,0:T(8,128)} %field.5, f32[8,128]{1,0:T(8,128)} %add_add_fusion.total, f32[1728,128]{1,0:T(8,128)} %bitcast.15, f32[2,36,3,8,128]{4,3,2,1,0:T(8,128)} %unpack.2.refs_1_.refs_0_, f32[2,36,3,8,128]{4,3,2,1,0:T(8,128)} %unpack.3.refs_1_), custom_call_target="tpu_custom_call" | custom-call | flops 6000000000 | bytes 18000000 | tf_op jit(solution)/shard_map/finish/pallas_call | solution.py:615
  (82 shorter events, 33.0 us)
Async XLA Ops:
  3.9 17.0 %copy-start.6 = (s32[660,4]{0,1:T(4,128)S(1)}, s32[660,4]{0,1:T(4,128)}, u32[]{:S(2)}) copy-start(s32[660,4]{0,1:T(4,128)} %param.11) | copy-start | bytes 31684
  3.9 23.3 %all-to-all-start.1 = ((f32[8,144,128]{2,1,0:T(8,128)}), f32[8,144,128]{2,1,0:T(8,128)S(1)}, u32[]{:S(2)}, u32[]{:S(2)}) async-start(f32[8,144,128]{2,1,0:T(8,128)} %bitcast.12), calls=%async_computation.1 | async-start | bytes 1179648 | tf_op jit(solution)/shard_map/all_to_all | solution.py:685
  16.5 5.3 %collective-permute-start.3 = (f32[2,3,8,128]{3,2,1,0:T(8,128)}, f32[2,3,8,128]{3,2,1,0:T(8,128)S(1)}, u32[]{:S(2)}, u32[]{:S(2)}) collective-permute-start(f32[2,3,8,128]{3,2,1,0:T(8,128)} %get-tuple-element.11.both), channel_id=1, source_target_pairs={{1,0},{2,1},{3,2},{5,4},{6,5},{7,6},{9,8},{10,9},{11,10},{13,12},{... | collective-permute-start | bytes 73736 | tf_op jit(solution)/shard_map/ppermute | solution.py:696
  17.8 4.1 %collective-permute-start.2 = (f32[2,3,8,128]{3,2,1,0:T(8,128)}, f32[2,3,8,128]{3,2,1,0:T(8,128)S(1)}, u32[]{:S(2)}, u32[]{:S(2)}) collective-permute-start(f32[2,3,8,128]{3,2,1,0:T(8,128)} %get-tuple-element.11.both), channel_id=1, source_target_pairs={{0,1},{1,2},{2,3},{4,5},{5,6},{6,7},{8,9},{9,10},{10,11},{12,13},{... | collective-permute-start | bytes 73736 | tf_op jit(solution)/shard_map/ppermute | solution.py:695
  27.1 8.0 %copy-start.5 = (f32[8,144,128]{2,1,0:T(8,128)}, f32[8,144,128]{2,1,0:T(8,128)S(1)}, u32[]{:S(2)}) copy-start(f32[8,144,128]{2,1,0:T(8,128)S(1)} %all-to-all-done.1) | copy-start | bytes 1769476
  27.2 33.0 %all-to-all-start = ((f32[8,288,128]{2,1,0:T(8,128)}), f32[8,288,128]{2,1,0:T(8,128)S(1)}, u32[]{:S(2)}, u32[]{:S(2)}) async-start(f32[8,288,128]{2,1,0:T(8,128)} %bitcast.1), calls=%async_computation | async-start | bytes 2359296 | tf_op jit(solution)/shard_map/all_to_all | solution.py:685
  30.8 15.2 %collective-permute-start.1 = (f32[1152,128]{1,0:T(8,128)S(1)}, f32[1152,128]{1,0:T(8,128)S(1)}, u32[]{:S(2)}, u32[]{:S(2)}) collective-permute-start(f32[1152,128]{1,0:T(8,128)S(1)} %bitcast.19), channel_id=1, source_target_pairs={{1,0},{2,1},{3,2},{5,4},{6,5},{7,6},{9,8},{10,9},{11,10},{13,12},{... | collective-permute-start | bytes 1769480 | tf_op jit(solution)/shard_map/ppermute | solution.py:688
  32.1 13.9 %collective-permute-start = (f32[1152,128]{1,0:T(8,128)S(1)}, f32[1152,128]{1,0:T(8,128)S(1)}, u32[]{:S(2)}, u32[]{:S(2)}) collective-permute-start(f32[1152,128]{1,0:T(8,128)S(1)} %bitcast.20), channel_id=1, source_target_pairs={{0,1},{1,2},{2,3},{4,5},{5,6},{6,7},{8,9},{9,10},{10,11},{12,13},{... | collective-permute-start | bytes 1769480 | tf_op jit(solution)/shard_map/ppermute | solution.py:688
  60.1 28.1 %all-to-all-start.2 = ((f32[8,216,128]{2,1,0:T(8,128)}), f32[8,216,128]{2,1,0:T(8,128)S(1)}, u32[]{:S(2)}, u32[]{:S(2)}) async-start(f32[8,216,128]{2,1,0:T(8,128)} %bitcast.18), calls=%async_computation.2 | async-start | bytes 1769472 | tf_op jit(solution)/shard_map/all_to_all | solution.py:685
  67.1 8.1 %collective-permute-start.7 = (f32[1152,128]{1,0:T(8,128)}, f32[1152,128]{1,0:T(8,128)S(1)}, u32[]{:S(2)}, u32[]{:S(2)}) collective-permute-start(f32[1152,128]{1,0:T(8,128)} %bitcast.27), channel_id=1, source_target_pairs={{1,0},{2,1},{3,2},{5,4},{6,5},{7,6},{9,8},{10,9},{11,10},{13,12},{... | collective-permute-start | bytes 1769480 | tf_op jit(solution)/shard_map/ppermute | solution.py:688
  68.6 6.6 %collective-permute-start.6 = (f32[1152,128]{1,0:T(8,128)}, f32[1152,128]{1,0:T(8,128)S(1)}, u32[]{:S(2)}, u32[]{:S(2)}) collective-permute-start(f32[1152,128]{1,0:T(8,128)} %bitcast.28), channel_id=1, source_target_pairs={{0,1},{1,2},{2,3},{4,5},{5,6},{6,7},{8,9},{9,10},{10,11},{12,13},{... | collective-permute-start | bytes 1769480 | tf_op jit(solution)/shard_map/ppermute | solution.py:688
  88.3 5.9 %copy-start.10 = (f32[8,144,128]{2,1,0:T(8,128)S(1)}, f32[8,144,128]{2,1,0:T(8,128)}, u32[]{:S(2)}) copy-start(f32[8,144,128]{2,1,0:T(8,128)} %part_component.2) | copy-start | bytes 1769476
  88.3 16.2 %copy-start.4 = (f32[8,216,128]{2,1,0:T(8,128)}, f32[8,216,128]{2,1,0:T(8,128)S(1)}, u32[]{:S(2)}) copy-start(f32[8,216,128]{2,1,0:T(8,128)S(1)} %all-to-all-done.2) | copy-start | bytes 2654212
  88.3 32.9 %all-to-all-start.4 = ((f32[8,216,128]{2,1,0:T(8,128)}), f32[8,216,128]{2,1,0:T(8,128)S(1)}, u32[]{:S(2)}, u32[]{:S(2)}) async-start(f32[8,216,128]{2,1,0:T(8,128)} %bitcast.17), calls=%async_computation.4 | async-start | bytes 1769472 | tf_op jit(solution)/shard_map/all_to_all | solution.py:685
  94.1 14.0 %collective-permute-start.5 = (f32[1152,128]{1,0:T(8,128)S(1)}, f32[1152,128]{1,0:T(8,128)S(1)}, u32[]{:S(2)}, u32[]{:S(2)}) collective-permute-start(f32[1152,128]{1,0:T(8,128)S(1)} %bitcast.25), channel_id=1, source_target_pairs={{1,0},{2,1},{3,2},{5,4},{6,5},{7,6},{9,8},{10,9},{11,10},{13,12},{... | collective-permute-start | bytes 1769480 | tf_op jit(solution)/shard_map/ppermute | solution.py:688
  95.4 12.7 %collective-permute-start.4 = (f32[1152,128]{1,0:T(8,128)S(1)}, f32[1152,128]{1,0:T(8,128)S(1)}, u32[]{:S(2)}, u32[]{:S(2)}) collective-permute-start(f32[1152,128]{1,0:T(8,128)S(1)} %bitcast.26), channel_id=1, source_target_pairs={{0,1},{1,2},{2,3},{4,5},{5,6},{6,7},{8,9},{9,10},{10,11},{12,13},{... | collective-permute-start | bytes 1769480 | tf_op jit(solution)/shard_map/ppermute | solution.py:688
  121.2 29.6 %copy-start.2 = (f32[8,216,128]{2,1,0:T(8,128)}, f32[8,216,128]{2,1,0:T(8,128)S(1)}, u32[]{:S(2)}) copy-start(f32[8,216,128]{2,1,0:T(8,128)S(1)} %all-to-all-done.4) | copy-start | bytes 2654212
  121.2 33.1 %all-to-all-start.3 = ((f32[8,216,128]{2,1,0:T(8,128)}), f32[8,216,128]{2,1,0:T(8,128)S(1)}, u32[]{:S(2)}, u32[]{:S(2)}) async-start(f32[8,216,128]{2,1,0:T(8,128)} %bitcast.14), calls=%async_computation.3 | async-start | bytes 1769472 | tf_op jit(solution)/shard_map/all_to_all | solution.py:685
  126.9 6.2 %collective-permute-start.8 = (f32[8,128]{1,0:T(8,128)S(1)}, f32[8,128]{1,0:T(8,128)S(1)}, u32[]{:S(2)}, u32[]{:S(2)}) collective-permute-start(f32[8,128]{1,0:T(8,128)S(1)} %copy-done.7), channel_id=1, source_target_pairs={{0,1},{1,0},{2,3},{3,2},{4,5},{5,4},{6,7},{7,6},{8,9},{9,8},{10,11... | collective-permute-start | bytes 12296 | tf_op jit(solution)/shard_map/ppermute | solution.py:670
  133.2 4.6 %collective-permute-start.9 = (f32[8,128]{1,0:T(8,128)S(1)}, f32[8,128]{1,0:T(8,128)S(1)}, u32[]{:S(2)}, u32[]{:S(2)}) collective-permute-start(f32[8,128]{1,0:T(8,128)S(1)} %add.37), channel_id=1, source_target_pairs={{0,2},{1,3},{2,0},{3,1},{4,6},{5,7},{6,4},{7,5},{8,10},{9,11},{10,... | collective-permute-start | bytes 12296 | tf_op jit(solution)/shard_map/ppermute | solution.py:670
  137.7 3.9 %collective-permute-start.10 = (f32[8,128]{1,0:T(8,128)S(1)}, f32[8,128]{1,0:T(8,128)S(1)}, u32[]{:S(2)}, u32[]{:S(2)}) collective-permute-start(f32[8,128]{1,0:T(8,128)S(1)} %add.38), channel_id=1, source_target_pairs={{0,4},{4,0},{8,12},{12,8},{16,20},{20,16},{24,28},{28,24},{1,5},{5... | collective-permute-start | bytes 12296 | tf_op jit(solution)/shard_map/ppermute | solution.py:670
  141.6 5.6 %collective-permute-start.13 = (f32[8,128]{1,0:T(8,128)S(1)}, f32[8,128]{1,0:T(8,128)S(1)}, u32[]{:S(2)}, u32[]{:S(2)}) collective-permute-start(f32[8,128]{1,0:T(8,128)S(1)} %add.39), channel_id=1, source_target_pairs={{0,24},{4,28},{8,16},{12,20},{16,8},{20,12},{24,0},{28,4},{1,25},{... | collective-permute-start | bytes 12296 | tf_op jit(solution)/shard_map/ppermute | solution.py:672
  145.5 4.7 %collective-permute-start.12 = (f32[8,128]{1,0:T(8,128)S(1)}, f32[8,128]{1,0:T(8,128)S(1)}, u32[]{:S(2)}, u32[]{:S(2)}) collective-permute-start(f32[8,128]{1,0:T(8,128)S(1)} %add.39), channel_id=1, source_target_pairs={{0,16},{4,20},{8,24},{12,28},{16,0},{20,4},{24,8},{28,12},{1,17},{... | collective-permute-start | bytes 12296 | tf_op jit(solution)/shard_map/ppermute | solution.py:672
  145.5 4.7 %collective-permute-start.11 = (f32[8,128]{1,0:T(8,128)S(1)}, f32[8,128]{1,0:T(8,128)S(1)}, u32[]{:S(2)}, u32[]{:S(2)}) collective-permute-start(f32[8,128]{1,0:T(8,128)S(1)} %add.39), channel_id=1, source_target_pairs={{0,8},{4,12},{8,0},{12,4},{16,24},{20,28},{24,16},{28,20},{1,9},{5... | collective-permute-start | bytes 12296 | tf_op jit(solution)/shard_map/ppermute | solution.py:672
  (12 other events, 23.2 us)

commit v11 on v10

--- a/solution.py
+++ b/solution.py
@@ -121,6 +121,8 @@
 PARTS = 8
 WIDE = 16
 ROWS = 4
+UPWARD = (1, 2, 3)
+DOWNWARD = (0, 1, 3)
 EVEN = 1 + VARS * (VARS + 1) // 2
 SPAN = VARS * EVEN
 FULL = 624
@@ -221,20 +223,33 @@
     goal[...] = source[...]
 
 
+def part_kernel(source, ready, own, upward, downward):
+    rows = own.shape[0]
+    slots = rows // ROWS
+    own[...] = source[...].reshape(rows, LANES)
+    for goal, planes in ((upward, UPWARD), (downward, DOWNWARD)):
+        for n, p in enumerate(planes):
+            goal[n * slots : (n + 1) * slots, :] = own[pl.ds(p, slots, stride=ROWS), :]
+
+
 def part_component(rows, n, ready):
     blocks = rows.reshape(PARTS, -1, LANES)
     part = (PARTS, blocks.shape[1] // (COMPS - 1), LANES)
-    whole = pl.BlockSpec(memory_space=pl.ANY)
+    count = part[0] * part[1]
+    vmem = pl.BlockSpec(memory_space=pltpu.VMEM)
     return pl.pallas_call(
-        copy_kernel,
+        part_kernel,
         grid=(1,),
-        out_shape=jax.ShapeDtypeStruct(part, jnp.float32),
-        in_specs=[pl.BlockSpec(part, lambda i: (0, n, 0)), whole],
-        out_specs=pl.BlockSpec(part, lambda i: (0, 0, 0)),
+        out_shape=[
+            jax.ShapeDtypeStruct((size, LANES), jnp.float32)
+            for size in (count, count * len(UPWARD) // ROWS, count * len(DOWNWARD) // ROWS)
+        ],
+        in_specs=[pl.BlockSpec(part, lambda i: (0, n, 0)), pl.BlockSpec(memory_space=pl.ANY)],
+        out_specs=[vmem] * 3,
         compiler_params=pltpu.CompilerParams(vmem_limit_bytes=VMEM),
         cost_estimate=estimate(0.5),
         name="part_component",
-    )(blocks, ready).reshape(-1, LANES)
+    )(blocks, ready)
 
 
 def after_rows(table, ready):
@@ -332,7 +347,7 @@
     return jnp.concatenate([high, low], axis=0)
 
 
-STEP = 32
+STEP = 48
 FACE = 16
 CENTRE = 6 * FACE
 EVEN_BLOCKS = ((0, 32), (32, EVEN))
@@ -360,7 +375,7 @@
                 )
 
 
-CHUNK = 4
+CHUNK = 8
 
 
 def chunks(count):
@@ -472,13 +487,16 @@
     lane = lax.broadcasted_iota(jnp.int32, (slots, LANES), 1)
     slot = lane % WIDE
     load = lambda ref, p: ref[pl.ds(p, slots, stride=ROWS), :]
-    left = pltpu.roll(load(before, 3), LANES - 3, 1)
-    right = pltpu.roll(load(after, 3), 3, 1)
+    whole = before.shape[0] == own.shape[0]
+    below = lambda p: load(before, p) if whole else before[pl.ds(UPWARD.index(p) * slots, slots), :]
+    above = lambda p: load(after, p) if whole else after[pl.ds(DOWNWARD.index(p) * slots, slots), :]
+    left = pltpu.roll(below(3), LANES - 3, 1)
+    right = pltpu.roll(above(3), 3, 1)
     halo = jnp.where((slot == 0) | (slot == 5), left, load(own, 3))
     halo = jnp.where((slot == 4) | (slot == 9), right, halo)
     ordered = [
-        load(own, 0), load(own, 1), load(own, 2), load(before, 2), load(after, 0), halo,
-        load(before, 1), load(after, 1),
+        load(own, 0), load(own, 1), load(own, 2), below(2), above(0), halo,
+        below(1), above(1),
     ]
     for t, tile in enumerate(ordered):
         field[:, tile_cols(t)] = tile * scale[...]
@@ -684,12 +702,13 @@
     def swap(rows):
         return lax.all_to_all(rows, "mode", 0, 0, tiled=True)
 
-    def halo(rows):
-        return rows, lax.ppermute(rows, "space", up), lax.ppermute(rows, "space", down)
+    def halo(rows, upward, downward):
+        return rows, lax.ppermute(upward, "space", up), lax.ppermute(downward, "space", down)
 
     (first,) = pack(right_side, (0,))
     both, others = pack(right_side, (1, 2), (mean_stiffness, ply_map), (first,))
-    first = halo(swap(first))
+    first = swap(first)
+    first = halo(first, first, first)
     others = swap(others)
     tables = mode_tables(after_rows(coupling_table, first[0]), slots)
     both_before = lax.ppermute(both, "space", up)
@@ -698,9 +717,9 @@
     image, partial = apply_twice(0, place, *first, tables, fields, fibre_weights)
     images = [swap(image)]
     parts = [part_component(others, n, partial) for n in range(COMPS - 1)]
-    halos = [halo(rows) for rows in parts]
+    halos = [halo(*part) for part in parts]
     modes = right_side.shape[0]
-    image, partial = apply_twice(1, place, *halos[0], tables, fields, fibre_weights, (partial,), parts[1:])
+    image, partial = apply_twice(1, place, *halos[0], tables, fields, fibre_weights, (partial,), parts[1][:1])
     images.append(swap(image))
     natural = [unpack(images[0], modes)]
     image, partial = apply_twice(2, place, *halos[1], tables, fields, fibre_weights, (partial,), natural)

time: 161 us -> 160 us (level); the launches traced: 160 us -> 157 us
  starting transfers between devices: 67.5 us -> 62 us
  waiting for transfers between devices: 12.6 us -> 16.4 us
    ppermute x3, starting transfers between devices: 10.4 us -> 6.31 us  [all_sum(): lax.ppermute(value, axis, [(i, i ^ bit) for i in range(devices)])]
    ppermute x3, waiting for transfers between devices: 4.34 us -> 6.44 us  [all_sum(): lax.ppermute(value, axis, [(i, i ^ bit) for i in range(devices)])]
    unnamed x35 -> x37, local copies, waits for them, and re-layouts: 4.65 us -> 4.36 us
  transfers between devices with their start and end apart: 19 -> 19, of which waited for: 8 -> 9; matrix products, arithmetic and copies ran while one was open for 7% -> 7% of each run, Pallas kernels for 35% -> 35%
where the time goes in v11:
time: 160 us; the launch traced here: 157 us
  Pallas kernels  62.9 us (39%)
  starting transfers between devices  62 us (39%)
  waiting for transfers between devices  16.4 us (10%)
  local copies, waits for them, and re-layouts  7.15 us (4%)
  other arithmetic  5.91 us (4%)
  matrix products  1.8 us (1%)
    pallas_call x3, Pallas kernels, apply_twice(): pl.pallas_call(functools.partial(apply_kernel, comp=comp), out_shape=[jax...  34.8 us
    all_to_all x5, starting transfers between devices, swap(): return lax.all_to_all(rows, 'mode', 0, 0, tiled=True)  27.4 us
    ppermute x3, starting transfers between devices, halo(): lax.ppermute(upward, 'space', up)  15.5 us
    pallas_call x2, Pallas kernels, pack(): pl.pallas_call(functools.partial(pack_kernel, comps=comps), grid=(1,), ou...  8.51 us
    pallas_call x2, Pallas kernels, unpack(): pl.pallas_call(unpack_kernel, out_shape=jax.ShapeDtypeStruct((2, modes, S...  7.23 us
    ppermute x3, waiting for transfers between devices, all_sum(): lax.ppermute(value, axis, [(i, i ^ bit) for i in range(devices)])  6.44 us
    ppermute x3, starting transfers between devices, all_sum(): lax.ppermute(value, axis, [(i, i ^ bit) for i in range(devices)])  6.31 us
    ppermute x3, waiting for transfers between devices, all_sum(): lax.ppermute(value, 'mode', [(i, i ^ bit) for i in range(PARTS)])  4.83 us
  transfers between devices with their start and end apart: 19, of which 9 were waited for; matrix products, arithmetic and copies ran while one was open for 7% of the time, Pallas kernels for 35%

profile of v11, /device:TPU:0, one launch (start us, length us, event | category | flops | bytes accessed | tf_op | source)
XLA Modules:
  0.0 157.1 jit_solution(14512974526615033923)
XLA Ops:
  0.6 3.2 %pack.2.refs_2_ = f32[1152,128]{1,0:T(8,128)} custom-call(f32[36,3,3,8,128]{4,3,2,1,0:T(8,128)} %field.5), custom_call_target="tpu_custom_call" | custom-call | flops 500000000 | bytes 1500000 | tf_op jit(solution)/shard_map/pack/pallas_call | solution.py:208
  3.9 7.4 %all-to-all-start.1 = ((f32[8,144,128]{2,1,0:T(8,128)}), f32[8,144,128]{2,1,0:T(8,128)S(1)}, u32[]{:S(2)}, u32[]{:S(2)}) async-start(f32[8,144,128]{2,1,0:T(8,128)} %bitcast.10), calls=%async_computation.1 | async-start | bytes 1179648 | tf_op jit(solution)/shard_map/all_to_all | solution.py:703
  11.3 5.3 %pack.3 = (f32[2,3,8,128]{3,2,1,0:T(8,128)}, f32[2304,128]{1,0:T(8,128)}) custom-call(f32[36,3,3,8,128]{4,3,2,1,0:T(8,128)} %field.5, f32[3,8,128]{2,1,0:T(8,128)} %refs_0_.1, s32[3,8,128]{2,1,0:T(8,128)} %refs_1_.1, f32[1152,128]{1,0:T(8,128)} %pack.2.refs_2_), custom_call_target="tpu_custom_call" | custom-call | flops 500000000 | bytes 1500000 | tf_op jit(solution)/shard_map/pack/pallas_call | solution.py:208
  17.8 3.0 %collective-permute-start.2 = (f32[2,3,8,128]{3,2,1,0:T(8,128)}, f32[2,3,8,128]{3,2,1,0:T(8,128)S(1)}, u32[]{:S(2)}, u32[]{:S(2)}) collective-permute-start(f32[2,3,8,128]{3,2,1,0:T(8,128)} %get-tuple-element.17.both), channel_id=1, source_target_pairs={{0,1},{1,2},{2,3},{4,5},{5,6},{6,7},{8,9},{9,10},{10,11},{12,13},{... | collective-permute-start | bytes 73736 | tf_op jit(solution)/shard_map/ppermute | solution.py:714
  24.2 3.0 %all-to-all-done.1 = f32[8,144,128]{2,1,0:T(8,128)S(1)} async-done(((f32[8,144,128]{2,1,0:T(8,128)}), f32[8,144,128]{2,1,0:T(8,128)S(1)}, u32[]{:S(2)}, u32[]{:S(2)}) %all-to-all-start.1) | async-done | bytes 589856 | tf_op jit(solution)/shard_map/all_to_all | solution.py:703
  27.2 3.6 %all-to-all-start = ((f32[8,288,128]{2,1,0:T(8,128)}), f32[8,288,128]{2,1,0:T(8,128)S(1)}, u32[]{:S(2)}, u32[]{:S(2)}) async-start(f32[8,288,128]{2,1,0:T(8,128)} %bitcast.1), calls=%async_computation | async-start | bytes 2359296 | tf_op jit(solution)/shard_map/all_to_all | solution.py:703
  32.1 3.1 %collective-permute-start = (f32[1152,128]{1,0:T(8,128)S(1)}, f32[1152,128]{1,0:T(8,128)S(1)}, u32[]{:S(2)}, u32[]{:S(2)}) collective-permute-start(f32[1152,128]{1,0:T(8,128)S(1)} %bitcast.18), channel_id=1, source_target_pairs={{0,1},{1,2},{2,3},{4,5},{5,6},{6,7},{8,9},{9,10},{10,11},{12,13},{... | collective-permute-start | bytes 1769480 | tf_op jit(solution)/shard_map/ppermute | solution.py:706
  47.0 11.6 %apply_twice.3 = (f32[1728,128]{1,0:T(8,128)}, f32[8,128]{1,0:T(8,128)}) custom-call(s32[1]{0:T(128)} %bitcast.place, f32[1152,128]{1,0:T(8,128)} %bitcast.20, f32[1152,128]{1,0:T(8,128)} %copy-done.9, f32[1152,128]{1,0:T(8,128)} %copy-done.8, f32[288,128]{1,0:T(8,128)} %broadcast_in_dim.90.scale, bf16[624,576]{1,0:T(8,128)(2,1)} %pad_maximum_fusion.to_even, ...), custom_call_target="tpu_custom_call" | custom-call | flops 2000000000 | bytes 6000000 | tf_op jit(solution)/shard_map/apply_twice/pallas_call | solution.py:530
  60.1 4.6 %all-to-all-start.2 = ((f32[8,216,128]{2,1,0:T(8,128)}), f32[8,216,128]{2,1,0:T(8,128)S(1)}, u32[]{:S(2)}, u32[]{:S(2)}) async-start(f32[8,216,128]{2,1,0:T(8,128)} %bitcast.15), calls=%async_computation.2 | async-start | bytes 1769472 | tf_op jit(solution)/shard_map/all_to_all | solution.py:703
  64.7 2.2 %part_component.3 = (f32[1152,128]{1,0:T(8,128)}, f32[864,128]{1,0:T(8,128)}, f32[864,128]{1,0:T(8,128)}) custom-call(f32[8,288,128]{2,1,0:T(8,128)} %copy-done.1, f32[8,128]{1,0:T(8,128)} %get-tuple-element.18.ready.refs_0_), custom_call_target="tpu_custom_call" | custom-call | flops 500000000 | bytes 1500000 | tf_op jit(solution)/shard_map/part_component/pallas_call | solution.py:240
  67.0 4.0 %collective-permute-start.6 = (f32[864,128]{1,0:T(8,128)}, f32[864,128]{1,0:T(8,128)S(1)}, u32[]{:S(2)}, u32[]{:S(2)}) collective-permute-start(f32[864,128]{1,0:T(8,128)} %get-tuple-element.23), channel_id=1, source_target_pairs={{0,1},{1,2},{2,3},{4,5},{5,6},{6,7},{8,9},{9,10},{10,11},{12,13},{... | collective-permute-start | bytes 1327112 | tf_op jit(solution)/shard_map/ppermute | solution.py:706
  72.3 2.3 %part_component.2 = (f32[1152,128]{1,0:T(8,128)}, f32[864,128]{1,0:T(8,128)}, f32[864,128]{1,0:T(8,128)}) custom-call(f32[8,288,128]{2,1,0:T(8,128)} %copy-done.1, f32[8,128]{1,0:T(8,128)} %get-tuple-element.18.ready.refs_0_), custom_call_target="tpu_custom_call" | custom-call | flops 500000000 | bytes 1500000 | tf_op jit(solution)/shard_map/part_component/pallas_call | solution.py:240
  75.9 11.6 %apply_twice.4 = (f32[1728,128]{1,0:T(8,128)}, f32[8,128]{1,0:T(8,128)}) custom-call(s32[1]{0:T(128)} %bitcast.place, f32[1152,128]{1,0:T(8,128)} %get-tuple-element.22.own, f32[864,128]{1,0:T(8,128)} %copy-done.13, f32[864,128]{1,0:T(8,128)} %copy-done.15, f32[288,128]{1,0:T(8,128)} %broadcast_in_dim.90.scale, bf16[624,576]{1,0:T(8,128)(2,1)} %pad_maximum_fusion.to_even, ...), custom_call_target="tpu_custom_call" | custom-call | flops 2000000000 | bytes 6000000 | tf_op jit(solution)/shard_map/apply_twice/pallas_call | solution.py:530
  87.6 6.1 %all-to-all-start.4 = ((f32[8,216,128]{2,1,0:T(8,128)}), f32[8,216,128]{2,1,0:T(8,128)S(1)}, u32[]{:S(2)}, u32[]{:S(2)}) async-start(f32[8,216,128]{2,1,0:T(8,128)} %bitcast.16), calls=%async_computation.4 | async-start | bytes 1769472 | tf_op jit(solution)/shard_map/all_to_all | solution.py:703
  93.7 8.4 %collective-permute-start.4 = (f32[864,128]{1,0:T(8,128)S(1)}, f32[864,128]{1,0:T(8,128)S(1)}, u32[]{:S(2)}, u32[]{:S(2)}) collective-permute-start(f32[864,128]{1,0:T(8,128)S(1)} %copy-done.11), channel_id=1, source_target_pairs={{0,1},{1,2},{2,3},{4,5},{5,6},{6,7},{8,9},{9,10},{10,11},{12,13},{... | collective-permute-start | bytes 1327112 | tf_op jit(solution)/shard_map/ppermute | solution.py:706
  103.6 3.6 %unpack.2.refs_1_.refs_0_ = f32[2,36,3,8,128]{4,3,2,1,0:T(8,128)} custom-call(f32[1728,128]{1,0:T(8,128)} %bitcast.14), custom_call_target="tpu_custom_call" | custom-call | flops 3000000000 | bytes 9000000 | tf_op jit(solution)/shard_map/unpack/pallas_call | solution.py:582
  108.2 11.6 %apply_twice.5 = (f32[1728,128]{1,0:T(8,128)}, f32[8,128]{1,0:T(8,128)}) custom-call(s32[1]{0:T(128)} %bitcast.place, f32[1152,128]{1,0:T(8,128)} %get-tuple-element.19.refs_1_.own, f32[864,128]{1,0:T(8,128)} %copy-done.12, f32[864,128]{1,0:T(8,128)} %copy-done.14, f32[288,128]{1,0:T(8,128)} %broadcast_in_dim.90.scale, ...), custom_call_target="tpu_custom_call" | custom-call | flops 2000000000 | bytes 6000000 | tf_op jit(solution)/shard_map/apply_twice/pallas_call | solution.py:530
  119.8 5.7 %all-to-all-start.3 = ((f32[8,216,128]{2,1,0:T(8,128)}), f32[8,216,128]{2,1,0:T(8,128)S(1)}, u32[]{:S(2)}, u32[]{:S(2)}) async-start(f32[8,216,128]{2,1,0:T(8,128)} %bitcast.12), calls=%async_computation.3 | async-start | bytes 1769472 | tf_op jit(solution)/shard_map/all_to_all | solution.py:703
  125.5 4.6 %collective-permute-start.8 = (f32[8,128]{1,0:T(8,128)S(1)}, f32[8,128]{1,0:T(8,128)S(1)}, u32[]{:S(2)}, u32[]{:S(2)}) collective-permute-start(f32[8,128]{1,0:T(8,128)S(1)} %copy-done.7), channel_id=1, source_target_pairs={{0,1},{1,0},{2,3},{3,2},{4,5},{5,4},{6,7},{7,6},{8,9},{9,8},{10,11... | collective-permute-start | bytes 12296 | tf_op jit(solution)/shard_map/ppermute | solution.py:688
  131.0 3.6 %collective-permute-done.9 = f32[8,128]{1,0:T(8,128)S(1)} collective-permute-done((f32[8,128]{1,0:T(8,128)S(1)}, f32[8,128]{1,0:T(8,128)S(1)}, u32[]{:S(2)}, u32[]{:S(2)}) %collective-permute-start.9) | collective-permute-done | bytes 4128 | tf_op jit(solution)/shard_map/ppermute | solution.py:688
  138.3 3.6 %collective-permute-start.13 = (f32[8,128]{1,0:T(8,128)S(1)}, f32[8,128]{1,0:T(8,128)S(1)}, u32[]{:S(2)}, u32[]{:S(2)}) collective-permute-start(f32[8,128]{1,0:T(8,128)S(1)} %add.39), channel_id=1, source_target_pairs={{0,24},{4,28},{8,16},{12,20},{16,8},{20,12},{24,0},{28,4},{1,25},{... | collective-permute-start | bytes 12296 | tf_op jit(solution)/shard_map/ppermute | solution.py:690
  143.8 3.7 %collective-permute-done.12 = f32[8,128]{1,0:T(8,128)S(1)} collective-permute-done((f32[8,128]{1,0:T(8,128)S(1)}, f32[8,128]{1,0:T(8,128)S(1)}, u32[]{:S(2)}, u32[]{:S(2)}) %collective-permute-start.12) | collective-permute-done | bytes 4128 | tf_op jit(solution)/shard_map/ppermute | solution.py:690
  148.1 3.6 %unpack.3.refs_1_ = f32[2,36,3,8,128]{4,3,2,1,0:T(8,128)} custom-call(f32[1728,128]{1,0:T(8,128)} %bitcast.11), custom_call_target="tpu_custom_call" | custom-call | flops 3000000000 | bytes 9000000 | tf_op jit(solution)/shard_map/unpack/pallas_call | solution.py:582
  152.7 4.4 %finish.1 = (f32[36,3,3,8,128]{4,3,2,1,0:T(8,128)}, f32[36,3,3,8,128]{4,3,2,1,0:T(8,128)}) custom-call(f32[36,3,3,8,128]{4,3,2,1,0:T(8,128)} %field.5, f32[8,128]{1,0:T(8,128)} %add_add_fusion.total, f32[1728,128]{1,0:T(8,128)} %bitcast.13, f32[2,36,3,8,128]{4,3,2,1,0:T(8,128)} %unpack.2.refs_1_.refs_0_, f32[2,36,3,8,128]{4,3,2,1,0:T(8,128)} %unpack.3.refs_1_), custom_call_target="tpu_custom_call" | custom-call | flops 6000000000 | bytes 18000000 | tf_op jit(solution)/shard_map/finish/pallas_call | solution.py:633
  (84 shorter events, 32.3 us)
Async XLA Ops:
  3.9 17.0 %copy-start.6 = (s32[660,4]{0,1:T(4,128)S(1)}, s32[660,4]{0,1:T(4,128)}, u32[]{:S(2)}) copy-start(s32[660,4]{0,1:T(4,128)} %param.11) | copy-start | bytes 31684
  3.9 23.3 %all-to-all-start.1 = ((f32[8,144,128]{2,1,0:T(8,128)}), f32[8,144,128]{2,1,0:T(8,128)S(1)}, u32[]{:S(2)}, u32[]{:S(2)}) async-start(f32[8,144,128]{2,1,0:T(8,128)} %bitcast.10), calls=%async_computation.1 | async-start | bytes 1179648 | tf_op jit(solution)/shard_map/all_to_all | solution.py:703
  16.5 5.3 %collective-permute-start.3 = (f32[2,3,8,128]{3,2,1,0:T(8,128)}, f32[2,3,8,128]{3,2,1,0:T(8,128)S(1)}, u32[]{:S(2)}, u32[]{:S(2)}) collective-permute-start(f32[2,3,8,128]{3,2,1,0:T(8,128)} %get-tuple-element.17.both), channel_id=1, source_target_pairs={{1,0},{2,1},{3,2},{5,4},{6,5},{7,6},{9,8},{10,9},{11,10},{13,12},{... | collective-permute-start | bytes 73736 | tf_op jit(solution)/shard_map/ppermute | solution.py:715
  17.8 4.1 %collective-permute-start.2 = (f32[2,3,8,128]{3,2,1,0:T(8,128)}, f32[2,3,8,128]{3,2,1,0:T(8,128)S(1)}, u32[]{:S(2)}, u32[]{:S(2)}) collective-permute-start(f32[2,3,8,128]{3,2,1,0:T(8,128)} %get-tuple-element.17.both), channel_id=1, source_target_pairs={{0,1},{1,2},{2,3},{4,5},{5,6},{6,7},{8,9},{9,10},{10,11},{12,13},{... | collective-permute-start | bytes 73736 | tf_op jit(solution)/shard_map/ppermute | solution.py:714
  27.1 8.0 %copy-start.5 = (f32[8,144,128]{2,1,0:T(8,128)}, f32[8,144,128]{2,1,0:T(8,128)S(1)}, u32[]{:S(2)}) copy-start(f32[8,144,128]{2,1,0:T(8,128)S(1)} %all-to-all-done.1) | copy-start | bytes 1769476
  27.2 33.0 %all-to-all-start = ((f32[8,288,128]{2,1,0:T(8,128)}), f32[8,288,128]{2,1,0:T(8,128)S(1)}, u32[]{:S(2)}, u32[]{:S(2)}) async-start(f32[8,288,128]{2,1,0:T(8,128)} %bitcast.1), calls=%async_computation | async-start | bytes 2359296 | tf_op jit(solution)/shard_map/all_to_all | solution.py:703
  30.8 15.2 %collective-permute-start.1 = (f32[1152,128]{1,0:T(8,128)S(1)}, f32[1152,128]{1,0:T(8,128)S(1)}, u32[]{:S(2)}, u32[]{:S(2)}) collective-permute-start(f32[1152,128]{1,0:T(8,128)S(1)} %bitcast.17), channel_id=1, source_target_pairs={{1,0},{2,1},{3,2},{5,4},{6,5},{7,6},{9,8},{10,9},{11,10},{13,12},{... | collective-permute-start | bytes 1769480 | tf_op jit(solution)/shard_map/ppermute | solution.py:706
  32.1 13.9 %collective-permute-start = (f32[1152,128]{1,0:T(8,128)S(1)}, f32[1152,128]{1,0:T(8,128)S(1)}, u32[]{:S(2)}, u32[]{:S(2)}) collective-permute-start(f32[1152,128]{1,0:T(8,128)S(1)} %bitcast.18), channel_id=1, source_target_pairs={{0,1},{1,2},{2,3},{4,5},{5,6},{6,7},{8,9},{9,10},{10,11},{12,13},{... | collective-permute-start | bytes 1769480 | tf_op jit(solution)/shard_map/ppermute | solution.py:706
  60.1 27.4 %all-to-all-start.2 = ((f32[8,216,128]{2,1,0:T(8,128)}), f32[8,216,128]{2,1,0:T(8,128)S(1)}, u32[]{:S(2)}, u32[]{:S(2)}) async-start(f32[8,216,128]{2,1,0:T(8,128)} %bitcast.15), calls=%async_computation.2 | async-start | bytes 1769472 | tf_op jit(solution)/shard_map/all_to_all | solution.py:703
  67.0 7.6 %collective-permute-start.6 = (f32[864,128]{1,0:T(8,128)}, f32[864,128]{1,0:T(8,128)S(1)}, u32[]{:S(2)}, u32[]{:S(2)}) collective-permute-start(f32[864,128]{1,0:T(8,128)} %get-tuple-element.23), channel_id=1, source_target_pairs={{0,1},{1,2},{2,3},{4,5},{5,6},{6,7},{8,9},{9,10},{10,11},{12,13},{... | collective-permute-start | bytes 1327112 | tf_op jit(solution)/shard_map/ppermute | solution.py:706
  71.0 4.2 %collective-permute-start.7 = (f32[864,128]{1,0:T(8,128)}, f32[864,128]{1,0:T(8,128)S(1)}, u32[]{:S(2)}, u32[]{:S(2)}) collective-permute-start(f32[864,128]{1,0:T(8,128)} %get-tuple-element.24), channel_id=1, source_target_pairs={{1,0},{2,1},{3,2},{5,4},{6,5},{7,6},{9,8},{10,9},{11,10},{13,12},{... | collective-permute-start | bytes 1327112 | tf_op jit(solution)/shard_map/ppermute | solution.py:706
  87.6 14.5 %copy-start.10 = (f32[864,128]{1,0:T(8,128)S(1)}, f32[864,128]{1,0:T(8,128)}, u32[]{:S(2)}) copy-start(f32[864,128]{1,0:T(8,128)} %get-tuple-element.21) | copy-start | bytes 1327108
  87.6 16.1 %copy-start.4 = (f32[8,216,128]{2,1,0:T(8,128)}, f32[8,216,128]{2,1,0:T(8,128)S(1)}, u32[]{:S(2)}) copy-start(f32[8,216,128]{2,1,0:T(8,128)S(1)} %all-to-all-done.2) | copy-start | bytes 2654212
  87.6 32.2 %all-to-all-start.4 = ((f32[8,216,128]{2,1,0:T(8,128)}), f32[8,216,128]{2,1,0:T(8,128)S(1)}, u32[]{:S(2)}, u32[]{:S(2)}) async-start(f32[8,216,128]{2,1,0:T(8,128)} %bitcast.16), calls=%async_computation.4 | async-start | bytes 1769472 | tf_op jit(solution)/shard_map/all_to_all | solution.py:703
  93.7 13.5 %collective-permute-start.4 = (f32[864,128]{1,0:T(8,128)S(1)}, f32[864,128]{1,0:T(8,128)S(1)}, u32[]{:S(2)}, u32[]{:S(2)}) collective-permute-start(f32[864,128]{1,0:T(8,128)S(1)} %copy-done.11), channel_id=1, source_target_pairs={{0,1},{1,2},{2,3},{4,5},{5,6},{6,7},{8,9},{9,10},{10,11},{12,13},{... | collective-permute-start | bytes 1327112 | tf_op jit(solution)/shard_map/ppermute | solution.py:706
  102.1 5.2 %collective-permute-start.5 = (f32[864,128]{1,0:T(8,128)S(1)}, f32[864,128]{1,0:T(8,128)S(1)}, u32[]{:S(2)}, u32[]{:S(2)}) collective-permute-start(f32[864,128]{1,0:T(8,128)S(1)} %copy-done.10), channel_id=1, source_target_pairs={{1,0},{2,1},{3,2},{5,4},{6,5},{7,6},{9,8},{10,9},{11,10},{13,12},{... | collective-permute-start | bytes 1327112 | tf_op jit(solution)/shard_map/ppermute | solution.py:706
  119.8 28.3 %copy-start.2 = (f32[8,216,128]{2,1,0:T(8,128)}, f32[8,216,128]{2,1,0:T(8,128)S(1)}, u32[]{:S(2)}) copy-start(f32[8,216,128]{2,1,0:T(8,128)S(1)} %all-to-all-done.4) | copy-start | bytes 2654212
  119.8 31.9 %all-to-all-start.3 = ((f32[8,216,128]{2,1,0:T(8,128)}), f32[8,216,128]{2,1,0:T(8,128)S(1)}, u32[]{:S(2)}, u32[]{:S(2)}) async-start(f32[8,216,128]{2,1,0:T(8,128)} %bitcast.12), calls=%async_computation.3 | async-start | bytes 1769472 | tf_op jit(solution)/shard_map/all_to_all | solution.py:703
  125.5 5.4 %collective-permute-start.8 = (f32[8,128]{1,0:T(8,128)S(1)}, f32[8,128]{1,0:T(8,128)S(1)}, u32[]{:S(2)}, u32[]{:S(2)}) collective-permute-start(f32[8,128]{1,0:T(8,128)S(1)} %copy-done.7), channel_id=1, source_target_pairs={{0,1},{1,0},{2,3},{3,2},{4,5},{5,4},{6,7},{7,6},{8,9},{9,8},{10,11... | collective-permute-start | bytes 12296 | tf_op jit(solution)/shard_map/ppermute | solution.py:688
  130.9 3.6 %collective-permute-start.9 = (f32[8,128]{1,0:T(8,128)S(1)}, f32[8,128]{1,0:T(8,128)S(1)}, u32[]{:S(2)}, u32[]{:S(2)}) collective-permute-start(f32[8,128]{1,0:T(8,128)S(1)} %add.37), channel_id=1, source_target_pairs={{0,2},{1,3},{2,0},{3,1},{4,6},{5,7},{6,4},{7,5},{8,10},{9,11},{10,... | collective-permute-start | bytes 12296 | tf_op jit(solution)/shard_map/ppermute | solution.py:688
  134.5 3.7 %collective-permute-start.10 = (f32[8,128]{1,0:T(8,128)S(1)}, f32[8,128]{1,0:T(8,128)S(1)}, u32[]{:S(2)}, u32[]{:S(2)}) collective-permute-start(f32[8,128]{1,0:T(8,128)S(1)} %add.38), channel_id=1, source_target_pairs={{0,4},{4,0},{8,12},{12,8},{16,20},{20,16},{24,28},{28,24},{1,5},{5... | collective-permute-start | bytes 12296 | tf_op jit(solution)/shard_map/ppermute | solution.py:688
  138.3 5.5 %collective-permute-start.13 = (f32[8,128]{1,0:T(8,128)S(1)}, f32[8,128]{1,0:T(8,128)S(1)}, u32[]{:S(2)}, u32[]{:S(2)}) collective-permute-start(f32[8,128]{1,0:T(8,128)S(1)} %add.39), channel_id=1, source_target_pairs={{0,24},{4,28},{8,16},{12,20},{16,8},{20,12},{24,0},{28,4},{1,25},{... | collective-permute-start | bytes 12296 | tf_op jit(solution)/shard_map/ppermute | solution.py:690
  141.9 5.6 %collective-permute-start.12 = (f32[8,128]{1,0:T(8,128)S(1)}, f32[8,128]{1,0:T(8,128)S(1)}, u32[]{:S(2)}, u32[]{:S(2)}) collective-permute-start(f32[8,128]{1,0:T(8,128)S(1)} %add.39), channel_id=1, source_target_pairs={{0,16},{4,20},{8,24},{12,28},{16,0},{20,4},{24,8},{28,12},{1,17},{... | collective-permute-start | bytes 12296 | tf_op jit(solution)/shard_map/ppermute | solution.py:690
  141.9 5.6 %collective-permute-start.11 = (f32[8,128]{1,0:T(8,128)S(1)}, f32[8,128]{1,0:T(8,128)S(1)}, u32[]{:S(2)}, u32[]{:S(2)}) collective-permute-start(f32[8,128]{1,0:T(8,128)S(1)} %add.39), channel_id=1, source_target_pairs={{0,8},{4,12},{8,0},{12,4},{16,24},{20,28},{24,16},{28,20},{1,9},{5... | collective-permute-start | bytes 12296 | tf_op jit(solution)/shard_map/ppermute | solution.py:690
  (13 other events, 28.5 us)

commit v12 on v11

--- a/solution.py
+++ b/solution.py
@@ -223,16 +223,17 @@
     goal[...] = source[...]
 
 
-def part_kernel(source, ready, own, upward, downward):
+def part_kernel(turns, source, ready, own, across, beside):
     rows = own.shape[0]
     slots = rows // ROWS
     own[...] = source[...].reshape(rows, LANES)
-    for goal, planes in ((upward, UPWARD), (downward, DOWNWARD)):
-        for n, p in enumerate(planes):
-            goal[n * slots : (n + 1) * slots, :] = own[pl.ds(p, slots, stride=ROWS), :]
-
-
-def part_component(rows, n, ready):
+    for n, goal in enumerate((across, beside)):
+        for m in range(len(UPWARD) - 1):
+            goal[m * slots : (m + 1) * slots, :] = own[pl.ds(m + turns[n], slots, stride=ROWS), :]
+        goal[(len(UPWARD) - 1) * slots :, :] = own[pl.ds(UPWARD[-1], slots, stride=ROWS), :]
+
+
+def part_component(turns, rows, n, ready):
     blocks = rows.reshape(PARTS, -1, LANES)
     part = (PARTS, blocks.shape[1] // (COMPS - 1), LANES)
     count = part[0] * part[1]
@@ -244,12 +245,16 @@
             jax.ShapeDtypeStruct((size, LANES), jnp.float32)
             for size in (count, count * len(UPWARD) // ROWS, count * len(DOWNWARD) // ROWS)
         ],
-        in_specs=[pl.BlockSpec(part, lambda i: (0, n, 0)), pl.BlockSpec(memory_space=pl.ANY)],
+        in_specs=[
+            pl.BlockSpec(memory_space=pltpu.SMEM),
+            pl.BlockSpec(part, lambda i: (0, n, 0)),
+            pl.BlockSpec(memory_space=pl.ANY),
+        ],
         out_specs=[vmem] * 3,
         compiler_params=pltpu.CompilerParams(vmem_limit_bytes=VMEM),
         cost_estimate=estimate(0.5),
         name="part_component",
-    )(blocks, ready)
+    )(turns, blocks, ready)
 
 
 def after_rows(table, ready):
@@ -488,8 +493,10 @@
     slot = lane % WIDE
     load = lambda ref, p: ref[pl.ds(p, slots, stride=ROWS), :]
     whole = before.shape[0] == own.shape[0]
-    below = lambda p: load(before, p) if whole else before[pl.ds(UPWARD.index(p) * slots, slots), :]
-    above = lambda p: load(after, p) if whole else after[pl.ds(DOWNWARD.index(p) * slots, slots), :]
+    odd = place[1] == 1
+    pick = lambda one, two, n: jnp.where(odd, two[pl.ds(n * slots, slots), :], one[pl.ds(n * slots, slots), :])
+    below = lambda p: load(before, p) if whole else pick(before, after, UPWARD.index(p))
+    above = lambda p: load(after, p) if whole else pick(after, before, DOWNWARD.index(p))
     left = pltpu.roll(below(3), LANES - 3, 1)
     right = pltpu.roll(above(3), 3, 1)
     halo = jnp.where((slot == 0) | (slot == 5), left, load(own, 3))
@@ -697,18 +704,21 @@
     devices = lax.axis_size("space")
     up = [(i, i + 1) for i in range(devices - 1)]
     down = [(j, i) for i, j in up]
-    place = lax.axis_index("mode").astype(jnp.int32).reshape(1)
+    slab = lax.axis_index("space").astype(jnp.int32)
+    place = jnp.stack([lax.axis_index("mode").astype(jnp.int32), slab % 2])
+    turns = jnp.stack([(slab == 1).astype(jnp.int32), 1 - slab % 2])
 
     def swap(rows):
         return lax.all_to_all(rows, "mode", 0, 0, tiled=True)
 
-    def halo(rows, upward, downward):
-        return rows, lax.ppermute(upward, "space", up), lax.ppermute(downward, "space", down)
+    def halo(rows, across, beside):
+        across = lax.ppermute(across, "space", [(1, 2), (2, 1)])
+        return rows, across, lax.ppermute(beside, "space", [(0, 1), (1, 0), (2, 3), (3, 2)])
 
     (first,) = pack(right_side, (0,))
     both, others = pack(right_side, (1, 2), (mean_stiffness, ply_map), (first,))
     first = swap(first)
-    first = halo(first, first, first)
+    first = (first, lax.ppermute(first, "space", up), lax.ppermute(first, "space", down))
     others = swap(others)
     tables = mode_tables(after_rows(coupling_table, first[0]), slots)
     both_before = lax.ppermute(both, "space", up)
@@ -716,7 +726,7 @@
     fields = stiffness_fields(place, both_before, both, both_after, ply_stiffness)
     image, partial = apply_twice(0, place, *first, tables, fields, fibre_weights)
     images = [swap(image)]
-    parts = [part_component(others, n, partial) for n in range(COMPS - 1)]
+    parts = [part_component(turns, others, n, partial) for n in range(COMPS - 1)]
     halos = [halo(*part) for part in parts]
     modes = right_side.shape[0]
     image, partial = apply_twice(1, place, *halos[0], tables, fields, fibre_weights, (partial,), parts[1][:1])

time: 160 us -> 158 us (0.988)
  starting transfers between devices: 62 us -> 57 us
  waiting for transfers between devices: 16.4 us -> 18.4 us
    ppermute x3, waiting for transfers between devices: 4.83 us -> 7.95 us  [all_sum(): lax.ppermute(value, 'mode', [(i, i ^ bit) for i in range(PARTS)])]
    ppermute x6, starting transfers between devices: 19.6 us -> 16.8 us  [the longest x2 10.5 us: halo(): lax.ppermute(beside, 'space', [(0, 1), (1, 0), (2, 3), (3, 2)])]
    all_to_all x5, starting transfers between devices: 27.4 us -> 25.7 us  [swap(): return lax.all_to_all(rows, 'mode', 0, 0, tiled=True)]
    ppermute x3, waiting for transfers between devices: 6.44 us -> 4.83 us  [all_sum(): lax.ppermute(value, axis, [(i, i ^ bit) for i in range(devices)])]
  transfers between devices with their start and end apart: 19 -> 19, of which waited for: 9 -> 8; matrix products, arithmetic and copies ran while one was open for 7% -> 8% of each run, Pallas kernels for 35% -> 35%
where the time goes in v12:
time: 158 us; the launch traced here: 156 us
  Pallas kernels  62.8 us (40%)
  starting transfers between devices  57 us (36%)
  waiting for transfers between devices  18.4 us (12%)
  local copies, waits for them, and re-layouts  7.88 us (5%)
  other arithmetic  7.11 us (4%)
  matrix products  1.8 us (1%)
    pallas_call x3, Pallas kernels, apply_twice(): pl.pallas_call(functools.partial(apply_kernel, comp=comp), out_shape=[jax...  34.8 us
    all_to_all x5, starting transfers between devices, swap(): return lax.all_to_all(rows, 'mode', 0, 0, tiled=True)  25.7 us
    ppermute x2, starting transfers between devices, halo(): lax.ppermute(beside, 'space', [(0, 1), (1, 0), (2, 3), (3, 2)])  10.5 us
    pallas_call x2, Pallas kernels, pack(): pl.pallas_call(functools.partial(pack_kernel, comps=comps), grid=(1,), ou...  8.51 us
    ppermute x3, waiting for transfers between devices, all_sum(): lax.ppermute(value, 'mode', [(i, i ^ bit) for i in range(PARTS)])  7.95 us
    pallas_call x2, Pallas kernels, unpack(): pl.pallas_call(unpack_kernel, out_shape=jax.ShapeDtypeStruct((2, modes, S...  7.22 us
    ppermute x3, starting transfers between devices, all_sum(): lax.ppermute(value, axis, [(i, i ^ bit) for i in range(devices)])  5.76 us
    all_to_all x5, waiting for transfers between devices, swap(): return lax.all_to_all(rows, 'mode', 0, 0, tiled=True)  5.56 us
  transfers between devices with their start and end apart: 19, of which 8 were waited for; matrix products, arithmetic and copies ran while one was open for 8% of the time, Pallas kernels for 35%

profile of v12, /device:TPU:0, one launch (start us, length us, event | category | flops | bytes accessed | tf_op | source)
XLA Modules:
  0.0 155.8 jit_solution(1404334496197725500)
XLA Ops:
  0.6 3.2 %pack.2.refs_2_ = f32[1152,128]{1,0:T(8,128)} custom-call(f32[36,3,3,8,128]{4,3,2,1,0:T(8,128)} %field.5), custom_call_target="tpu_custom_call" | custom-call | flops 500000000 | bytes 1500000 | tf_op jit(solution)/shard_map/pack/pallas_call | solution.py:208
  3.9 7.4 %all-to-all-start.1 = ((f32[8,144,128]{2,1,0:T(8,128)}), f32[8,144,128]{2,1,0:T(8,128)S(1)}, u32[]{:S(2)}, u32[]{:S(2)}) async-start(f32[8,144,128]{2,1,0:T(8,128)} %bitcast.13), calls=%async_computation.1 | async-start | bytes 1179648 | tf_op jit(solution)/shard_map/all_to_all | solution.py:712
  11.3 5.3 %pack.3 = (f32[2,3,8,128]{3,2,1,0:T(8,128)}, f32[2304,128]{1,0:T(8,128)}) custom-call(f32[36,3,3,8,128]{4,3,2,1,0:T(8,128)} %field.5, f32[3,8,128]{2,1,0:T(8,128)} %refs_0_.1, s32[3,8,128]{2,1,0:T(8,128)} %refs_1_.1, f32[1152,128]{1,0:T(8,128)} %pack.2.refs_2_), custom_call_target="tpu_custom_call" | custom-call | flops 500000000 | bytes 1500000 | tf_op jit(solution)/shard_map/pack/pallas_call | solution.py:208
  17.8 3.0 %collective-permute-start.2 = (f32[2,3,8,128]{3,2,1,0:T(8,128)}, f32[2,3,8,128]{3,2,1,0:T(8,128)S(1)}, u32[]{:S(2)}, u32[]{:S(2)}) collective-permute-start(f32[2,3,8,128]{3,2,1,0:T(8,128)} %get-tuple-element.17.both), channel_id=1, source_target_pairs={{0,1},{1,2},{2,3},{4,5},{5,6},{6,7},{8,9},{9,10},{10,11},{12,13},{... | collective-permute-start | bytes 73736 | tf_op jit(solution)/shard_map/ppermute | solution.py:724
  27.2 4.2 %all-to-all-start = ((f32[8,288,128]{2,1,0:T(8,128)}), f32[8,288,128]{2,1,0:T(8,128)S(1)}, u32[]{:S(2)}, u32[]{:S(2)}) async-start(f32[8,288,128]{2,1,0:T(8,128)} %bitcast.4), calls=%async_computation | async-start | bytes 2359296 | tf_op jit(solution)/shard_map/all_to_all | solution.py:712
  32.6 3.4 %collective-permute-start = (f32[1152,128]{1,0:T(8,128)S(1)}, f32[1152,128]{1,0:T(8,128)S(1)}, u32[]{:S(2)}, u32[]{:S(2)}) collective-permute-start(f32[1152,128]{1,0:T(8,128)S(1)} %bitcast.21), channel_id=1, source_target_pairs={{0,1},{1,2},{2,3},{4,5},{5,6},{6,7},{8,9},{9,10},{10,11},{12,13},{... | collective-permute-start | bytes 1769480 | tf_op jit(solution)/shard_map/ppermute | solution.py:721
  47.9 11.6 %apply_twice.3 = (f32[1728,128]{1,0:T(8,128)}, f32[8,128]{1,0:T(8,128)}) custom-call(s32[2]{0:T(128)} %pad_add_fusion.place, f32[1152,128]{1,0:T(8,128)} %bitcast.23, f32[1152,128]{1,0:T(8,128)} %copy-done.9, f32[1152,128]{1,0:T(8,128)} %copy-done.8, f32[288,128]{1,0:T(8,128)} %broadcast_in_dim.90.scale, bf16[624,576]{1,0:T(8,128)(2,1)} %pad_maximum_fusion.to_even, ...), custom_call_target="tpu_custom_call" | custom-call | flops 2000000000 | bytes 6000000 | tf_op jit(solution)/shard_map/apply_twice/pallas_call | solution.py:537
  61.5 3.8 %all-to-all-start.2 = ((f32[8,216,128]{2,1,0:T(8,128)}), f32[8,216,128]{2,1,0:T(8,128)S(1)}, u32[]{:S(2)}, u32[]{:S(2)}) async-start(f32[8,216,128]{2,1,0:T(8,128)} %bitcast.18), calls=%async_computation.2 | async-start | bytes 1769472 | tf_op jit(solution)/shard_map/all_to_all | solution.py:712
  65.9 2.2 %part_component.3 = (f32[1152,128]{1,0:T(8,128)}, f32[864,128]{1,0:T(8,128)}, f32[864,128]{1,0:T(8,128)}) custom-call(s32[2]{0:T(128)} %pad_add_fusion.1.turns, f32[8,288,128]{2,1,0:T(8,128)} %copy-done.1, f32[8,128]{1,0:T(8,128)} %get-tuple-element.18.ready.refs_0_), custom_call_target="tpu_custom_call" | custom-call | flops 500000000 | bytes 1500000 | tf_op jit(solution)/shard_map/part_component/pallas_call | solution.py:241
  68.8 3.6 %collective-permute-start.7 = (f32[864,128]{1,0:T(8,128)}, f32[864,128]{1,0:T(8,128)S(1)}, u32[]{:S(2)}, u32[]{:S(2)}) collective-permute-start(f32[864,128]{1,0:T(8,128)} %get-tuple-element.24), channel_id=1, source_target_pairs={{0,1},{1,0},{2,3},{3,2},{4,5},{5,4},{6,7},{7,6},{8,9},{9,8},{10,11... | collective-permute-start | bytes 1327112 | tf_op jit(solution)/shard_map/ppermute | solution.py:716
  72.4 2.2 %part_component.2 = (f32[1152,128]{1,0:T(8,128)}, f32[864,128]{1,0:T(8,128)}, f32[864,128]{1,0:T(8,128)}) custom-call(s32[2]{0:T(128)} %pad_add_fusion.1.turns, f32[8,288,128]{2,1,0:T(8,128)} %copy-done.1, f32[8,128]{1,0:T(8,128)} %get-tuple-element.18.ready.refs_0_), custom_call_target="tpu_custom_call" | custom-call | flops 500000000 | bytes 1500000 | tf_op jit(solution)/shard_map/part_component/pallas_call | solution.py:241
  75.5 11.6 %apply_twice.4 = (f32[1728,128]{1,0:T(8,128)}, f32[8,128]{1,0:T(8,128)}) custom-call(s32[2]{0:T(128)} %pad_add_fusion.place, f32[1152,128]{1,0:T(8,128)} %get-tuple-element.22.own, f32[864,128]{1,0:T(8,128)} %copy-done.13, f32[864,128]{1,0:T(8,128)} %copy-done.15, f32[288,128]{1,0:T(8,128)} %broadcast_in_dim.90.scale, ...), custom_call_target="tpu_custom_call" | custom-call | flops 2000000000 | bytes 6000000 | tf_op jit(solution)/shard_map/apply_twice/pallas_call | solution.py:537
  88.9 4.4 %all-to-all-start.4 = ((f32[8,216,128]{2,1,0:T(8,128)}), f32[8,216,128]{2,1,0:T(8,128)S(1)}, u32[]{:S(2)}, u32[]{:S(2)}) async-start(f32[8,216,128]{2,1,0:T(8,128)} %bitcast.19), calls=%async_computation.4 | async-start | bytes 1769472 | tf_op jit(solution)/shard_map/all_to_all | solution.py:712
  94.2 6.9 %collective-permute-start.5 = (f32[864,128]{1,0:T(8,128)S(1)}, f32[864,128]{1,0:T(8,128)S(1)}, u32[]{:S(2)}, u32[]{:S(2)}) collective-permute-start(f32[864,128]{1,0:T(8,128)S(1)} %copy-done.10), channel_id=1, source_target_pairs={{0,1},{1,0},{2,3},{3,2},{4,5},{5,4},{6,7},{7,6},{8,9},{9,8},{10,11... | collective-permute-start | bytes 1327112 | tf_op jit(solution)/shard_map/ppermute | solution.py:716
  101.1 3.6 %unpack.2.refs_1_.refs_0_ = f32[2,36,3,8,128]{4,3,2,1,0:T(8,128)} custom-call(f32[1728,128]{1,0:T(8,128)} %bitcast.17), custom_call_target="tpu_custom_call" | custom-call | flops 3000000000 | bytes 9000000 | tf_op jit(solution)/shard_map/unpack/pallas_call | solution.py:589
  105.7 11.6 %apply_twice.5 = (f32[1728,128]{1,0:T(8,128)}, f32[8,128]{1,0:T(8,128)}) custom-call(s32[2]{0:T(128)} %pad_add_fusion.place, f32[1152,128]{1,0:T(8,128)} %get-tuple-element.19.refs_1_.own, f32[864,128]{1,0:T(8,128)} %copy-done.12, f32[864,128]{1,0:T(8,128)} %copy-done.14, f32[288,128]{1,0:T(8,128)} %broadcast_in_dim.90.scale, ...), custom_call_target="tpu_custom_call" | custom-call | flops 2000000000 | bytes 6000000 | tf_op jit(solution)/shard_map/apply_twice/pallas_call | solution.py:537
  117.2 6.0 %all-to-all-start.3 = ((f32[8,216,128]{2,1,0:T(8,128)}), f32[8,216,128]{2,1,0:T(8,128)S(1)}, u32[]{:S(2)}, u32[]{:S(2)}) async-start(f32[8,216,128]{2,1,0:T(8,128)} %bitcast.15), calls=%async_computation.3 | async-start | bytes 1769472 | tf_op jit(solution)/shard_map/all_to_all | solution.py:712
  123.2 2.5 %collective-permute-start.8 = (f32[8,128]{1,0:T(8,128)S(1)}, f32[8,128]{1,0:T(8,128)S(1)}, u32[]{:S(2)}, u32[]{:S(2)}) collective-permute-start(f32[8,128]{1,0:T(8,128)S(1)} %copy-done.7), channel_id=1, source_target_pairs={{0,1},{1,0},{2,3},{3,2},{4,5},{5,4},{6,7},{7,6},{8,9},{9,8},{10,11... | collective-permute-start | bytes 12296 | tf_op jit(solution)/shard_map/ppermute | solution.py:695
  128.2 2.0 %collective-permute-done.9 = f32[8,128]{1,0:T(8,128)S(1)} collective-permute-done((f32[8,128]{1,0:T(8,128)S(1)}, f32[8,128]{1,0:T(8,128)S(1)}, u32[]{:S(2)}, u32[]{:S(2)}) %collective-permute-start.9) | collective-permute-done | bytes 4128 | tf_op jit(solution)/shard_map/ppermute | solution.py:695
  133.9 3.8 %collective-permute-start.13 = (f32[8,128]{1,0:T(8,128)S(1)}, f32[8,128]{1,0:T(8,128)S(1)}, u32[]{:S(2)}, u32[]{:S(2)}) collective-permute-start(f32[8,128]{1,0:T(8,128)S(1)} %add.45), channel_id=1, source_target_pairs={{0,24},{4,28},{8,16},{12,20},{16,8},{20,12},{24,0},{28,4},{1,25},{... | collective-permute-start | bytes 12296 | tf_op jit(solution)/shard_map/ppermute | solution.py:697
  138.3 3.9 %collective-permute-done.13 = f32[8,128]{1,0:T(8,128)S(1)} collective-permute-done((f32[8,128]{1,0:T(8,128)S(1)}, f32[8,128]{1,0:T(8,128)S(1)}, u32[]{:S(2)}, u32[]{:S(2)}) %collective-permute-start.13) | collective-permute-done | bytes 4128 | tf_op jit(solution)/shard_map/ppermute | solution.py:697
  142.1 4.1 %collective-permute-done.12 = f32[8,128]{1,0:T(8,128)S(1)} collective-permute-done((f32[8,128]{1,0:T(8,128)S(1)}, f32[8,128]{1,0:T(8,128)S(1)}, u32[]{:S(2)}, u32[]{:S(2)}) %collective-permute-start.12) | collective-permute-done | bytes 4128 | tf_op jit(solution)/shard_map/ppermute | solution.py:697
  146.8 3.6 %unpack.3.refs_1_ = f32[2,36,3,8,128]{4,3,2,1,0:T(8,128)} custom-call(f32[1728,128]{1,0:T(8,128)} %bitcast.14), custom_call_target="tpu_custom_call" | custom-call | flops 3000000000 | bytes 9000000 | tf_op jit(solution)/shard_map/unpack/pallas_call | solution.py:589
  151.4 4.4 %finish.1 = (f32[36,3,3,8,128]{4,3,2,1,0:T(8,128)}, f32[36,3,3,8,128]{4,3,2,1,0:T(8,128)}) custom-call(f32[36,3,3,8,128]{4,3,2,1,0:T(8,128)} %field.5, f32[8,128]{1,0:T(8,128)} %add_add_fusion.total, f32[1728,128]{1,0:T(8,128)} %bitcast.16, f32[2,36,3,8,128]{4,3,2,1,0:T(8,128)} %unpack.2.refs_1_.refs_0_, f32[2,36,3,8,128]{4,3,2,1,0:T(8,128)} %unpack.3.refs_1_), custom_call_target="tpu_custom_call" | custom-call | flops 6000000000 | bytes 18000000 | tf_op jit(solution)/shard_map/finish/pallas_call | solution.py:640
  (86 shorter events, 36.5 us)
Async XLA Ops:
  3.9 17.7 %copy-start.6 = (s32[660,4]{0,1:T(4,128)S(1)}, s32[660,4]{0,1:T(4,128)}, u32[]{:S(2)}) copy-start(s32[660,4]{0,1:T(4,128)} %param.11) | copy-start | bytes 31684
  3.9 23.3 %all-to-all-start.1 = ((f32[8,144,128]{2,1,0:T(8,128)}), f32[8,144,128]{2,1,0:T(8,128)S(1)}, u32[]{:S(2)}, u32[]{:S(2)}) async-start(f32[8,144,128]{2,1,0:T(8,128)} %bitcast.13), calls=%async_computation.1 | async-start | bytes 1179648 | tf_op jit(solution)/shard_map/all_to_all | solution.py:712
  16.5 5.9 %collective-permute-start.3 = (f32[2,3,8,128]{3,2,1,0:T(8,128)}, f32[2,3,8,128]{3,2,1,0:T(8,128)S(1)}, u32[]{:S(2)}, u32[]{:S(2)}) collective-permute-start(f32[2,3,8,128]{3,2,1,0:T(8,128)} %get-tuple-element.17.both), channel_id=1, source_target_pairs={{1,0},{2,1},{3,2},{5,4},{6,5},{7,6},{9,8},{10,9},{11,10},{13,12},{... | collective-permute-start | bytes 73736 | tf_op jit(solution)/shard_map/ppermute | solution.py:725
  17.8 4.6 %collective-permute-start.2 = (f32[2,3,8,128]{3,2,1,0:T(8,128)}, f32[2,3,8,128]{3,2,1,0:T(8,128)S(1)}, u32[]{:S(2)}, u32[]{:S(2)}) collective-permute-start(f32[2,3,8,128]{3,2,1,0:T(8,128)} %get-tuple-element.17.both), channel_id=1, source_target_pairs={{0,1},{1,2},{2,3},{4,5},{5,6},{6,7},{8,9},{9,10},{10,11},{12,13},{... | collective-permute-start | bytes 73736 | tf_op jit(solution)/shard_map/ppermute | solution.py:724
  27.1 8.9 %copy-start.5 = (f32[8,144,128]{2,1,0:T(8,128)}, f32[8,144,128]{2,1,0:T(8,128)S(1)}, u32[]{:S(2)}) copy-start(f32[8,144,128]{2,1,0:T(8,128)S(1)} %all-to-all-done.1) | copy-start | bytes 1769476
  27.2 34.3 %all-to-all-start = ((f32[8,288,128]{2,1,0:T(8,128)}), f32[8,288,128]{2,1,0:T(8,128)S(1)}, u32[]{:S(2)}, u32[]{:S(2)}) async-start(f32[8,288,128]{2,1,0:T(8,128)} %bitcast.4), calls=%async_computation | async-start | bytes 2359296 | tf_op jit(solution)/shard_map/all_to_all | solution.py:712
  31.3 15.5 %collective-permute-start.1 = (f32[1152,128]{1,0:T(8,128)S(1)}, f32[1152,128]{1,0:T(8,128)S(1)}, u32[]{:S(2)}, u32[]{:S(2)}) collective-permute-start(f32[1152,128]{1,0:T(8,128)S(1)} %bitcast.20), channel_id=1, source_target_pairs={{1,0},{2,1},{3,2},{5,4},{6,5},{7,6},{9,8},{10,9},{11,10},{13,12},{... | collective-permute-start | bytes 1769480 | tf_op jit(solution)/shard_map/ppermute | solution.py:721
  32.6 14.2 %collective-permute-start = (f32[1152,128]{1,0:T(8,128)S(1)}, f32[1152,128]{1,0:T(8,128)S(1)}, u32[]{:S(2)}, u32[]{:S(2)}) collective-permute-start(f32[1152,128]{1,0:T(8,128)S(1)} %bitcast.21), channel_id=1, source_target_pairs={{0,1},{1,2},{2,3},{4,5},{5,6},{6,7},{8,9},{9,10},{10,11},{12,13},{... | collective-permute-start | bytes 1769480 | tf_op jit(solution)/shard_map/ppermute | solution.py:721
  61.5 27.4 %all-to-all-start.2 = ((f32[8,216,128]{2,1,0:T(8,128)}), f32[8,216,128]{2,1,0:T(8,128)S(1)}, u32[]{:S(2)}, u32[]{:S(2)}) async-start(f32[8,216,128]{2,1,0:T(8,128)} %bitcast.18), calls=%async_computation.2 | async-start | bytes 1769472 | tf_op jit(solution)/shard_map/all_to_all | solution.py:712
  68.1 6.5 %collective-permute-start.6 = (f32[864,128]{1,0:T(8,128)}, f32[864,128]{1,0:T(8,128)S(1)}, u32[]{:S(2)}, u32[]{:S(2)}) collective-permute-start(f32[864,128]{1,0:T(8,128)} %get-tuple-element.23), channel_id=1, source_target_pairs={{1,2},{2,1},{5,6},{6,5},{9,10},{10,9},{13,14},{14,13},{17,18},{18,... | collective-permute-start | bytes 1327112 | tf_op jit(solution)/shard_map/ppermute | solution.py:715
  68.8 5.8 %collective-permute-start.7 = (f32[864,128]{1,0:T(8,128)}, f32[864,128]{1,0:T(8,128)S(1)}, u32[]{:S(2)}, u32[]{:S(2)}) collective-permute-start(f32[864,128]{1,0:T(8,128)} %get-tuple-element.24), channel_id=1, source_target_pairs={{0,1},{1,0},{2,3},{3,2},{4,5},{5,4},{6,7},{7,6},{8,9},{9,8},{10,11... | collective-permute-start | bytes 1327112 | tf_op jit(solution)/shard_map/ppermute | solution.py:716
  87.1 7.1 %copy-start.10 = (f32[864,128]{1,0:T(8,128)S(1)}, f32[864,128]{1,0:T(8,128)}, u32[]{:S(2)}) copy-start(f32[864,128]{1,0:T(8,128)} %get-tuple-element.21) | copy-start | bytes 1327108
  88.9 12.2 %copy-start.4 = (f32[8,216,128]{2,1,0:T(8,128)}, f32[8,216,128]{2,1,0:T(8,128)S(1)}, u32[]{:S(2)}) copy-start(f32[8,216,128]{2,1,0:T(8,128)S(1)} %all-to-all-done.2) | copy-start | bytes 2654212
  88.9 28.3 %all-to-all-start.4 = ((f32[8,216,128]{2,1,0:T(8,128)}), f32[8,216,128]{2,1,0:T(8,128)S(1)}, u32[]{:S(2)}, u32[]{:S(2)}) async-start(f32[8,216,128]{2,1,0:T(8,128)} %bitcast.19), calls=%async_computation.4 | async-start | bytes 1769472 | tf_op jit(solution)/shard_map/all_to_all | solution.py:712
  93.3 11.4 %collective-permute-start.4 = (f32[864,128]{1,0:T(8,128)S(1)}, f32[864,128]{1,0:T(8,128)S(1)}, u32[]{:S(2)}, u32[]{:S(2)}) collective-permute-start(f32[864,128]{1,0:T(8,128)S(1)} %copy-done.11), channel_id=1, source_target_pairs={{1,2},{2,1},{5,6},{6,5},{9,10},{10,9},{13,14},{14,13},{17,18},{18,... | collective-permute-start | bytes 1327112 | tf_op jit(solution)/shard_map/ppermute | solution.py:715
  94.2 10.5 %collective-permute-start.5 = (f32[864,128]{1,0:T(8,128)S(1)}, f32[864,128]{1,0:T(8,128)S(1)}, u32[]{:S(2)}, u32[]{:S(2)}) collective-permute-start(f32[864,128]{1,0:T(8,128)S(1)} %copy-done.10), channel_id=1, source_target_pairs={{0,1},{1,0},{2,3},{3,2},{4,5},{5,4},{6,7},{7,6},{8,9},{9,8},{10,11... | collective-permute-start | bytes 1327112 | tf_op jit(solution)/shard_map/ppermute | solution.py:716
  117.2 29.6 %copy-start.2 = (f32[8,216,128]{2,1,0:T(8,128)}, f32[8,216,128]{2,1,0:T(8,128)S(1)}, u32[]{:S(2)}) copy-start(f32[8,216,128]{2,1,0:T(8,128)S(1)} %all-to-all-done.4) | copy-start | bytes 2654212
  117.2 33.2 %all-to-all-start.3 = ((f32[8,216,128]{2,1,0:T(8,128)}), f32[8,216,128]{2,1,0:T(8,128)S(1)}, u32[]{:S(2)}, u32[]{:S(2)}) async-start(f32[8,216,128]{2,1,0:T(8,128)} %bitcast.15), calls=%async_computation.3 | async-start | bytes 1769472 | tf_op jit(solution)/shard_map/all_to_all | solution.py:712
  123.2 3.3 %collective-permute-start.8 = (f32[8,128]{1,0:T(8,128)S(1)}, f32[8,128]{1,0:T(8,128)S(1)}, u32[]{:S(2)}, u32[]{:S(2)}) collective-permute-start(f32[8,128]{1,0:T(8,128)S(1)} %copy-done.7), channel_id=1, source_target_pairs={{0,1},{1,0},{2,3},{3,2},{4,5},{5,4},{6,7},{7,6},{8,9},{9,8},{10,11... | collective-permute-start | bytes 12296 | tf_op jit(solution)/shard_map/ppermute | solution.py:695
  126.6 3.6 %collective-permute-start.9 = (f32[8,128]{1,0:T(8,128)S(1)}, f32[8,128]{1,0:T(8,128)S(1)}, u32[]{:S(2)}, u32[]{:S(2)}) collective-permute-start(f32[8,128]{1,0:T(8,128)S(1)} %add.43), channel_id=1, source_target_pairs={{0,2},{1,3},{2,0},{3,1},{4,6},{5,7},{6,4},{7,5},{8,10},{9,11},{10,... | collective-permute-start | bytes 12296 | tf_op jit(solution)/shard_map/ppermute | solution.py:695
  130.2 3.6 %collective-permute-start.10 = (f32[8,128]{1,0:T(8,128)S(1)}, f32[8,128]{1,0:T(8,128)S(1)}, u32[]{:S(2)}, u32[]{:S(2)}) collective-permute-start(f32[8,128]{1,0:T(8,128)S(1)} %add.44), channel_id=1, source_target_pairs={{0,4},{4,0},{8,12},{12,8},{16,20},{20,16},{24,28},{28,24},{1,5},{5... | collective-permute-start | bytes 12296 | tf_op jit(solution)/shard_map/ppermute | solution.py:695
  133.9 8.3 %collective-permute-start.13 = (f32[8,128]{1,0:T(8,128)S(1)}, f32[8,128]{1,0:T(8,128)S(1)}, u32[]{:S(2)}, u32[]{:S(2)}) collective-permute-start(f32[8,128]{1,0:T(8,128)S(1)} %add.45), channel_id=1, source_target_pairs={{0,24},{4,28},{8,16},{12,20},{16,8},{20,12},{24,0},{28,4},{1,25},{... | collective-permute-start | bytes 12296 | tf_op jit(solution)/shard_map/ppermute | solution.py:697
  137.7 8.5 %collective-permute-start.12 = (f32[8,128]{1,0:T(8,128)S(1)}, f32[8,128]{1,0:T(8,128)S(1)}, u32[]{:S(2)}, u32[]{:S(2)}) collective-permute-start(f32[8,128]{1,0:T(8,128)S(1)} %add.45), channel_id=1, source_target_pairs={{0,16},{4,20},{8,24},{12,28},{16,0},{20,4},{24,8},{28,12},{1,17},{... | collective-permute-start | bytes 12296 | tf_op jit(solution)/shard_map/ppermute | solution.py:697
  137.7 8.5 %collective-permute-start.11 = (f32[8,128]{1,0:T(8,128)S(1)}, f32[8,128]{1,0:T(8,128)S(1)}, u32[]{:S(2)}, u32[]{:S(2)}) collective-permute-start(f32[8,128]{1,0:T(8,128)S(1)} %add.45), channel_id=1, source_target_pairs={{0,8},{4,12},{8,0},{12,4},{16,24},{20,28},{24,16},{28,20},{1,9},{5... | collective-permute-start | bytes 12296 | tf_op jit(solution)/shard_map/ppermute | solution.py:697
  (13 other events, 28.7 us)

commit v13 on v12

--- a/solution.py
+++ b/solution.py
@@ -600,8 +600,8 @@
 STEPS = 2
 
 
-def finish_kernel(field, total, image, *refs):
-    *natural, solution_field, residual, factors = refs
+def finish_kernel(field, total, natural, *refs):
+    *images, solution_field, residual, factors = refs
     modes = field.shape[0]
     per_part = STEPS * modes * 2 * SLAB
 
@@ -620,9 +620,10 @@
             for comp in range(COMPS):
                 for p in range(SLAB):
                     b = field[mode, comp, p]
-                    if comp < len(natural):
-                        q, w = natural[comp][0, mode, p], natural[comp][1, mode, p]
+                    if comp == 0:
+                        q, w = natural[0, mode, p], natural[1, mode, p]
                     else:
+                        image = images[comp - 1]
                         row = (first + mode) * 2 * SLAB + p
                         q = swap_back(image[pl.ds(row, PARTS, stride=per_part), :])
                         w = swap_back(image[pl.ds(row + SLAB, PARTS, stride=per_part), :])
@@ -633,7 +634,7 @@
     lax.fori_loop(0, modes // (2 * UNROLL), body, 0)
 
 
-def finish(field, total, image, *natural):
+def finish(field, total, natural, *images):
     rows = field.shape[0] // STEPS
     block = pl.BlockSpec((rows,) + field.shape[1:], lambda i: (i, 0, 0, 0, 0))
     vmem = pl.BlockSpec(memory_space=pltpu.VMEM)
@@ -641,14 +642,14 @@
         finish_kernel,
         grid=(STEPS,),
         out_shape=[jax.ShapeDtypeStruct(field.shape, jnp.float32)] * 2,
-        in_specs=[block, vmem, vmem]
-        + [pl.BlockSpec((2, rows) + field.shape[2:], lambda i: (0, i, 0, 0, 0))] * len(natural),
+        in_specs=[block, vmem, pl.BlockSpec((2, rows) + field.shape[2:], lambda i: (0, i, 0, 0, 0))]
+        + [vmem] * len(images),
         out_specs=[block, block],
         scratch_shapes=[pltpu.VMEM((16, LANES), jnp.float32)],
         compiler_params=pltpu.CompilerParams(vmem_limit_bytes=VMEM),
         cost_estimate=estimate(6),
         name="finish",
-    )(field, total, image, *natural)
+    )(field, total, natural, *images)
 
 
 def mode_tables(coupling_table, slots):
@@ -731,11 +732,10 @@
     modes = right_side.shape[0]
     image, partial = apply_twice(1, place, *halos[0], tables, fields, fibre_weights, (partial,), parts[1][:1])
     images.append(swap(image))
-    natural = [unpack(images[0], modes)]
-    image, partial = apply_twice(2, place, *halos[1], tables, fields, fibre_weights, (partial,), natural)
+    natural = unpack(images[0], modes)
+    image, partial = apply_twice(2, place, *halos[1], tables, fields, fibre_weights, (partial,), (natural,))
     images.append(swap(image))
-    natural.append(unpack(images[1], modes))
-    return tuple(finish(right_side, all_sum(partial), images[2], *natural))
+    return tuple(finish(right_side, all_sum(partial), natural, *images[1:]))
 
 
 def on_device(right_side, mean_stiffness, ply_stiffness, fibre_weights, ply_map, coupling_table):

time: 158 us -> 155 us (0.981)
  Pallas kernels: 62.8 us -> 60.1 us
    pallas_call x2 -> x1, Pallas kernels: 7.22 us -> 3.61 us  [unpack(): pl.pallas_call(unpack_kernel, out_shape=jax.ShapeDtypeStruct((2, modes, S...]
  transfers between devices with their start and end apart: 19 -> 19, of which waited for: 8 -> 8; matrix products, arithmetic and copies ran while one was open for 8% -> 8% of each run, Pallas kernels for 35% -> 34%
where the time goes in v13:
time: 155 us; the launch traced here: 153 us
  Pallas kernels  60.1 us (39%)
  starting transfers between devices  57 us (37%)
  waiting for transfers between devices  18.4 us (12%)
  local copies, waits for them, and re-layouts  7.86 us (5%)
  other arithmetic  7.11 us (5%)
  matrix products  1.8 us (1%)
    pallas_call x3, Pallas kernels, apply_twice(): pl.pallas_call(functools.partial(apply_kernel, comp=comp), out_shape=[jax...  34.8 us
    all_to_all x5, starting transfers between devices, swap(): return lax.all_to_all(rows, 'mode', 0, 0, tiled=True)  25.7 us
    ppermute x2, starting transfers between devices, halo(): lax.ppermute(beside, 'space', [(0, 1), (1, 0), (2, 3), (3, 2)])  10.5 us
    pallas_call x2, Pallas kernels, pack(): pl.pallas_call(functools.partial(pack_kernel, comps=comps), grid=(1,), ou...  8.51 us
    ppermute x3, waiting for transfers between devices, all_sum(): lax.ppermute(value, 'mode', [(i, i ^ bit) for i in range(PARTS)])  7.95 us
    ppermute x3, starting transfers between devices, all_sum(): lax.ppermute(value, axis, [(i, i ^ bit) for i in range(devices)])  5.76 us
    all_to_all x5, waiting for transfers between devices, swap(): return lax.all_to_all(rows, 'mode', 0, 0, tiled=True)  5.56 us
    pallas_call x1, Pallas kernels, finish(): pl.pallas_call(finish_kernel, grid=(STEPS,), out_shape=[jax.ShapeDtypeStr...  5.37 us
  transfers between devices with their start and end apart: 19, of which 8 were waited for; matrix products, arithmetic and copies ran while one was open for 8% of the time, Pallas kernels for 34%

profile of v13, /device:TPU:0, one launch (start us, length us, event | category | flops | bytes accessed | tf_op | source)
XLA Modules:
  0.0 153.1 jit_solution(14591982189718901501)
XLA Ops:
  0.6 3.2 %pack.2.refs_2_ = f32[1152,128]{1,0:T(8,128)} custom-call(f32[36,3,3,8,128]{4,3,2,1,0:T(8,128)} %field.5), custom_call_target="tpu_custom_call" | custom-call | flops 500000000 | bytes 1500000 | tf_op jit(solution)/shard_map/pack/pallas_call | solution.py:208
  3.9 7.4 %all-to-all-start.1 = ((f32[8,144,128]{2,1,0:T(8,128)}), f32[8,144,128]{2,1,0:T(8,128)S(1)}, u32[]{:S(2)}, u32[]{:S(2)}) async-start(f32[8,144,128]{2,1,0:T(8,128)} %bitcast.13), calls=%async_computation.1 | async-start | bytes 1179648 | tf_op jit(solution)/shard_map/all_to_all | solution.py:713
  11.3 5.3 %pack.3 = (f32[2,3,8,128]{3,2,1,0:T(8,128)}, f32[2304,128]{1,0:T(8,128)}) custom-call(f32[36,3,3,8,128]{4,3,2,1,0:T(8,128)} %field.5, f32[3,8,128]{2,1,0:T(8,128)} %refs_0_.1, s32[3,8,128]{2,1,0:T(8,128)} %refs_1_.1, f32[1152,128]{1,0:T(8,128)} %pack.2.refs_2_), custom_call_target="tpu_custom_call" | custom-call | flops 500000000 | bytes 1500000 | tf_op jit(solution)/shard_map/pack/pallas_call | solution.py:208
  17.8 3.0 %collective-permute-start.2 = (f32[2,3,8,128]{3,2,1,0:T(8,128)}, f32[2,3,8,128]{3,2,1,0:T(8,128)S(1)}, u32[]{:S(2)}, u32[]{:S(2)}) collective-permute-start(f32[2,3,8,128]{3,2,1,0:T(8,128)} %get-tuple-element.17.both), channel_id=1, source_target_pairs={{0,1},{1,2},{2,3},{4,5},{5,6},{6,7},{8,9},{9,10},{10,11},{12,13},{... | collective-permute-start | bytes 73736 | tf_op jit(solution)/shard_map/ppermute | solution.py:725
  27.2 4.2 %all-to-all-start = ((f32[8,288,128]{2,1,0:T(8,128)}), f32[8,288,128]{2,1,0:T(8,128)S(1)}, u32[]{:S(2)}, u32[]{:S(2)}) async-start(f32[8,288,128]{2,1,0:T(8,128)} %bitcast.4), calls=%async_computation | async-start | bytes 2359296 | tf_op jit(solution)/shard_map/all_to_all | solution.py:713
  32.6 3.4 %collective-permute-start = (f32[1152,128]{1,0:T(8,128)S(1)}, f32[1152,128]{1,0:T(8,128)S(1)}, u32[]{:S(2)}, u32[]{:S(2)}) collective-permute-start(f32[1152,128]{1,0:T(8,128)S(1)} %bitcast.21), channel_id=1, source_target_pairs={{0,1},{1,2},{2,3},{4,5},{5,6},{6,7},{8,9},{9,10},{10,11},{12,13},{... | collective-permute-start | bytes 1769480 | tf_op jit(solution)/shard_map/ppermute | solution.py:722
  47.9 11.6 %apply_twice.3 = (f32[1728,128]{1,0:T(8,128)}, f32[8,128]{1,0:T(8,128)}) custom-call(s32[2]{0:T(128)} %pad_add_fusion.place, f32[1152,128]{1,0:T(8,128)} %bitcast.23, f32[1152,128]{1,0:T(8,128)} %copy-done.9, f32[1152,128]{1,0:T(8,128)} %copy-done.8, f32[288,128]{1,0:T(8,128)} %broadcast_in_dim.90.scale, bf16[624,576]{1,0:T(8,128)(2,1)} %pad_maximum_fusion.to_even, ...), custom_call_target="tpu_custom_call" | custom-call | flops 2000000000 | bytes 6000000 | tf_op jit(solution)/shard_map/apply_twice/pallas_call | solution.py:537
  61.5 3.8 %all-to-all-start.2 = ((f32[8,216,128]{2,1,0:T(8,128)}), f32[8,216,128]{2,1,0:T(8,128)S(1)}, u32[]{:S(2)}, u32[]{:S(2)}) async-start(f32[8,216,128]{2,1,0:T(8,128)} %bitcast.18), calls=%async_computation.2 | async-start | bytes 1769472 | tf_op jit(solution)/shard_map/all_to_all | solution.py:713
  65.9 2.2 %part_component.3 = (f32[1152,128]{1,0:T(8,128)}, f32[864,128]{1,0:T(8,128)}, f32[864,128]{1,0:T(8,128)}) custom-call(s32[2]{0:T(128)} %pad_add_fusion.1.turns, f32[8,288,128]{2,1,0:T(8,128)} %copy-done.1, f32[8,128]{1,0:T(8,128)} %get-tuple-element.18.ready.refs_0_), custom_call_target="tpu_custom_call" | custom-call | flops 500000000 | bytes 1500000 | tf_op jit(solution)/shard_map/part_component/pallas_call | solution.py:241
  68.8 3.6 %collective-permute-start.7 = (f32[864,128]{1,0:T(8,128)}, f32[864,128]{1,0:T(8,128)S(1)}, u32[]{:S(2)}, u32[]{:S(2)}) collective-permute-start(f32[864,128]{1,0:T(8,128)} %get-tuple-element.24), channel_id=1, source_target_pairs={{0,1},{1,0},{2,3},{3,2},{4,5},{5,4},{6,7},{7,6},{8,9},{9,8},{10,11... | collective-permute-start | bytes 1327112 | tf_op jit(solution)/shard_map/ppermute | solution.py:717
  72.4 2.2 %part_component.2 = (f32[1152,128]{1,0:T(8,128)}, f32[864,128]{1,0:T(8,128)}, f32[864,128]{1,0:T(8,128)}) custom-call(s32[2]{0:T(128)} %pad_add_fusion.1.turns, f32[8,288,128]{2,1,0:T(8,128)} %copy-done.1, f32[8,128]{1,0:T(8,128)} %get-tuple-element.18.ready.refs_0_), custom_call_target="tpu_custom_call" | custom-call | flops 500000000 | bytes 1500000 | tf_op jit(solution)/shard_map/part_component/pallas_call | solution.py:241
  75.5 11.6 %apply_twice.4 = (f32[1728,128]{1,0:T(8,128)}, f32[8,128]{1,0:T(8,128)}) custom-call(s32[2]{0:T(128)} %pad_add_fusion.place, f32[1152,128]{1,0:T(8,128)} %get-tuple-element.22.own, f32[864,128]{1,0:T(8,128)} %copy-done.13, f32[864,128]{1,0:T(8,128)} %copy-done.15, f32[288,128]{1,0:T(8,128)} %broadcast_in_dim.90.scale, ...), custom_call_target="tpu_custom_call" | custom-call | flops 2000000000 | bytes 6000000 | tf_op jit(solution)/shard_map/apply_twice/pallas_call | solution.py:537
  88.9 4.4 %all-to-all-start.3 = ((f32[8,216,128]{2,1,0:T(8,128)}), f32[8,216,128]{2,1,0:T(8,128)S(1)}, u32[]{:S(2)}, u32[]{:S(2)}) async-start(f32[8,216,128]{2,1,0:T(8,128)} %bitcast.19), calls=%async_computation.3 | async-start | bytes 1769472 | tf_op jit(solution)/shard_map/all_to_all | solution.py:713
  94.2 6.9 %collective-permute-start.5 = (f32[864,128]{1,0:T(8,128)S(1)}, f32[864,128]{1,0:T(8,128)S(1)}, u32[]{:S(2)}, u32[]{:S(2)}) collective-permute-start(f32[864,128]{1,0:T(8,128)S(1)} %copy-done.10), channel_id=1, source_target_pairs={{0,1},{1,0},{2,3},{3,2},{4,5},{5,4},{6,7},{7,6},{8,9},{9,8},{10,11... | collective-permute-start | bytes 1327112 | tf_op jit(solution)/shard_map/ppermute | solution.py:717
  101.1 3.6 %unpack.1.refs_1_.natural = f32[2,36,3,8,128]{4,3,2,1,0:T(8,128)} custom-call(f32[1728,128]{1,0:T(8,128)} %bitcast.17), custom_call_target="tpu_custom_call" | custom-call | flops 3000000000 | bytes 9000000 | tf_op jit(solution)/shard_map/unpack/pallas_call | solution.py:589
  105.7 11.6 %apply_twice.5 = (f32[1728,128]{1,0:T(8,128)}, f32[8,128]{1,0:T(8,128)}) custom-call(s32[2]{0:T(128)} %pad_add_fusion.place, f32[1152,128]{1,0:T(8,128)} %get-tuple-element.19.refs_1_.own, f32[864,128]{1,0:T(8,128)} %copy-done.12, f32[864,128]{1,0:T(8,128)} %copy-done.14, f32[288,128]{1,0:T(8,128)} %broadcast_in_dim.90.scale, ...), custom_call_target="tpu_custom_call" | custom-call | flops 2000000000 | bytes 6000000 | tf_op jit(solution)/shard_map/apply_twice/pallas_call | solution.py:537
  117.2 6.0 %all-to-all-start.4 = ((f32[8,216,128]{2,1,0:T(8,128)}), f32[8,216,128]{2,1,0:T(8,128)S(1)}, u32[]{:S(2)}, u32[]{:S(2)}) async-start(f32[8,216,128]{2,1,0:T(8,128)} %bitcast.15), calls=%async_computation.4 | async-start | bytes 1769472 | tf_op jit(solution)/shard_map/all_to_all | solution.py:713
  123.2 2.5 %collective-permute-start.8 = (f32[8,128]{1,0:T(8,128)S(1)}, f32[8,128]{1,0:T(8,128)S(1)}, u32[]{:S(2)}, u32[]{:S(2)}) collective-permute-start(f32[8,128]{1,0:T(8,128)S(1)} %copy-done.7), channel_id=1, source_target_pairs={{0,1},{1,0},{2,3},{3,2},{4,5},{5,4},{6,7},{7,6},{8,9},{9,8},{10,11... | collective-permute-start | bytes 12296 | tf_op jit(solution)/shard_map/ppermute | solution.py:696
  128.2 2.0 %collective-permute-done.9 = f32[8,128]{1,0:T(8,128)S(1)} collective-permute-done((f32[8,128]{1,0:T(8,128)S(1)}, f32[8,128]{1,0:T(8,128)S(1)}, u32[]{:S(2)}, u32[]{:S(2)}) %collective-permute-start.9) | collective-permute-done | bytes 4128 | tf_op jit(solution)/shard_map/ppermute | solution.py:696
  131.9 2.0 %collective-permute-done.10 = f32[8,128]{1,0:T(8,128)S(1)} collective-permute-done((f32[8,128]{1,0:T(8,128)S(1)}, f32[8,128]{1,0:T(8,128)S(1)}, u32[]{:S(2)}, u32[]{:S(2)}) %collective-permute-start.10) | collective-permute-done | bytes 4128 | tf_op jit(solution)/shard_map/ppermute | solution.py:696
  133.9 3.8 %collective-permute-start.13 = (f32[8,128]{1,0:T(8,128)S(1)}, f32[8,128]{1,0:T(8,128)S(1)}, u32[]{:S(2)}, u32[]{:S(2)}) collective-permute-start(f32[8,128]{1,0:T(8,128)S(1)} %add.45), channel_id=1, source_target_pairs={{0,24},{4,28},{8,16},{12,20},{16,8},{20,12},{24,0},{28,4},{1,25},{... | collective-permute-start | bytes 12296 | tf_op jit(solution)/shard_map/ppermute | solution.py:698
  138.3 3.9 %collective-permute-done.13 = f32[8,128]{1,0:T(8,128)S(1)} collective-permute-done((f32[8,128]{1,0:T(8,128)S(1)}, f32[8,128]{1,0:T(8,128)S(1)}, u32[]{:S(2)}, u32[]{:S(2)}) %collective-permute-start.13) | collective-permute-done | bytes 4128 | tf_op jit(solution)/shard_map/ppermute | solution.py:698
  142.1 4.1 %collective-permute-done.12 = f32[8,128]{1,0:T(8,128)S(1)} collective-permute-done((f32[8,128]{1,0:T(8,128)S(1)}, f32[8,128]{1,0:T(8,128)S(1)}, u32[]{:S(2)}, u32[]{:S(2)}) %collective-permute-start.12) | collective-permute-done | bytes 4128 | tf_op jit(solution)/shard_map/ppermute | solution.py:698
  147.7 5.4 %finish.1 = (f32[36,3,3,8,128]{4,3,2,1,0:T(8,128)}, f32[36,3,3,8,128]{4,3,2,1,0:T(8,128)}) custom-call(f32[36,3,3,8,128]{4,3,2,1,0:T(8,128)} %field.5, f32[8,128]{1,0:T(8,128)} %add_add_fusion.total, f32[2,36,3,8,128]{4,3,2,1,0:T(8,128)} %unpack.1.refs_1_.natural, f32[1728,128]{1,0:T(8,128)} %bitcast.14, f32[1728,128]{1,0:T(8,128)} %bitcast.16), custom_call_target="tpu_custom_call" | custom-call | flops 6000000000 | bytes 18000000 | tf_op jit(solution)/shard_map/finish/pallas_call | solution.py:641
  (85 shorter events, 34.5 us)
Async XLA Ops:
  3.9 17.7 %copy-start.6 = (s32[660,4]{0,1:T(4,128)S(1)}, s32[660,4]{0,1:T(4,128)}, u32[]{:S(2)}) copy-start(s32[660,4]{0,1:T(4,128)} %param.11) | copy-start | bytes 31684
  3.9 23.3 %all-to-all-start.1 = ((f32[8,144,128]{2,1,0:T(8,128)}), f32[8,144,128]{2,1,0:T(8,128)S(1)}, u32[]{:S(2)}, u32[]{:S(2)}) async-start(f32[8,144,128]{2,1,0:T(8,128)} %bitcast.13), calls=%async_computation.1 | async-start | bytes 1179648 | tf_op jit(solution)/shard_map/all_to_all | solution.py:713
  16.5 5.9 %collective-permute-start.3 = (f32[2,3,8,128]{3,2,1,0:T(8,128)}, f32[2,3,8,128]{3,2,1,0:T(8,128)S(1)}, u32[]{:S(2)}, u32[]{:S(2)}) collective-permute-start(f32[2,3,8,128]{3,2,1,0:T(8,128)} %get-tuple-element.17.both), channel_id=1, source_target_pairs={{1,0},{2,1},{3,2},{5,4},{6,5},{7,6},{9,8},{10,9},{11,10},{13,12},{... | collective-permute-start | bytes 73736 | tf_op jit(solution)/shard_map/ppermute | solution.py:726
  17.8 4.6 %collective-permute-start.2 = (f32[2,3,8,128]{3,2,1,0:T(8,128)}, f32[2,3,8,128]{3,2,1,0:T(8,128)S(1)}, u32[]{:S(2)}, u32[]{:S(2)}) collective-permute-start(f32[2,3,8,128]{3,2,1,0:T(8,128)} %get-tuple-element.17.both), channel_id=1, source_target_pairs={{0,1},{1,2},{2,3},{4,5},{5,6},{6,7},{8,9},{9,10},{10,11},{12,13},{... | collective-permute-start | bytes 73736 | tf_op jit(solution)/shard_map/ppermute | solution.py:725
  27.1 8.9 %copy-start.5 = (f32[8,144,128]{2,1,0:T(8,128)}, f32[8,144,128]{2,1,0:T(8,128)S(1)}, u32[]{:S(2)}) copy-start(f32[8,144,128]{2,1,0:T(8,128)S(1)} %all-to-all-done.1) | copy-start | bytes 1769476
  27.2 34.3 %all-to-all-start = ((f32[8,288,128]{2,1,0:T(8,128)}), f32[8,288,128]{2,1,0:T(8,128)S(1)}, u32[]{:S(2)}, u32[]{:S(2)}) async-start(f32[8,288,128]{2,1,0:T(8,128)} %bitcast.4), calls=%async_computation | async-start | bytes 2359296 | tf_op jit(solution)/shard_map/all_to_all | solution.py:713
  31.3 15.5 %collective-permute-start.1 = (f32[1152,128]{1,0:T(8,128)S(1)}, f32[1152,128]{1,0:T(8,128)S(1)}, u32[]{:S(2)}, u32[]{:S(2)}) collective-permute-start(f32[1152,128]{1,0:T(8,128)S(1)} %bitcast.20), channel_id=1, source_target_pairs={{1,0},{2,1},{3,2},{5,4},{6,5},{7,6},{9,8},{10,9},{11,10},{13,12},{... | collective-permute-start | bytes 1769480 | tf_op jit(solution)/shard_map/ppermute | solution.py:722
  32.6 14.2 %collective-permute-start = (f32[1152,128]{1,0:T(8,128)S(1)}, f32[1152,128]{1,0:T(8,128)S(1)}, u32[]{:S(2)}, u32[]{:S(2)}) collective-permute-start(f32[1152,128]{1,0:T(8,128)S(1)} %bitcast.21), channel_id=1, source_target_pairs={{0,1},{1,2},{2,3},{4,5},{5,6},{6,7},{8,9},{9,10},{10,11},{12,13},{... | collective-permute-start | bytes 1769480 | tf_op jit(solution)/shard_map/ppermute | solution.py:722
  61.5 27.4 %all-to-all-start.2 = ((f32[8,216,128]{2,1,0:T(8,128)}), f32[8,216,128]{2,1,0:T(8,128)S(1)}, u32[]{:S(2)}, u32[]{:S(2)}) async-start(f32[8,216,128]{2,1,0:T(8,128)} %bitcast.18), calls=%async_computation.2 | async-start | bytes 1769472 | tf_op jit(solution)/shard_map/all_to_all | solution.py:713
  68.1 6.5 %collective-permute-start.6 = (f32[864,128]{1,0:T(8,128)}, f32[864,128]{1,0:T(8,128)S(1)}, u32[]{:S(2)}, u32[]{:S(2)}) collective-permute-start(f32[864,128]{1,0:T(8,128)} %get-tuple-element.23), channel_id=1, source_target_pairs={{1,2},{2,1},{5,6},{6,5},{9,10},{10,9},{13,14},{14,13},{17,18},{18,... | collective-permute-start | bytes 1327112 | tf_op jit(solution)/shard_map/ppermute | solution.py:716
  68.8 5.8 %collective-permute-start.7 = (f32[864,128]{1,0:T(8,128)}, f32[864,128]{1,0:T(8,128)S(1)}, u32[]{:S(2)}, u32[]{:S(2)}) collective-permute-start(f32[864,128]{1,0:T(8,128)} %get-tuple-element.24), channel_id=1, source_target_pairs={{0,1},{1,0},{2,3},{3,2},{4,5},{5,4},{6,7},{7,6},{8,9},{9,8},{10,11... | collective-permute-start | bytes 1327112 | tf_op jit(solution)/shard_map/ppermute | solution.py:717
  87.1 7.1 %copy-start.10 = (f32[864,128]{1,0:T(8,128)S(1)}, f32[864,128]{1,0:T(8,128)}, u32[]{:S(2)}) copy-start(f32[864,128]{1,0:T(8,128)} %get-tuple-element.21) | copy-start | bytes 1327108
  88.9 12.2 %copy-start.4 = (f32[8,216,128]{2,1,0:T(8,128)}, f32[8,216,128]{2,1,0:T(8,128)S(1)}, u32[]{:S(2)}) copy-start(f32[8,216,128]{2,1,0:T(8,128)S(1)} %all-to-all-done.2) | copy-start | bytes 2654212
  88.9 28.3 %all-to-all-start.3 = ((f32[8,216,128]{2,1,0:T(8,128)}), f32[8,216,128]{2,1,0:T(8,128)S(1)}, u32[]{:S(2)}, u32[]{:S(2)}) async-start(f32[8,216,128]{2,1,0:T(8,128)} %bitcast.19), calls=%async_computation.3 | async-start | bytes 1769472 | tf_op jit(solution)/shard_map/all_to_all | solution.py:713
  93.3 11.4 %collective-permute-start.4 = (f32[864,128]{1,0:T(8,128)S(1)}, f32[864,128]{1,0:T(8,128)S(1)}, u32[]{:S(2)}, u32[]{:S(2)}) collective-permute-start(f32[864,128]{1,0:T(8,128)S(1)} %copy-done.11), channel_id=1, source_target_pairs={{1,2},{2,1},{5,6},{6,5},{9,10},{10,9},{13,14},{14,13},{17,18},{18,... | collective-permute-start | bytes 1327112 | tf_op jit(solution)/shard_map/ppermute | solution.py:716
  94.2 10.5 %collective-permute-start.5 = (f32[864,128]{1,0:T(8,128)S(1)}, f32[864,128]{1,0:T(8,128)S(1)}, u32[]{:S(2)}, u32[]{:S(2)}) collective-permute-start(f32[864,128]{1,0:T(8,128)S(1)} %copy-done.10), channel_id=1, source_target_pairs={{0,1},{1,0},{2,3},{3,2},{4,5},{5,4},{6,7},{7,6},{8,9},{9,8},{10,11... | collective-permute-start | bytes 1327112 | tf_op jit(solution)/shard_map/ppermute | solution.py:717
  117.2 29.6 %copy-start.2 = (f32[8,216,128]{2,1,0:T(8,128)}, f32[8,216,128]{2,1,0:T(8,128)S(1)}, u32[]{:S(2)}) copy-start(f32[8,216,128]{2,1,0:T(8,128)S(1)} %all-to-all-done.3) | copy-start | bytes 2654212
  117.2 29.6 %all-to-all-start.4 = ((f32[8,216,128]{2,1,0:T(8,128)}), f32[8,216,128]{2,1,0:T(8,128)S(1)}, u32[]{:S(2)}, u32[]{:S(2)}) async-start(f32[8,216,128]{2,1,0:T(8,128)} %bitcast.15), calls=%async_computation.4 | async-start | bytes 1769472 | tf_op jit(solution)/shard_map/all_to_all | solution.py:713
  123.2 3.3 %collective-permute-start.8 = (f32[8,128]{1,0:T(8,128)S(1)}, f32[8,128]{1,0:T(8,128)S(1)}, u32[]{:S(2)}, u32[]{:S(2)}) collective-permute-start(f32[8,128]{1,0:T(8,128)S(1)} %copy-done.7), channel_id=1, source_target_pairs={{0,1},{1,0},{2,3},{3,2},{4,5},{5,4},{6,7},{7,6},{8,9},{9,8},{10,11... | collective-permute-start | bytes 12296 | tf_op jit(solution)/shard_map/ppermute | solution.py:696
  126.6 3.6 %collective-permute-start.9 = (f32[8,128]{1,0:T(8,128)S(1)}, f32[8,128]{1,0:T(8,128)S(1)}, u32[]{:S(2)}, u32[]{:S(2)}) collective-permute-start(f32[8,128]{1,0:T(8,128)S(1)} %add.43), channel_id=1, source_target_pairs={{0,2},{1,3},{2,0},{3,1},{4,6},{5,7},{6,4},{7,5},{8,10},{9,11},{10,... | collective-permute-start | bytes 12296 | tf_op jit(solution)/shard_map/ppermute | solution.py:696
  130.2 3.6 %collective-permute-start.10 = (f32[8,128]{1,0:T(8,128)S(1)}, f32[8,128]{1,0:T(8,128)S(1)}, u32[]{:S(2)}, u32[]{:S(2)}) collective-permute-start(f32[8,128]{1,0:T(8,128)S(1)} %add.44), channel_id=1, source_target_pairs={{0,4},{4,0},{8,12},{12,8},{16,20},{20,16},{24,28},{28,24},{1,5},{5... | collective-permute-start | bytes 12296 | tf_op jit(solution)/shard_map/ppermute | solution.py:696
  133.9 8.3 %collective-permute-start.13 = (f32[8,128]{1,0:T(8,128)S(1)}, f32[8,128]{1,0:T(8,128)S(1)}, u32[]{:S(2)}, u32[]{:S(2)}) collective-permute-start(f32[8,128]{1,0:T(8,128)S(1)} %add.45), channel_id=1, source_target_pairs={{0,24},{4,28},{8,16},{12,20},{16,8},{20,12},{24,0},{28,4},{1,25},{... | collective-permute-start | bytes 12296 | tf_op jit(solution)/shard_map/ppermute | solution.py:698
  137.7 8.5 %collective-permute-start.12 = (f32[8,128]{1,0:T(8,128)S(1)}, f32[8,128]{1,0:T(8,128)S(1)}, u32[]{:S(2)}, u32[]{:S(2)}) collective-permute-start(f32[8,128]{1,0:T(8,128)S(1)} %add.45), channel_id=1, source_target_pairs={{0,16},{4,20},{8,24},{12,28},{16,0},{20,4},{24,8},{28,12},{1,17},{... | collective-permute-start | bytes 12296 | tf_op jit(solution)/shard_map/ppermute | solution.py:698
  137.7 8.5 %collective-permute-start.11 = (f32[8,128]{1,0:T(8,128)S(1)}, f32[8,128]{1,0:T(8,128)S(1)}, u32[]{:S(2)}, u32[]{:S(2)}) collective-permute-start(f32[8,128]{1,0:T(8,128)S(1)} %add.45), channel_id=1, source_target_pairs={{0,8},{4,12},{8,0},{12,4},{16,24},{20,28},{24,16},{28,20},{1,9},{5... | collective-permute-start | bytes 12296 | tf_op jit(solution)/shard_map/ppermute | solution.py:698
  (13 other events, 28.7 us)
